TPU v7x, 32 devices: a whole 2x2x4 slice. The times are simulated.
32 devices in a mesh: tm: 8 (over z, x), space: 4 (over y, core).
Axes of the slice: x: 2, y: 2, z: 4, core: 2. Of those that a mesh axis runs over, the one named last changes fastest.
Arguments:
- ensembles: bfloat16 [128, 80, 8192], P('tm', None, 'space'), may hold values from -6 to 6
- cotangents: bfloat16 [128, 80, 8192], P('tm', None, 'space'), may hold values from -6 to 6
- transforms: float32 [128, 80, 80], P('tm'), may hold values from -1.5 to 1.5
Outputs:
- smoothed: bfloat16 [128, 80, 8192], P('tm', None, 'space')
- ensemble_grad: bfloat16 [128, 80, 8192], P('tm', None, 'space')
- transform_grad: float32 [128, 80, 80], P('tm')
All inputs are finite; a program needn't handle non-finite values.
Results may differ from a plain program's by a relative error of at most 0.0049.
Values sent between devices are 32-bit elements; how exact they have to be, the bound alone decides.
No kernel may reach another device: no remote copies, remote signals or barrier semaphores. Data moves between devices by JAX's collectives and lax.ppermute only.
A program may use at most 64 MiB of HBM per device.

v0:
```python
import functools
import math

import jax
import jax.numpy as jnp
from jax import lax
from jax.experimental import pallas as pl
from jax.experimental.pallas import tpu as pltpu
from jax.sharding import PartitionSpec as P

F32 = jnp.float32
BF16 = jnp.bfloat16
VMEM = pl.BlockSpec(memory_space=pltpu.VMEM)
HBM = pl.BlockSpec(memory_space=pltpu.HBM)
DEPTH = 256
PIECES = 3
NORMAL = (((1,), (0,)), ((), ()))
ROWS = (((1,), (1,)), ((), ()))


def split(value):
    high = value.astype(BF16)
    return high, (value - high.astype(F32)).astype(BF16)


def mul(left, right, dims=NORMAL):
    return lax.dot_general(left, right, dims, preferred_element_type=F32)


def mul_pairs(left, right, dims=NORMAL):
    return mul(left[0], right[0], dims) + (
        mul(left[0], right[1], dims) + mul(left[1], right[0], dims)
    )


def mul_exact(left, right, dims=NORMAL):
    return mul_pairs(split(left), split(right), dims)


def product_of(factors):
    while len(factors) > 1:
        joined = [mul_exact(*factors[at : at + 2]) for at in range(0, len(factors) - 1, 2)]
        factors = joined + factors[len(joined) * 2 :]
    return factors[0]


def suffix_scan(ref, count, members, stop):
    width = 1
    while width < stop:
        for start in range(0, count, 2 * width):
            middle = start + width
            if middle < count:
                rows = slice(start * members, middle * members)
                ref[rows] = mul_exact(ref[rows], ref[middle * members : (middle + 1) * members])
        width *= 2


def scan_steps(count):
    steps = []
    width = 1
    while width < count:
        for middle in range(width, count, 2 * width):
            for at in range(middle, min(middle + width, count)):
                steps.append((middle - 1, at))
        width *= 2
    return steps


class Plan:
    def __init__(self, count, members):
        self.count, self.members, self.half = count, members, count // 2
        self.stack = DEPTH // members
        self.groups = [
            (start, min(start + self.stack, base + self.half))
            for base in (0, self.half)
            for start in range(base, base + self.half, self.stack)
        ]
        bounds = [len(self.groups) * at // PIECES for at in range(PIECES + 1)]
        self.piece_groups = [self.groups[a:b] for a, b in zip(bounds, bounds[1:])]
        self.pieces = [(part[0][0], part[-1][1]) for part in self.piece_groups]
        self.first_group = bounds[:-1]
        self.width = -(-self.slot(self.half + 1).stop // 128) * 128

    def slot(self, at):
        start = at // self.stack * DEPTH + at % self.stack * self.members
        return slice(start, start + self.members)

    def rows(self, first, last):
        return slice(first * self.members, last * self.members)


def on_blocks(members, size):
    rows = lax.broadcasted_iota(jnp.int32, (size, size), 0) // members
    columns = lax.broadcasted_iota(jnp.int32, (size, size), 1) // members
    return rows == columns


def loads(values, buffer, sems, first, last):
    copies = [
        pltpu.make_async_copy(values.at[at], buffer.at[at - first], sems.at[at - first])
        for at in range(first, last)
    ]
    for copy in copies:
        copy.start()
    return copies


def chain_kernel(plan, transforms, ensembles, cotangents, kept, halves, total, ens, cot, sems, ens_sem, cot_sem):
    count, members = plan.count, plan.members
    reads = loads(transforms, kept, sems, 0, count)
    more = loads(ensembles, ens, ens_sem, *plan.pieces[0])
    more += loads(cotangents, cot, cot_sem, *plan.pieces[0])
    for at, copy in enumerate(reads):
        copy.wait()
        halves[plan.rows(at, at + 1)] = kept[at]
    suffix_scan(halves, count, members, plan.half)
    total[...] = mul_exact(halves[plan.rows(0, 1)], halves[plan.rows(plan.half, plan.half + 1)])
    for copy in more:
        copy.wait()


def gram_kernel(plan, piece, *refs):
    members, half = plan.members, plan.half
    ens, cot, halves = refs[:3]
    refs = refs[3:]
    last = piece == PIECES - 1
    copies = []
    if last:
        earlier, refs = refs[: 2 * piece], refs[2 * piece :]
        sent, kept = refs
    else:
        ensembles, cotangents, grams, offsets, next_ens, next_cot, ens_sem, cot_sem = refs
        copies = loads(ensembles, next_ens, ens_sem, *plan.pieces[piece + 1])
        copies += loads(cotangents, next_cot, cot_sem, *plan.pieces[piece + 1])
    base = plan.pieces[piece][0]
    sums = [jnp.zeros((members, members), F32)] * 2
    packed = []
    for start, stop in plan.piece_groups[piece]:
        size = (stop - start) * members
        stacked = [ref[start - base : stop - base].reshape(size, ref.shape[2]) for ref in (cot, ens)]
        wide = jnp.where(on_blocks(members, size), mul(*stacked, ROWS), 0.0)
        gram = wide[:members]
        for at in range(1, stop - start):
            gram = gram + wide[at * members : (at + 1) * members]
        side = start // half
        sums[side] = sums[side] + mul_exact(gram, halves[plan.rows(start, stop)])
        packed.append(jnp.pad(gram, ((0, 0), (0, DEPTH - size))))
    if not last:
        for at, gram in enumerate(packed):
            grams[at] = gram
        for side in range(2):
            offsets[side] = sums[side]
    else:
        groups = []
        for at in range(piece):
            groups += [earlier[2 * at][i] for i in range(len(plan.piece_groups[at]))]
            sums = [sums[side] + earlier[2 * at + 1][side] for side in range(2)]
        groups += packed
        whole = sums[1] + mul_exact(sums[0], halves[plan.rows(half, half + 1)])
        core = lax.rem(lax.axis_index("space"), 2)
        side_groups = len(groups) // 2
        for ref, side in ((kept, core), (sent, 1 - core)):
            for at in range(side_groups):
                lanes = slice(at * DEPTH, min((at + 1) * DEPTH, plan.width))
                chosen = jnp.where(side == 0, groups[at], groups[side_groups + at])
                ref[:, lanes] = chosen[:, : lanes.stop - lanes.start]
            if plan.width > side_groups * DEPTH:
                ref[:, side_groups * DEPTH :] = jnp.zeros(
                    (members, plan.width - side_groups * DEPTH), F32
                )
            ref[:, plan.slot(half)] = whole
            ref[:, plan.slot(half + 1)] = sums[0]
    for copy in copies:
        copy.wait()


def upper_half(level):
    return lax.rem(lax.axis_index("tm") // (1 << level), 2) == 1


def join_kernel(level, total, other, later, before, new_total, new_later, new_before, upper_total):
    upper = upper_half(level)
    left = jnp.where(upper, other[...], total[...])
    right = jnp.where(upper, total[...], other[...])
    new_total[...] = mul_exact(left, right)
    upper_total[...] = right
    new_later[...] = jnp.where(upper, later[...], mul_exact(later[...], other[...]))
    new_before[...] = jnp.where(upper, mul_exact(other[...], before[...]), before[...])


def pass_kernel(level, own, other, carry, upper_total, before, new_own, new_carry):
    upper = upper_half(level)
    left = jnp.where(upper, other[...], own[...])
    right = jnp.where(upper, own[...], other[...])
    new_own[...] = mul_exact(left, upper_total[...]) + right
    new_carry[...] = carry[...] + jnp.where(upper, mul_exact(left, before[...]), 0.0)


def carry_kernel(plan, level, transforms, halves, later, other, ens_factors, cot_factors, follow, steps):
    count, members, half = plan.count, plan.members, plan.half
    core = lax.rem(lax.axis_index("space"), 2)
    entering = later[...]
    entering = jnp.where(upper_half(level), entering, mul_exact(entering, other[...]))
    middle = mul_exact(halves[plan.rows(half, half + 1)], entering)
    mask = on_blocks(members, plan.stack * members)
    follows = [[], []]
    for side, end in ((0, middle), (1, entering)):
        rows = plan.rows(side * half, (side + 1) * half)
        wide = mul_exact(halves[rows], jnp.concatenate([end] * plan.stack, axis=1))
        follows[side] = jnp.concatenate([wide[members:, :members], end], axis=0)
        for at, (start, stop) in enumerate(plan.groups):
            if start // half == side:
                size = (stop - start) * members
                offset = (start - side * half) * members
                part = jnp.where(mask[:size, :size], wide[offset : offset + size, :size], 0.0)
                cot_factors[at, :size, :size] = part.astype(BF16)
                ens_factors[at, :size, :size] = part.T.astype(BF16)
    for at, part in enumerate(split(jnp.where(core == 0, follows[0], follows[1]))):
        follow[at] = part
    for at, (first, last) in enumerate(scan_steps(half)):
        factors = [transforms[core * half + i] for i in range(first, last)]
        for side, part in enumerate(split(product_of(factors).T)):
            steps[side, plan.rows(at, at + 1)] = part


def apply_kernel(plan, piece, factors, values, *refs):
    out, out_buf, out_sem = refs[-3:]
    members = plan.members
    base = plan.pieces[piece][0]
    writes = []
    for at, (start, stop) in enumerate(plan.piece_groups[piece]):
        size = (stop - start) * members
        part = slice(start - base, stop - base)
        stacked = values[part].reshape(size, values.shape[2])
        result = mul(factors[plan.first_group[piece] + at, :size, :size], stacked)
        out_buf[part] = result.astype(BF16).reshape(stop - start, members, values.shape[2])
        copy = pltpu.make_async_copy(out_buf.at[part], out.at[start:stop], out_sem.at[at])
        copy.start()
        writes.append(copy)
    for copy in writes:
        copy.wait()


def final_kernel(plan, level, scale, message, own, other, carry, before, halves, follow, steps, out):
    members, half = plan.members, plan.half
    core = lax.rem(lax.axis_index("space"), 2)
    entering = carry[...] + jnp.where(
        upper_half(level), mul_exact(other[...], before[...]), 0.0
    )
    middle = mul_exact(entering, halves[plan.rows(0, 1)]) + message[:, plan.slot(half + 1)]
    entering = jnp.where(core == 0, entering, middle)
    totals = []
    for start in range(0, half, plan.stack):
        at = start // plan.stack
        tall = message[:, at * DEPTH : (at + 1) * DEPTH].T
        for i in range(min(plan.stack, half - start)):
            totals.append(tall[i * members : (i + 1) * members])
    totals[0] = totals[0] + entering.T
    number = 0
    width = 1
    while width < half:
        for start in range(width, half, 2 * width):
            size = min(width, half - start)
            rows = plan.rows(number, number + size)
            added = mul_pairs((steps[0, rows], steps[1, rows]), split(totals[start - 1]))
            for at in range(size):
                totals[start + at] = totals[start + at] + added[at * members : (at + 1) * members]
            number += size
        width *= 2
    for at in range(half):
        rows = plan.rows(at, at + 1)
        out[at] = mul_pairs(split(totals[at]), (follow[0, rows], follow[1, rows]), ROWS) * scale


def place_kernel(half, mine, other, out, sems):
    core = lax.rem(lax.axis_index("space"), 2)
    copies = [
        pltpu.make_async_copy(mine, out.at[pl.ds(core * half, half)], sems.at[0]),
        pltpu.make_async_copy(other, out.at[pl.ds((1 - core) * half, half)], sems.at[1]),
    ]
    for copy in copies:
        copy.start()
    for copy in copies:
        copy.wait()


def call(kernel, outs, ins, out_specs, scratch, micros, name, limit=16, aliases=None):
    return pl.pallas_call(
        kernel,
        out_shape=outs,
        in_specs=ins,
        out_specs=out_specs,
        scratch_shapes=scratch,
        input_output_aliases=aliases or {},
        compiler_params=pltpu.CompilerParams(vmem_limit_bytes=limit << 20),
        cost_estimate=pl.CostEstimate(
            flops=0, bytes_accessed=int(micros * 3.6e6), transcendentals=0
        ),
        name=name,
    )


def shape(*dims, kind=F32):
    return jax.ShapeDtypeStruct(dims, kind)


def shards(ensembles, cotangents, transforms):
    count, members, cells = ensembles.shape
    blocks, lanes = lax.axis_size("tm"), lax.axis_size("space")
    chips, half = lanes // 2, count // 2
    scale = 1.0 / math.sqrt(cells * lanes * count * blocks)
    plan = Plan(count, members)
    levels = blocks.bit_length() - 1
    square = shape(members, members)

    def exchange(value, axis, size, bit):
        return lax.ppermute(value, axis, [(at, at ^ bit) for at in range(size)])

    def loaded(piece):
        first, last = plan.pieces[piece]
        return [shape(last - first, members, cells, kind=BF16)] * 2

    def sems(piece):
        first, last = plan.pieces[piece]
        return [pltpu.SemaphoreType.DMA((last - first,))] * 2

    kept, halves, total, *first_part = call(
        functools.partial(chain_kernel, plan),
        [shape(count, members, members), shape(count * members, members), square] + loaded(0),
        [HBM] * 3, [VMEM] * 5,
        [pltpu.SemaphoreType.DMA((count,))] + sems(0), 2, "transform_chain",
    )(transforms, ensembles, cotangents)

    later = before = jnp.eye(members, dtype=F32)
    parts, grams, uppers, befores = [first_part], [], [], []
    for level in range(levels):
        other = exchange(total, "tm", blocks, 1 << level)
        if level < PIECES - 1:
            *sums, ens, cot = call(
                functools.partial(gram_kernel, plan, level),
                [shape(len(plan.piece_groups[level]), members, DEPTH), shape(2, members, members)]
                + loaded(level + 1),
                [VMEM] * 3 + [HBM] * 2, [VMEM] * 4, sems(level + 1), 1.5, f"gram_{level}",
            )(*parts[-1], halves, ensembles, cotangents)
            parts.append((ens, cot))
            grams += sums
        befores.append(before)
        if level < levels - 1:
            total, later, before, upper = call(
                functools.partial(join_kernel, level),
                [square] * 4, [VMEM] * 4, [VMEM] * 4, [], 0.4, f"join_{level}",
            )(total, other, later, before)
            uppers.append(upper)
    sent, mine = call(
        functools.partial(gram_kernel, plan, PIECES - 1),
        [shape(members, plan.width)] * 2,
        [VMEM] * (3 + len(grams)), [VMEM] * 2, [], 1.5, "gram_last",
    )(*parts[-1], halves, *grams)
    message = mine + exchange(sent, "space", lanes, 1)

    size = plan.stack * members
    steps = len(scan_steps(half))
    ens_factors, cot_factors, follow, steps = call(
        functools.partial(carry_kernel, plan, levels - 1),
        [shape(len(plan.groups), size, size, kind=BF16)] * 2
        + [shape(2, half * members, members, kind=BF16), shape(2, steps * members, members, kind=BF16)],
        [VMEM] * 4, [VMEM] * 4, [], 1.5, "carries",
    )(kept, halves, later, other)

    whole = message
    for d in range(1, chips):
        whole = whole + lax.ppermute(
            message, "space", [(at, (at + 2 * d) % lanes) for at in range(lanes)]
        )
    own = whole[:, plan.slot(half)]

    def apply(factors, which, name):
        out = []
        for piece in range(PIECES):
            first, last = plan.pieces[piece]
            out = [call(
                functools.partial(apply_kernel, plan, piece),
                shape(count, members, cells, kind=BF16),
                [VMEM] * 2 + [HBM] * len(out), HBM,
                [pltpu.VMEM((last - first, members, cells), BF16),
                 pltpu.SemaphoreType.DMA((len(plan.piece_groups[piece]),))],
                1.2, f"{name}_{piece}", aliases={2: 0} if out else None,
            )(factors, parts[piece][which], *out)]
        return out[0]

    smoothed = apply(ens_factors, 0, "smoothed")
    ensemble_grad = apply(cot_factors, 1, "ensemble_grad")

    carry = jnp.zeros((members, members), F32)
    for level in range(levels):
        other = exchange(own, "tm", blocks, 1 << level)
        if level < levels - 1:
            own, carry = call(
                functools.partial(pass_kernel, level),
                [square] * 2, [VMEM] * 5, [VMEM] * 2, [], 0.4, f"pass_{level}",
            )(own, other, carry, uppers[level], befores[level])
    mine = call(
        functools.partial(final_kernel, plan, levels - 1, scale),
        shape(half, members, members),
        [VMEM] * 8, VMEM, [], 1.5, "transform_grad",
    )(whole, own, other, carry, befores[-1], halves, follow, steps)
    transform_grad = call(
        functools.partial(place_kernel, half),
        shape(count, members, members),
        [VMEM] * 2, HBM, [pltpu.SemaphoreType.DMA((2,))], 0.5, "place",
    )(mine, exchange(mine, "space", lanes, 1))
    return (smoothed, ensemble_grad, transform_grad)


def solution(mesh):
    return jax.shard_map(
        shards,
        mesh=mesh,
        in_specs=(P("tm", None, "space"), P("tm", None, "space"), P("tm", None, None)),
        out_specs=(P("tm", None, "space"), P("tm", None, "space"), P("tm", None, None)),
        check_vma=False,
    )
```

profile of v0, /device:TPU:0, one launch (start us, length us, event | category | flops | bytes accessed | tf_op | source)
XLA Modules:
  0.0 55.6 jit_solution(13629747149575505741)
XLA Ops:
  0.6 0.0 copy-start
  0.6 2.5 %copy-done = bf16[16,80,2048]{2,1,0:T(8,128)(2,1)S(1)} copy-done((bf16[16,80,2048]{2,1,0:T(8,128)(2,1)S(1)}, bf16[16,80,2048]{2,1,0:T(8,128)(2,1)}, u32[]{:S(2)}) %copy-start) | copy-done | bytes 5242904
  3.1 0.0 copy-start.2
  3.1 2.5 %copy-done.2 = bf16[16,80,2048]{2,1,0:T(8,128)(2,1)S(1)} copy-done((bf16[16,80,2048]{2,1,0:T(8,128)(2,1)S(1)}, bf16[16,80,2048]{2,1,0:T(8,128)(2,1)}, u32[]{:S(2)}) %copy-start.2) | copy-done | bytes 5242904
  5.6 0.0 copy-start.4
  5.6 1.1 %copy-done.4 = f32[16,80,80]{2,1,0:T(8,128)S(1)} copy-done((f32[16,80,80]{2,1,0:T(8,128)S(1)}, f32[16,80,80]{2,1,0:T(8,128)}, u32[]{:S(2)}) %copy-start.4) | copy-done | bytes 409624
  6.7 0.0 copy-start.1
  6.7 0.0 copy-start.3
  6.7 3.4 %transform_chain.1 = (f32[16,80,80]{2,1,0:T(8,128)S(1)}, f32[1280,80]{1,0:T(8,128)S(1)}, f32[80,80]{1,0:T(8,128)S(1)}, bf16[6,80,2048]{2,1,0:T(8,128)(2,1)S(1)}, bf16[6,80,2048]{2,1,0:T(8,128)(2,1)S(1)}) custom-call(f32[16,80,80]{2,1,0:T(8,128)S(1)} %copy-done.4, bf16[16,80,2048]{2,1,0:T(8,128)(2,1)S(1)} %copy-done, bf16[16,80,2048]{2,1,0:T(8,128)(2,1)S(1)} %copy-done.2), custom_call_target="tpu_custom_call" | custom-call | bytes 7200000 | tf_op jit(solution)/shard_map/transform_chain/pallas_call | solution.py:327
  10.1 0.0 copy-done.1
  10.1 0.6 %copy-done.3 = bf16[16,80,2048]{2,1,0:T(8,128)(2,1)S(1)} copy-done((bf16[16,80,2048]{2,1,0:T(8,128)(2,1)S(1)}, bf16[16,80,2048]{2,1,0:T(8,128)(2,1)}, u32[]{:S(2)}) %copy-start.3) | copy-done | bytes 5242904
  10.8 2.7 %gram_0.1 = (f32[2,80,256]{2,1,0:T(8,128)S(1)}, f32[2,80,80]{2,1,0:T(8,128)S(1)}, bf16[5,80,2048]{2,1,0:T(8,128)(2,1)S(1)}, bf16[5,80,2048]{2,1,0:T(8,128)(2,1)S(1)}) custom-call(bf16[6,80,2048]{2,1,0:T(8,128)(2,1)S(1)} %get-tuple-element.43.refs_0_.values, bf16[6,80,2048]{2,1,0:T(8,128)(2,1)S(1)} %get-tuple-element.44.refs_1_.values, ...), custom_call_target="tpu_custom_call" | custom-call | bytes 5400000 | tf_op jit(solution)/shard_map/gram_0/pallas_call | solution.py:339
  13.4 2.5 %gram_1.1 = (f32[2,80,256]{2,1,0:T(8,128)S(1)}, f32[2,80,80]{2,1,0:T(8,128)S(1)}, bf16[5,80,2048]{2,1,0:T(8,128)(2,1)S(1)}, bf16[5,80,2048]{2,1,0:T(8,128)(2,1)S(1)}) custom-call(bf16[5,80,2048]{2,1,0:T(8,128)(2,1)S(1)} %get-tuple-element.45.refs_0_.values, bf16[5,80,2048]{2,1,0:T(8,128)(2,1)S(1)} %get-tuple-element.46.refs_1_.values, ...), custom_call_target="tpu_custom_call" | custom-call | bytes 5400000 | tf_op jit(solution)/shard_map/gram_1/pallas_call | solution.py:339
  15.9 1.5 %gram_last.1 = (f32[80,896]{1,0:T(8,128)S(1)}, f32[80,896]{1,0:T(8,128)S(1)}) custom-call(bf16[5,80,2048]{2,1,0:T(8,128)(2,1)S(1)} %get-tuple-element.47.values.refs_0_, bf16[5,80,2048]{2,1,0:T(8,128)(2,1)S(1)} %get-tuple-element.49.values.refs_1_, f32[1280,80]{1,0:T(8,128)S(1)} %get-tuple-element.35.halves.refs_2_, ...), custom_call_target="tpu_custom_call" | custom-call | bytes 5400000 | tf_op jit(solution)/shard_map/gram_last/pallas_call | solution.py:354
  17.4 0.5 collective-permute-start.3
  17.9 1.2 %collective-permute-done.3 = f32[80,896]{1,0:T(8,128)S(1)} collective-permute-done((f32[80,896]{1,0:T(8,128)S(1)}, f32[80,896]{1,0:T(8,128)S(1)}, u32[]{:S(2)}, u32[]{:S(2)}) %collective-permute-start.3) | collective-permute-done | bytes 286752 | tf_op jit(solution)/shard_map/ppermute | solution.py:317
  19.2 3.0 %collective-permute-start.4 = (f32[80,896]{1,0:T(8,128)S(1)}, f32[80,896]{1,0:T(8,128)S(1)}, u32[]{:S(2)}, u32[]{:S(2)}) collective-permute-start(f32[80,896]{1,0:T(8,128)S(1)} %add.6), channel_id=1, source_target_pairs={{0,2},{1,3},{2,0},{3,1},{4,6},{5,7},{6,4},{7,5},{8,10},{9,11},{10,... | collective-permute-start | bytes 860168 | tf_op jit(solution)/shard_map/ppermute | solution.py:372
  22.1 1.5 %collective-permute-start = (f32[80,80]{1,0:T(8,128)S(1)}, f32[80,80]{1,0:T(8,128)S(1)}, u32[]{:S(2)}, u32[]{:S(2)}) collective-permute-start(f32[80,80]{1,0:T(8,128)S(1)} %get-tuple-element.36.total), channel_id=1, source_target_pairs={{0,4},{4,0},{8,12},{12,8},{16,20},{20,16},{24,28},{28,24},{1,5},{5... | collective-permute-start | bytes 76808 | tf_op jit(solution)/shard_map/ppermute | solution.py:317
  23.6 5.6 %collective-permute-done.4 = f32[80,896]{1,0:T(8,128)S(1)} collective-permute-done((f32[80,896]{1,0:T(8,128)S(1)}, f32[80,896]{1,0:T(8,128)S(1)}, u32[]{:S(2)}, u32[]{:S(2)}) %collective-permute-start.4) | collective-permute-done | bytes 286752 | tf_op jit(solution)/shard_map/ppermute | solution.py:372
  29.3 0.1 slice.4.own
  29.4 1.7 %collective-permute-start.5 = (f32[80,80]{1,0:T(8,128)S(1)}, f32[80,80]{1,0:T(8,128)S(1)}, u32[]{:S(2)}, u32[]{:S(2)}) collective-permute-start(f32[80,80]{1,0:T(8,128)S(1)} %slice.4.own), channel_id=1, source_target_pairs={{0,4},{4,0},{8,12},{12,8},{16,20},{20,16},{24,28},{28,24},{1,5},{5... | collective-permute-start | bytes 76808 | tf_op jit(solution)/shard_map/ppermute | solution.py:317
  31.1 0.0 collective-permute-done.other
  31.1 0.3 join_0.1
  31.4 1.6 %collective-permute-start.1 = (f32[80,80]{1,0:T(8,128)S(1)}, f32[80,80]{1,0:T(8,128)S(1)}, u32[]{:S(2)}, u32[]{:S(2)}) collective-permute-start(f32[80,80]{1,0:T(8,128)S(1)} %get-tuple-element.37.total), channel_id=1, source_target_pairs={{0,8},{4,12},{8,0},{12,4},{16,24},{20,28},{24,16},{28,20},{1,9},{5... | collective-permute-start | bytes 76808 | tf_op jit(solution)/shard_map/ppermute | solution.py:317
  33.0 0.4 collective-permute-done.5.other
  33.4 0.2 pass_0.1
  33.6 1.9 %collective-permute-start.6 = (f32[80,80]{1,0:T(8,128)S(1)}, f32[80,80]{1,0:T(8,128)S(1)}, u32[]{:S(2)}, u32[]{:S(2)}) collective-permute-start(f32[80,80]{1,0:T(8,128)S(1)} %get-tuple-element.57.own), channel_id=1, source_target_pairs={{0,8},{4,12},{8,0},{12,4},{16,24},{20,28},{24,16},{28,20},{1,9},{5... | collective-permute-start | bytes 76808 | tf_op jit(solution)/shard_map/ppermute | solution.py:317
  35.5 0.2 collective-permute-done.1.other
  35.6 0.3 join_1.1
  35.9 2.6 %collective-permute-start.2 = (f32[80,80]{1,0:T(8,128)S(1)}, f32[80,80]{1,0:T(8,128)S(1)}, u32[]{:S(2)}, u32[]{:S(2)}) collective-permute-start(f32[80,80]{1,0:T(8,128)S(1)} %get-tuple-element.41), channel_id=1, source_target_pairs={{0,16},{4,20},{8,24},{12,28},{16,0},{20,4},{24,8},{28,12},{1,17},{... | collective-permute-start | bytes 76808 | tf_op jit(solution)/shard_map/ppermute | solution.py:317
  38.4 0.0 collective-permute-done.6.other
  38.4 0.2 pass_1.1
  38.7 2.1 %collective-permute-start.7 = (f32[80,80]{1,0:T(8,128)S(1)}, f32[80,80]{1,0:T(8,128)S(1)}, u32[]{:S(2)}, u32[]{:S(2)}) collective-permute-start(f32[80,80]{1,0:T(8,128)S(1)} %get-tuple-element.60.own), channel_id=1, source_target_pairs={{0,16},{4,20},{8,24},{12,28},{16,0},{20,4},{24,8},{28,12},{1,17},{... | collective-permute-start | bytes 76808 | tf_op jit(solution)/shard_map/ppermute | solution.py:317
  40.8 0.1 collective-permute-done.2.other
  40.9 1.6 %carries.1 = (bf16[6,240,240]{2,1,0:T(8,128)(2,1)S(1)}, bf16[6,240,240]{2,1,0:T(8,128)(2,1)S(1)}, bf16[2,640,80]{2,1,0:T(8,128)(2,1)S(1)}, bf16[2,960,80]{2,1,0:T(8,128)(2,1)S(1)}) custom-call(f32[16,80,80]{2,1,0:T(8,128)S(1)} %get-tuple-element.34.transforms, f32[1280,80]{1,0:T(8,128)S(1)} %get-tuple-element.35.halves.refs_2_, ...), custom_call_target="tpu_custom_call" | custom-call | bytes 5400000 | tf_op jit(solution)/shard_map/carries/pallas_call | solution.py:363
  42.5 1.1 %collective-permute-done.7.other = f32[80,80]{1,0:T(8,128)S(1)} collective-permute-done((f32[80,80]{1,0:T(8,128)S(1)}, f32[80,80]{1,0:T(8,128)S(1)}, u32[]{:S(2)}, u32[]{:S(2)}) %collective-permute-start.7) | collective-permute-done | bytes 25632 | tf_op jit(solution)/shard_map/ppermute | solution.py:317
  43.6 1.3 %transform_grad.1.mine = f32[8,80,80]{2,1,0:T(8,128)S(1)} custom-call(f32[80,896]{1,0:T(8,128)S(1)} %add.7.message, f32[80,80]{1,0:T(8,128)S(1)} %get-tuple-element.60.own, f32[80,80]{1,0:T(8,128)S(1)} %collective-permute-done.7.other, f32[80,80]{1,0:T(8,128)S(1)} %get-tuple-element.61.carry, f32[80,80]{1,0:T(8,128)S(1)} %get-tuple-element.62.before, ...), custom_call_target="tpu_custom_call" | custom-call | bytes 5400000 | tf_op jit(solution)/shard_map/transform_grad/pallas_call | solution.py:402
  44.9 0.1 collective-permute-start.8
  45.0 1.7 %ensemble_grad_0.1.refs_0_ = bf16[16,80,2048]{2,1,0:T(8,128)(2,1)} custom-call(bf16[6,240,240]{2,1,0:T(8,128)(2,1)S(1)} %get-tuple-element.48.factors, bf16[6,80,2048]{2,1,0:T(8,128)(2,1)S(1)} %get-tuple-element.44.refs_1_.values), custom_call_target="tpu_custom_call" | custom-call | bytes 4320000 | tf_op jit(solution)/shard_map/ensemble_grad_0/pallas_call | solution.py:381
  46.7 1.5 %ensemble_grad_1.1.refs_0_ = bf16[16,80,2048]{2,1,0:T(8,128)(2,1)} custom-call(bf16[6,240,240]{2,1,0:T(8,128)(2,1)S(1)} %get-tuple-element.48.factors, bf16[5,80,2048]{2,1,0:T(8,128)(2,1)S(1)} %get-tuple-element.46.refs_1_.values, bf16[16,80,2048]{2,1,0:T(8,128)(2,1)} %ensemble_grad_0.1.refs_0_), custom_call_target="tpu_custom_call", output_to_operand_aliasing={{}: (2, {})} | custom-call | bytes 4320000 | tf_op jit(solution)/shard_map/ensemble_grad_1/pallas_call | solution.py:381
  48.2 1.6 %ensemble_grad_2.1 = bf16[16,80,2048]{2,1,0:T(8,128)(2,1)} custom-call(bf16[6,240,240]{2,1,0:T(8,128)(2,1)S(1)} %get-tuple-element.48.factors, bf16[5,80,2048]{2,1,0:T(8,128)(2,1)S(1)} %get-tuple-element.49.values.refs_1_, bf16[16,80,2048]{2,1,0:T(8,128)(2,1)} %ensemble_grad_1.1.refs_0_), custom_call_target="tpu_custom_call", output_to_operand_aliasing={{}: (2, {})} | custom-call | bytes 4320000 | tf_op jit(solution)/shard_map/ensemble_grad_2/pallas_call | solution.py:381
  49.8 1.7 %smoothed_0.1.refs_0_ = bf16[16,80,2048]{2,1,0:T(8,128)(2,1)} custom-call(bf16[6,240,240]{2,1,0:T(8,128)(2,1)S(1)} %get-tuple-element.42.factors, bf16[6,80,2048]{2,1,0:T(8,128)(2,1)S(1)} %get-tuple-element.43.refs_0_.values), custom_call_target="tpu_custom_call" | custom-call | bytes 4320000 | tf_op jit(solution)/shard_map/smoothed_0/pallas_call | solution.py:381
  51.5 1.5 %smoothed_1.1.refs_0_ = bf16[16,80,2048]{2,1,0:T(8,128)(2,1)} custom-call(bf16[6,240,240]{2,1,0:T(8,128)(2,1)S(1)} %get-tuple-element.42.factors, bf16[5,80,2048]{2,1,0:T(8,128)(2,1)S(1)} %get-tuple-element.45.refs_0_.values, bf16[16,80,2048]{2,1,0:T(8,128)(2,1)} %smoothed_0.1.refs_0_), custom_call_target="tpu_custom_call", output_to_operand_aliasing={{}: (2, {})} | custom-call | bytes 4320000 | tf_op jit(solution)/shard_map/smoothed_1/pallas_call | solution.py:381
  53.1 1.6 %smoothed_2.1 = bf16[16,80,2048]{2,1,0:T(8,128)(2,1)} custom-call(bf16[6,240,240]{2,1,0:T(8,128)(2,1)S(1)} %get-tuple-element.42.factors, bf16[5,80,2048]{2,1,0:T(8,128)(2,1)S(1)} %get-tuple-element.47.values.refs_0_, bf16[16,80,2048]{2,1,0:T(8,128)(2,1)} %smoothed_1.1.refs_0_), custom_call_target="tpu_custom_call", output_to_operand_aliasing={{}: (2, {})} | custom-call | bytes 4320000 | tf_op jit(solution)/shard_map/smoothed_2/pallas_call | solution.py:381
  54.7 0.0 collective-permute-done.8.other
  54.7 0.9 %place.1 = f32[16,80,80]{2,1,0:T(8,128)} custom-call(f32[8,80,80]{2,1,0:T(8,128)S(1)} %transform_grad.1.mine, f32[8,80,80]{2,1,0:T(8,128)S(1)} %collective-permute-done.8.other), custom_call_target="tpu_custom_call" | custom-call | bytes 1800000 | tf_op jit(solution)/shard_map/place/pallas_call | solution.py:407
  (4 shorter events, 0.1 us)
Async XLA Ops:
  0.6 2.5 %copy-start = (bf16[16,80,2048]{2,1,0:T(8,128)(2,1)S(1)}, bf16[16,80,2048]{2,1,0:T(8,128)(2,1)}, u32[]{:S(2)}) copy-start(bf16[16,80,2048]{2,1,0:T(8,128)(2,1)} %refs_3_.3) | copy-start | bytes 15728644
  3.1 2.5 %copy-start.2 = (bf16[16,80,2048]{2,1,0:T(8,128)(2,1)S(1)}, bf16[16,80,2048]{2,1,0:T(8,128)(2,1)}, u32[]{:S(2)}) copy-start(bf16[16,80,2048]{2,1,0:T(8,128)(2,1)} %refs_4_.3) | copy-start | bytes 15728644
  5.6 1.1 %copy-start.4 = (f32[16,80,80]{2,1,0:T(8,128)S(1)}, f32[16,80,80]{2,1,0:T(8,128)}, u32[]{:S(2)}) copy-start(f32[16,80,80]{2,1,0:T(8,128)} %transforms.1) | copy-start | bytes 1228804
  6.7 3.4 %copy-start.1 = (bf16[16,80,2048]{2,1,0:T(8,128)(2,1)S(1)}, bf16[16,80,2048]{2,1,0:T(8,128)(2,1)}, u32[]{:S(2)}) copy-start(bf16[16,80,2048]{2,1,0:T(8,128)(2,1)} %refs_3_.3) | copy-start | bytes 15728644
  6.7 4.1 %copy-start.3 = (bf16[16,80,2048]{2,1,0:T(8,128)(2,1)S(1)}, bf16[16,80,2048]{2,1,0:T(8,128)(2,1)}, u32[]{:S(2)}) copy-start(bf16[16,80,2048]{2,1,0:T(8,128)(2,1)} %refs_4_.3) | copy-start | bytes 15728644
  17.4 1.7 %collective-permute-start.3 = (f32[80,896]{1,0:T(8,128)S(1)}, f32[80,896]{1,0:T(8,128)S(1)}, u32[]{:S(2)}, u32[]{:S(2)}) collective-permute-start(f32[80,896]{1,0:T(8,128)S(1)} %get-tuple-element.55), channel_id=1, source_target_pairs={{0,1},{1,0},{2,3},{3,2},{4,5},{5,4},{6,7},{7,6},{8,9},{9,8},{10,11... | collective-permute-start | bytes 860168 | tf_op jit(solution)/shard_map/ppermute | solution.py:317
  19.2 10.1 %collective-permute-start.4 = (f32[80,896]{1,0:T(8,128)S(1)}, f32[80,896]{1,0:T(8,128)S(1)}, u32[]{:S(2)}, u32[]{:S(2)}) collective-permute-start(f32[80,896]{1,0:T(8,128)S(1)} %add.6), channel_id=1, source_target_pairs={{0,2},{1,3},{2,0},{3,1},{4,6},{5,7},{6,4},{7,5},{8,10},{9,11},{10,... | collective-permute-start | bytes 860168 | tf_op jit(solution)/shard_map/ppermute | solution.py:372
  22.1 9.0 %collective-permute-start = (f32[80,80]{1,0:T(8,128)S(1)}, f32[80,80]{1,0:T(8,128)S(1)}, u32[]{:S(2)}, u32[]{:S(2)}) collective-permute-start(f32[80,80]{1,0:T(8,128)S(1)} %get-tuple-element.36.total), channel_id=1, source_target_pairs={{0,4},{4,0},{8,12},{12,8},{16,20},{20,16},{24,28},{28,24},{1,5},{5... | collective-permute-start | bytes 76808 | tf_op jit(solution)/shard_map/ppermute | solution.py:317
  29.4 4.0 %collective-permute-start.5 = (f32[80,80]{1,0:T(8,128)S(1)}, f32[80,80]{1,0:T(8,128)S(1)}, u32[]{:S(2)}, u32[]{:S(2)}) collective-permute-start(f32[80,80]{1,0:T(8,128)S(1)} %slice.4.own), channel_id=1, source_target_pairs={{0,4},{4,0},{8,12},{12,8},{16,20},{20,16},{24,28},{28,24},{1,5},{5... | collective-permute-start | bytes 76808 | tf_op jit(solution)/shard_map/ppermute | solution.py:317
  31.4 4.2 %collective-permute-start.1 = (f32[80,80]{1,0:T(8,128)S(1)}, f32[80,80]{1,0:T(8,128)S(1)}, u32[]{:S(2)}, u32[]{:S(2)}) collective-permute-start(f32[80,80]{1,0:T(8,128)S(1)} %get-tuple-element.37.total), channel_id=1, source_target_pairs={{0,8},{4,12},{8,0},{12,4},{16,24},{20,28},{24,16},{28,20},{1,9},{5... | collective-permute-start | bytes 76808 | tf_op jit(solution)/shard_map/ppermute | solution.py:317
  33.6 4.8 %collective-permute-start.6 = (f32[80,80]{1,0:T(8,128)S(1)}, f32[80,80]{1,0:T(8,128)S(1)}, u32[]{:S(2)}, u32[]{:S(2)}) collective-permute-start(f32[80,80]{1,0:T(8,128)S(1)} %get-tuple-element.57.own), channel_id=1, source_target_pairs={{0,8},{4,12},{8,0},{12,4},{16,24},{20,28},{24,16},{28,20},{1,9},{5... | collective-permute-start | bytes 76808 | tf_op jit(solution)/shard_map/ppermute | solution.py:317
  35.9 5.0 %collective-permute-start.2 = (f32[80,80]{1,0:T(8,128)S(1)}, f32[80,80]{1,0:T(8,128)S(1)}, u32[]{:S(2)}, u32[]{:S(2)}) collective-permute-start(f32[80,80]{1,0:T(8,128)S(1)} %get-tuple-element.41), channel_id=1, source_target_pairs={{0,16},{4,20},{8,24},{12,28},{16,0},{20,4},{24,8},{28,12},{1,17},{... | collective-permute-start | bytes 76808 | tf_op jit(solution)/shard_map/ppermute | solution.py:317
  38.7 5.0 %collective-permute-start.7 = (f32[80,80]{1,0:T(8,128)S(1)}, f32[80,80]{1,0:T(8,128)S(1)}, u32[]{:S(2)}, u32[]{:S(2)}) collective-permute-start(f32[80,80]{1,0:T(8,128)S(1)} %get-tuple-element.60.own), channel_id=1, source_target_pairs={{0,16},{4,20},{8,24},{12,28},{16,0},{20,4},{24,8},{28,12},{1,17},{... | collective-permute-start | bytes 76808 | tf_op jit(solution)/shard_map/ppermute | solution.py:317
  44.9 9.8 %collective-permute-start.8 = (f32[8,80,80]{2,1,0:T(8,128)S(1)}, f32[8,80,80]{2,1,0:T(8,128)S(1)}, u32[]{:S(2)}, u32[]{:S(2)}) collective-permute-start(f32[8,80,80]{2,1,0:T(8,128)S(1)} %transform_grad.1.mine), channel_id=1, source_target_pairs={{0,1},{1,0},{2,3},{3,2},{4,5},{5,4},{6,7},{7,6},{8,9},{9,8},{10,11... | collective-permute-start | bytes 614408 | tf_op jit(solution)/shard_map/ppermute | solution.py:317
where the time goes:
time: 55.9 us; the launch traced here: 55.6 us
  Pallas kernels  24.4 us (44%)
  starting transfers between devices  14.9 us (27%)
  waiting for transfers between devices  8.61 us (15%)
  local copies, waits for them, and re-layouts  6.77 us (12%)
  between operations  0.8 us (1%)
    ppermute x8, starting transfers between devices, exchange(): return lax.ppermute(value, axis, [(at, at ^ bit) for at in range(size)])  12 us
    pallas_call x6, Pallas kernels, apply(): call(functools.partial(apply_kernel, plan, piece), shape(count, members,...  9.69 us
    unnamed x10, local copies, waits for them, and re-layouts  6.69 us
    ppermute x1, waiting for transfers between devices, shards(): lax.ppermute(message, 'space', [(at, (at + 2 * d) % lanes) for at in rang...  5.64 us
    pallas_call x2, Pallas kernels, shards(): call(functools.partial(gram_kernel, plan, level), [shape(len(plan.piece_g...  5.13 us
    pallas_call x1, Pallas kernels, shards(): call(functools.partial(chain_kernel, plan), [shape(count, members, member...  3.4 us
    ppermute x8, waiting for transfers between devices, exchange(): return lax.ppermute(value, axis, [(at, at ^ bit) for at in range(size)])  2.97 us
    ppermute x1, starting transfers between devices, shards(): lax.ppermute(message, 'space', [(at, (at + 2 * d) % lanes) for at in rang...  2.95 us
  transfers between devices with their start and end apart: 9, of which 6 were waited for; matrix products, arithmetic and copies ran while one was open for 0% of the time, Pallas kernels for 22%

commit v1 on v0

v1 whole, which is shorter than its diff:
```python
import functools
import math

import jax
import jax.numpy as jnp
from jax import lax
from jax.experimental import pallas as pl
from jax.experimental.pallas import tpu as pltpu
from jax.sharding import PartitionSpec as P

F32 = jnp.float32
BF16 = jnp.bfloat16
VMEM = pl.BlockSpec(memory_space=pltpu.VMEM)
HBM = pl.BlockSpec(memory_space=pltpu.HBM)
ANY = pl.BlockSpec(memory_space=pl.ANY)
DEPTH = 256
PIECES = 3
NORMAL = (((1,), (0,)), ((), ()))
ROWS = (((1,), (1,)), ((), ()))


def split(value):
    high = value.astype(BF16)
    return high, (value - high.astype(F32)).astype(BF16)


def mul(left, right, dims=NORMAL):
    return lax.dot_general(left, right, dims, preferred_element_type=F32)


def mul_pairs(left, right, dims=NORMAL):
    return mul(left[0], right[0], dims) + (
        mul(left[0], right[1], dims) + mul(left[1], right[0], dims)
    )


def mul_exact(left, right, dims=NORMAL):
    return mul_pairs(split(left), split(right), dims)


def product_of(factors):
    while len(factors) > 1:
        joined = [mul_exact(*factors[at : at + 2]) for at in range(0, len(factors) - 1, 2)]
        factors = joined + factors[len(joined) * 2 :]
    return factors[0]


def suffix_scan(ref, count, members, stop):
    width = 1
    while width < stop:
        for start in range(0, count, 2 * width):
            middle = start + width
            if middle < count:
                rows = slice(start * members, middle * members)
                ref[rows] = mul_exact(ref[rows], ref[middle * members : (middle + 1) * members])
        width *= 2


class Plan:
    def __init__(self, count, members):
        self.count, self.members = count, members
        self.stack = DEPTH // members
        self.groups = [
            (start, min(start + self.stack, count)) for start in range(0, count, self.stack)
        ]
        bounds = [-(-len(self.groups) * at // PIECES) for at in range(PIECES + 1)]
        self.piece_groups = [self.groups[a:b] for a, b in zip(bounds, bounds[1:])]
        self.pieces = [(part[0][0], part[-1][1]) for part in self.piece_groups]
        self.first_group = bounds[:-1]
        self.widths = [-(-(stop - start) * members // 128) * 128 for start, stop in self.groups]
        self.width = sum(self.widths)

    def lanes(self, at):
        start = sum(self.widths[:at])
        return slice(start, start + self.widths[at])

    def rows(self, first, last):
        return slice(first * self.members, last * self.members)


def on_blocks(members, size):
    rows = lax.broadcasted_iota(jnp.int32, (size, size), 0) // members
    columns = lax.broadcasted_iota(jnp.int32, (size, size), 1) // members
    return rows == columns


def loads(values, buffer, sems, first, last):
    copies = [
        pltpu.make_async_copy(values.at[at], buffer.at[at - first], sems.at[at - first])
        for at in range(first, last)
    ]
    for copy in copies:
        copy.start()
    return copies


def chain_kernel(plan, transforms, ensembles, cotangents, suffixes, total, steps, ens, cot, kept, runs, sems, ens_sem, cot_sem):
    count, members = plan.count, plan.members
    reads = loads(transforms, kept, sems, 0, count)
    more = loads(ensembles, ens, ens_sem, *plan.pieces[0])
    more += loads(cotangents, cot, cot_sem, *plan.pieces[0])
    for at, copy in enumerate(reads):
        copy.wait()
        suffixes[plan.rows(at, at + 1)] = kept[at]
        if at + 1 < count:
            runs[plan.rows(at + 1, at + 2)] = kept[at].T
    suffix_scan(suffixes, count, members, count)
    total[...] = suffixes[plan.rows(0, 1)]
    number = 0
    width = 1
    while width < count:
        for middle in range(width, count, 2 * width):
            size = min(width, count - middle)
            for side, part in enumerate(split(runs[plan.rows(middle, middle + size)])):
                steps[side, plan.rows(number, number + size)] = part
            number += size
        for start in range(2 * width, count, 2 * width):
            if start + width < count:
                rows = plan.rows(start + width, min(start + 2 * width, count))
                runs[rows] = mul_exact(runs[rows], runs[plan.rows(start + width - 1, start + width)])
        width *= 2
    for copy in more:
        copy.wait()


def count_steps(count):
    total = 0
    width = 1
    while width < count:
        total += sum(min(width, count - middle) for middle in range(width, count, 2 * width))
        width *= 2
    return total


def gram_kernel(plan, piece, *refs):
    members = plan.members
    ens, cot, suffixes = refs[:3]
    refs = refs[3:]
    last = piece == PIECES - 1
    copies = []
    if last:
        earlier, refs = refs[: 2 * piece], refs[2 * piece :]
        _, grams, offsets = refs
    else:
        ensembles, cotangents, _, grams, offsets, next_ens, next_cot, ens_sem, cot_sem = refs
        copies = loads(ensembles, next_ens, ens_sem, *plan.pieces[piece + 1])
        copies += loads(cotangents, next_cot, cot_sem, *plan.pieces[piece + 1])
    base = plan.pieces[piece][0]
    offset = jnp.zeros((members, members), F32)
    first = plan.first_group[piece]
    if last:
        for at in range(piece):
            group = plan.first_group[at]
            lanes = slice(plan.lanes(group).start, plan.lanes(plan.first_group[at + 1]).start)
            grams[:, lanes] = earlier[2 * at][...]
            offset = offset + earlier[2 * at + 1][...]
        origin = 0
    else:
        origin = plan.lanes(first).start
    for at, (start, stop) in enumerate(plan.piece_groups[piece]):
        size = (stop - start) * members
        stacked = [ref[start - base : stop - base].reshape(size, ref.shape[2]) for ref in (cot, ens)]
        wide = jnp.where(on_blocks(members, size), mul(*stacked, ROWS), 0.0)
        gram = wide[:members]
        for i in range(1, stop - start):
            gram = gram + wide[i * members : (i + 1) * members]
        offset = offset + mul_exact(gram, suffixes[plan.rows(start, stop)])
        lanes = plan.lanes(first + at)
        width = lanes.stop - lanes.start
        grams[:, lanes.start - origin : lanes.stop - origin] = jnp.pad(gram, ((0, 0), (0, width - size)))
    offsets[...] = offset
    for copy in copies:
        copy.wait()


def upper_half(level):
    return lax.rem(lax.axis_index("tm") // (1 << level), 2) == 1


def join_kernel(level, total, other, later, before, _, new_total, new_later, new_before, upper_total):
    upper = upper_half(level)
    left = jnp.where(upper, other[...], total[...])
    right = jnp.where(upper, total[...], other[...])
    new_total[...] = mul_exact(left, right)
    upper_total[...] = right
    new_later[...] = jnp.where(upper, later[...], mul_exact(later[...], other[...]))
    new_before[...] = jnp.where(upper, mul_exact(other[...], before[...]), before[...])


def sum_kernel(number, *refs):
    out = refs[-1]
    total = refs[0][...]
    for ref in refs[1:number]:
        total = total + ref[...]
    out[...] = total


def pass_kernel(level, own, other, carry, upper_total, before, _, new_own, new_carry):
    upper = upper_half(level)
    left = jnp.where(upper, other[...], own[...])
    right = jnp.where(upper, own[...], other[...])
    new_own[...] = mul_exact(left, upper_total[...]) + right
    new_carry[...] = carry[...] + jnp.where(upper, mul_exact(left, before[...]), 0.0)


def carry_kernel(plan, level, suffixes, later, other, _, ens_factors, cot_factors, follow, __):
    count, members = plan.count, plan.members
    entering = later[...]
    entering = jnp.where(upper_half(level), entering, mul_exact(entering, other[...]))
    mask = on_blocks(members, plan.stack * members)
    repeated = split(jnp.concatenate([entering] * plan.stack, axis=1))
    for at, (start, stop) in enumerate(plan.groups):
        size = (stop - start) * members
        wide = mul_pairs(split(suffixes[plan.rows(start, stop)]), repeated)
        part = jnp.where(mask[:size, :size], wide[:, :size], 0.0)
        cot_factors[at, :size, :size] = part.astype(BF16)
        ens_factors[at, :size, :size] = part.T.astype(BF16)
        first = max(start - 1, 0)
        kept = wide[(first + 1 - start) * members :, :members]
        for side, value in enumerate(split(kept)):
            follow[side, plan.rows(first, stop - 1)] = value
    for side, value in enumerate(split(entering)):
        follow[side, plan.rows(count - 1, count)] = value


def apply_kernel(plan, pieces, factors, *refs):
    out, marker, out_buf, out_sem = refs[-4:]
    members = plan.members
    marker[...] = jnp.zeros_like(marker)
    base = plan.pieces[pieces[0]][0]
    chunk = out_buf.shape[2] // 2
    writes = []
    for values, piece in zip(refs, pieces):
        for at, (start, stop) in enumerate(plan.piece_groups[piece]):
            size = (stop - start) * members
            first = plan.pieces[piece][0]
            for side in range(2):
                columns = slice(side * chunk, (side + 1) * chunk)
                stacked = values[start - first : stop - first, :, columns].reshape(size, chunk)
                result = mul(factors[plan.first_group[piece] + at, :size, :size], stacked)
                out_buf[start - base : stop - base, :, columns] = result.astype(BF16).reshape(
                    stop - start, members, chunk
                )
                copy = pltpu.make_async_copy(
                    out_buf.at[start - base : stop - base, :, columns],
                    out.at[start:stop, :, columns],
                    out_sem.at[len(writes)],
                )
                copy.start()
                writes.append(copy)
    for copy in writes:
        copy.wait()


def final_kernel(plan, level, scale, number, *refs):
    messages = refs[:number]
    other, carry, before, follow, steps, _, out, buffer, sems = refs[number:]
    count, members = plan.count, plan.members
    entering = carry[...] + jnp.where(
        upper_half(level), mul_exact(other[...], before[...]), 0.0
    )
    totals = []
    for at, (start, stop) in enumerate(plan.groups):
        wide = messages[0][:, plan.lanes(at)]
        for ref in messages[1:]:
            wide = wide + ref[:, plan.lanes(at)]
        tall = wide.T
        for i in range(stop - start):
            totals.append(tall[i * members : (i + 1) * members])
    totals[0] = totals[0] + entering.T
    number = 0
    width = 1
    while width < count:
        for start in range(width, count, 2 * width):
            size = min(width, count - start)
            rows = plan.rows(number, number + size)
            added = mul_pairs((steps[0, rows], steps[1, rows]), split(totals[start - 1]))
            for at in range(size):
                totals[start + at] = totals[start + at] + added[at * members : (at + 1) * members]
            number += size
        width *= 2
    copies = []
    for at in range(count):
        rows = plan.rows(at, at + 1)
        buffer[at] = mul_pairs(split(totals[at]), (follow[0, rows], follow[1, rows]), ROWS) * scale
        copy = pltpu.make_async_copy(buffer.at[at], out.at[at], sems.at[at])
        copy.start()
        copies.append(copy)
    for copy in copies:
        copy.wait()


def call(kernel, outs, ins, out_specs, scratch, micros, name, limit=16, aliases=None):
    return pl.pallas_call(
        kernel,
        out_shape=outs,
        in_specs=ins,
        out_specs=out_specs,
        scratch_shapes=scratch,
        input_output_aliases=aliases or {},
        compiler_params=pltpu.CompilerParams(vmem_limit_bytes=limit << 20),
        cost_estimate=pl.CostEstimate(
            flops=0, bytes_accessed=int(micros * 3.6e6), transcendentals=0
        ),
        name=name,
    )


def shape(*dims, kind=F32):
    return jax.ShapeDtypeStruct(dims, kind)


def shards(ensembles, cotangents, transforms):
    count, members, cells = ensembles.shape
    blocks, lanes = lax.axis_size("tm"), lax.axis_size("space")
    chips = lanes // 2
    scale = 1.0 / math.sqrt(cells * lanes * count * blocks)
    plan = Plan(count, members)
    levels = blocks.bit_length() - 1
    square = shape(members, members)
    ensembles, cotangents, transforms = (
        pltpu.with_memory_space_constraint(value, pltpu.HBM)
        for value in (ensembles, cotangents, transforms)
    )

    def exchange(value, axis, size, bit):
        return lax.ppermute(value, axis, [(at, at ^ bit) for at in range(size)])

    def around(value):
        return [
            lax.ppermute(value, "space", [(at, (at + 2 * d) % lanes) for at in range(lanes)])
            for d in range(1, chips)
        ]

    def loaded(piece):
        first, last = plan.pieces[piece]
        return [shape(last - first, members, cells, kind=BF16)] * 2

    def sems(piece):
        first, last = plan.pieces[piece]
        return [pltpu.SemaphoreType.DMA((last - first,))] * 2

    steps_shape = shape(2, count_steps(count) * members, members, kind=BF16)
    suffixes, total, steps, *first_part = call(
        functools.partial(chain_kernel, plan),
        [shape(count * members, members), square, steps_shape] + loaded(0),
        [HBM] * 3, [VMEM] * 5,
        [pltpu.VMEM((count, members, members), F32), pltpu.VMEM((count * members, members), F32),
         pltpu.SemaphoreType.DMA((count,))] + sems(0), 2, "transform_chain",
    )(transforms, ensembles, cotangents)

    later = before = jnp.eye(members, dtype=F32)
    parts, grams, uppers, befores = [first_part], [], [], []
    done = suffixes
    for level in range(levels):
        other = exchange(total, "tm", blocks, 1 << level)
        if level < PIECES - 1:
            first, last = plan.first_group[level : level + 2]
            width = plan.lanes(last).start - plan.lanes(first).start
            *sums, ens, cot = call(
                functools.partial(gram_kernel, plan, level),
                [shape(members, width), square] + loaded(level + 1),
                [VMEM] * 3 + [HBM] * 2 + [ANY], [VMEM] * 4, sems(level + 1), 1.5, f"gram_{level}",
            )(*parts[-1], suffixes, ensembles, cotangents, done)
            parts.append((ens, cot))
            grams += sums
            done = sums[1]
        befores.append(before)
        if level < levels - 1:
            total, later, before, upper = call(
                functools.partial(join_kernel, level),
                [square] * 4, [VMEM] * 4 + [ANY], [VMEM] * 4, [], 0.3, f"join_{level}",
            )(total, other, later, before, done)
            uppers.append(upper)
            done = later
    gram, offset = call(
        functools.partial(gram_kernel, plan, PIECES - 1),
        [shape(members, plan.width), square],
        [VMEM] * (3 + len(grams)) + [ANY], [VMEM] * 2, [], 1.5, "gram_last",
    )(*parts[-1], suffixes, *grams, done)
    offset_core = exchange(offset, "space", lanes, 1)

    size = plan.stack * members
    ens_factors, cot_factors, follow, gram = call(
        functools.partial(carry_kernel, plan, levels - 1),
        [shape(len(plan.groups), size, size, kind=BF16)] * 2
        + [shape(2, count * members, members, kind=BF16), shape(members, plan.width)],
        [VMEM] * 3 + [ANY], [VMEM] * 3 + [ANY], [], 1.5, "carries", aliases={3: 3},
    )(suffixes, later, other, gram)
    gram_core = exchange(gram, "space", lanes, 1)

    def add(values, after, name):
        return call(
            functools.partial(sum_kernel, len(values)), shape(*values[0].shape),
            [VMEM] * len(values) + [ANY], VMEM, [], 0.1, name,
        )(*values, after)

    offset = add([offset, offset_core], follow, "chip_offset")
    offsets = [offset] + around(offset)

    def apply(factors, which, pieces, out, after, name):
        first, last = plan.pieces[pieces[0]][0], plan.pieces[pieces[-1]][1]
        number = 2 * sum(len(plan.piece_groups[piece]) for piece in pieces)
        return call(
            functools.partial(apply_kernel, plan, pieces),
            [shape(count, members, cells, kind=BF16), shape(8, 128)],
            [VMEM] * (1 + len(pieces)) + [ANY] + [HBM] * len(out), [HBM, VMEM],
            [pltpu.VMEM((last - first, members, cells), BF16),
             pltpu.SemaphoreType.DMA((number,))],
            1.5, name, aliases={2 + len(pieces): 0} if out else None,
        )(factors, *(parts[piece][which] for piece in pieces), after, *out)

    later_pieces = tuple(range(1, PIECES))
    smoothed, done = apply(ens_factors, 0, (0,), (), offset, "smoothed_0")
    own = add(offsets, done, "own_offset")
    gram = add([gram, gram_core], done, "chip_gram")
    grams = [gram] + around(gram)
    carry = jnp.zeros((members, members), F32)
    for level in range(levels):
        other = exchange(own, "tm", blocks, 1 << level)
        if level == 0:
            smoothed, done = apply(ens_factors, 0, later_pieces, (smoothed,), own, "smoothed_1")
        if level == 1:
            ensemble_grad, done = apply(cot_factors, 1, (0,), (), own, "ensemble_grad_0")
        if level == 2:
            ensemble_grad, done = apply(
                cot_factors, 1, later_pieces, (ensemble_grad,), own, "ensemble_grad_1"
            )
        if level < levels - 1:
            own, carry = call(
                functools.partial(pass_kernel, level),
                [square] * 2, [VMEM] * 5 + [ANY], [VMEM] * 2, [], 0.3, f"pass_{level}",
            )(own, other, carry, uppers[level], befores[level], done)
    transform_grad = call(
        functools.partial(final_kernel, plan, levels - 1, scale, chips),
        shape(count, members, members),
        [VMEM] * (chips + 5) + [ANY], HBM,
        [pltpu.VMEM((count, members, members), F32), pltpu.SemaphoreType.DMA((count,))],
        2, "transform_grad",
    )(*grams, other, carry, befores[-1], follow, steps, done)
    return (smoothed, ensemble_grad, transform_grad)


def solution(mesh):
    return jax.shard_map(
        shards,
        mesh=mesh,
        in_specs=(P("tm", None, "space"), P("tm", None, "space"), P("tm", None, None)),
        out_specs=(P("tm", None, "space"), P("tm", None, "space"), P("tm", None, None)),
        check_vma=False,
    )
```

time: 55.9 us -> 55.6 us (level)
  waiting for transfers between devices: 8.61 us -> 16.3 us
  local copies, waits for them, and re-layouts: 6.77 us -> 0.01 us
  Pallas kernels: 24.4 us -> 23.3 us
    unnamed x10 -> x0, local copies, waits for them, and re-layouts: 6.69 us -> none
    ppermute x1 -> x2, waiting for transfers between devices: 5.64 us -> 11.2 us  [around(): lax.ppermute(value, 'space', [(at, (at + 2 * d) % lanes) for at in range(...]
    ppermute x8, waiting for transfers between devices: 2.97 us -> 5.04 us  [exchange(): return lax.ppermute(value, axis, [(at, at ^ bit) for at in range(size)])]
    ppermute x8, starting transfers between devices: 12 us -> 13 us  [exchange(): return lax.ppermute(value, axis, [(at, at ^ bit) for at in range(size)])]
    ppermute x1 -> x2, starting transfers between devices: 2.95 us -> 2.09 us  [around(): lax.ppermute(value, 'space', [(at, (at + 2 * d) % lanes) for at in range(...]
  transfers between devices with their start and end apart: 9 -> 10, of which waited for: 6 -> 5; matrix products, arithmetic and copies ran while one was open for 0% -> 0% of each run, Pallas kernels for 22% -> 27%
where the time goes in v1:
time: 55.6 us; the launch traced here: 55.4 us
  Pallas kernels  23.3 us (42%)
  waiting for transfers between devices  16.3 us (29%)
  starting transfers between devices  15.1 us (27%)
  between operations  0.78 us (1%)
    ppermute x8, starting transfers between devices, exchange(): return lax.ppermute(value, axis, [(at, at ^ bit) for at in range(size)])  13 us
    ppermute x2, waiting for transfers between devices, around(): lax.ppermute(value, 'space', [(at, (at + 2 * d) % lanes) for at in range(...  11.2 us
    pallas_call x4, Pallas kernels, apply(): call(functools.partial(apply_kernel, plan, pieces), [shape(count, members...  7.29 us
    pallas_call x2, Pallas kernels, shards(): call(functools.partial(gram_kernel, plan, level), [shape(members, width),...  6.1 us
    ppermute x8, waiting for transfers between devices, exchange(): return lax.ppermute(value, axis, [(at, at ^ bit) for at in range(size)])  5.04 us
    pallas_call x1, Pallas kernels, shards(): call(functools.partial(chain_kernel, plan), [shape(count * members, membe...  4.23 us
    pallas_call x1, Pallas kernels, shards(): call(functools.partial(final_kernel, plan, levels - 1, scale, chips), sha...  2.47 us
    ppermute x2, starting transfers between devices, around(): lax.ppermute(value, 'space', [(at, (at + 2 * d) % lanes) for at in range(...  2.09 us
  transfers between devices with their start and end apart: 10, of which 5 were waited for; matrix products, arithmetic and copies ran while one was open for 0% of the time, Pallas kernels for 27%

profile of v1, /device:TPU:0, one launch (start us, length us, event | category | flops | bytes accessed | tf_op | source)
XLA Modules:
  0.0 55.4 jit_solution(12829779462069018902)
XLA Ops:
  0.6 4.2 %transform_chain.1 = (f32[1280,80]{1,0:T(8,128)S(1)}, f32[80,80]{1,0:T(8,128)S(1)}, bf16[2,2560,80]{2,1,0:T(8,128)(2,1)S(1)}, bf16[6,80,2048]{2,1,0:T(8,128)(2,1)S(1)}, bf16[6,80,2048]{2,1,0:T(8,128)(2,1)S(1)}) custom-call(f32[16,80,80]{2,1,0:T(8,128)} %transforms.1, bf16[16,80,2048]{2,1,0:T(8,128)(2,1)} %refs_3_.3, bf16[16,80,2048]{2,1,0:T(8,128)(2,1)} %refs_4_.3), custom_call_target="tpu_custom_call" | custom-call | bytes 7200000 | tf_op jit(solution)/shard_map/transform_chain/pallas_call | solution.py:344
  4.9 3.0 %collective-permute-start = (f32[80,80]{1,0:T(8,128)S(1)}, f32[80,80]{1,0:T(8,128)S(1)}, u32[]{:S(2)}, u32[]{:S(2)}) collective-permute-start(f32[80,80]{1,0:T(8,128)S(1)} %get-tuple-element.43.total), channel_id=1, source_target_pairs={{0,4},{4,0},{8,12},{12,8},{16,20},{20,16},{24,28},{28,24},{1,5},{5... | collective-permute-start | bytes 76808 | tf_op jit(solution)/shard_map/ppermute | solution.py:327
  7.9 3.3 %gram_0.1 = (f32[80,512]{1,0:T(8,128)S(1)}, f32[80,80]{1,0:T(8,128)S(1)}, bf16[6,80,2048]{2,1,0:T(8,128)(2,1)S(1)}, bf16[6,80,2048]{2,1,0:T(8,128)(2,1)S(1)}) custom-call(bf16[6,80,2048]{2,1,0:T(8,128)(2,1)S(1)} %get-tuple-element.44.refs_0_, bf16[6,80,2048]{2,1,0:T(8,128)(2,1)S(1)} %get-tuple-element.45.refs_1_.refs_0_, ...), custom_call_target="tpu_custom_call" | custom-call | bytes 5400000 | tf_op jit(solution)/shard_map/gram_0/pallas_call | solution.py:360
  11.2 0.0 collective-permute-done.other
  11.2 0.3 join_0.1
  11.4 1.6 %collective-permute-start.1 = (f32[80,80]{1,0:T(8,128)S(1)}, f32[80,80]{1,0:T(8,128)S(1)}, u32[]{:S(2)}, u32[]{:S(2)}) collective-permute-start(f32[80,80]{1,0:T(8,128)S(1)} %get-tuple-element.47.total), channel_id=1, source_target_pairs={{0,8},{4,12},{8,0},{12,4},{16,24},{20,28},{24,16},{28,20},{1,9},{5... | collective-permute-start | bytes 76808 | tf_op jit(solution)/shard_map/ppermute | solution.py:327
  13.1 2.8 %gram_1.1 = (f32[80,512]{1,0:T(8,128)S(1)}, f32[80,80]{1,0:T(8,128)S(1)}, bf16[4,80,2048]{2,1,0:T(8,128)(2,1)S(1)}, bf16[4,80,2048]{2,1,0:T(8,128)(2,1)S(1)}) custom-call(bf16[6,80,2048]{2,1,0:T(8,128)(2,1)S(1)} %get-tuple-element.50.refs_0_, bf16[6,80,2048]{2,1,0:T(8,128)(2,1)S(1)} %get-tuple-element.51.refs_1_.refs_0_, ...), custom_call_target="tpu_custom_call" | custom-call | bytes 5400000 | tf_op jit(solution)/shard_map/gram_1/pallas_call | solution.py:360
  15.9 0.0 collective-permute-done.1.other
  15.9 0.3 join_1.1
  16.2 2.7 %collective-permute-start.2 = (f32[80,80]{1,0:T(8,128)S(1)}, f32[80,80]{1,0:T(8,128)S(1)}, u32[]{:S(2)}, u32[]{:S(2)}) collective-permute-start(f32[80,80]{1,0:T(8,128)S(1)} %get-tuple-element.54), channel_id=1, source_target_pairs={{0,16},{4,20},{8,24},{12,28},{16,0},{20,4},{24,8},{28,12},{1,17},{... | collective-permute-start | bytes 76808 | tf_op jit(solution)/shard_map/ppermute | solution.py:327
  18.9 1.1 %gram_last.1 = (f32[80,1408]{1,0:T(8,128)S(1)}, f32[80,80]{1,0:T(8,128)S(1)}) custom-call(bf16[4,80,2048]{2,1,0:T(8,128)(2,1)S(1)} %get-tuple-element.55.refs_0_.refs_1_, bf16[4,80,2048]{2,1,0:T(8,128)(2,1)S(1)} %get-tuple-element.56.refs_1_, f32[1280,80]{1,0:T(8,128)S(1)} %get-tuple-element.42.refs_2_.refs_5_.suffixes, ...), custom_call_target="tpu_custom_call" | custom-call | bytes 5400000 | tf_op jit(solution)/shard_map/gram_last/pallas_call | solution.py:376
  20.0 1.2 %collective-permute-done.2.other = f32[80,80]{1,0:T(8,128)S(1)} collective-permute-done((f32[80,80]{1,0:T(8,128)S(1)}, f32[80,80]{1,0:T(8,128)S(1)}, u32[]{:S(2)}, u32[]{:S(2)}) %collective-permute-start.2) | collective-permute-done | bytes 25632 | tf_op jit(solution)/shard_map/ppermute | solution.py:327
  21.2 1.1 %carries.1 = (bf16[6,240,240]{2,1,0:T(8,128)(2,1)S(1)}, bf16[6,240,240]{2,1,0:T(8,128)(2,1)S(1)}, bf16[2,1280,80]{2,1,0:T(8,128)(2,1)S(1)}, f32[80,1408]{1,0:T(8,128)S(1)}) custom-call(f32[1280,80]{1,0:T(8,128)S(1)} %get-tuple-element.42.refs_2_.refs_5_.suffixes, f32[80,80]{1,0:T(8,128)S(1)} %get-tuple-element.53.refs_7_.later, ...), custom_call_target="tpu_custom_call", output_to_operand_aliasing={{3}: (3, {})} | custom-call | bytes 5400000 | tf_op jit(solution)/shard_map/carries/pallas_call | solution.py:384
  22.2 0.1 collective-permute-start.7
  22.3 0.5 collective-permute-start.3
  22.8 1.4 %collective-permute-done.3.refs_1_ = f32[80,80]{1,0:T(8,128)S(1)} collective-permute-done((f32[80,80]{1,0:T(8,128)S(1)}, f32[80,80]{1,0:T(8,128)S(1)}, u32[]{:S(2)}, u32[]{:S(2)}) %collective-permute-start.3) | collective-permute-done | bytes 25632 | tf_op jit(solution)/shard_map/ppermute | solution.py:327
  24.2 1.6 %smoothed_0.1 = (bf16[16,80,2048]{2,1,0:T(8,128)(2,1)}, f32[8,128]{1,0:T(8,128)S(1)}) custom-call(bf16[6,240,240]{2,1,0:T(8,128)(2,1)S(1)} %get-tuple-element.60.factors, bf16[6,80,2048]{2,1,0:T(8,128)(2,1)S(1)} %get-tuple-element.44.refs_0_, f32[80,80]{1,0:T(8,128)S(1)} %chip_offset.1.refs_1_.refs_0_), custom_call_target="tpu_custom_call" | custom-call | bytes 5400000 | tf_op jit(solution)/shard_map/smoothed_0/pallas_call | solution.py:404
  25.8 0.0 collective-permute-done.7.refs_1_
  25.8 0.1 chip_gram.1.refs_0_
  25.8 1.6 %collective-permute-start.8 = (f32[80,1408]{1,0:T(8,128)S(1)}, f32[80,1408]{1,0:T(8,128)S(1)}, u32[]{:S(2)}, u32[]{:S(2)}) collective-permute-start(f32[80,1408]{1,0:T(8,128)S(1)} %chip_gram.1.refs_0_), channel_id=1, source_target_pairs={{0,2},{1,3},{2,0},{3,1},{4,6},{5,7},{6,4},{7,5},{8,10},{9,11},{10,... | collective-permute-start | bytes 1351688 | tf_op jit(solution)/shard_map/ppermute | solution.py:331
  27.4 0.5 collective-permute-start.4
  27.9 11.2 %collective-permute-done.4.refs_1_ = f32[80,80]{1,0:T(8,128)S(1)} collective-permute-done((f32[80,80]{1,0:T(8,128)S(1)}, f32[80,80]{1,0:T(8,128)S(1)}, u32[]{:S(2)}, u32[]{:S(2)}) %collective-permute-start.4) | collective-permute-done | bytes 25632 | tf_op jit(solution)/shard_map/ppermute | solution.py:331
  39.2 0.8 %collective-permute-start.5 = (f32[80,80]{1,0:T(8,128)S(1)}, f32[80,80]{1,0:T(8,128)S(1)}, u32[]{:S(2)}, u32[]{:S(2)}) collective-permute-start(f32[80,80]{1,0:T(8,128)S(1)} %own_offset.1.refs_2_.own), channel_id=1, source_target_pairs={{0,4},{4,0},{8,12},{12,8},{16,20},{20,16},{24,28},{28,24},{1,5},{5... | collective-permute-start | bytes 76808 | tf_op jit(solution)/shard_map/ppermute | solution.py:327
  39.9 2.1 %smoothed_1.1 = (bf16[16,80,2048]{2,1,0:T(8,128)(2,1)}, f32[8,128]{1,0:T(8,128)S(1)}) custom-call(bf16[6,240,240]{2,1,0:T(8,128)(2,1)S(1)} %get-tuple-element.60.factors, bf16[6,80,2048]{2,1,0:T(8,128)(2,1)S(1)} %get-tuple-element.50.refs_0_, bf16[4,80,2048]{2,1,0:T(8,128)(2,1)S(1)} %get-tuple-element.55.refs_0_.refs_1_, ...), custom_call_target="tpu_custom_call", output_to_operand_aliasing={{0}: (4, {})} | custom-call | bytes 5400000 | tf_op jit(solution)/shard_map/smoothed_1/pallas_call | solution.py:404
  42.0 1.2 %collective-permute-done.5.other = f32[80,80]{1,0:T(8,128)S(1)} collective-permute-done((f32[80,80]{1,0:T(8,128)S(1)}, f32[80,80]{1,0:T(8,128)S(1)}, u32[]{:S(2)}, u32[]{:S(2)}) %collective-permute-start.5) | collective-permute-done | bytes 25632 | tf_op jit(solution)/shard_map/ppermute | solution.py:327
  43.2 0.2 pass_0.1
  43.5 1.2 %collective-permute-start.6 = (f32[80,80]{1,0:T(8,128)S(1)}, f32[80,80]{1,0:T(8,128)S(1)}, u32[]{:S(2)}, u32[]{:S(2)}) collective-permute-start(f32[80,80]{1,0:T(8,128)S(1)} %get-tuple-element.69.refs_1_.own), channel_id=1, source_target_pairs={{0,8},{4,12},{8,0},{12,4},{16,24},{20,28},{24,16},{28,20},{1,9},{5... | collective-permute-start | bytes 76808 | tf_op jit(solution)/shard_map/ppermute | solution.py:327
  44.7 1.6 %ensemble_grad_0.1 = (bf16[16,80,2048]{2,1,0:T(8,128)(2,1)}, f32[8,128]{1,0:T(8,128)S(1)}) custom-call(bf16[6,240,240]{2,1,0:T(8,128)(2,1)S(1)} %get-tuple-element.66.factors, bf16[6,80,2048]{2,1,0:T(8,128)(2,1)S(1)} %get-tuple-element.45.refs_1_.refs_0_, f32[80,80]{1,0:T(8,128)S(1)} %get-tuple-element.69.refs_1_.own), custom_call_target="tpu_custom_call" | custom-call | bytes 5400000 | tf_op jit(solution)/shard_map/ensemble_grad_0/pallas_call | solution.py:404
  46.3 1.3 %collective-permute-done.6.other = f32[80,80]{1,0:T(8,128)S(1)} collective-permute-done((f32[80,80]{1,0:T(8,128)S(1)}, f32[80,80]{1,0:T(8,128)S(1)}, u32[]{:S(2)}, u32[]{:S(2)}) %collective-permute-start.6) | collective-permute-done | bytes 25632 | tf_op jit(solution)/shard_map/ppermute | solution.py:327
  47.5 0.2 pass_1.1
  47.7 3.1 %collective-permute-start.9 = (f32[80,80]{1,0:T(8,128)S(1)}, f32[80,80]{1,0:T(8,128)S(1)}, u32[]{:S(2)}, u32[]{:S(2)}) collective-permute-start(f32[80,80]{1,0:T(8,128)S(1)} %get-tuple-element.73.refs_2_), channel_id=1, source_target_pairs={{0,16},{4,20},{8,24},{12,28},{16,0},{20,4},{24,8},{28,12},{1,17},{... | collective-permute-start | bytes 76808 | tf_op jit(solution)/shard_map/ppermute | solution.py:327
  50.9 2.1 %ensemble_grad_1.1 = (bf16[16,80,2048]{2,1,0:T(8,128)(2,1)}, f32[8,128]{1,0:T(8,128)S(1)}) custom-call(bf16[6,240,240]{2,1,0:T(8,128)(2,1)S(1)} %get-tuple-element.66.factors, bf16[6,80,2048]{2,1,0:T(8,128)(2,1)S(1)} %get-tuple-element.51.refs_1_.refs_0_, bf16[4,80,2048]{2,1,0:T(8,128)(2,1)S(1)} %get-tuple-element.56.refs_1_, ...), custom_call_target="tpu_custom_call", output_to_operand_aliasing={{0}: (4, {})} | custom-call | bytes 5400000 | tf_op jit(solution)/shard_map/ensemble_grad_1/pallas_call | solution.py:404
  52.9 0.0 collective-permute-done.9.refs_2_
  52.9 0.0 collective-permute-done.8.refs_1_
  53.0 2.5 %transform_grad.1 = f32[16,80,80]{2,1,0:T(8,128)} custom-call(f32[80,1408]{1,0:T(8,128)S(1)} %chip_gram.1.refs_0_, f32[80,1408]{1,0:T(8,128)S(1)} %collective-permute-done.8.refs_1_, f32[80,80]{1,0:T(8,128)S(1)} %collective-permute-done.9.refs_2_, f32[80,80]{1,0:T(8,128)S(1)} %get-tuple-element.77.refs_3_, f32[80,80]{1,0:T(8,128)S(1)} %get-tuple-element.78.refs_4_, ...), custom_call_target="tpu_custom_call" | custom-call | bytes 7200000 | tf_op jit(solution)/shard_map/transform_grad/pallas_call | solution.py:434
  (4 shorter events, 0.0 us)
Async XLA Ops:
  4.9 6.3 %collective-permute-start = (f32[80,80]{1,0:T(8,128)S(1)}, f32[80,80]{1,0:T(8,128)S(1)}, u32[]{:S(2)}, u32[]{:S(2)}) collective-permute-start(f32[80,80]{1,0:T(8,128)S(1)} %get-tuple-element.43.total), channel_id=1, source_target_pairs={{0,4},{4,0},{8,12},{12,8},{16,20},{20,16},{24,28},{28,24},{1,5},{5... | collective-permute-start | bytes 76808 | tf_op jit(solution)/shard_map/ppermute | solution.py:327
  11.4 4.5 %collective-permute-start.1 = (f32[80,80]{1,0:T(8,128)S(1)}, f32[80,80]{1,0:T(8,128)S(1)}, u32[]{:S(2)}, u32[]{:S(2)}) collective-permute-start(f32[80,80]{1,0:T(8,128)S(1)} %get-tuple-element.47.total), channel_id=1, source_target_pairs={{0,8},{4,12},{8,0},{12,4},{16,24},{20,28},{24,16},{28,20},{1,9},{5... | collective-permute-start | bytes 76808 | tf_op jit(solution)/shard_map/ppermute | solution.py:327
  16.2 5.0 %collective-permute-start.2 = (f32[80,80]{1,0:T(8,128)S(1)}, f32[80,80]{1,0:T(8,128)S(1)}, u32[]{:S(2)}, u32[]{:S(2)}) collective-permute-start(f32[80,80]{1,0:T(8,128)S(1)} %get-tuple-element.54), channel_id=1, source_target_pairs={{0,16},{4,20},{8,24},{12,28},{16,0},{20,4},{24,8},{28,12},{1,17},{... | collective-permute-start | bytes 76808 | tf_op jit(solution)/shard_map/ppermute | solution.py:327
  22.2 3.5 %collective-permute-start.7 = (f32[80,1408]{1,0:T(8,128)S(1)}, f32[80,1408]{1,0:T(8,128)S(1)}, u32[]{:S(2)}, u32[]{:S(2)}) collective-permute-start(f32[80,1408]{1,0:T(8,128)S(1)} %get-tuple-element.76.refs_0_), channel_id=1, source_target_pairs={{0,1},{1,0},{2,3},{3,2},{4,5},{5,4},{6,7},{7,6},{8,9},{9,8},{10,11... | collective-permute-start | bytes 1351688 | tf_op jit(solution)/shard_map/ppermute | solution.py:327
  22.3 1.9 %collective-permute-start.3 = (f32[80,80]{1,0:T(8,128)S(1)}, f32[80,80]{1,0:T(8,128)S(1)}, u32[]{:S(2)}, u32[]{:S(2)}) collective-permute-start(f32[80,80]{1,0:T(8,128)S(1)} %get-tuple-element.61.refs_0_), channel_id=1, source_target_pairs={{0,1},{1,0},{2,3},{3,2},{4,5},{5,4},{6,7},{7,6},{8,9},{9,8},{10,11... | collective-permute-start | bytes 76808 | tf_op jit(solution)/shard_map/ppermute | solution.py:327
  25.8 27.1 %collective-permute-start.8 = (f32[80,1408]{1,0:T(8,128)S(1)}, f32[80,1408]{1,0:T(8,128)S(1)}, u32[]{:S(2)}, u32[]{:S(2)}) collective-permute-start(f32[80,1408]{1,0:T(8,128)S(1)} %chip_gram.1.refs_0_), channel_id=1, source_target_pairs={{0,2},{1,3},{2,0},{3,1},{4,6},{5,7},{6,4},{7,5},{8,10},{9,11},{10,... | collective-permute-start | bytes 1351688 | tf_op jit(solution)/shard_map/ppermute | solution.py:331
  27.4 11.7 %collective-permute-start.4 = (f32[80,80]{1,0:T(8,128)S(1)}, f32[80,80]{1,0:T(8,128)S(1)}, u32[]{:S(2)}, u32[]{:S(2)}) collective-permute-start(f32[80,80]{1,0:T(8,128)S(1)} %chip_offset.1.refs_1_.refs_0_), channel_id=1, source_target_pairs={{0,2},{1,3},{2,0},{3,1},{4,6},{5,7},{6,4},{7,5},{8,10},{9,11},{10,... | collective-permute-start | bytes 76808 | tf_op jit(solution)/shard_map/ppermute | solution.py:331
  39.2 4.1 %collective-permute-start.5 = (f32[80,80]{1,0:T(8,128)S(1)}, f32[80,80]{1,0:T(8,128)S(1)}, u32[]{:S(2)}, u32[]{:S(2)}) collective-permute-start(f32[80,80]{1,0:T(8,128)S(1)} %own_offset.1.refs_2_.own), channel_id=1, source_target_pairs={{0,4},{4,0},{8,12},{12,8},{16,20},{20,16},{24,28},{28,24},{1,5},{5... | collective-permute-start | bytes 76808 | tf_op jit(solution)/shard_map/ppermute | solution.py:327
  43.5 4.1 %collective-permute-start.6 = (f32[80,80]{1,0:T(8,128)S(1)}, f32[80,80]{1,0:T(8,128)S(1)}, u32[]{:S(2)}, u32[]{:S(2)}) collective-permute-start(f32[80,80]{1,0:T(8,128)S(1)} %get-tuple-element.69.refs_1_.own), channel_id=1, source_target_pairs={{0,8},{4,12},{8,0},{12,4},{16,24},{20,28},{24,16},{28,20},{1,9},{5... | collective-permute-start | bytes 76808 | tf_op jit(solution)/shard_map/ppermute | solution.py:327
  47.7 5.2 %collective-permute-start.9 = (f32[80,80]{1,0:T(8,128)S(1)}, f32[80,80]{1,0:T(8,128)S(1)}, u32[]{:S(2)}, u32[]{:S(2)}) collective-permute-start(f32[80,80]{1,0:T(8,128)S(1)} %get-tuple-element.73.refs_2_), channel_id=1, source_target_pairs={{0,16},{4,20},{8,24},{12,28},{16,0},{20,4},{24,8},{28,12},{1,17},{... | collective-permute-start | bytes 76808 | tf_op jit(solution)/shard_map/ppermute | solution.py:327

commit v2 on v1

--- a/solution.py
+++ b/solution.py
@@ -84,23 +84,26 @@
     return rows == columns
 
 
-def loads(values, buffer, sems, first, last):
-    copies = [
-        pltpu.make_async_copy(values.at[at], buffer.at[at - first], sems.at[at - first])
-        for at in range(first, last)
-    ]
+def loads(values, buffers, sems, plan):
+    copies = []
+    for (base, _), buffer, groups in zip(plan.pieces, buffers, plan.piece_groups):
+        for start, stop in groups:
+            part = buffer.at[start - base : stop - base]
+            copies.append(pltpu.make_async_copy(values.at[start:stop], part, sems.at[len(copies)]))
     for copy in copies:
         copy.start()
     return copies
 
 
-def chain_kernel(plan, transforms, ensembles, cotangents, suffixes, total, steps, ens, cot, kept, runs, sems, ens_sem, cot_sem):
+def chain_kernel(plan, transforms, ensembles, cotangents, suffixes, total, steps, *refs):
     count, members = plan.count, plan.members
-    reads = loads(transforms, kept, sems, 0, count)
-    more = loads(ensembles, ens, ens_sem, *plan.pieces[0])
-    more += loads(cotangents, cot, cot_sem, *plan.pieces[0])
-    for at, copy in enumerate(reads):
-        copy.wait()
+    kept, runs, sem, ens_sem, cot_sem = refs[2 * PIECES :]
+    read = pltpu.make_async_copy(transforms, kept, sem)
+    read.start()
+    more = loads(ensembles, refs[:PIECES], ens_sem, plan)
+    more += loads(cotangents, refs[PIECES : 2 * PIECES], cot_sem, plan)
+    read.wait()
+    for at in range(count):
         suffixes[plan.rows(at, at + 1)] = kept[at]
         if at + 1 < count:
             runs[plan.rows(at + 1, at + 2)] = kept[at].T
@@ -137,14 +140,9 @@
     ens, cot, suffixes = refs[:3]
     refs = refs[3:]
     last = piece == PIECES - 1
-    copies = []
     if last:
         earlier, refs = refs[: 2 * piece], refs[2 * piece :]
-        _, grams, offsets = refs
-    else:
-        ensembles, cotangents, _, grams, offsets, next_ens, next_cot, ens_sem, cot_sem = refs
-        copies = loads(ensembles, next_ens, ens_sem, *plan.pieces[piece + 1])
-        copies += loads(cotangents, next_cot, cot_sem, *plan.pieces[piece + 1])
+    _, grams, offsets = refs
     base = plan.pieces[piece][0]
     offset = jnp.zeros((members, members), F32)
     first = plan.first_group[piece]
@@ -169,8 +167,6 @@
         width = lanes.stop - lanes.start
         grams[:, lanes.start - origin : lanes.stop - origin] = jnp.pad(gram, ((0, 0), (0, width - size)))
     offsets[...] = offset
-    for copy in copies:
-        copy.wait()
 
 
 def upper_half(level):
@@ -188,7 +184,7 @@
 
 
 def sum_kernel(number, *refs):
-    out = refs[-1]
+    out = refs[-2]
     total = refs[0][...]
     for ref in refs[1:number]:
         total = total + ref[...]
@@ -203,7 +199,7 @@
     new_carry[...] = carry[...] + jnp.where(upper, mul_exact(left, before[...]), 0.0)
 
 
-def carry_kernel(plan, level, suffixes, later, other, _, ens_factors, cot_factors, follow, __):
+def carry_kernel(plan, level, suffixes, later, other, _, ens_factors, cot_factors, follow):
     count, members = plan.count, plan.members
     entering = later[...]
     entering = jnp.where(upper_half(level), entering, mul_exact(entering, other[...]))
@@ -332,37 +328,31 @@
             for d in range(1, chips)
         ]
 
-    def loaded(piece):
-        first, last = plan.pieces[piece]
-        return [shape(last - first, members, cells, kind=BF16)] * 2
-
-    def sems(piece):
-        first, last = plan.pieces[piece]
-        return [pltpu.SemaphoreType.DMA((last - first,))] * 2
-
     steps_shape = shape(2, count_steps(count) * members, members, kind=BF16)
-    suffixes, total, steps, *first_part = call(
+    buffers = [shape(last - first, members, cells, kind=BF16) for first, last in plan.pieces] * 2
+    suffixes, total, steps, *loaded = call(
         functools.partial(chain_kernel, plan),
-        [shape(count * members, members), square, steps_shape] + loaded(0),
-        [HBM] * 3, [VMEM] * 5,
+        [shape(count * members, members), square, steps_shape] + buffers,
+        [HBM] * 3, [VMEM] * (3 + len(buffers)),
         [pltpu.VMEM((count, members, members), F32), pltpu.VMEM((count * members, members), F32),
-         pltpu.SemaphoreType.DMA((count,))] + sems(0), 2, "transform_chain",
+         pltpu.SemaphoreType.DMA] + [pltpu.SemaphoreType.DMA((len(plan.groups),))] * 2,
+        4, "transform_chain",
     )(transforms, ensembles, cotangents)
+    parts = list(zip(loaded[:PIECES], loaded[PIECES:]))
 
     later = before = jnp.eye(members, dtype=F32)
-    parts, grams, uppers, befores = [first_part], [], [], []
+    grams, uppers, befores = [], [], []
     done = suffixes
     for level in range(levels):
         other = exchange(total, "tm", blocks, 1 << level)
         if level < PIECES - 1:
             first, last = plan.first_group[level : level + 2]
             width = plan.lanes(last).start - plan.lanes(first).start
-            *sums, ens, cot = call(
+            sums = call(
                 functools.partial(gram_kernel, plan, level),
-                [shape(members, width), square] + loaded(level + 1),
-                [VMEM] * 3 + [HBM] * 2 + [ANY], [VMEM] * 4, sems(level + 1), 1.5, f"gram_{level}",
-            )(*parts[-1], suffixes, ensembles, cotangents, done)
-            parts.append((ens, cot))
+                [shape(members, width), square],
+                [VMEM] * 3 + [ANY], [VMEM] * 2, [], 1.5, f"gram_{level}",
+            )(*parts[level], suffixes, done)
             grams += sums
             done = sums[1]
         befores.append(before)
@@ -381,21 +371,23 @@
     offset_core = exchange(offset, "space", lanes, 1)
 
     size = plan.stack * members
-    ens_factors, cot_factors, follow, gram = call(
+    ens_factors, cot_factors, follow = call(
         functools.partial(carry_kernel, plan, levels - 1),
         [shape(len(plan.groups), size, size, kind=BF16)] * 2
-        + [shape(2, count * members, members, kind=BF16), shape(members, plan.width)],
-        [VMEM] * 3 + [ANY], [VMEM] * 3 + [ANY], [], 1.5, "carries", aliases={3: 3},
-    )(suffixes, later, other, gram)
+        + [shape(2, count * members, members, kind=BF16)],
+        [VMEM] * 3 + [ANY], [VMEM] * 3, [], 1.5, "carries",
+    )(suffixes, later, other, offset)
+
+    def add(values, after, name, through):
+        number = len(values)
+        return call(
+            functools.partial(sum_kernel, number),
+            [shape(*values[0].shape), shape(*through.shape)],
+            [VMEM] * number + [ANY] * 2, [VMEM, ANY], [], 0.1, name, aliases={number + 1: 1},
+        )(*values, after, through)
+
+    offset, gram = add([offset, offset_core], follow, "chip_offset", gram)
     gram_core = exchange(gram, "space", lanes, 1)
-
-    def add(values, after, name):
-        return call(
-            functools.partial(sum_kernel, len(values)), shape(*values[0].shape),
-            [VMEM] * len(values) + [ANY], VMEM, [], 0.1, name,
-        )(*values, after)
-
-    offset = add([offset, offset_core], follow, "chip_offset")
     offsets = [offset] + around(offset)
 
     def apply(factors, which, pieces, out, after, name):
@@ -412,8 +404,8 @@
 
     later_pieces = tuple(range(1, PIECES))
     smoothed, done = apply(ens_factors, 0, (0,), (), offset, "smoothed_0")
-    own = add(offsets, done, "own_offset")
-    gram = add([gram, gram_core], done, "chip_gram")
+    own, gram_core = add(offsets, done, "own_offset", gram_core)
+    gram = gram + gram_core
     grams = [gram] + around(gram)
     carry = jnp.zeros((members, members), F32)
     for level in range(levels):

time: 55.6 us -> 44.7 us (0.80)
  waiting for transfers between devices: 16.3 us -> 3.78 us
  starting transfers between devices: 15.1 us -> 18 us
  Pallas kernels: 23.3 us -> 21.9 us
    ppermute x2, waiting for transfers between devices: 11.2 us -> 0.56 us  [around(): lax.ppermute(value, 'space', [(at, (at + 2 * d) % lanes) for at in range(...]
    pallas_call x2, Pallas kernels: 6.1 us -> 3.05 us  [shards(): call(functools.partial(gram_kernel, plan, level), [shape(members, width),...]
    ppermute x8, waiting for transfers between devices: 5.04 us -> 3.21 us  [exchange(): return lax.ppermute(value, axis, [(at, at ^ bit) for at in range(size)])]
    pallas_call x1, Pallas kernels: 4.23 us -> 5.98 us  [shards(): call(functools.partial(chain_kernel, plan), [shape(count * members, membe...]
    ppermute x2, starting transfers between devices: 2.09 us -> 3.83 us  [around(): lax.ppermute(value, 'space', [(at, (at + 2 * d) % lanes) for at in range(...]
    ppermute x8, starting transfers between devices: 13 us -> 14.2 us  [exchange(): return lax.ppermute(value, axis, [(at, at ^ bit) for at in range(size)])]
  transfers between devices with their start and end apart: 10 -> 10, of which waited for: 5 -> 7; matrix products, arithmetic and copies ran while one was open for 0% -> 0% of each run, Pallas kernels for 27% -> 29%
where the time goes in v2:
time: 44.7 us; the launch traced here: 44.5 us
  Pallas kernels  21.9 us (49%)
  starting transfers between devices  18 us (40%)
  waiting for transfers between devices  3.78 us (8%)
  between operations  0.77 us (2%)
    ppermute x8, starting transfers between devices, exchange(): return lax.ppermute(value, axis, [(at, at ^ bit) for at in range(size)])  14.2 us
    pallas_call x4, Pallas kernels, apply(): call(functools.partial(apply_kernel, plan, pieces), [shape(count, members...  7.28 us
    pallas_call x1, Pallas kernels, shards(): call(functools.partial(chain_kernel, plan), [shape(count * members, membe...  5.98 us
    ppermute x2, starting transfers between devices, around(): lax.ppermute(value, 'space', [(at, (at + 2 * d) % lanes) for at in range(...  3.83 us
    ppermute x8, waiting for transfers between devices, exchange(): return lax.ppermute(value, axis, [(at, at ^ bit) for at in range(size)])  3.21 us
    pallas_call x2, Pallas kernels, shards(): call(functools.partial(gram_kernel, plan, level), [shape(members, width),...  3.05 us
    pallas_call x1, Pallas kernels, shards(): call(functools.partial(final_kernel, plan, levels - 1, scale, chips), sha...  2.47 us
    pallas_call x1, Pallas kernels, shards(): call(functools.partial(gram_kernel, plan, PIECES - 1), [shape(members, pl...  1.14 us
  transfers between devices with their start and end apart: 10, of which 7 were waited for; matrix products, arithmetic and copies ran while one was open for 0% of the time, Pallas kernels for 29%

profile of v2, /device:TPU:0, one launch (start us, length us, event | category | flops | bytes accessed | tf_op | source)
XLA Modules:
  0.0 44.5 jit_solution(427238870742836075)
XLA Ops:
  0.6 6.0 %transform_chain.1 = (f32[1280,80]{1,0:T(8,128)S(1)}, f32[80,80]{1,0:T(8,128)S(1)}, bf16[2,2560,80]{2,1,0:T(8,128)(2,1)S(1)}, bf16[6,80,2048]{2,1,0:T(8,128)(2,1...) custom-call(f32[16,80,80]{2,1,0:T(8,128)} %transforms.1, ...), custom_call_target="tpu_custom_call" | custom-call | bytes 14400000 | tf_op jit(solution)/shard_map/transform_chain/pallas_call | solution.py:333
  6.6 3.0 %collective-permute-start = (f32[80,80]{1,0:T(8,128)S(1)}, f32[80,80]{1,0:T(8,128)S(1)}, u32[]{:S(2)}, u32[]{:S(2)}) collective-permute-start(f32[80,80]{1,0:T(8,128)S(1)} %get-tuple-element.46.total), channel_id=1, source_target_pairs={{0,4},{4,0},{8,12},{12,8},{16,20},{20,16},{24,28},{28,24},{1,5},{5... | collective-permute-start | bytes 76808 | tf_op jit(solution)/shard_map/ppermute | solution.py:323
  9.6 1.5 %gram_0.1 = (f32[80,512]{1,0:T(8,128)S(1)}, f32[80,80]{1,0:T(8,128)S(1)}) custom-call(bf16[6,80,2048]{2,1,0:T(8,128)(2,1)S(1)} %get-tuple-element.47.refs_0_, bf16[6,80,2048]{2,1,0:T(8,128)(2,1)S(1)} %get-tuple-element.48.refs_1_.refs_0_, f32[1280,80]{1,0:T(8,128)S(1)} %get-tuple-element.45.refs_2_.refs_3_.suffixes, ...), custom_call_target="tpu_custom_call" | custom-call | bytes 5400000 | tf_op jit(solution)/shard_map/gram_0/pallas_call | solution.py:351
  11.2 0.4 collective-permute-done.other
  11.6 0.3 join_0.1
  11.9 2.2 %collective-permute-start.1 = (f32[80,80]{1,0:T(8,128)S(1)}, f32[80,80]{1,0:T(8,128)S(1)}, u32[]{:S(2)}, u32[]{:S(2)}) collective-permute-start(f32[80,80]{1,0:T(8,128)S(1)} %get-tuple-element.50.total), channel_id=1, source_target_pairs={{0,8},{4,12},{8,0},{12,4},{16,24},{20,28},{24,16},{28,20},{1,9},{5... | collective-permute-start | bytes 76808 | tf_op jit(solution)/shard_map/ppermute | solution.py:323
  14.0 1.5 %gram_1.1 = (f32[80,512]{1,0:T(8,128)S(1)}, f32[80,80]{1,0:T(8,128)S(1)}) custom-call(bf16[6,80,2048]{2,1,0:T(8,128)(2,1)S(1)} %get-tuple-element.53.refs_0_, bf16[6,80,2048]{2,1,0:T(8,128)(2,1)S(1)} %get-tuple-element.54.refs_1_.refs_0_, f32[1280,80]{1,0:T(8,128)S(1)} %get-tuple-element.45.refs_2_.refs_3_.suffixes, f32[80,80]{1,0:T(8,128)S(1)} %get-tuple-element.51.refs_3_.later), custom_call_target="tpu_custom_call" | custom-call | bytes 5400000 | tf_op jit(solution)/shard_map/gram_1/pallas_call | solution.py:351
  15.6 0.5 %collective-permute-done.1.other = f32[80,80]{1,0:T(8,128)S(1)} collective-permute-done((f32[80,80]{1,0:T(8,128)S(1)}, f32[80,80]{1,0:T(8,128)S(1)}, u32[]{:S(2)}, u32[]{:S(2)}) %collective-permute-start.1) | collective-permute-done | bytes 25632 | tf_op jit(solution)/shard_map/ppermute | solution.py:323
  16.0 0.3 join_1.1
  16.3 3.1 %collective-permute-start.2 = (f32[80,80]{1,0:T(8,128)S(1)}, f32[80,80]{1,0:T(8,128)S(1)}, u32[]{:S(2)}, u32[]{:S(2)}) collective-permute-start(f32[80,80]{1,0:T(8,128)S(1)} %get-tuple-element.57), channel_id=1, source_target_pairs={{0,16},{4,20},{8,24},{12,28},{16,0},{20,4},{24,8},{28,12},{1,17},{... | collective-permute-start | bytes 76808 | tf_op jit(solution)/shard_map/ppermute | solution.py:323
  19.4 1.1 %gram_last.1 = (f32[80,1408]{1,0:T(8,128)S(1)}, f32[80,80]{1,0:T(8,128)S(1)}) custom-call(bf16[4,80,2048]{2,1,0:T(8,128)(2,1)S(1)} %get-tuple-element.58.refs_0_.refs_1_, bf16[4,80,2048]{2,1,0:T(8,128)(2,1)S(1)} %get-tuple-element.59.refs_1_, f32[1280,80]{1,0:T(8,128)S(1)} %get-tuple-element.45.refs_2_.refs_3_.suffixes, ...), custom_call_target="tpu_custom_call" | custom-call | bytes 5400000 | tf_op jit(solution)/shard_map/gram_last/pallas_call | solution.py:366
  20.5 0.1 collective-permute-start.3
  20.6 0.8 %collective-permute-done.2.other = f32[80,80]{1,0:T(8,128)S(1)} collective-permute-done((f32[80,80]{1,0:T(8,128)S(1)}, f32[80,80]{1,0:T(8,128)S(1)}, u32[]{:S(2)}, u32[]{:S(2)}) %collective-permute-start.2) | collective-permute-done | bytes 25632 | tf_op jit(solution)/shard_map/ppermute | solution.py:323
  21.3 1.1 %carries.1 = (bf16[6,240,240]{2,1,0:T(8,128)(2,1)S(1)}, bf16[6,240,240]{2,1,0:T(8,128)(2,1)S(1)}, bf16[2,1280,80]{2,1,0:T(8,128)(2,1)S(1)}) custom-call(f32[1280,80]{1,0:T(8,128)S(1)} %get-tuple-element.45.refs_2_.refs_3_.suffixes, f32[80,80]{1,0:T(8,128)S(1)} %get-tuple-element.56.refs_7_.later, f32[80,80]{1,0:T(8,128)S(1)} %collective-permute-done.2.other, ...), custom_call_target="tpu_custom_call" | custom-call | bytes 5400000 | tf_op jit(solution)/shard_map/carries/pallas_call | solution.py:374
  22.4 0.0 collective-permute-done.3.refs_1_
  22.4 0.1 collective-permute-start.5
  22.5 1.9 %collective-permute-start.4 = (f32[80,80]{1,0:T(8,128)S(1)}, f32[80,80]{1,0:T(8,128)S(1)}, u32[]{:S(2)}, u32[]{:S(2)}) collective-permute-start(f32[80,80]{1,0:T(8,128)S(1)} %get-tuple-element.66.refs_1_.refs_0_), channel_id=1, source_target_pairs={{0,2},{1,3},{2,0},{3,1},{4,6},{5,7},{6,4},{7,5},{8,10},{9,11},{10,... | collective-permute-start | bytes 76808 | tf_op jit(solution)/shard_map/ppermute | solution.py:327
  24.4 1.6 %smoothed_0.1 = (bf16[16,80,2048]{2,1,0:T(8,128)(2,1)}, f32[8,128]{1,0:T(8,128)S(1)}) custom-call(bf16[6,240,240]{2,1,0:T(8,128)(2,1)S(1)} %get-tuple-element.63.factors, bf16[6,80,2048]{2,1,0:T(8,128)(2,1)S(1)} %get-tuple-element.47.refs_0_, f32[80,80]{1,0:T(8,128)S(1)} %get-tuple-element.66.refs_1_.refs_0_), custom_call_target="tpu_custom_call" | custom-call | bytes 5400000 | tf_op jit(solution)/shard_map/smoothed_0/pallas_call | solution.py:396
  26.0 0.6 %collective-permute-done.4.refs_1_ = f32[80,80]{1,0:T(8,128)S(1)} collective-permute-done((f32[80,80]{1,0:T(8,128)S(1)}, f32[80,80]{1,0:T(8,128)S(1)}, u32[]{:S(2)}, u32[]{:S(2)}) %collective-permute-start.4) | collective-permute-done | bytes 25632 | tf_op jit(solution)/shard_map/ppermute | solution.py:327
  26.6 0.0 collective-permute-done.5.refs_3_
  26.6 0.1 add.3.refs_0_
  26.7 1.9 %collective-permute-start.8 = (f32[80,1408]{1,0:T(8,128)S(1)}, f32[80,1408]{1,0:T(8,128)S(1)}, u32[]{:S(2)}, u32[]{:S(2)}) collective-permute-start(f32[80,1408]{1,0:T(8,128)S(1)} %add.3.refs_0_), channel_id=1, source_target_pairs={{0,2},{1,3},{2,0},{3,1},{4,6},{5,7},{6,4},{7,5},{8,10},{9,11},{10,... | collective-permute-start | bytes 1351688 | tf_op jit(solution)/shard_map/ppermute | solution.py:327
  28.6 1.5 %collective-permute-start.6 = (f32[80,80]{1,0:T(8,128)S(1)}, f32[80,80]{1,0:T(8,128)S(1)}, u32[]{:S(2)}, u32[]{:S(2)}) collective-permute-start(f32[80,80]{1,0:T(8,128)S(1)} %get-tuple-element.69.refs_2_.own), channel_id=1, source_target_pairs={{0,4},{4,0},{8,12},{12,8},{16,20},{20,16},{24,28},{28,24},{1,5},{5... | collective-permute-start | bytes 76808 | tf_op jit(solution)/shard_map/ppermute | solution.py:323
  30.1 2.1 %smoothed_1.1 = (bf16[16,80,2048]{2,1,0:T(8,128)(2,1)}, f32[8,128]{1,0:T(8,128)S(1)}) custom-call(bf16[6,240,240]{2,1,0:T(8,128)(2,1)S(1)} %get-tuple-element.63.factors, bf16[6,80,2048]{2,1,0:T(8,128)(2,1)S(1)} %get-tuple-element.53.refs_0_, bf16[4,80,2048]{2,1,0:T(8,128)(2,1)S(1)} %get-tuple-element.58.refs_0_.refs_1_, ...), custom_call_target="tpu_custom_call", output_to_operand_aliasing={{0}: (4, {})} | custom-call | bytes 5400000 | tf_op jit(solution)/shard_map/smoothed_1/pallas_call | solution.py:396
  32.1 0.5 %collective-permute-done.6.other = f32[80,80]{1,0:T(8,128)S(1)} collective-permute-done((f32[80,80]{1,0:T(8,128)S(1)}, f32[80,80]{1,0:T(8,128)S(1)}, u32[]{:S(2)}, u32[]{:S(2)}) %collective-permute-start.6) | collective-permute-done | bytes 25632 | tf_op jit(solution)/shard_map/ppermute | solution.py:323
  32.6 0.2 pass_0.1
  32.8 1.6 %collective-permute-start.7 = (f32[80,80]{1,0:T(8,128)S(1)}, f32[80,80]{1,0:T(8,128)S(1)}, u32[]{:S(2)}, u32[]{:S(2)}) collective-permute-start(f32[80,80]{1,0:T(8,128)S(1)} %get-tuple-element.75.refs_1_.own), channel_id=1, source_target_pairs={{0,8},{4,12},{8,0},{12,4},{16,24},{20,28},{24,16},{28,20},{1,9},{5... | collective-permute-start | bytes 76808 | tf_op jit(solution)/shard_map/ppermute | solution.py:323
  34.4 1.6 %ensemble_grad_0.1 = (bf16[16,80,2048]{2,1,0:T(8,128)(2,1)}, f32[8,128]{1,0:T(8,128)S(1)}) custom-call(bf16[6,240,240]{2,1,0:T(8,128)(2,1)S(1)} %get-tuple-element.72.factors, bf16[6,80,2048]{2,1,0:T(8,128)(2,1)S(1)} %get-tuple-element.48.refs_1_.refs_0_, f32[80,80]{1,0:T(8,128)S(1)} %get-tuple-element.75.refs_1_.own), custom_call_target="tpu_custom_call" | custom-call | bytes 5400000 | tf_op jit(solution)/shard_map/ensemble_grad_0/pallas_call | solution.py:396
  36.0 0.8 %collective-permute-done.7.other = f32[80,80]{1,0:T(8,128)S(1)} collective-permute-done((f32[80,80]{1,0:T(8,128)S(1)}, f32[80,80]{1,0:T(8,128)S(1)}, u32[]{:S(2)}, u32[]{:S(2)}) %collective-permute-start.7) | collective-permute-done | bytes 25632 | tf_op jit(solution)/shard_map/ppermute | solution.py:323
  36.9 0.2 pass_1.1
  37.1 2.7 %collective-permute-start.9 = (f32[80,80]{1,0:T(8,128)S(1)}, f32[80,80]{1,0:T(8,128)S(1)}, u32[]{:S(2)}, u32[]{:S(2)}) collective-permute-start(f32[80,80]{1,0:T(8,128)S(1)} %get-tuple-element.79.refs_2_), channel_id=1, source_target_pairs={{0,16},{4,20},{8,24},{12,28},{16,0},{20,4},{24,8},{28,12},{1,17},{... | collective-permute-start | bytes 76808 | tf_op jit(solution)/shard_map/ppermute | solution.py:323
  39.7 2.0 %ensemble_grad_1.1 = (bf16[16,80,2048]{2,1,0:T(8,128)(2,1)}, f32[8,128]{1,0:T(8,128)S(1)}) custom-call(bf16[6,240,240]{2,1,0:T(8,128)(2,1)S(1)} %get-tuple-element.72.factors, bf16[6,80,2048]{2,1,0:T(8,128)(2,1)S(1)} %get-tuple-element.54.refs_1_.refs_0_, bf16[4,80,2048]{2,1,0:T(8,128)(2,1)S(1)} %get-tuple-element.59.refs_1_, ...), custom_call_target="tpu_custom_call", output_to_operand_aliasing={{0}: (4, {})} | custom-call | bytes 5400000 | tf_op jit(solution)/shard_map/ensemble_grad_1/pallas_call | solution.py:396
  41.8 0.3 collective-permute-done.9.refs_2_
  42.1 0.0 collective-permute-done.8.refs_1_
  42.1 2.5 %transform_grad.1 = f32[16,80,80]{2,1,0:T(8,128)} custom-call(f32[80,1408]{1,0:T(8,128)S(1)} %add.3.refs_0_, f32[80,1408]{1,0:T(8,128)S(1)} %collective-permute-done.8.refs_1_, f32[80,80]{1,0:T(8,128)S(1)} %collective-permute-done.9.refs_2_, f32[80,80]{1,0:T(8,128)S(1)} %get-tuple-element.83.refs_3_, f32[80,80]{1,0:T(8,128)S(1)} %get-tuple-element.84.refs_4_, ...), custom_call_target="tpu_custom_call" | custom-call | bytes 7200000 | tf_op jit(solution)/shard_map/transform_grad/pallas_call | solution.py:426
  (4 shorter events, 0.0 us)
Async XLA Ops:
  6.6 5.0 %collective-permute-start = (f32[80,80]{1,0:T(8,128)S(1)}, f32[80,80]{1,0:T(8,128)S(1)}, u32[]{:S(2)}, u32[]{:S(2)}) collective-permute-start(f32[80,80]{1,0:T(8,128)S(1)} %get-tuple-element.46.total), channel_id=1, source_target_pairs={{0,4},{4,0},{8,12},{12,8},{16,20},{20,16},{24,28},{28,24},{1,5},{5... | collective-permute-start | bytes 76808 | tf_op jit(solution)/shard_map/ppermute | solution.py:323
  11.9 4.1 %collective-permute-start.1 = (f32[80,80]{1,0:T(8,128)S(1)}, f32[80,80]{1,0:T(8,128)S(1)}, u32[]{:S(2)}, u32[]{:S(2)}) collective-permute-start(f32[80,80]{1,0:T(8,128)S(1)} %get-tuple-element.50.total), channel_id=1, source_target_pairs={{0,8},{4,12},{8,0},{12,4},{16,24},{20,28},{24,16},{28,20},{1,9},{5... | collective-permute-start | bytes 76808 | tf_op jit(solution)/shard_map/ppermute | solution.py:323
  16.3 5.1 %collective-permute-start.2 = (f32[80,80]{1,0:T(8,128)S(1)}, f32[80,80]{1,0:T(8,128)S(1)}, u32[]{:S(2)}, u32[]{:S(2)}) collective-permute-start(f32[80,80]{1,0:T(8,128)S(1)} %get-tuple-element.57), channel_id=1, source_target_pairs={{0,16},{4,20},{8,24},{12,28},{16,0},{20,4},{24,8},{28,12},{1,17},{... | collective-permute-start | bytes 76808 | tf_op jit(solution)/shard_map/ppermute | solution.py:323
  20.5 1.9 %collective-permute-start.3 = (f32[80,80]{1,0:T(8,128)S(1)}, f32[80,80]{1,0:T(8,128)S(1)}, u32[]{:S(2)}, u32[]{:S(2)}) collective-permute-start(f32[80,80]{1,0:T(8,128)S(1)} %get-tuple-element.62._.refs_0_), channel_id=1, source_target_pairs={{0,1},{1,0},{2,3},{3,2},{4,5},{5,4},{6,7},{7,6},{8,9},{9,8},{10,11... | collective-permute-start | bytes 76808 | tf_op jit(solution)/shard_map/ppermute | solution.py:323
  22.4 4.2 %collective-permute-start.5 = (f32[80,1408]{1,0:T(8,128)S(1)}, f32[80,1408]{1,0:T(8,128)S(1)}, u32[]{:S(2)}, u32[]{:S(2)}) collective-permute-start(f32[80,1408]{1,0:T(8,128)S(1)} %get-tuple-element.68), channel_id=1, source_target_pairs={{0,1},{1,0},{2,3},{3,2},{4,5},{5,4},{6,7},{7,6},{8,9},{9,8},{10,11... | collective-permute-start | bytes 1351688 | tf_op jit(solution)/shard_map/ppermute | solution.py:323
  22.5 4.1 %collective-permute-start.4 = (f32[80,80]{1,0:T(8,128)S(1)}, f32[80,80]{1,0:T(8,128)S(1)}, u32[]{:S(2)}, u32[]{:S(2)}) collective-permute-start(f32[80,80]{1,0:T(8,128)S(1)} %get-tuple-element.66.refs_1_.refs_0_), channel_id=1, source_target_pairs={{0,2},{1,3},{2,0},{3,1},{4,6},{5,7},{6,4},{7,5},{8,10},{9,11},{10,... | collective-permute-start | bytes 76808 | tf_op jit(solution)/shard_map/ppermute | solution.py:327
  26.7 15.4 %collective-permute-start.8 = (f32[80,1408]{1,0:T(8,128)S(1)}, f32[80,1408]{1,0:T(8,128)S(1)}, u32[]{:S(2)}, u32[]{:S(2)}) collective-permute-start(f32[80,1408]{1,0:T(8,128)S(1)} %add.3.refs_0_), channel_id=1, source_target_pairs={{0,2},{1,3},{2,0},{3,1},{4,6},{5,7},{6,4},{7,5},{8,10},{9,11},{10,... | collective-permute-start | bytes 1351688 | tf_op jit(solution)/shard_map/ppermute | solution.py:327
  28.6 4.0 %collective-permute-start.6 = (f32[80,80]{1,0:T(8,128)S(1)}, f32[80,80]{1,0:T(8,128)S(1)}, u32[]{:S(2)}, u32[]{:S(2)}) collective-permute-start(f32[80,80]{1,0:T(8,128)S(1)} %get-tuple-element.69.refs_2_.own), channel_id=1, source_target_pairs={{0,4},{4,0},{8,12},{12,8},{16,20},{20,16},{24,28},{28,24},{1,5},{5... | collective-permute-start | bytes 76808 | tf_op jit(solution)/shard_map/ppermute | solution.py:323
  32.8 4.1 %collective-permute-start.7 = (f32[80,80]{1,0:T(8,128)S(1)}, f32[80,80]{1,0:T(8,128)S(1)}, u32[]{:S(2)}, u32[]{:S(2)}) collective-permute-start(f32[80,80]{1,0:T(8,128)S(1)} %get-tuple-element.75.refs_1_.own), channel_id=1, source_target_pairs={{0,8},{4,12},{8,0},{12,4},{16,24},{20,28},{24,16},{28,20},{1,9},{5... | collective-permute-start | bytes 76808 | tf_op jit(solution)/shard_map/ppermute | solution.py:323
  37.1 5.0 %collective-permute-start.9 = (f32[80,80]{1,0:T(8,128)S(1)}, f32[80,80]{1,0:T(8,128)S(1)}, u32[]{:S(2)}, u32[]{:S(2)}) collective-permute-start(f32[80,80]{1,0:T(8,128)S(1)} %get-tuple-element.79.refs_2_), channel_id=1, source_target_pairs={{0,16},{4,20},{8,24},{12,28},{16,0},{20,4},{24,8},{28,12},{1,17},{... | collective-permute-start | bytes 76808 | tf_op jit(solution)/shard_map/ppermute | solution.py:323

commit v3 on v2

--- a/solution.py
+++ b/solution.py
@@ -63,7 +63,7 @@
         self.groups = [
             (start, min(start + self.stack, count)) for start in range(0, count, self.stack)
         ]
-        bounds = [-(-len(self.groups) * at // PIECES) for at in range(PIECES + 1)]
+        bounds = [len(self.groups) * at // PIECES for at in range(PIECES + 1)]
         self.piece_groups = [self.groups[a:b] for a, b in zip(bounds, bounds[1:])]
         self.pieces = [(part[0][0], part[-1][1]) for part in self.piece_groups]
         self.first_group = bounds[:-1]
@@ -84,31 +84,37 @@
     return rows == columns
 
 
-def loads(values, buffers, sems, plan):
-    copies = []
-    for (base, _), buffer, groups in zip(plan.pieces, buffers, plan.piece_groups):
-        for start, stop in groups:
-            part = buffer.at[start - base : stop - base]
-            copies.append(pltpu.make_async_copy(values.at[start:stop], part, sems.at[len(copies)]))
+def loads(plan, piece, values, buffer, sems):
+    base = plan.pieces[piece][0]
+    copies = [
+        pltpu.make_async_copy(values.at[start:stop], buffer.at[start - base : stop - base], sems.at[at])
+        for at, (start, stop) in enumerate(plan.piece_groups[piece])
+    ]
     for copy in copies:
         copy.start()
     return copies
 
 
-def chain_kernel(plan, transforms, ensembles, cotangents, suffixes, total, steps, *refs):
+def chain_kernel(
+    plan, transforms, ensembles, cotangents, suffixes, total, kept, ens, cot, sem, ens_sem, cot_sem
+):
     count, members = plan.count, plan.members
-    kept, runs, sem, ens_sem, cot_sem = refs[2 * PIECES :]
     read = pltpu.make_async_copy(transforms, kept, sem)
     read.start()
-    more = loads(ensembles, refs[:PIECES], ens_sem, plan)
-    more += loads(cotangents, refs[PIECES : 2 * PIECES], cot_sem, plan)
     read.wait()
+    more = loads(plan, 0, ensembles, ens, ens_sem) + loads(plan, 0, cotangents, cot, cot_sem)
     for at in range(count):
         suffixes[plan.rows(at, at + 1)] = kept[at]
-        if at + 1 < count:
-            runs[plan.rows(at + 1, at + 2)] = kept[at].T
     suffix_scan(suffixes, count, members, count)
     total[...] = suffixes[plan.rows(0, 1)]
+    for copy in more:
+        copy.wait()
+
+
+def windows_kernel(plan, kept, _, steps, runs):
+    count = plan.count
+    for at in range(count - 1):
+        runs[plan.rows(at + 1, at + 2)] = kept[at].T
     number = 0
     width = 1
     while width < count:
@@ -122,8 +128,6 @@
                 rows = plan.rows(start + width, min(start + 2 * width, count))
                 runs[rows] = mul_exact(runs[rows], runs[plan.rows(start + width - 1, start + width)])
         width *= 2
-    for copy in more:
-        copy.wait()
 
 
 def count_steps(count):
@@ -135,27 +139,16 @@
     return total
 
 
-def gram_kernel(plan, piece, *refs):
+def core_index():
+    return lax.rem(lax.axis_index("space"), 2)
+
+
+def gram_of(plan, piece, cot, ens, suffixes, whole, ready=lambda: None):
     members = plan.members
-    ens, cot, suffixes = refs[:3]
-    refs = refs[3:]
-    last = piece == PIECES - 1
-    if last:
-        earlier, refs = refs[: 2 * piece], refs[2 * piece :]
-    _, grams, offsets = refs
     base = plan.pieces[piece][0]
     offset = jnp.zeros((members, members), F32)
-    first = plan.first_group[piece]
-    if last:
-        for at in range(piece):
-            group = plan.first_group[at]
-            lanes = slice(plan.lanes(group).start, plan.lanes(plan.first_group[at + 1]).start)
-            grams[:, lanes] = earlier[2 * at][...]
-            offset = offset + earlier[2 * at + 1][...]
-        origin = 0
-    else:
-        origin = plan.lanes(first).start
     for at, (start, stop) in enumerate(plan.piece_groups[piece]):
+        ready()
         size = (stop - start) * members
         stacked = [ref[start - base : stop - base].reshape(size, ref.shape[2]) for ref in (cot, ens)]
         wide = jnp.where(on_blocks(members, size), mul(*stacked, ROWS), 0.0)
@@ -163,10 +156,52 @@
         for i in range(1, stop - start):
             gram = gram + wide[i * members : (i + 1) * members]
         offset = offset + mul_exact(gram, suffixes[plan.rows(start, stop)])
-        lanes = plan.lanes(first + at)
+        lanes = plan.lanes(plan.first_group[piece] + at)
         width = lanes.stop - lanes.start
-        grams[:, lanes.start - origin : lanes.stop - origin] = jnp.pad(gram, ((0, 0), (0, width - size)))
-    offsets[...] = offset
+        whole[:, lanes] = jnp.pad(gram, ((0, 0), (0, width - size)))
+    return offset
+
+
+def early_gram_kernel(plan, ensembles, cotangents, suffixes, ens, cot, whole, offset, *refs):
+    buffers, sems = refs[: 2 * (PIECES - 1)], refs[2 * (PIECES - 1) :]
+    copies = []
+    for piece in range(1, PIECES):
+        pair = buffers[2 * piece - 2 : 2 * piece]
+        own = sems[2 * piece - 2 : 2 * piece]
+        copies.append(list(zip(
+            loads(plan, piece, ensembles, pair[0], own[0]),
+            loads(plan, piece, cotangents, pair[1], own[1]),
+        )))
+    total = gram_of(plan, 0, cot, ens, suffixes, whole)
+    for piece in range(1, PIECES - 1):
+        waiting = iter(copies[piece - 1])
+
+        def ready():
+            for copy in next(waiting):
+                copy.wait()
+
+        ens, cot = buffers[2 * piece - 2 : 2 * piece]
+        total = total + gram_of(plan, piece, cot, ens, suffixes, whole, ready)
+    offset[...] = total
+    for pair in copies[-1]:
+        for copy in pair:
+            copy.wait()
+
+
+def late_gram_kernel(
+    plan, ens, cot, suffixes, early, offset, _,
+    gram_kept, gram_sent, offset_kept, offset_sent, whole, offsets,
+):
+    members = plan.members
+    whole[:, : early.shape[1]] = early[...]
+    offsets[...] = offset[...] + gram_of(plan, PIECES - 1, cot, ens, suffixes, whole)
+    half = members // 2
+    core = lax.rem(lax.axis_index("space"), 2)
+    mine, other = pl.ds(core * half, half), pl.ds((1 - core) * half, half)
+    gram_kept[...] = whole[mine]
+    gram_sent[...] = whole[other]
+    offset_kept[...] = offsets[mine]
+    offset_sent[...] = offsets[other]
 
 
 def upper_half(level):
@@ -183,20 +218,25 @@
     new_before[...] = jnp.where(upper, mul_exact(other[...], before[...]), before[...])
 
 
-def sum_kernel(number, *refs):
-    out = refs[-2]
+def sum_kernel(number, out, *refs):
     total = refs[0][...]
     for ref in refs[1:number]:
         total = total + ref[...]
-    out[...] = total
-
-
-def pass_kernel(level, own, other, carry, upper_total, before, _, new_own, new_carry):
+    refs[out][...] = total
+
+
+def pass_kernel(level, last, own, other, carry, upper_total, before, *refs):
+    new_own, new_carry = refs[2:4] if last else refs[1:3]
     upper = upper_half(level)
     left = jnp.where(upper, other[...], own[...])
     right = jnp.where(upper, own[...], other[...])
     new_own[...] = mul_exact(left, upper_total[...]) + right
     new_carry[...] = carry[...] + jnp.where(upper, mul_exact(left, before[...]), 0.0)
+
+
+def last_pass_kernel(level, other, carry, before, _, new_carry):
+    added = mul_exact(other[...], before[...])
+    new_carry[...] = carry[...] + jnp.where(upper_half(level), added, 0.0)
 
 
 def carry_kernel(plan, level, suffixes, later, other, _, ens_factors, cot_factors, follow):
@@ -227,9 +267,9 @@
     chunk = out_buf.shape[2] // 2
     writes = []
     for values, piece in zip(refs, pieces):
+        first = plan.pieces[piece][0]
         for at, (start, stop) in enumerate(plan.piece_groups[piece]):
             size = (stop - start) * members
-            first = plan.pieces[piece][0]
             for side in range(2):
                 columns = slice(side * chunk, (side + 1) * chunk)
                 stacked = values[start - first : stop - first, :, columns].reshape(size, chunk)
@@ -248,22 +288,22 @@
         copy.wait()
 
 
-def final_kernel(plan, level, scale, number, *refs):
-    messages = refs[:number]
-    other, carry, before, follow, steps, _, out, buffer, sems = refs[number:]
+def final_kernel(
+    plan, scale, gram_mine, gram_other, carry_mine, carry_other, follow, steps, _, out, buffer, sems
+):
     count, members = plan.count, plan.members
-    entering = carry[...] + jnp.where(
-        upper_half(level), mul_exact(other[...], before[...]), 0.0
-    )
+    first = lax.rem(lax.axis_index("space"), 2) == 0
+
+    def whole(mine, other):
+        return jnp.concatenate([jnp.where(first, mine, other), jnp.where(first, other, mine)], axis=0)
+
     totals = []
     for at, (start, stop) in enumerate(plan.groups):
-        wide = messages[0][:, plan.lanes(at)]
-        for ref in messages[1:]:
-            wide = wide + ref[:, plan.lanes(at)]
-        tall = wide.T
+        lanes = plan.lanes(at)
+        tall = whole(gram_mine[:, lanes], gram_other[:, lanes]).T
         for i in range(stop - start):
             totals.append(tall[i * members : (i + 1) * members])
-    totals[0] = totals[0] + entering.T
+    totals[0] = totals[0] + whole(carry_mine[...], carry_other[...]).T
     number = 0
     width = 1
     while width < count:
@@ -328,67 +368,87 @@
             for d in range(1, chips)
         ]
 
-    steps_shape = shape(2, count_steps(count) * members, members, kind=BF16)
-    buffers = [shape(last - first, members, cells, kind=BF16) for first, last in plan.pieces] * 2
-    suffixes, total, steps, *loaded = call(
+    def piece_shape(piece):
+        first, last = plan.pieces[piece]
+        return shape(last - first, members, cells, kind=BF16)
+
+    def piece_sems(piece):
+        return [pltpu.SemaphoreType.DMA((len(plan.piece_groups[piece]),))] * 2
+
+    suffixes, total, kept, *first_part = call(
         functools.partial(chain_kernel, plan),
-        [shape(count * members, members), square, steps_shape] + buffers,
-        [HBM] * 3, [VMEM] * (3 + len(buffers)),
-        [pltpu.VMEM((count, members, members), F32), pltpu.VMEM((count * members, members), F32),
-         pltpu.SemaphoreType.DMA] + [pltpu.SemaphoreType.DMA((len(plan.groups),))] * 2,
-        4, "transform_chain",
+        [shape(count * members, members), square, shape(count, members, members)] + [piece_shape(0)] * 2,
+        [HBM] * 3, [VMEM] * 5, [pltpu.SemaphoreType.DMA] + piece_sems(0), 3.5, "transform_chain",
     )(transforms, ensembles, cotangents)
-    parts = list(zip(loaded[:PIECES], loaded[PIECES:]))
-
+
+    half = members // 2
     later = before = jnp.eye(members, dtype=F32)
-    grams, uppers, befores = [], [], []
-    done = suffixes
-    for level in range(levels):
-        other = exchange(total, "tm", blocks, 1 << level)
-        if level < PIECES - 1:
-            first, last = plan.first_group[level : level + 2]
-            width = plan.lanes(last).start - plan.lanes(first).start
-            sums = call(
-                functools.partial(gram_kernel, plan, level),
-                [shape(members, width), square],
-                [VMEM] * 3 + [ANY], [VMEM] * 2, [], 1.5, f"gram_{level}",
-            )(*parts[level], suffixes, done)
-            grams += sums
-            done = sums[1]
+    uppers, befores = [], []
+
+    def join(level, total, other, later, before, after):
         befores.append(before)
-        if level < levels - 1:
-            total, later, before, upper = call(
-                functools.partial(join_kernel, level),
-                [square] * 4, [VMEM] * 4 + [ANY], [VMEM] * 4, [], 0.3, f"join_{level}",
-            )(total, other, later, before, done)
-            uppers.append(upper)
-            done = later
-    gram, offset = call(
-        functools.partial(gram_kernel, plan, PIECES - 1),
-        [shape(members, plan.width), square],
-        [VMEM] * (3 + len(grams)) + [ANY], [VMEM] * 2, [], 1.5, "gram_last",
-    )(*parts[-1], suffixes, *grams, done)
-    offset_core = exchange(offset, "space", lanes, 1)
-
+        *new, upper = call(
+            functools.partial(join_kernel, level),
+            [square] * 4, [VMEM] * 4 + [ANY], [VMEM] * 4, [], 0.3, f"join_{level}",
+        )(total, other, later, before, after)
+        uppers.append(upper)
+        return new
+
+    def add(values, after, name, *through):
+        number = len(values)
+        return call(
+            functools.partial(sum_kernel, number, number + 1 + len(through)),
+            [shape(*values[0].shape)] + [shape(*value.shape) for value in through],
+            [VMEM] * number + [ANY] * (1 + len(through)), [VMEM] + [ANY] * len(through), [], 0.1, name,
+            aliases={number + 1 + at: 1 + at for at in range(len(through))},
+        )(*values, after, *through)
+
+    other = exchange(total, "tm", blocks, 1)
+    early_width = plan.lanes(plan.first_group[-1]).start
+    early, offset, *loaded = call(
+        functools.partial(early_gram_kernel, plan),
+        [shape(members, early_width), square]
+        + [piece_shape(piece) for piece in range(1, PIECES) for _ in range(2)],
+        [HBM] * 2 + [VMEM] * 3, [VMEM] * (2 * PIECES),
+        [sem for piece in range(1, PIECES) for sem in piece_sems(piece)], 3, "early_gram",
+    )(ensembles, cotangents, suffixes, *first_part)
+    parts = [first_part] + [loaded[at : at + 2] for at in range(0, len(loaded), 2)]
+    total, later, before = join(0, total, other, later, before, offset)
+
+    other = exchange(total, "tm", blocks, 2)
+    gram, gram_sent, offset, offset_sent = call(
+        functools.partial(late_gram_kernel, plan),
+        [shape(half, plan.width)] * 2 + [shape(half, members)] * 2,
+        [VMEM] * 5 + [ANY], [VMEM] * 4,
+        [pltpu.VMEM((members, plan.width), F32), pltpu.VMEM((members, members), F32)],
+        1.2, "late_gram",
+    )(*parts[-1], suffixes, early, offset, total)
+    offset_core = exchange(offset_sent, "space", lanes, 1)
+    for level in range(1, levels - 1):
+        total, later, before = join(level, total, other, later, before, offset)
+        other = exchange(total, "tm", blocks, 2 << level)
+    befores.append(before)
+
+    offset, gram_sent = add([offset, offset_core], total, "chip_offset", gram_sent)
+    gram_core = exchange(gram_sent, "space", lanes, 1)
+    offsets = [offset] + around(offset)
+    steps = call(
+        functools.partial(windows_kernel, plan),
+        shape(2, count_steps(count) * members, members, kind=BF16), [VMEM, ANY], VMEM,
+        [pltpu.VMEM((count * members, members), F32)], 1.5, "windows",
+    )(kept, offset)
+    own, gram_core, other = add(offsets, steps, "own_offset", gram_core, other)
+
+    other_own = exchange(own, "tm", blocks, 1)
+    gram = gram + gram_core
+    grams = around(gram)
     size = plan.stack * members
     ens_factors, cot_factors, follow = call(
         functools.partial(carry_kernel, plan, levels - 1),
         [shape(len(plan.groups), size, size, kind=BF16)] * 2
         + [shape(2, count * members, members, kind=BF16)],
-        [VMEM] * 3 + [ANY], [VMEM] * 3, [], 1.5, "carries",
-    )(suffixes, later, other, offset)
-
-    def add(values, after, name, through):
-        number = len(values)
-        return call(
-            functools.partial(sum_kernel, number),
-            [shape(*values[0].shape), shape(*through.shape)],
-            [VMEM] * number + [ANY] * 2, [VMEM, ANY], [], 0.1, name, aliases={number + 1: 1},
-        )(*values, after, through)
-
-    offset, gram = add([offset, offset_core], follow, "chip_offset", gram)
-    gram_core = exchange(gram, "space", lanes, 1)
-    offsets = [offset] + around(offset)
+        [VMEM] * 3 + [ANY], [VMEM] * 3, [], 1.0, "carries",
+    )(suffixes, later, other, own)
 
     def apply(factors, which, pieces, out, after, name):
         first, last = plan.pieces[pieces[0]][0], plan.pieces[pieces[-1]][1]
@@ -397,39 +457,43 @@
             functools.partial(apply_kernel, plan, pieces),
             [shape(count, members, cells, kind=BF16), shape(8, 128)],
             [VMEM] * (1 + len(pieces)) + [ANY] + [HBM] * len(out), [HBM, VMEM],
-            [pltpu.VMEM((last - first, members, cells), BF16),
-             pltpu.SemaphoreType.DMA((number,))],
-            1.5, name, aliases={2 + len(pieces): 0} if out else None,
+            [pltpu.VMEM((last - first, members, cells), BF16), pltpu.SemaphoreType.DMA((number,))],
+            1.8, name, aliases={2 + len(pieces): 0} if out else None,
         )(factors, *(parts[piece][which] for piece in pieces), after, *out)
 
-    later_pieces = tuple(range(1, PIECES))
-    smoothed, done = apply(ens_factors, 0, (0,), (), offset, "smoothed_0")
-    own, gram_core = add(offsets, done, "own_offset", gram_core)
-    gram = gram + gram_core
-    grams = [gram] + around(gram)
-    carry = jnp.zeros((members, members), F32)
-    for level in range(levels):
-        other = exchange(own, "tm", blocks, 1 << level)
+    front, rear = tuple(range(PIECES - 1)), (PIECES - 1,)
+    smoothed, done = apply(ens_factors, 0, front, (), follow, "smoothed_0")
+    carry = jnp.zeros((half, members), F32)
+    for level in range(levels - 1):
+        last = level == levels - 2
+        own, carry, *rest = call(
+            functools.partial(pass_kernel, level, last),
+            [shape(half, members)] * 2 + [shape(half, plan.width)] * last,
+            [VMEM] * 5 + [ANY] * (1 + last), [VMEM] * 2 + [ANY] * last, [], 0.3, f"pass_{level}",
+            aliases={6: 2} if last else None,
+        )(own, other_own, carry, uppers[level], befores[level], done, *grams[:last])
+        other_own = exchange(own, "tm", blocks, 2 << level)
         if level == 0:
-            smoothed, done = apply(ens_factors, 0, later_pieces, (smoothed,), own, "smoothed_1")
+            smoothed, done = apply(ens_factors, 0, rear, (smoothed,), own, "smoothed_1")
         if level == 1:
-            ensemble_grad, done = apply(cot_factors, 1, (0,), (), own, "ensemble_grad_0")
-        if level == 2:
-            ensemble_grad, done = apply(
-                cot_factors, 1, later_pieces, (ensemble_grad,), own, "ensemble_grad_1"
-            )
-        if level < levels - 1:
-            own, carry = call(
-                functools.partial(pass_kernel, level),
-                [square] * 2, [VMEM] * 5 + [ANY], [VMEM] * 2, [], 0.3, f"pass_{level}",
-            )(own, other, carry, uppers[level], befores[level], done)
+            ensemble_grad, done = apply(cot_factors, 1, front, (), own, "ensemble_grad_0")
+    grams[0] = rest[0]
+    for part in grams:
+        gram = gram + part
+    gram_other = exchange(gram, "space", lanes, 1)
+    carry = call(
+        functools.partial(last_pass_kernel, levels - 1),
+        shape(half, members), [VMEM] * 3 + [ANY], VMEM, [], 0.2, "pass_last",
+    )(other_own, carry, befores[-1], done)
+    carry_other = exchange(carry, "space", lanes, 1)
+    ensemble_grad, done = apply(cot_factors, 1, rear, (ensemble_grad,), carry, "ensemble_grad_1")
     transform_grad = call(
-        functools.partial(final_kernel, plan, levels - 1, scale, chips),
+        functools.partial(final_kernel, plan, scale),
         shape(count, members, members),
-        [VMEM] * (chips + 5) + [ANY], HBM,
+        [VMEM] * 6 + [ANY], HBM,
         [pltpu.VMEM((count, members, members), F32), pltpu.SemaphoreType.DMA((count,))],
-        2, "transform_grad",
-    )(*grams, other, carry, befores[-1], follow, steps, done)
+        2.5, "transform_grad",
+    )(gram, gram_other, carry, carry_other, follow, steps, done)
     return (smoothed, ensemble_grad, transform_grad)
 
 

time: 44.7 us -> 40.7 us (0.911)
  starting transfers between devices: 18 us -> 14.3 us
  Pallas kernels: 21.9 us -> 20.9 us
  waiting for transfers between devices: 3.78 us -> 4.36 us
    ppermute x8 -> x10, starting transfers between devices: 14.2 us -> 11.2 us  [exchange(): return lax.ppermute(value, axis, [(at, at ^ bit) for at in range(size)])]
    pallas_call x1, Pallas kernels: 5.98 us -> 3.22 us  [shards(): call(functools.partial(chain_kernel, plan), [shape(count * members, membe...]
    pallas_call x10 -> x11, Pallas kernels: 7.6 us -> 9.29 us  [the longest x1 3.85 us: shards(): call(functools.partial(early_gram_kernel, plan), [shape(members, early_wi...]
    ppermute x2, waiting for transfers between devices: 0.56 us -> 1.31 us  [around(): lax.ppermute(value, 'space', [(at, (at + 2 * d) % lanes) for at in range(...]
    ppermute x2, starting transfers between devices: 3.83 us -> 3.12 us  [around(): lax.ppermute(value, 'space', [(at, (at + 2 * d) % lanes) for at in range(...]
    ppermute x8 -> x10, waiting for transfers between devices: 3.21 us -> 3.06 us  [exchange(): return lax.ppermute(value, axis, [(at, at ^ bit) for at in range(size)])]
  transfers between devices with their start and end apart: 10 -> 12, of which waited for: 7 -> 4; matrix products, arithmetic and copies ran while one was open for 0% -> 0% of each run, Pallas kernels for 29% -> 37%
where the time goes in v3:
time: 40.7 us; the launch traced here: 40.4 us
  Pallas kernels  20.9 us (51%)
  starting transfers between devices  14.3 us (35%)
  waiting for transfers between devices  4.36 us (11%)
  between operations  0.83 us (2%)
    ppermute x10, starting transfers between devices, exchange(): return lax.ppermute(value, axis, [(at, at ^ bit) for at in range(size)])  11.2 us
    pallas_call x4, Pallas kernels, apply(): call(functools.partial(apply_kernel, plan, pieces), [shape(count, members...  7.3 us
    pallas_call x1, Pallas kernels, shards(): call(functools.partial(early_gram_kernel, plan), [shape(members, early_wi...  3.85 us
    pallas_call x1, Pallas kernels, shards(): call(functools.partial(chain_kernel, plan), [shape(count * members, membe...  3.22 us
    ppermute x2, starting transfers between devices, around(): lax.ppermute(value, 'space', [(at, (at + 2 * d) % lanes) for at in range(...  3.12 us
    ppermute x10, waiting for transfers between devices, exchange(): return lax.ppermute(value, axis, [(at, at ^ bit) for at in range(size)])  3.06 us
    pallas_call x1, Pallas kernels, shards(): call(functools.partial(final_kernel, plan, scale), shape(count, members,...  2.29 us
    ppermute x2, waiting for transfers between devices, around(): lax.ppermute(value, 'space', [(at, (at + 2 * d) % lanes) for at in range(...  1.31 us
  transfers between devices with their start and end apart: 12, of which 4 were waited for; matrix products, arithmetic and copies ran while one was open for 0% of the time, Pallas kernels for 37%

profile of v3, /device:TPU:0, one launch (start us, length us, event | category | flops | bytes accessed | tf_op | source)
XLA Modules:
  0.0 40.4 jit_solution(2173730470474860261)
XLA Ops:
  0.6 3.2 %transform_chain.1 = (f32[1280,80]{1,0:T(8,128)S(1)}, f32[80,80]{1,0:T(8,128)S(1)}, f32[16,80,80]{2,1,0:T(8,128)S(1)}, bf16[6,80,2048]{2,1,0:T(8,128)(2,1)S(1)}, bf16[6,80,2048]{2,1,0:T(8,128)(2,1)S(1)}) custom-call(f32[16,80,80]{2,1,0:T(8,128)} %transforms.1, bf16[16,80,2048]{2,1,0:T(8,128)(2,1)} %ensembles.3, bf16[16,80,2048]{2,1,0:T(8,128)(2,1)} %cotangents.3), custom_call_target="tpu_custom_call" | custom-call | bytes 12600000 | tf_op jit(solution)/shard_map/transform_chain/pallas_call | solution.py:378
  3.9 3.0 %collective-permute-start = (f32[80,80]{1,0:T(8,128)S(1)}, f32[80,80]{1,0:T(8,128)S(1)}, u32[]{:S(2)}, u32[]{:S(2)}) collective-permute-start(f32[80,80]{1,0:T(8,128)S(1)} %get-tuple-element.48.total), channel_id=1, source_target_pairs={{0,4},{4,0},{8,12},{12,8},{16,20},{20,16},{24,28},{28,24},{1,5},{5... | collective-permute-start | bytes 76808 | tf_op jit(solution)/shard_map/ppermute | solution.py:363
  6.9 3.8 %early_gram.1 = (f32[80,1024]{1,0:T(8,128)S(1)}, f32[80,80]{1,0:T(8,128)S(1)}, bf16[6,80,2048]{2,1,0:T(8,128)(2,1)S(1)}, bf16[6,80,2048]{2,1,0:T(8,128)(2,1)S(1)...) custom-call(bf16[16,80,2048]{2,1,0:T(8,128)(2,1)} %ensembles.3, bf16[16,80,2048]{2,1,0:T(8,128)(2,1)} %cotangents.3, ...), custom_call_target="tpu_custom_call" | custom-call | bytes 10800000 | tf_op jit(solution)/shard_map/early_gram/pallas_call | solution.py:408
  10.7 0.0 collective-permute-done.other
  10.7 0.3 join_0.1
  11.0 1.6 %collective-permute-start.1 = (f32[80,80]{1,0:T(8,128)S(1)}, f32[80,80]{1,0:T(8,128)S(1)}, u32[]{:S(2)}, u32[]{:S(2)}) collective-permute-start(f32[80,80]{1,0:T(8,128)S(1)} %get-tuple-element.52._.total), channel_id=1, source_target_pairs={{0,8},{4,12},{8,0},{12,4},{16,24},{20,28},{24,16},{28,20},{1,9},{5... | collective-permute-start | bytes 76808 | tf_op jit(solution)/shard_map/ppermute | solution.py:363
  12.6 1.2 %late_gram.1 = (f32[40,1408]{1,0:T(8,128)S(1)}, f32[40,1408]{1,0:T(8,128)S(1)}, f32[40,80]{1,0:T(8,128)S(1)}, f32[40,80]{1,0:T(8,128)S(1)}) custom-call(bf16[4,80,2048]{2,1,0:T(8,128)(2,1)S(1)} %get-tuple-element.55.ens.refs_0_, bf16[4,80,2048]{2,1,0:T(8,128)(2,1)S(1)} %get-tuple-element.56.cot.refs_0_, f32[1280,80]{1,0:T(8,128)S(1)} %get-tuple-element.47.suffixes, ...), custom_call_target="tpu_custom_call" | custom-call | bytes 4320000 | tf_op jit(solution)/shard_map/late_gram/pallas_call | solution.py:419
  13.8 0.1 collective-permute-start.2
  13.9 1.2 %collective-permute-done.1.other = f32[80,80]{1,0:T(8,128)S(1)} collective-permute-done((f32[80,80]{1,0:T(8,128)S(1)}, f32[80,80]{1,0:T(8,128)S(1)}, u32[]{:S(2)}, u32[]{:S(2)}) %collective-permute-start.1) | collective-permute-done | bytes 25632 | tf_op jit(solution)/shard_map/ppermute | solution.py:363
  15.1 0.2 join_1.1
  15.3 0.0 collective-permute-done.2.refs_1_
  15.4 0.1 collective-permute-start.4
  15.4 2.6 %collective-permute-start.5 = (f32[80,80]{1,0:T(8,128)S(1)}, f32[80,80]{1,0:T(8,128)S(1)}, u32[]{:S(2)}, u32[]{:S(2)}) collective-permute-start(f32[80,80]{1,0:T(8,128)S(1)} %get-tuple-element.61.refs_2_), channel_id=1, source_target_pairs={{0,16},{4,20},{8,24},{12,28},{16,0},{20,4},{24,8},{28,12},{1,17},{... | collective-permute-start | bytes 76808 | tf_op jit(solution)/shard_map/ppermute | solution.py:363
  18.1 1.5 %collective-permute-start.3 = (f32[40,80]{1,0:T(8,128)S(1)}, f32[40,80]{1,0:T(8,128)S(1)}, u32[]{:S(2)}, u32[]{:S(2)}) collective-permute-start(f32[40,80]{1,0:T(8,128)S(1)} %get-tuple-element.63._.refs_0_), channel_id=1, source_target_pairs={{0,2},{1,3},{2,0},{3,1},{4,6},{5,7},{6,4},{7,5},{8,10},{9,11},{10,... | collective-permute-start | bytes 38408 | tf_op jit(solution)/shard_map/ppermute | solution.py:367
  19.6 0.9 %windows.1.refs_2_.steps = bf16[2,2560,80]{2,1,0:T(8,128)(2,1)S(1)} custom-call(f32[16,80,80]{2,1,0:T(8,128)S(1)} %get-tuple-element.64.kept, f32[40,80]{1,0:T(8,128)S(1)} %get-tuple-element.63._.refs_0_), custom_call_target="tpu_custom_call" | custom-call | bytes 5400000 | tf_op jit(solution)/shard_map/windows/pallas_call | solution.py:435
  20.6 1.3 %collective-permute-done.3.refs_1_ = f32[40,80]{1,0:T(8,128)S(1)} collective-permute-done((f32[40,80]{1,0:T(8,128)S(1)}, f32[40,80]{1,0:T(8,128)S(1)}, u32[]{:S(2)}, u32[]{:S(2)}) %collective-permute-start.3) | collective-permute-done | bytes 12832 | tf_op jit(solution)/shard_map/ppermute | solution.py:367
  21.9 0.0 collective-permute-done.5.refs_4_
  21.9 0.0 collective-permute-done.4.refs_3_
  21.9 1.6 %collective-permute-start.8 = (f32[40,1408]{1,0:T(8,128)S(1)}, f32[40,1408]{1,0:T(8,128)S(1)}, u32[]{:S(2)}, u32[]{:S(2)}) collective-permute-start(f32[40,1408]{1,0:T(8,128)S(1)} %add.6), channel_id=1, source_target_pairs={{0,2},{1,3},{2,0},{3,1},{4,6},{5,7},{6,4},{7,5},{8,10},{9,11},{10,... | collective-permute-start | bytes 675848 | tf_op jit(solution)/shard_map/ppermute | solution.py:367
  23.5 0.5 %collective-permute-start.6 = (f32[40,80]{1,0:T(8,128)S(1)}, f32[40,80]{1,0:T(8,128)S(1)}, u32[]{:S(2)}, u32[]{:S(2)}) collective-permute-start(f32[40,80]{1,0:T(8,128)S(1)} %get-tuple-element.67._.own), channel_id=1, source_target_pairs={{0,4},{4,0},{8,12},{12,8},{16,20},{20,16},{24,28},{28,24},{1,5},{5... | collective-permute-start | bytes 38408 | tf_op jit(solution)/shard_map/ppermute | solution.py:363
  24.0 1.1 %carries.1 = (bf16[6,240,240]{2,1,0:T(8,128)(2,1)S(1)}, bf16[6,240,240]{2,1,0:T(8,128)(2,1)S(1)}, bf16[2,1280,80]{2,1,0:T(8,128)(2,1)S(1)}) custom-call(f32[1280,80]{1,0:T(8,128)S(1)} %get-tuple-element.47.suffixes, f32[80,80]{1,0:T(8,128)S(1)} %get-tuple-element.59.later, f32[80,80]{1,0:T(8,128)S(1)} %get-tuple-element.66.other, ...), custom_call_target="tpu_custom_call" | custom-call | bytes 3600000 | tf_op jit(solution)/shard_map/carries/pallas_call | solution.py:446
  25.1 2.3 %smoothed_0.1 = (bf16[16,80,2048]{2,1,0:T(8,128)(2,1)}, f32[8,128]{1,0:T(8,128)S(1)}) custom-call(bf16[6,240,240]{2,1,0:T(8,128)(2,1)S(1)} %get-tuple-element.68.factors, bf16[6,80,2048]{2,1,0:T(8,128)(2,1)S(1)} %get-tuple-element.49.ens.refs_0_, bf16[6,80,2048]{2,1,0:T(8,128)(2,1)S(1)} %get-tuple-element.70.refs_1_, ...), custom_call_target="tpu_custom_call" | custom-call | bytes 6480000 | tf_op jit(solution)/shard_map/smoothed_0/pallas_call | solution.py:456
  27.4 0.0 collective-permute-done.6.other
  27.4 0.2 pass_0.1
  27.6 1.6 %collective-permute-start.7 = (f32[40,80]{1,0:T(8,128)S(1)}, f32[40,80]{1,0:T(8,128)S(1)}, u32[]{:S(2)}, u32[]{:S(2)}) collective-permute-start(f32[40,80]{1,0:T(8,128)S(1)} %get-tuple-element.73.refs_1_.own), channel_id=1, source_target_pairs={{0,8},{4,12},{8,0},{12,4},{16,24},{20,28},{24,16},{28,20},{1,9},{5... | collective-permute-start | bytes 38408 | tf_op jit(solution)/shard_map/ppermute | solution.py:363
  29.3 1.4 %smoothed_1.1 = (bf16[16,80,2048]{2,1,0:T(8,128)(2,1)}, f32[8,128]{1,0:T(8,128)S(1)}) custom-call(bf16[6,240,240]{2,1,0:T(8,128)(2,1)S(1)} %get-tuple-element.68.factors, bf16[4,80,2048]{2,1,0:T(8,128)(2,1)S(1)} %get-tuple-element.55.ens.refs_0_, f32[40,80]{1,0:T(8,128)S(1)} %get-tuple-element.73.refs_1_.own, ...), custom_call_target="tpu_custom_call", output_to_operand_aliasing={{0}: (3, {})} | custom-call | bytes 6480000 | tf_op jit(solution)/shard_map/smoothed_1/pallas_call | solution.py:456
  30.6 0.8 %collective-permute-done.7.other = f32[40,80]{1,0:T(8,128)S(1)} collective-permute-done((f32[40,80]{1,0:T(8,128)S(1)}, f32[40,80]{1,0:T(8,128)S(1)}, u32[]{:S(2)}, u32[]{:S(2)}) %collective-permute-start.7) | collective-permute-done | bytes 12832 | tf_op jit(solution)/shard_map/ppermute | solution.py:363
  31.5 0.0 collective-permute-done.8.refs_1_
  31.5 0.2 pass_1.1
  31.7 0.1 collective-permute-start.10
  31.8 1.4 %collective-permute-start.9 = (f32[40,80]{1,0:T(8,128)S(1)}, f32[40,80]{1,0:T(8,128)S(1)}, u32[]{:S(2)}, u32[]{:S(2)}) collective-permute-start(f32[40,80]{1,0:T(8,128)S(1)} %get-tuple-element.82.refs_2_), channel_id=1, source_target_pairs={{0,16},{4,20},{8,24},{12,28},{16,0},{20,4},{24,8},{28,12},{1,17},{... | collective-permute-start | bytes 38408 | tf_op jit(solution)/shard_map/ppermute | solution.py:363
  33.2 2.3 %ensemble_grad_0.1 = (bf16[16,80,2048]{2,1,0:T(8,128)(2,1)}, f32[8,128]{1,0:T(8,128)S(1)}) custom-call(bf16[6,240,240]{2,1,0:T(8,128)(2,1)S(1)} %get-tuple-element.76.factors, bf16[6,80,2048]{2,1,0:T(8,128)(2,1)S(1)} %get-tuple-element.50.cot.refs_0_, bf16[6,80,2048]{2,1,0:T(8,128)(2,1)S(1)} %get-tuple-element.85.refs_1_, f32[40,80]{1,0:T(8,128)S(1)} %get-tuple-element.82.refs_2_), custom_call_target="tpu_custom_call" | custom-call | bytes 6480000 | tf_op jit(solution)/shard_map/ensemble_grad_0/pallas_call | solution.py:456
  35.5 1.0 %collective-permute-done.9.other = f32[40,80]{1,0:T(8,128)S(1)} collective-permute-done((f32[40,80]{1,0:T(8,128)S(1)}, f32[40,80]{1,0:T(8,128)S(1)}, u32[]{:S(2)}, u32[]{:S(2)}) %collective-permute-start.9) | collective-permute-done | bytes 12832 | tf_op jit(solution)/shard_map/ppermute | solution.py:363
  36.5 0.1 pass_last.1.refs_1_.carry_mine
  36.7 0.1 collective-permute-start.11
  36.7 1.4 %ensemble_grad_1.1 = (bf16[16,80,2048]{2,1,0:T(8,128)(2,1)}, f32[8,128]{1,0:T(8,128)S(1)}) custom-call(bf16[6,240,240]{2,1,0:T(8,128)(2,1)S(1)} %get-tuple-element.76.factors, bf16[4,80,2048]{2,1,0:T(8,128)(2,1)S(1)} %get-tuple-element.56.cot.refs_0_, f32[40,80]{1,0:T(8,128)S(1)} %pass_last.1.refs_1_.carry_mine, ...), custom_call_target="tpu_custom_call", output_to_operand_aliasing={{0}: (3, {})} | custom-call | bytes 6480000 | tf_op jit(solution)/shard_map/ensemble_grad_1/pallas_call | solution.py:456
  38.1 0.0 collective-permute-done.11.carry_other
  38.1 0.0 collective-permute-done.10.gram_other
  38.1 2.3 %transform_grad.1 = f32[16,80,80]{2,1,0:T(8,128)} custom-call(f32[40,1408]{1,0:T(8,128)S(1)} %add.7.gram_mine, f32[40,1408]{1,0:T(8,128)S(1)} %collective-permute-done.10.gram_other, f32[40,80]{1,0:T(8,128)S(1)} %pass_last.1.refs_1_.carry_mine, f32[40,80]{1,0:T(8,128)S(1)} %collective-permute-done.11.carry_other, ...), custom_call_target="tpu_custom_call" | custom-call | bytes 9000000 | tf_op jit(solution)/shard_map/transform_grad/pallas_call | solution.py:490
  (6 shorter events, 0.1 us)
Async XLA Ops:
  3.9 6.9 %collective-permute-start = (f32[80,80]{1,0:T(8,128)S(1)}, f32[80,80]{1,0:T(8,128)S(1)}, u32[]{:S(2)}, u32[]{:S(2)}) collective-permute-start(f32[80,80]{1,0:T(8,128)S(1)} %get-tuple-element.48.total), channel_id=1, source_target_pairs={{0,4},{4,0},{8,12},{12,8},{16,20},{20,16},{24,28},{28,24},{1,5},{5... | collective-permute-start | bytes 76808 | tf_op jit(solution)/shard_map/ppermute | solution.py:363
  11.0 4.1 %collective-permute-start.1 = (f32[80,80]{1,0:T(8,128)S(1)}, f32[80,80]{1,0:T(8,128)S(1)}, u32[]{:S(2)}, u32[]{:S(2)}) collective-permute-start(f32[80,80]{1,0:T(8,128)S(1)} %get-tuple-element.52._.total), channel_id=1, source_target_pairs={{0,8},{4,12},{8,0},{12,4},{16,24},{20,28},{24,16},{28,20},{1,9},{5... | collective-permute-start | bytes 76808 | tf_op jit(solution)/shard_map/ppermute | solution.py:363
  13.8 1.5 %collective-permute-start.2 = (f32[40,80]{1,0:T(8,128)S(1)}, f32[40,80]{1,0:T(8,128)S(1)}, u32[]{:S(2)}, u32[]{:S(2)}) collective-permute-start(f32[40,80]{1,0:T(8,128)S(1)} %get-tuple-element.60), channel_id=1, source_target_pairs={{0,1},{1,0},{2,3},{3,2},{4,5},{5,4},{6,7},{7,6},{8,9},{9,8},{10,11... | collective-permute-start | bytes 38408 | tf_op jit(solution)/shard_map/ppermute | solution.py:363
  15.4 6.5 %collective-permute-start.4 = (f32[40,1408]{1,0:T(8,128)S(1)}, f32[40,1408]{1,0:T(8,128)S(1)}, u32[]{:S(2)}, u32[]{:S(2)}) collective-permute-start(f32[40,1408]{1,0:T(8,128)S(1)} %get-tuple-element.65), channel_id=1, source_target_pairs={{0,1},{1,0},{2,3},{3,2},{4,5},{5,4},{6,7},{7,6},{8,9},{9,8},{10,11... | collective-permute-start | bytes 675848 | tf_op jit(solution)/shard_map/ppermute | solution.py:363
  15.4 6.4 %collective-permute-start.5 = (f32[80,80]{1,0:T(8,128)S(1)}, f32[80,80]{1,0:T(8,128)S(1)}, u32[]{:S(2)}, u32[]{:S(2)}) collective-permute-start(f32[80,80]{1,0:T(8,128)S(1)} %get-tuple-element.61.refs_2_), channel_id=1, source_target_pairs={{0,16},{4,20},{8,24},{12,28},{16,0},{20,4},{24,8},{28,12},{1,17},{... | collective-permute-start | bytes 76808 | tf_op jit(solution)/shard_map/ppermute | solution.py:363
  18.1 3.8 %collective-permute-start.3 = (f32[40,80]{1,0:T(8,128)S(1)}, f32[40,80]{1,0:T(8,128)S(1)}, u32[]{:S(2)}, u32[]{:S(2)}) collective-permute-start(f32[40,80]{1,0:T(8,128)S(1)} %get-tuple-element.63._.refs_0_), channel_id=1, source_target_pairs={{0,2},{1,3},{2,0},{3,1},{4,6},{5,7},{6,4},{7,5},{8,10},{9,11},{10,... | collective-permute-start | bytes 38408 | tf_op jit(solution)/shard_map/ppermute | solution.py:367
  21.9 9.5 %collective-permute-start.8 = (f32[40,1408]{1,0:T(8,128)S(1)}, f32[40,1408]{1,0:T(8,128)S(1)}, u32[]{:S(2)}, u32[]{:S(2)}) collective-permute-start(f32[40,1408]{1,0:T(8,128)S(1)} %add.6), channel_id=1, source_target_pairs={{0,2},{1,3},{2,0},{3,1},{4,6},{5,7},{6,4},{7,5},{8,10},{9,11},{10,... | collective-permute-start | bytes 675848 | tf_op jit(solution)/shard_map/ppermute | solution.py:367
  23.5 3.9 %collective-permute-start.6 = (f32[40,80]{1,0:T(8,128)S(1)}, f32[40,80]{1,0:T(8,128)S(1)}, u32[]{:S(2)}, u32[]{:S(2)}) collective-permute-start(f32[40,80]{1,0:T(8,128)S(1)} %get-tuple-element.67._.own), channel_id=1, source_target_pairs={{0,4},{4,0},{8,12},{12,8},{16,20},{20,16},{24,28},{28,24},{1,5},{5... | collective-permute-start | bytes 38408 | tf_op jit(solution)/shard_map/ppermute | solution.py:363
  27.6 3.8 %collective-permute-start.7 = (f32[40,80]{1,0:T(8,128)S(1)}, f32[40,80]{1,0:T(8,128)S(1)}, u32[]{:S(2)}, u32[]{:S(2)}) collective-permute-start(f32[40,80]{1,0:T(8,128)S(1)} %get-tuple-element.73.refs_1_.own), channel_id=1, source_target_pairs={{0,8},{4,12},{8,0},{12,4},{16,24},{20,28},{24,16},{28,20},{1,9},{5... | collective-permute-start | bytes 38408 | tf_op jit(solution)/shard_map/ppermute | solution.py:363
  31.7 6.4 %collective-permute-start.10 = (f32[40,1408]{1,0:T(8,128)S(1)}, f32[40,1408]{1,0:T(8,128)S(1)}, u32[]{:S(2)}, u32[]{:S(2)}) collective-permute-start(f32[40,1408]{1,0:T(8,128)S(1)} %add.7.gram_mine), channel_id=1, source_target_pairs={{0,1},{1,0},{2,3},{3,2},{4,5},{5,4},{6,7},{7,6},{8,9},{9,8},{10,11... | collective-permute-start | bytes 675848 | tf_op jit(solution)/shard_map/ppermute | solution.py:363
  31.8 4.7 %collective-permute-start.9 = (f32[40,80]{1,0:T(8,128)S(1)}, f32[40,80]{1,0:T(8,128)S(1)}, u32[]{:S(2)}, u32[]{:S(2)}) collective-permute-start(f32[40,80]{1,0:T(8,128)S(1)} %get-tuple-element.82.refs_2_), channel_id=1, source_target_pairs={{0,16},{4,20},{8,24},{12,28},{16,0},{20,4},{24,8},{28,12},{1,17},{... | collective-permute-start | bytes 38408 | tf_op jit(solution)/shard_map/ppermute | solution.py:363
  36.7 1.5 %collective-permute-start.11 = (f32[40,80]{1,0:T(8,128)S(1)}, f32[40,80]{1,0:T(8,128)S(1)}, u32[]{:S(2)}, u32[]{:S(2)}) collective-permute-start(f32[40,80]{1,0:T(8,128)S(1)} %pass_last.1.refs_1_.carry_mine), channel_id=1, source_target_pairs={{0,1},{1,0},{2,3},{3,2},{4,5},{5,4},{6,7},{7,6},{8,9},{9,8},{10,11... | collective-permute-start | bytes 38408 | tf_op jit(solution)/shard_map/ppermute | solution.py:363

commit v4 on v3

--- a/solution.py
+++ b/solution.py
@@ -188,20 +188,13 @@
             copy.wait()
 
 
-def late_gram_kernel(
-    plan, ens, cot, suffixes, early, offset, _,
-    gram_kept, gram_sent, offset_kept, offset_sent, whole, offsets,
-):
-    members = plan.members
-    whole[:, : early.shape[1]] = early[...]
-    offsets[...] = offset[...] + gram_of(plan, PIECES - 1, cot, ens, suffixes, whole)
-    half = members // 2
-    core = lax.rem(lax.axis_index("space"), 2)
-    mine, other = pl.ds(core * half, half), pl.ds((1 - core) * half, half)
-    gram_kept[...] = whole[mine]
-    gram_sent[...] = whole[other]
-    offset_kept[...] = offsets[mine]
-    offset_sent[...] = offsets[other]
+def late_gram_kernel(plan, ens, cot, suffixes, early, offset, _, grams, offsets):
+    grams[:, : early.shape[1]] = early[...]
+    offsets[...] = offset[...] + gram_of(plan, PIECES - 1, cot, ens, suffixes, grams)
+
+
+def chip_kernel(mine, other, _, __, offset, ___):
+    offset[...] = mine[...] + other[...]
 
 
 def upper_half(level):
@@ -218,15 +211,8 @@
     new_before[...] = jnp.where(upper, mul_exact(other[...], before[...]), before[...])
 
 
-def sum_kernel(number, out, *refs):
-    total = refs[0][...]
-    for ref in refs[1:number]:
-        total = total + ref[...]
-    refs[out][...] = total
-
-
-def pass_kernel(level, last, own, other, carry, upper_total, before, *refs):
-    new_own, new_carry = refs[2:4] if last else refs[1:3]
+def pass_kernel(level, own, other, carry, upper_total, before, *refs):
+    new_own, new_carry = refs[len(refs) // 2 : len(refs) // 2 + 2] if len(refs) > 3 else refs[1:]
     upper = upper_half(level)
     left = jnp.where(upper, other[...], own[...])
     right = jnp.where(upper, own[...], other[...])
@@ -234,15 +220,24 @@
     new_carry[...] = carry[...] + jnp.where(upper, mul_exact(left, before[...]), 0.0)
 
 
-def last_pass_kernel(level, other, carry, before, _, new_carry):
+def last_pass_kernel(level, other, carry, before, _, __, new_carry, ___):
     added = mul_exact(other[...], before[...])
     new_carry[...] = carry[...] + jnp.where(upper_half(level), added, 0.0)
 
 
-def carry_kernel(plan, level, suffixes, later, other, _, ens_factors, cot_factors, follow):
+def enter_kernel(level, number, later, other, *refs):
+    values, (_, __, entering, own, ___) = refs[:number], refs[number:]
+    joined = mul_exact(later[...], other[...])
+    entering[...] = jnp.where(upper_half(level), later[...], joined)
+    total = values[0][...]
+    for ref in values[1:]:
+        total = total + ref[...]
+    own[...] = total
+
+
+def carry_kernel(plan, suffixes, mine, other, _, ens_factors, cot_factors, follow):
     count, members = plan.count, plan.members
-    entering = later[...]
-    entering = jnp.where(upper_half(level), entering, mul_exact(entering, other[...]))
+    entering = jnp.where(lax.rem(lax.axis_index("space"), 2) == 1, mine[...], other[...])
     mask = on_blocks(members, plan.stack * members)
     repeated = split(jnp.concatenate([entering] * plan.stack, axis=1))
     for at, (start, stop) in enumerate(plan.groups):
@@ -293,17 +288,15 @@
 ):
     count, members = plan.count, plan.members
     first = lax.rem(lax.axis_index("space"), 2) == 0
-
-    def whole(mine, other):
-        return jnp.concatenate([jnp.where(first, mine, other), jnp.where(first, other, mine)], axis=0)
+    carry = jnp.where(first, carry_other[...], carry_mine[...])
 
     totals = []
     for at, (start, stop) in enumerate(plan.groups):
         lanes = plan.lanes(at)
-        tall = whole(gram_mine[:, lanes], gram_other[:, lanes]).T
+        tall = jnp.where(first, gram_mine[:, lanes], gram_other[:, lanes]).T
         for i in range(stop - start):
             totals.append(tall[i * members : (i + 1) * members])
-    totals[0] = totals[0] + whole(carry_mine[...], carry_other[...]).T
+    totals[0] = totals[0] + carry.T
     number = 0
     width = 1
     while width < count:
@@ -359,12 +352,24 @@
         for value in (ensembles, cotangents, transforms)
     )
 
-    def exchange(value, axis, size, bit):
-        return lax.ppermute(value, axis, [(at, at ^ bit) for at in range(size)])
-
-    def around(value):
+    def send(value, target, core):
+        pairs = []
+        for at in range(blocks * lanes):
+            block, lane = divmod(at, lanes)
+            if lane % 2 in core:
+                block, lane = target(block, lane)
+                pairs.append((at, block * lanes + lane))
+        return lax.ppermute(value, ("tm", "space"), pairs)
+
+    def exchange(value, bit):
+        return send(value, lambda block, lane: (block ^ bit, lane), (1,))
+
+    def hand_over(value, *core):
+        return send(value, lambda block, lane: (block, lane ^ 1), core)
+
+    def around(value, *core):
         return [
-            lax.ppermute(value, "space", [(at, (at + 2 * d) % lanes) for at in range(lanes)])
+            send(value, lambda block, lane: (block, (lane + 2 * d) % lanes), core)
             for d in range(1, chips)
         ]
 
@@ -381,7 +386,7 @@
         [HBM] * 3, [VMEM] * 5, [pltpu.SemaphoreType.DMA] + piece_sems(0), 3.5, "transform_chain",
     )(transforms, ensembles, cotangents)
 
-    half = members // 2
+    wide = shape(members, plan.width)
     later = before = jnp.eye(members, dtype=F32)
     uppers, befores = [], []
 
@@ -389,21 +394,12 @@
         befores.append(before)
         *new, upper = call(
             functools.partial(join_kernel, level),
-            [square] * 4, [VMEM] * 4 + [ANY], [VMEM] * 4, [], 0.3, f"join_{level}",
+            [square] * 4, [VMEM] * 4 + [ANY], [VMEM] * 4, [], 3, f"join_{level}",
         )(total, other, later, before, after)
         uppers.append(upper)
         return new
 
-    def add(values, after, name, *through):
-        number = len(values)
-        return call(
-            functools.partial(sum_kernel, number, number + 1 + len(through)),
-            [shape(*values[0].shape)] + [shape(*value.shape) for value in through],
-            [VMEM] * number + [ANY] * (1 + len(through)), [VMEM] + [ANY] * len(through), [], 0.1, name,
-            aliases={number + 1 + at: 1 + at for at in range(len(through))},
-        )(*values, after, *through)
-
-    other = exchange(total, "tm", blocks, 1)
+    other = exchange(total, 1)
     early_width = plan.lanes(plan.first_group[-1]).start
     early, offset, *loaded = call(
         functools.partial(early_gram_kernel, plan),
@@ -415,42 +411,46 @@
     parts = [first_part] + [loaded[at : at + 2] for at in range(0, len(loaded), 2)]
     total, later, before = join(0, total, other, later, before, offset)
 
-    other = exchange(total, "tm", blocks, 2)
-    gram, gram_sent, offset, offset_sent = call(
+    other = exchange(total, 2)
+    gram, offset = call(
         functools.partial(late_gram_kernel, plan),
-        [shape(half, plan.width)] * 2 + [shape(half, members)] * 2,
-        [VMEM] * 5 + [ANY], [VMEM] * 4,
-        [pltpu.VMEM((members, plan.width), F32), pltpu.VMEM((members, members), F32)],
-        1.2, "late_gram",
+        [wide, square], [VMEM] * 5 + [ANY], [VMEM] * 2, [], 1.2, "late_gram",
     )(*parts[-1], suffixes, early, offset, total)
-    offset_core = exchange(offset_sent, "space", lanes, 1)
+    offset_core = hand_over(offset, 0)
     for level in range(1, levels - 1):
-        total, later, before = join(level, total, other, later, before, offset)
-        other = exchange(total, "tm", blocks, 2 << level)
+        total, later, before = join(level, total, other, later, before, gram)
+        other = exchange(total, 2 << level)
     befores.append(before)
-
-    offset, gram_sent = add([offset, offset_core], total, "chip_offset", gram_sent)
-    gram_core = exchange(gram_sent, "space", lanes, 1)
-    offsets = [offset] + around(offset)
+    offset, gram = call(
+        chip_kernel, [square, wide], [VMEM] * 2 + [ANY] * 2, [VMEM, ANY], [], 0.2, "chip_offset",
+        aliases={3: 1},
+    )(offset, offset_core, total, gram)
+    gram_core = hand_over(gram, 1)
+    offsets = [offset] + around(offset, 1)
+
     steps = call(
         functools.partial(windows_kernel, plan),
         shape(2, count_steps(count) * members, members, kind=BF16), [VMEM, ANY], VMEM,
-        [pltpu.VMEM((count * members, members), F32)], 1.5, "windows",
+        [pltpu.VMEM((count * members, members), F32)], 10, "windows",
     )(kept, offset)
-    own, gram_core, other = add(offsets, steps, "own_offset", gram_core, other)
-
-    other_own = exchange(own, "tm", blocks, 1)
+    entering, own, gram_core = call(
+        functools.partial(enter_kernel, levels - 1, chips),
+        [square] * 2 + [wide], [VMEM] * (2 + chips) + [ANY] * 2, [VMEM] * 2 + [ANY], [], 0.2,
+        "entering", aliases={3 + chips: 2},
+    )(later, other, *offsets, steps, gram_core)
+    other_own = exchange(own, 1)
     gram = gram + gram_core
-    grams = around(gram)
+    grams = around(gram, 0)
+    entering_core = hand_over(entering, 1)
     size = plan.stack * members
     ens_factors, cot_factors, follow = call(
-        functools.partial(carry_kernel, plan, levels - 1),
+        functools.partial(carry_kernel, plan),
         [shape(len(plan.groups), size, size, kind=BF16)] * 2
         + [shape(2, count * members, members, kind=BF16)],
-        [VMEM] * 3 + [ANY], [VMEM] * 3, [], 1.0, "carries",
-    )(suffixes, later, other, own)
-
-    def apply(factors, which, pieces, out, after, name):
+        [VMEM] * 3 + [ANY], [VMEM] * 3, [], 0.1, "carries",
+    )(suffixes, entering, entering_core, own)
+
+    def apply(factors, which, pieces, out, after, name, micros):
         first, last = plan.pieces[pieces[0]][0], plan.pieces[pieces[-1]][1]
         number = 2 * sum(len(plan.piece_groups[piece]) for piece in pieces)
         return call(
@@ -458,35 +458,36 @@
             [shape(count, members, cells, kind=BF16), shape(8, 128)],
             [VMEM] * (1 + len(pieces)) + [ANY] + [HBM] * len(out), [HBM, VMEM],
             [pltpu.VMEM((last - first, members, cells), BF16), pltpu.SemaphoreType.DMA((number,))],
-            1.8, name, aliases={2 + len(pieces): 0} if out else None,
+            micros, name, aliases={2 + len(pieces): 0} if out else None,
         )(factors, *(parts[piece][which] for piece in pieces), after, *out)
 
     front, rear = tuple(range(PIECES - 1)), (PIECES - 1,)
-    smoothed, done = apply(ens_factors, 0, front, (), follow, "smoothed_0")
-    carry = jnp.zeros((half, members), F32)
+    smoothed, done = apply(ens_factors, 0, rear, (), follow, "smoothed_0", 0.1)
+    carry = jnp.zeros((members, members), F32)
     for level in range(levels - 1):
-        last = level == levels - 2
+        waits = level > 0
         own, carry, *rest = call(
-            functools.partial(pass_kernel, level, last),
-            [shape(half, members)] * 2 + [shape(half, plan.width)] * last,
-            [VMEM] * 5 + [ANY] * (1 + last), [VMEM] * 2 + [ANY] * last, [], 0.3, f"pass_{level}",
-            aliases={6: 2} if last else None,
-        )(own, other_own, carry, uppers[level], befores[level], done, *grams[:last])
-        other_own = exchange(own, "tm", blocks, 2 << level)
+            functools.partial(pass_kernel, level),
+            [square] * 2 + [wide] * waits,
+            [VMEM] * 5 + [ANY] * (1 + waits), [VMEM] * 2 + [ANY] * waits, [], 0.3, f"pass_{level}",
+            aliases={6: 2} if waits else None,
+        )(own, other_own, carry, uppers[level], befores[level], done, *grams[:waits])
+        grams[:waits] = rest
+        other_own = exchange(own, 2 << level)
         if level == 0:
-            smoothed, done = apply(ens_factors, 0, rear, (smoothed,), own, "smoothed_1")
+            smoothed, done = apply(ens_factors, 0, front, (smoothed,), own, "smoothed_1", 2.4)
         if level == 1:
-            ensemble_grad, done = apply(cot_factors, 1, front, (), own, "ensemble_grad_0")
-    grams[0] = rest[0]
+            ensemble_grad, done = apply(cot_factors, 1, front, (), own, "ensemble_grad_0", 2.4)
+    carry, grams[0] = call(
+        functools.partial(last_pass_kernel, levels - 1),
+        [square, wide], [VMEM] * 3 + [ANY] * 2, [VMEM, ANY], [], 0.2, "pass_last",
+        aliases={4: 1},
+    )(other_own, carry, befores[-1], done, grams[0])
     for part in grams:
         gram = gram + part
-    gram_other = exchange(gram, "space", lanes, 1)
-    carry = call(
-        functools.partial(last_pass_kernel, levels - 1),
-        shape(half, members), [VMEM] * 3 + [ANY], VMEM, [], 0.2, "pass_last",
-    )(other_own, carry, befores[-1], done)
-    carry_other = exchange(carry, "space", lanes, 1)
-    ensemble_grad, done = apply(cot_factors, 1, rear, (ensemble_grad,), carry, "ensemble_grad_1")
+    gram_other = hand_over(gram, 0)
+    carry_other = hand_over(carry, 1)
+    ensemble_grad, done = apply(cot_factors, 1, rear, (ensemble_grad,), carry, "ensemble_grad_1", 1.4)
     transform_grad = call(
         functools.partial(final_kernel, plan, scale),
         shape(count, members, members),

time: 40.7 us -> 57.9 us (1.42)
  starting transfers between devices: 14.3 us -> 28.3 us
  waiting for transfers between devices: 4.36 us -> 6.92 us
    ppermute x12 -> x13, starting transfers between devices: 14.3 us -> 28.3 us  [send(): return lax.ppermute(value, ('tm', 'space'), pairs)]
    ppermute x12 -> x13, waiting for transfers between devices: 4.36 us -> 6.92 us  [send(): return lax.ppermute(value, ('tm', 'space'), pairs)]
  transfers between devices with their start and end apart: 12 -> 13, of which waited for: 4 -> 4; matrix products, arithmetic and copies ran while one was open for 0% -> 0% of each run, Pallas kernels for 37% -> 25%
where the time goes in v4:
time: 57.9 us; the launch traced here: 57.2 us
  starting transfers between devices  28.3 us (49%)
  Pallas kernels  20.9 us (36%)
  waiting for transfers between devices  6.92 us (12%)
  between operations  0.93 us (2%)
    ppermute x13, starting transfers between devices, send(): return lax.ppermute(value, ('tm', 'space'), pairs)  28.3 us
    pallas_call x4, Pallas kernels, apply(): call(functools.partial(apply_kernel, plan, pieces), [shape(count, members...  7.3 us
    ppermute x13, waiting for transfers between devices, send(): return lax.ppermute(value, ('tm', 'space'), pairs)  6.92 us
    pallas_call x1, Pallas kernels, shards(): call(functools.partial(early_gram_kernel, plan), [shape(members, early_wi...  3.85 us
    pallas_call x1, Pallas kernels, shards(): call(functools.partial(chain_kernel, plan), [shape(count * members, membe...  3.22 us
    pallas_call x1, Pallas kernels, shards(): call(functools.partial(final_kernel, plan, scale), shape(count, members,...  2.29 us
  transfers between devices with their start and end apart: 13, of which 4 were waited for; matrix products, arithmetic and copies ran while one was open for 0% of the time, Pallas kernels for 25%

profile of v4, /device:TPU:0, one launch (start us, length us, event | category | flops | bytes accessed | tf_op | source)
XLA Modules:
  0.0 57.2 jit_solution(6249753772352099865)
XLA Ops:
  0.6 3.2 %transform_chain.1 = (f32[1280,80]{1,0:T(8,128)S(1)}, f32[80,80]{1,0:T(8,128)S(1)}, f32[16,80,80]{2,1,0:T(8,128)S(1)}, bf16[6,80,2048]{2,1,0:T(8,128)(2,1)S(1)}, bf16[6,80,2048]{2,1,0:T(8,128)(2,1)S(1)}) custom-call(f32[16,80,80]{2,1,0:T(8,128)} %transforms.1, bf16[16,80,2048]{2,1,0:T(8,128)(2,1)} %ensembles.3, bf16[16,80,2048]{2,1,0:T(8,128)(2,1)} %cotangents.3), custom_call_target="tpu_custom_call" | custom-call | bytes 12600000 | tf_op jit(solution)/shard_map/transform_chain/pallas_call | solution.py:383
  3.9 0.7 %collective-permute-start = (f32[80,80]{1,0:T(8,128)S(1)}, f32[80,80]{1,0:T(8,128)S(1)}, u32[]{:S(2)}, u32[]{:S(2)}) collective-permute-start(f32[80,80]{1,0:T(8,128)S(1)} %get-tuple-element.48.total), channel_id=1, source_target_pairs={{1,5},{3,7},{5,1},{7,3},{9,13},{11,15},{13,9},{15,11},{17,21},{19,... | collective-permute-start | bytes 76808 | tf_op jit(solution)/shard_map/ppermute | solution.py:362
  4.5 3.9 %early_gram.1 = (f32[80,1024]{1,0:T(8,128)S(1)}, f32[80,80]{1,0:T(8,128)S(1)}, bf16[6,80,2048]{2,1,0:T(8,128)(2,1)S(1)}, bf16[6,80,2048]{2,1,0:T(8,128)(2,1)S(1)...) custom-call(bf16[16,80,2048]{2,1,0:T(8,128)(2,1)} %ensembles.3, bf16[16,80,2048]{2,1,0:T(8,128)(2,1)} %cotangents.3, ...), custom_call_target="tpu_custom_call" | custom-call | bytes 10800000 | tf_op jit(solution)/shard_map/early_gram/pallas_call | solution.py:404
  8.4 0.0 collective-permute-done.other
  8.4 0.3 join_0.1
  8.7 0.7 %collective-permute-start.1 = (f32[80,80]{1,0:T(8,128)S(1)}, f32[80,80]{1,0:T(8,128)S(1)}, u32[]{:S(2)}, u32[]{:S(2)}) collective-permute-start(f32[80,80]{1,0:T(8,128)S(1)} %get-tuple-element.52._.total), channel_id=1, source_target_pairs={{1,9},{3,11},{5,13},{7,15},{9,1},{11,3},{13,5},{15,7},{17,25},{19,... | collective-permute-start | bytes 76808 | tf_op jit(solution)/shard_map/ppermute | solution.py:362
  9.4 1.1 %late_gram.1 = (f32[80,1408]{1,0:T(8,128)S(1)}, f32[80,80]{1,0:T(8,128)S(1)}) custom-call(bf16[4,80,2048]{2,1,0:T(8,128)(2,1)S(1)} %get-tuple-element.55.ens.refs_0_, bf16[4,80,2048]{2,1,0:T(8,128)(2,1)S(1)} %get-tuple-element.56.cot.refs_0_, f32[1280,80]{1,0:T(8,128)S(1)} %get-tuple-element.47.suffixes, f32[80,1024]{1,0:T(8,128)S(1)} %get-tuple-element.57.early, ...), custom_call_target="tpu_custom_call" | custom-call | bytes 4320000 | tf_op jit(solution)/shard_map/late_gram/pallas_call | solution.py:415
  10.5 8.2 %collective-permute-start.3 = (f32[80,80]{1,0:T(8,128)S(1)}, f32[80,80]{1,0:T(8,128)S(1)}, u32[]{:S(2)}, u32[]{:S(2)}) collective-permute-start(f32[80,80]{1,0:T(8,128)S(1)} %get-tuple-element.61.mine), channel_id=1, source_target_pairs={{0,1},{2,3},{4,5},{6,7},{8,9},{10,11},{12,13},{14,15},{16,17},{18,... | collective-permute-start | bytes 76808 | tf_op jit(solution)/shard_map/ppermute | solution.py:362
  18.7 0.0 collective-permute-done.1.other
  18.7 0.3 join_1.1
  19.0 0.6 collective-permute-done.3.other
  19.6 1.3 %collective-permute-start.5 = (f32[80,1408]{1,0:T(8,128)S(1)}, f32[80,1408]{1,0:T(8,128)S(1)}, u32[]{:S(2)}, u32[]{:S(2)}) collective-permute-start(f32[80,1408]{1,0:T(8,128)S(1)} %get-tuple-element.64), channel_id=1, source_target_pairs={{1,0},{3,2},{5,4},{7,6},{9,8},{11,10},{13,12},{15,14},{17,16},{19,... | collective-permute-start | bytes 1351688 | tf_op jit(solution)/shard_map/ppermute | solution.py:362
  20.8 0.7 %collective-permute-start.2 = (f32[80,80]{1,0:T(8,128)S(1)}, f32[80,80]{1,0:T(8,128)S(1)}, u32[]{:S(2)}, u32[]{:S(2)}) collective-permute-start(f32[80,80]{1,0:T(8,128)S(1)} %get-tuple-element.60._), channel_id=1, source_target_pairs={{1,17},{3,19},{5,21},{7,23},{9,25},{11,27},{13,29},{15,31},{17,1},... | collective-permute-start | bytes 76808 | tf_op jit(solution)/shard_map/ppermute | solution.py:362
  21.5 0.7 %collective-permute-start.4 = (f32[80,80]{1,0:T(8,128)S(1)}, f32[80,80]{1,0:T(8,128)S(1)}, u32[]{:S(2)}, u32[]{:S(2)}) collective-permute-start(f32[80,80]{1,0:T(8,128)S(1)} %get-tuple-element.62._.refs_0_), channel_id=1, source_target_pairs={{1,3},{3,1},{5,7},{7,5},{9,11},{11,9},{13,15},{15,13},{17,19},{19,... | collective-permute-start | bytes 76808 | tf_op jit(solution)/shard_map/ppermute | solution.py:362
  22.2 0.9 %windows.1.refs_2_.steps = bf16[2,2560,80]{2,1,0:T(8,128)(2,1)S(1)} custom-call(f32[16,80,80]{2,1,0:T(8,128)S(1)} %get-tuple-element.63.kept, f32[80,80]{1,0:T(8,128)S(1)} %get-tuple-element.62._.refs_0_), custom_call_target="tpu_custom_call" | custom-call | bytes 36000000 | tf_op jit(solution)/shard_map/windows/pallas_call | solution.py:431
  23.1 0.0 collective-permute-done.2.other
  23.1 0.0 collective-permute-done.4.refs_1_
  23.2 0.1 collective-permute-done.5.refs_3_
  23.2 0.2 entering.1
  23.4 0.1 add.6
  23.5 3.4 %collective-permute-start.9 = (f32[80,1408]{1,0:T(8,128)S(1)}, f32[80,1408]{1,0:T(8,128)S(1)}, u32[]{:S(2)}, u32[]{:S(2)}) collective-permute-start(f32[80,1408]{1,0:T(8,128)S(1)} %add.6), channel_id=1, source_target_pairs={{0,2},{2,0},{4,6},{6,4},{8,10},{10,8},{12,14},{14,12},{16,18},{18,... | collective-permute-start | bytes 1351688 | tf_op jit(solution)/shard_map/ppermute | solution.py:362
  26.9 1.3 %collective-permute-start.6 = (f32[80,80]{1,0:T(8,128)S(1)}, f32[80,80]{1,0:T(8,128)S(1)}, u32[]{:S(2)}, u32[]{:S(2)}) collective-permute-start(f32[80,80]{1,0:T(8,128)S(1)} %get-tuple-element.65.mine), channel_id=1, source_target_pairs={{1,0},{3,2},{5,4},{7,6},{9,8},{11,10},{13,12},{15,14},{17,16},{19,... | collective-permute-start | bytes 76808 | tf_op jit(solution)/shard_map/ppermute | solution.py:362
  28.2 0.7 %collective-permute-start.7 = (f32[80,80]{1,0:T(8,128)S(1)}, f32[80,80]{1,0:T(8,128)S(1)}, u32[]{:S(2)}, u32[]{:S(2)}) collective-permute-start(f32[80,80]{1,0:T(8,128)S(1)} %get-tuple-element.66._.own), channel_id=1, source_target_pairs={{1,5},{3,7},{5,1},{7,3},{9,13},{11,15},{13,9},{15,11},{17,21},{19,... | collective-permute-start | bytes 76808 | tf_op jit(solution)/shard_map/ppermute | solution.py:362
  28.9 5.8 %collective-permute-done.6.other = f32[80,80]{1,0:T(8,128)S(1)} collective-permute-done((f32[80,80]{1,0:T(8,128)S(1)}, f32[80,80]{1,0:T(8,128)S(1)}, u32[]{:S(2)}, u32[]{:S(2)}) %collective-permute-start.6) | collective-permute-done | bytes 25632 | tf_op jit(solution)/shard_map/ppermute | solution.py:362
  34.7 0.9 %carries.1 = (bf16[6,240,240]{2,1,0:T(8,128)(2,1)S(1)}, bf16[6,240,240]{2,1,0:T(8,128)(2,1)S(1)}, bf16[2,1280,80]{2,1,0:T(8,128)(2,1)S(1)}) custom-call(f32[1280,80]{1,0:T(8,128)S(1)} %get-tuple-element.47.suffixes, f32[80,80]{1,0:T(8,128)S(1)} %get-tuple-element.65.mine, f32[80,80]{1,0:T(8,128)S(1)} %collective-permute-done.6.other, ...), custom_call_target="tpu_custom_call" | custom-call | bytes 360000 | tf_op jit(solution)/shard_map/carries/pallas_call | solution.py:446
  35.6 1.4 %smoothed_0.1 = (bf16[16,80,2048]{2,1,0:T(8,128)(2,1)}, f32[8,128]{1,0:T(8,128)S(1)}) custom-call(bf16[6,240,240]{2,1,0:T(8,128)(2,1)S(1)} %get-tuple-element.67.factors, bf16[4,80,2048]{2,1,0:T(8,128)(2,1)S(1)} %get-tuple-element.55.ens.refs_0_, bf16[2,1280,80]{2,1,0:T(8,128)(2,1)S(1)} %get-tuple-element.70.refs_1_.follow), custom_call_target="tpu_custom_call" | custom-call | bytes 360000 | tf_op jit(solution)/shard_map/smoothed_0/pallas_call | solution.py:456
  36.9 0.0 collective-permute-done.7.other
  37.0 0.2 pass_0.1
  37.2 0.7 %collective-permute-start.8 = (f32[80,80]{1,0:T(8,128)S(1)}, f32[80,80]{1,0:T(8,128)S(1)}, u32[]{:S(2)}, u32[]{:S(2)}) collective-permute-start(f32[80,80]{1,0:T(8,128)S(1)} %get-tuple-element.72.refs_2_.own), channel_id=1, source_target_pairs={{1,9},{3,11},{5,13},{7,15},{9,1},{11,3},{13,5},{15,7},{17,25},{19,... | collective-permute-start | bytes 76808 | tf_op jit(solution)/shard_map/ppermute | solution.py:362
  37.8 2.3 %smoothed_1.1 = (bf16[16,80,2048]{2,1,0:T(8,128)(2,1)}, f32[8,128]{1,0:T(8,128)S(1)}) custom-call(bf16[6,240,240]{2,1,0:T(8,128)(2,1)S(1)} %get-tuple-element.67.factors, bf16[6,80,2048]{2,1,0:T(8,128)(2,1)S(1)} %get-tuple-element.49.ens.refs_0_, bf16[6,80,2048]{2,1,0:T(8,128)(2,1)S(1)} %get-tuple-element.68.refs_1_, ...), custom_call_target="tpu_custom_call", output_to_operand_aliasing={{0}: (4, {})} | custom-call | bytes 8640000 | tf_op jit(solution)/shard_map/smoothed_1/pallas_call | solution.py:456
  40.1 0.0 collective-permute-done.8.other
  40.1 0.0 collective-permute-done.9.refs_1_
  40.1 0.2 pass_1.1
  40.4 0.7 %collective-permute-start.10 = (f32[80,80]{1,0:T(8,128)S(1)}, f32[80,80]{1,0:T(8,128)S(1)}, u32[]{:S(2)}, u32[]{:S(2)}) collective-permute-start(f32[80,80]{1,0:T(8,128)S(1)} %get-tuple-element.80.refs_2_), channel_id=1, source_target_pairs={{1,17},{3,19},{5,21},{7,23},{9,25},{11,27},{13,29},{15,31},{17,1},... | collective-permute-start | bytes 76808 | tf_op jit(solution)/shard_map/ppermute | solution.py:362
  41.0 2.3 %ensemble_grad_0.1 = (bf16[16,80,2048]{2,1,0:T(8,128)(2,1)}, f32[8,128]{1,0:T(8,128)S(1)}) custom-call(bf16[6,240,240]{2,1,0:T(8,128)(2,1)S(1)} %get-tuple-element.75.factors, bf16[6,80,2048]{2,1,0:T(8,128)(2,1)S(1)} %get-tuple-element.50.cot.refs_0_, bf16[6,80,2048]{2,1,0:T(8,128)(2,1)S(1)} %get-tuple-element.83.refs_1_, f32[80,80]{1,0:T(8,128)S(1)} %get-tuple-element.80.refs_2_), custom_call_target="tpu_custom_call" | custom-call | bytes 8640000 | tf_op jit(solution)/shard_map/ensemble_grad_0/pallas_call | solution.py:456
  43.3 0.0 collective-permute-done.10.other
  43.3 0.2 pass_last.1
  43.5 0.1 add.7.gram_mine
  43.6 8.2 %collective-permute-start.11 = (f32[80,1408]{1,0:T(8,128)S(1)}, f32[80,1408]{1,0:T(8,128)S(1)}, u32[]{:S(2)}, u32[]{:S(2)}) collective-permute-start(f32[80,1408]{1,0:T(8,128)S(1)} %add.7.gram_mine), channel_id=1, source_target_pairs={{0,1},{2,3},{4,5},{6,7},{8,9},{10,11},{12,13},{14,15},{16,17},{18,... | collective-permute-start | bytes 1351688 | tf_op jit(solution)/shard_map/ppermute | solution.py:362
  51.8 1.3 %collective-permute-start.12 = (f32[80,80]{1,0:T(8,128)S(1)}, f32[80,80]{1,0:T(8,128)S(1)}, u32[]{:S(2)}, u32[]{:S(2)}) collective-permute-start(f32[80,80]{1,0:T(8,128)S(1)} %get-tuple-element.86.refs_1_.carry_mine), channel_id=1, source_target_pairs={{1,0},{3,2},{5,4},{7,6},{9,8},{11,10},{13,12},{15,14},{17,16},{19,... | collective-permute-start | bytes 76808 | tf_op jit(solution)/shard_map/ppermute | solution.py:362
  53.1 1.4 %ensemble_grad_1.1 = (bf16[16,80,2048]{2,1,0:T(8,128)(2,1)}, f32[8,128]{1,0:T(8,128)S(1)}) custom-call(bf16[6,240,240]{2,1,0:T(8,128)(2,1)S(1)} %get-tuple-element.75.factors, bf16[4,80,2048]{2,1,0:T(8,128)(2,1)S(1)} %get-tuple-element.56.cot.refs_0_, f32[80,80]{1,0:T(8,128)S(1)} %get-tuple-element.86.refs_1_.carry_mine, ...), custom_call_target="tpu_custom_call", output_to_operand_aliasing={{0}: (3, {})} | custom-call | bytes 5040000 | tf_op jit(solution)/shard_map/ensemble_grad_1/pallas_call | solution.py:456
  54.4 0.4 collective-permute-done.12.carry_other
  54.9 0.0 collective-permute-done.11.gram_other
  54.9 2.3 %transform_grad.1 = f32[16,80,80]{2,1,0:T(8,128)} custom-call(f32[80,1408]{1,0:T(8,128)S(1)} %add.7.gram_mine, f32[80,1408]{1,0:T(8,128)S(1)} %collective-permute-done.11.gram_other, f32[80,80]{1,0:T(8,128)S(1)} %get-tuple-element.86.refs_1_.carry_mine, f32[80,80]{1,0:T(8,128)S(1)} %collective-permute-done.12.carry_other, ...), custom_call_target="tpu_custom_call" | custom-call | bytes 9000000 | tf_op jit(solution)/shard_map/transform_grad/pallas_call | solution.py:491
  (3 shorter events, 0.0 us)
Async XLA Ops:
  3.9 4.6 %collective-permute-start = (f32[80,80]{1,0:T(8,128)S(1)}, f32[80,80]{1,0:T(8,128)S(1)}, u32[]{:S(2)}, u32[]{:S(2)}) collective-permute-start(f32[80,80]{1,0:T(8,128)S(1)} %get-tuple-element.48.total), channel_id=1, source_target_pairs={{1,5},{3,7},{5,1},{7,3},{9,13},{11,15},{13,9},{15,11},{17,21},{19,... | collective-permute-start | bytes 76808 | tf_op jit(solution)/shard_map/ppermute | solution.py:362
  8.7 10.0 %collective-permute-start.1 = (f32[80,80]{1,0:T(8,128)S(1)}, f32[80,80]{1,0:T(8,128)S(1)}, u32[]{:S(2)}, u32[]{:S(2)}) collective-permute-start(f32[80,80]{1,0:T(8,128)S(1)} %get-tuple-element.52._.total), channel_id=1, source_target_pairs={{1,9},{3,11},{5,13},{7,15},{9,1},{11,3},{13,5},{15,7},{17,25},{19,... | collective-permute-start | bytes 76808 | tf_op jit(solution)/shard_map/ppermute | solution.py:362
  10.5 9.0 %collective-permute-start.3 = (f32[80,80]{1,0:T(8,128)S(1)}, f32[80,80]{1,0:T(8,128)S(1)}, u32[]{:S(2)}, u32[]{:S(2)}) collective-permute-start(f32[80,80]{1,0:T(8,128)S(1)} %get-tuple-element.61.mine), channel_id=1, source_target_pairs={{0,1},{2,3},{4,5},{6,7},{8,9},{10,11},{12,13},{14,15},{16,17},{18,... | collective-permute-start | bytes 76808 | tf_op jit(solution)/shard_map/ppermute | solution.py:362
  19.6 3.7 %collective-permute-start.5 = (f32[80,1408]{1,0:T(8,128)S(1)}, f32[80,1408]{1,0:T(8,128)S(1)}, u32[]{:S(2)}, u32[]{:S(2)}) collective-permute-start(f32[80,1408]{1,0:T(8,128)S(1)} %get-tuple-element.64), channel_id=1, source_target_pairs={{1,0},{3,2},{5,4},{7,6},{9,8},{11,10},{13,12},{15,14},{17,16},{19,... | collective-permute-start | bytes 1351688 | tf_op jit(solution)/shard_map/ppermute | solution.py:362
  20.8 2.3 %collective-permute-start.2 = (f32[80,80]{1,0:T(8,128)S(1)}, f32[80,80]{1,0:T(8,128)S(1)}, u32[]{:S(2)}, u32[]{:S(2)}) collective-permute-start(f32[80,80]{1,0:T(8,128)S(1)} %get-tuple-element.60._), channel_id=1, source_target_pairs={{1,17},{3,19},{5,21},{7,23},{9,25},{11,27},{13,29},{15,31},{17,1},... | collective-permute-start | bytes 76808 | tf_op jit(solution)/shard_map/ppermute | solution.py:362
  21.5 1.6 %collective-permute-start.4 = (f32[80,80]{1,0:T(8,128)S(1)}, f32[80,80]{1,0:T(8,128)S(1)}, u32[]{:S(2)}, u32[]{:S(2)}) collective-permute-start(f32[80,80]{1,0:T(8,128)S(1)} %get-tuple-element.62._.refs_0_), channel_id=1, source_target_pairs={{1,3},{3,1},{5,7},{7,5},{9,11},{11,9},{13,15},{15,13},{17,19},{19,... | collective-permute-start | bytes 76808 | tf_op jit(solution)/shard_map/ppermute | solution.py:362
  23.5 16.7 %collective-permute-start.9 = (f32[80,1408]{1,0:T(8,128)S(1)}, f32[80,1408]{1,0:T(8,128)S(1)}, u32[]{:S(2)}, u32[]{:S(2)}) collective-permute-start(f32[80,1408]{1,0:T(8,128)S(1)} %add.6), channel_id=1, source_target_pairs={{0,2},{2,0},{4,6},{6,4},{8,10},{10,8},{12,14},{14,12},{16,18},{18,... | collective-permute-start | bytes 1351688 | tf_op jit(solution)/shard_map/ppermute | solution.py:362
  26.9 7.8 %collective-permute-start.6 = (f32[80,80]{1,0:T(8,128)S(1)}, f32[80,80]{1,0:T(8,128)S(1)}, u32[]{:S(2)}, u32[]{:S(2)}) collective-permute-start(f32[80,80]{1,0:T(8,128)S(1)} %get-tuple-element.65.mine), channel_id=1, source_target_pairs={{1,0},{3,2},{5,4},{7,6},{9,8},{11,10},{13,12},{15,14},{17,16},{19,... | collective-permute-start | bytes 76808 | tf_op jit(solution)/shard_map/ppermute | solution.py:362
  28.2 8.7 %collective-permute-start.7 = (f32[80,80]{1,0:T(8,128)S(1)}, f32[80,80]{1,0:T(8,128)S(1)}, u32[]{:S(2)}, u32[]{:S(2)}) collective-permute-start(f32[80,80]{1,0:T(8,128)S(1)} %get-tuple-element.66._.own), channel_id=1, source_target_pairs={{1,5},{3,7},{5,1},{7,3},{9,13},{11,15},{13,9},{15,11},{17,21},{19,... | collective-permute-start | bytes 76808 | tf_op jit(solution)/shard_map/ppermute | solution.py:362
  37.2 3.0 %collective-permute-start.8 = (f32[80,80]{1,0:T(8,128)S(1)}, f32[80,80]{1,0:T(8,128)S(1)}, u32[]{:S(2)}, u32[]{:S(2)}) collective-permute-start(f32[80,80]{1,0:T(8,128)S(1)} %get-tuple-element.72.refs_2_.own), channel_id=1, source_target_pairs={{1,9},{3,11},{5,13},{7,15},{9,1},{11,3},{13,5},{15,7},{17,25},{19,... | collective-permute-start | bytes 76808 | tf_op jit(solution)/shard_map/ppermute | solution.py:362
  40.4 3.0 %collective-permute-start.10 = (f32[80,80]{1,0:T(8,128)S(1)}, f32[80,80]{1,0:T(8,128)S(1)}, u32[]{:S(2)}, u32[]{:S(2)}) collective-permute-start(f32[80,80]{1,0:T(8,128)S(1)} %get-tuple-element.80.refs_2_), channel_id=1, source_target_pairs={{1,17},{3,19},{5,21},{7,23},{9,25},{11,27},{13,29},{15,31},{17,1},... | collective-permute-start | bytes 76808 | tf_op jit(solution)/shard_map/ppermute | solution.py:362
  43.6 11.3 %collective-permute-start.11 = (f32[80,1408]{1,0:T(8,128)S(1)}, f32[80,1408]{1,0:T(8,128)S(1)}, u32[]{:S(2)}, u32[]{:S(2)}) collective-permute-start(f32[80,1408]{1,0:T(8,128)S(1)} %add.7.gram_mine), channel_id=1, source_target_pairs={{0,1},{2,3},{4,5},{6,7},{8,9},{10,11},{12,13},{14,15},{16,17},{18,... | collective-permute-start | bytes 1351688 | tf_op jit(solution)/shard_map/ppermute | solution.py:362
  51.8 3.1 %collective-permute-start.12 = (f32[80,80]{1,0:T(8,128)S(1)}, f32[80,80]{1,0:T(8,128)S(1)}, u32[]{:S(2)}, u32[]{:S(2)}) collective-permute-start(f32[80,80]{1,0:T(8,128)S(1)} %get-tuple-element.86.refs_1_.carry_mine), channel_id=1, source_target_pairs={{1,0},{3,2},{5,4},{7,6},{9,8},{11,10},{13,12},{15,14},{17,16},{19,... | collective-permute-start | bytes 76808 | tf_op jit(solution)/shard_map/ppermute | solution.py:362

commit v5 on v4

--- a/solution.py
+++ b/solution.py
@@ -358,14 +358,14 @@
             block, lane = divmod(at, lanes)
             if lane % 2 in core:
                 block, lane = target(block, lane)
-                pairs.append((at, block * lanes + lane))
+            pairs.append((at, block * lanes + lane))
         return lax.ppermute(value, ("tm", "space"), pairs)
 
     def exchange(value, bit):
         return send(value, lambda block, lane: (block ^ bit, lane), (1,))
 
-    def hand_over(value, *core):
-        return send(value, lambda block, lane: (block, lane ^ 1), core)
+    def hand_over(value):
+        return send(value, lambda block, lane: (block, lane ^ 1), (0, 1))
 
     def around(value, *core):
         return [
@@ -416,7 +416,7 @@
         functools.partial(late_gram_kernel, plan),
         [wide, square], [VMEM] * 5 + [ANY], [VMEM] * 2, [], 1.2, "late_gram",
     )(*parts[-1], suffixes, early, offset, total)
-    offset_core = hand_over(offset, 0)
+    offset_core = hand_over(offset)
     for level in range(1, levels - 1):
         total, later, before = join(level, total, other, later, before, gram)
         other = exchange(total, 2 << level)
@@ -425,7 +425,7 @@
         chip_kernel, [square, wide], [VMEM] * 2 + [ANY] * 2, [VMEM, ANY], [], 0.2, "chip_offset",
         aliases={3: 1},
     )(offset, offset_core, total, gram)
-    gram_core = hand_over(gram, 1)
+    gram_core = hand_over(gram)
     offsets = [offset] + around(offset, 1)
 
     steps = call(
@@ -441,7 +441,7 @@
     other_own = exchange(own, 1)
     gram = gram + gram_core
     grams = around(gram, 0)
-    entering_core = hand_over(entering, 1)
+    entering_core = hand_over(entering)
     size = plan.stack * members
     ens_factors, cot_factors, follow = call(
         functools.partial(carry_kernel, plan),
@@ -485,8 +485,8 @@
     )(other_own, carry, befores[-1], done, grams[0])
     for part in grams:
         gram = gram + part
-    gram_other = hand_over(gram, 0)
-    carry_other = hand_over(carry, 1)
+    gram_other = hand_over(gram)
+    carry_other = hand_over(carry)
     ensemble_grad, done = apply(cot_factors, 1, rear, (ensemble_grad,), carry, "ensemble_grad_1", 1.4)
     transform_grad = call(
         functools.partial(final_kernel, plan, scale),

time: 57.9 us -> 49 us (0.85)
  waiting for transfers between devices: 6.92 us -> 0.87 us
  starting transfers between devices: 28.3 us -> 25.9 us
    ppermute x13, waiting for transfers between devices: 6.92 us -> 0.87 us  [send(): return lax.ppermute(value, ('tm', 'space'), pairs)]
    ppermute x13, starting transfers between devices: 28.3 us -> 25.9 us  [send(): return lax.ppermute(value, ('tm', 'space'), pairs)]
  transfers between devices with their start and end apart: 13 -> 13, of which waited for: 4 -> 2; matrix products, arithmetic and copies ran while one was open for 0% -> 0% of each run, Pallas kernels for 25% -> 30%
where the time goes in v5:
time: 49 us; the launch traced here: 48.6 us
  starting transfers between devices  25.9 us (53%)
  Pallas kernels  20.9 us (43%)
  between operations  0.89 us (2%)
  waiting for transfers between devices  0.87 us (2%)
    ppermute x13, starting transfers between devices, send(): return lax.ppermute(value, ('tm', 'space'), pairs)  25.9 us
    pallas_call x4, Pallas kernels, apply(): call(functools.partial(apply_kernel, plan, pieces), [shape(count, members...  7.29 us
    pallas_call x1, Pallas kernels, shards(): call(functools.partial(early_gram_kernel, plan), [shape(members, early_wi...  3.85 us
    pallas_call x1, Pallas kernels, shards(): call(functools.partial(chain_kernel, plan), [shape(count * members, membe...  3.22 us
    pallas_call x1, Pallas kernels, shards(): call(functools.partial(final_kernel, plan, scale), shape(count, members,...  2.29 us
    pallas_call x1, Pallas kernels, shards(): call(functools.partial(late_gram_kernel, plan), [wide, square], [VMEM] *...  1.15 us
  transfers between devices with their start and end apart: 13, of which 2 were waited for; matrix products, arithmetic and copies ran while one was open for 0% of the time, Pallas kernels for 30%

profile of v5, /device:TPU:0, one launch (start us, length us, event | category | flops | bytes accessed | tf_op | source)
XLA Modules:
  0.0 48.6 jit_solution(1399748694383991676)
XLA Ops:
  0.6 3.2 %transform_chain.1 = (f32[1280,80]{1,0:T(8,128)S(1)}, f32[80,80]{1,0:T(8,128)S(1)}, f32[16,80,80]{2,1,0:T(8,128)S(1)}, bf16[6,80,2048]{2,1,0:T(8,128)(2,1)S(1)}, bf16[6,80,2048]{2,1,0:T(8,128)(2,1)S(1)}) custom-call(f32[16,80,80]{2,1,0:T(8,128)} %transforms.1, bf16[16,80,2048]{2,1,0:T(8,128)(2,1)} %ensembles.3, bf16[16,80,2048]{2,1,0:T(8,128)(2,1)} %cotangents.3), custom_call_target="tpu_custom_call" | custom-call | bytes 12600000 | tf_op jit(solution)/shard_map/transform_chain/pallas_call | solution.py:383
  3.9 0.7 %collective-permute-start = (f32[80,80]{1,0:T(8,128)S(1)}, f32[80,80]{1,0:T(8,128)S(1)}, u32[]{:S(2)}, u32[]{:S(2)}) collective-permute-start(f32[80,80]{1,0:T(8,128)S(1)} %get-tuple-element.48.total), channel_id=1, source_target_pairs={{0,0},{1,5},{2,2},{3,7},{4,4},{5,1},{6,6},{7,3},{8,8},{9,13},{10,1... | collective-permute-start | bytes 76808 | tf_op jit(solution)/shard_map/ppermute | solution.py:362
  4.5 3.9 %early_gram.1 = (f32[80,1024]{1,0:T(8,128)S(1)}, f32[80,80]{1,0:T(8,128)S(1)}, bf16[6,80,2048]{2,1,0:T(8,128)(2,1)S(1)}, bf16[6,80,2048]{2,1,0:T(8,128)(2,1)S(1)...) custom-call(bf16[16,80,2048]{2,1,0:T(8,128)(2,1)} %ensembles.3, bf16[16,80,2048]{2,1,0:T(8,128)(2,1)} %cotangents.3, ...), custom_call_target="tpu_custom_call" | custom-call | bytes 10800000 | tf_op jit(solution)/shard_map/early_gram/pallas_call | solution.py:404
  8.4 0.0 collective-permute-done.other
  8.4 0.3 join_0.1
  8.7 0.7 %collective-permute-start.1 = (f32[80,80]{1,0:T(8,128)S(1)}, f32[80,80]{1,0:T(8,128)S(1)}, u32[]{:S(2)}, u32[]{:S(2)}) collective-permute-start(f32[80,80]{1,0:T(8,128)S(1)} %get-tuple-element.52._.total), channel_id=1, source_target_pairs={{0,0},{1,9},{2,2},{3,11},{4,4},{5,13},{6,6},{7,15},{8,8},{9,1},{10... | collective-permute-start | bytes 76808 | tf_op jit(solution)/shard_map/ppermute | solution.py:362
  9.4 1.1 %late_gram.1 = (f32[80,1408]{1,0:T(8,128)S(1)}, f32[80,80]{1,0:T(8,128)S(1)}) custom-call(bf16[4,80,2048]{2,1,0:T(8,128)(2,1)S(1)} %get-tuple-element.55.ens.refs_0_, bf16[4,80,2048]{2,1,0:T(8,128)(2,1)S(1)} %get-tuple-element.56.cot.refs_0_, f32[1280,80]{1,0:T(8,128)S(1)} %get-tuple-element.47.suffixes, f32[80,1024]{1,0:T(8,128)S(1)} %get-tuple-element.57.early, ...), custom_call_target="tpu_custom_call" | custom-call | bytes 4320000 | tf_op jit(solution)/shard_map/late_gram/pallas_call | solution.py:415
  10.5 6.3 %collective-permute-start.3 = (f32[80,80]{1,0:T(8,128)S(1)}, f32[80,80]{1,0:T(8,128)S(1)}, u32[]{:S(2)}, u32[]{:S(2)}) collective-permute-start(f32[80,80]{1,0:T(8,128)S(1)} %get-tuple-element.61.mine), channel_id=1, source_target_pairs={{0,1},{1,0},{2,3},{3,2},{4,5},{5,4},{6,7},{7,6},{8,9},{9,8},{10,11... | collective-permute-start | bytes 76808 | tf_op jit(solution)/shard_map/ppermute | solution.py:362
  16.9 0.0 collective-permute-done.1.other
  16.9 0.3 join_1.1
  17.1 0.6 %collective-permute-done.3.other = f32[80,80]{1,0:T(8,128)S(1)} collective-permute-done((f32[80,80]{1,0:T(8,128)S(1)}, f32[80,80]{1,0:T(8,128)S(1)}, u32[]{:S(2)}, u32[]{:S(2)}) %collective-permute-start.3) | collective-permute-done | bytes 25632 | tf_op jit(solution)/shard_map/ppermute | solution.py:362
  17.7 0.4 collective-permute-start.5
  18.1 0.7 %collective-permute-start.2 = (f32[80,80]{1,0:T(8,128)S(1)}, f32[80,80]{1,0:T(8,128)S(1)}, u32[]{:S(2)}, u32[]{:S(2)}) collective-permute-start(f32[80,80]{1,0:T(8,128)S(1)} %get-tuple-element.60._), channel_id=1, source_target_pairs={{0,0},{1,17},{2,2},{3,19},{4,4},{5,21},{6,6},{7,23},{8,8},{9,25},{... | collective-permute-start | bytes 76808 | tf_op jit(solution)/shard_map/ppermute | solution.py:362
  18.8 0.7 %collective-permute-start.4 = (f32[80,80]{1,0:T(8,128)S(1)}, f32[80,80]{1,0:T(8,128)S(1)}, u32[]{:S(2)}, u32[]{:S(2)}) collective-permute-start(f32[80,80]{1,0:T(8,128)S(1)} %get-tuple-element.62._.refs_0_), channel_id=1, source_target_pairs={{0,0},{1,3},{2,2},{3,1},{4,4},{5,7},{6,6},{7,5},{8,8},{9,11},{10,1... | collective-permute-start | bytes 76808 | tf_op jit(solution)/shard_map/ppermute | solution.py:362
  19.5 0.9 %windows.1.refs_2_.steps = bf16[2,2560,80]{2,1,0:T(8,128)(2,1)S(1)} custom-call(f32[16,80,80]{2,1,0:T(8,128)S(1)} %get-tuple-element.63.kept, f32[80,80]{1,0:T(8,128)S(1)} %get-tuple-element.62._.refs_0_), custom_call_target="tpu_custom_call" | custom-call | bytes 36000000 | tf_op jit(solution)/shard_map/windows/pallas_call | solution.py:431
  20.4 0.0 collective-permute-done.2.other
  20.4 0.0 collective-permute-done.4.refs_1_
  20.4 0.0 collective-permute-done.5.refs_3_
  20.4 0.2 entering.1
  20.6 0.1 add.6
  20.7 3.4 %collective-permute-start.9 = (f32[80,1408]{1,0:T(8,128)S(1)}, f32[80,1408]{1,0:T(8,128)S(1)}, u32[]{:S(2)}, u32[]{:S(2)}) collective-permute-start(f32[80,1408]{1,0:T(8,128)S(1)} %add.6), channel_id=1, source_target_pairs={{0,2},{1,1},{2,0},{3,3},{4,6},{5,5},{6,4},{7,7},{8,10},{9,9},{10,8... | collective-permute-start | bytes 1351688 | tf_op jit(solution)/shard_map/ppermute | solution.py:362
  24.1 4.8 %collective-permute-start.6 = (f32[80,80]{1,0:T(8,128)S(1)}, f32[80,80]{1,0:T(8,128)S(1)}, u32[]{:S(2)}, u32[]{:S(2)}) collective-permute-start(f32[80,80]{1,0:T(8,128)S(1)} %get-tuple-element.65.mine), channel_id=1, source_target_pairs={{0,1},{1,0},{2,3},{3,2},{4,5},{5,4},{6,7},{7,6},{8,9},{9,8},{10,11... | collective-permute-start | bytes 76808 | tf_op jit(solution)/shard_map/ppermute | solution.py:362
  28.9 0.7 %collective-permute-start.7 = (f32[80,80]{1,0:T(8,128)S(1)}, f32[80,80]{1,0:T(8,128)S(1)}, u32[]{:S(2)}, u32[]{:S(2)}) collective-permute-start(f32[80,80]{1,0:T(8,128)S(1)} %get-tuple-element.66._.own), channel_id=1, source_target_pairs={{0,0},{1,5},{2,2},{3,7},{4,4},{5,1},{6,6},{7,3},{8,8},{9,13},{10,1... | collective-permute-start | bytes 76808 | tf_op jit(solution)/shard_map/ppermute | solution.py:362
  29.6 0.2 collective-permute-done.6.other
  29.8 0.9 %carries.1 = (bf16[6,240,240]{2,1,0:T(8,128)(2,1)S(1)}, bf16[6,240,240]{2,1,0:T(8,128)(2,1)S(1)}, bf16[2,1280,80]{2,1,0:T(8,128)(2,1)S(1)}) custom-call(f32[1280,80]{1,0:T(8,128)S(1)} %get-tuple-element.47.suffixes, f32[80,80]{1,0:T(8,128)S(1)} %get-tuple-element.65.mine, f32[80,80]{1,0:T(8,128)S(1)} %collective-permute-done.6.other, ...), custom_call_target="tpu_custom_call" | custom-call | bytes 360000 | tf_op jit(solution)/shard_map/carries/pallas_call | solution.py:446
  30.6 1.4 %smoothed_0.1 = (bf16[16,80,2048]{2,1,0:T(8,128)(2,1)}, f32[8,128]{1,0:T(8,128)S(1)}) custom-call(bf16[6,240,240]{2,1,0:T(8,128)(2,1)S(1)} %get-tuple-element.67.factors, bf16[4,80,2048]{2,1,0:T(8,128)(2,1)S(1)} %get-tuple-element.55.ens.refs_0_, bf16[2,1280,80]{2,1,0:T(8,128)(2,1)S(1)} %get-tuple-element.70.refs_1_.follow), custom_call_target="tpu_custom_call" | custom-call | bytes 360000 | tf_op jit(solution)/shard_map/smoothed_0/pallas_call | solution.py:456
  32.0 0.0 collective-permute-done.7.other
  32.0 0.2 pass_0.1
  32.3 0.7 %collective-permute-start.8 = (f32[80,80]{1,0:T(8,128)S(1)}, f32[80,80]{1,0:T(8,128)S(1)}, u32[]{:S(2)}, u32[]{:S(2)}) collective-permute-start(f32[80,80]{1,0:T(8,128)S(1)} %get-tuple-element.72.refs_2_.own), channel_id=1, source_target_pairs={{0,0},{1,9},{2,2},{3,11},{4,4},{5,13},{6,6},{7,15},{8,8},{9,1},{10... | collective-permute-start | bytes 76808 | tf_op jit(solution)/shard_map/ppermute | solution.py:362
  32.9 2.3 %smoothed_1.1 = (bf16[16,80,2048]{2,1,0:T(8,128)(2,1)}, f32[8,128]{1,0:T(8,128)S(1)}) custom-call(bf16[6,240,240]{2,1,0:T(8,128)(2,1)S(1)} %get-tuple-element.67.factors, bf16[6,80,2048]{2,1,0:T(8,128)(2,1)S(1)} %get-tuple-element.49.ens.refs_0_, bf16[6,80,2048]{2,1,0:T(8,128)(2,1)S(1)} %get-tuple-element.68.refs_1_, ...), custom_call_target="tpu_custom_call", output_to_operand_aliasing={{0}: (4, {})} | custom-call | bytes 8640000 | tf_op jit(solution)/shard_map/smoothed_1/pallas_call | solution.py:456
  35.2 0.0 collective-permute-done.8.other
  35.2 0.0 collective-permute-done.9.refs_1_
  35.2 0.2 pass_1.1
  35.4 0.7 %collective-permute-start.10 = (f32[80,80]{1,0:T(8,128)S(1)}, f32[80,80]{1,0:T(8,128)S(1)}, u32[]{:S(2)}, u32[]{:S(2)}) collective-permute-start(f32[80,80]{1,0:T(8,128)S(1)} %get-tuple-element.80.refs_2_), channel_id=1, source_target_pairs={{0,0},{1,17},{2,2},{3,19},{4,4},{5,21},{6,6},{7,23},{8,8},{9,25},{... | collective-permute-start | bytes 76808 | tf_op jit(solution)/shard_map/ppermute | solution.py:362
  36.1 2.3 %ensemble_grad_0.1 = (bf16[16,80,2048]{2,1,0:T(8,128)(2,1)}, f32[8,128]{1,0:T(8,128)S(1)}) custom-call(bf16[6,240,240]{2,1,0:T(8,128)(2,1)S(1)} %get-tuple-element.75.factors, bf16[6,80,2048]{2,1,0:T(8,128)(2,1)S(1)} %get-tuple-element.50.cot.refs_0_, bf16[6,80,2048]{2,1,0:T(8,128)(2,1)S(1)} %get-tuple-element.83.refs_1_, f32[80,80]{1,0:T(8,128)S(1)} %get-tuple-element.80.refs_2_), custom_call_target="tpu_custom_call" | custom-call | bytes 8640000 | tf_op jit(solution)/shard_map/ensemble_grad_0/pallas_call | solution.py:456
  38.4 0.0 collective-permute-done.10.other
  38.4 0.2 pass_last.1
  38.6 0.1 add.7.gram_mine
  38.7 6.2 %collective-permute-start.11 = (f32[80,1408]{1,0:T(8,128)S(1)}, f32[80,1408]{1,0:T(8,128)S(1)}, u32[]{:S(2)}, u32[]{:S(2)}) collective-permute-start(f32[80,1408]{1,0:T(8,128)S(1)} %add.7.gram_mine), channel_id=1, source_target_pairs={{0,1},{1,0},{2,3},{3,2},{4,5},{5,4},{6,7},{7,6},{8,9},{9,8},{10,11... | collective-permute-start | bytes 1351688 | tf_op jit(solution)/shard_map/ppermute | solution.py:362
  44.9 0.1 collective-permute-start.12
  44.9 1.4 %ensemble_grad_1.1 = (bf16[16,80,2048]{2,1,0:T(8,128)(2,1)}, f32[8,128]{1,0:T(8,128)S(1)}) custom-call(bf16[6,240,240]{2,1,0:T(8,128)(2,1)S(1)} %get-tuple-element.75.factors, bf16[4,80,2048]{2,1,0:T(8,128)(2,1)S(1)} %get-tuple-element.56.cot.refs_0_, f32[80,80]{1,0:T(8,128)S(1)} %get-tuple-element.86.refs_1_.carry_mine, ...), custom_call_target="tpu_custom_call", output_to_operand_aliasing={{0}: (3, {})} | custom-call | bytes 5040000 | tf_op jit(solution)/shard_map/ensemble_grad_1/pallas_call | solution.py:456
  46.3 0.0 collective-permute-done.12.carry_other
  46.3 0.0 collective-permute-done.11.gram_other
  46.4 2.3 %transform_grad.1 = f32[16,80,80]{2,1,0:T(8,128)} custom-call(f32[80,1408]{1,0:T(8,128)S(1)} %add.7.gram_mine, f32[80,1408]{1,0:T(8,128)S(1)} %collective-permute-done.11.gram_other, f32[80,80]{1,0:T(8,128)S(1)} %get-tuple-element.86.refs_1_.carry_mine, f32[80,80]{1,0:T(8,128)S(1)} %collective-permute-done.12.carry_other, ...), custom_call_target="tpu_custom_call" | custom-call | bytes 9000000 | tf_op jit(solution)/shard_map/transform_grad/pallas_call | solution.py:491
  (3 shorter events, 0.0 us)
Async XLA Ops:
  3.9 4.6 %collective-permute-start = (f32[80,80]{1,0:T(8,128)S(1)}, f32[80,80]{1,0:T(8,128)S(1)}, u32[]{:S(2)}, u32[]{:S(2)}) collective-permute-start(f32[80,80]{1,0:T(8,128)S(1)} %get-tuple-element.48.total), channel_id=1, source_target_pairs={{0,0},{1,5},{2,2},{3,7},{4,4},{5,1},{6,6},{7,3},{8,8},{9,13},{10,1... | collective-permute-start | bytes 76808 | tf_op jit(solution)/shard_map/ppermute | solution.py:362
  8.7 8.2 %collective-permute-start.1 = (f32[80,80]{1,0:T(8,128)S(1)}, f32[80,80]{1,0:T(8,128)S(1)}, u32[]{:S(2)}, u32[]{:S(2)}) collective-permute-start(f32[80,80]{1,0:T(8,128)S(1)} %get-tuple-element.52._.total), channel_id=1, source_target_pairs={{0,0},{1,9},{2,2},{3,11},{4,4},{5,13},{6,6},{7,15},{8,8},{9,1},{10... | collective-permute-start | bytes 76808 | tf_op jit(solution)/shard_map/ppermute | solution.py:362
  10.5 7.2 %collective-permute-start.3 = (f32[80,80]{1,0:T(8,128)S(1)}, f32[80,80]{1,0:T(8,128)S(1)}, u32[]{:S(2)}, u32[]{:S(2)}) collective-permute-start(f32[80,80]{1,0:T(8,128)S(1)} %get-tuple-element.61.mine), channel_id=1, source_target_pairs={{0,1},{1,0},{2,3},{3,2},{4,5},{5,4},{6,7},{7,6},{8,9},{9,8},{10,11... | collective-permute-start | bytes 76808 | tf_op jit(solution)/shard_map/ppermute | solution.py:362
  17.7 2.7 %collective-permute-start.5 = (f32[80,1408]{1,0:T(8,128)S(1)}, f32[80,1408]{1,0:T(8,128)S(1)}, u32[]{:S(2)}, u32[]{:S(2)}) collective-permute-start(f32[80,1408]{1,0:T(8,128)S(1)} %get-tuple-element.64), channel_id=1, source_target_pairs={{0,1},{1,0},{2,3},{3,2},{4,5},{5,4},{6,7},{7,6},{8,9},{9,8},{10,11... | collective-permute-start | bytes 1351688 | tf_op jit(solution)/shard_map/ppermute | solution.py:362
  18.1 2.3 %collective-permute-start.2 = (f32[80,80]{1,0:T(8,128)S(1)}, f32[80,80]{1,0:T(8,128)S(1)}, u32[]{:S(2)}, u32[]{:S(2)}) collective-permute-start(f32[80,80]{1,0:T(8,128)S(1)} %get-tuple-element.60._), channel_id=1, source_target_pairs={{0,0},{1,17},{2,2},{3,19},{4,4},{5,21},{6,6},{7,23},{8,8},{9,25},{... | collective-permute-start | bytes 76808 | tf_op jit(solution)/shard_map/ppermute | solution.py:362
  18.8 1.6 %collective-permute-start.4 = (f32[80,80]{1,0:T(8,128)S(1)}, f32[80,80]{1,0:T(8,128)S(1)}, u32[]{:S(2)}, u32[]{:S(2)}) collective-permute-start(f32[80,80]{1,0:T(8,128)S(1)} %get-tuple-element.62._.refs_0_), channel_id=1, source_target_pairs={{0,0},{1,3},{2,2},{3,1},{4,4},{5,7},{6,6},{7,5},{8,8},{9,11},{10,1... | collective-permute-start | bytes 76808 | tf_op jit(solution)/shard_map/ppermute | solution.py:362
  20.7 14.5 %collective-permute-start.9 = (f32[80,1408]{1,0:T(8,128)S(1)}, f32[80,1408]{1,0:T(8,128)S(1)}, u32[]{:S(2)}, u32[]{:S(2)}) collective-permute-start(f32[80,1408]{1,0:T(8,128)S(1)} %add.6), channel_id=1, source_target_pairs={{0,2},{1,1},{2,0},{3,3},{4,6},{5,5},{6,4},{7,7},{8,10},{9,9},{10,8... | collective-permute-start | bytes 1351688 | tf_op jit(solution)/shard_map/ppermute | solution.py:362
  24.1 5.7 %collective-permute-start.6 = (f32[80,80]{1,0:T(8,128)S(1)}, f32[80,80]{1,0:T(8,128)S(1)}, u32[]{:S(2)}, u32[]{:S(2)}) collective-permute-start(f32[80,80]{1,0:T(8,128)S(1)} %get-tuple-element.65.mine), channel_id=1, source_target_pairs={{0,1},{1,0},{2,3},{3,2},{4,5},{5,4},{6,7},{7,6},{8,9},{9,8},{10,11... | collective-permute-start | bytes 76808 | tf_op jit(solution)/shard_map/ppermute | solution.py:362
  28.9 3.1 %collective-permute-start.7 = (f32[80,80]{1,0:T(8,128)S(1)}, f32[80,80]{1,0:T(8,128)S(1)}, u32[]{:S(2)}, u32[]{:S(2)}) collective-permute-start(f32[80,80]{1,0:T(8,128)S(1)} %get-tuple-element.66._.own), channel_id=1, source_target_pairs={{0,0},{1,5},{2,2},{3,7},{4,4},{5,1},{6,6},{7,3},{8,8},{9,13},{10,1... | collective-permute-start | bytes 76808 | tf_op jit(solution)/shard_map/ppermute | solution.py:362
  32.3 3.0 %collective-permute-start.8 = (f32[80,80]{1,0:T(8,128)S(1)}, f32[80,80]{1,0:T(8,128)S(1)}, u32[]{:S(2)}, u32[]{:S(2)}) collective-permute-start(f32[80,80]{1,0:T(8,128)S(1)} %get-tuple-element.72.refs_2_.own), channel_id=1, source_target_pairs={{0,0},{1,9},{2,2},{3,11},{4,4},{5,13},{6,6},{7,15},{8,8},{9,1},{10... | collective-permute-start | bytes 76808 | tf_op jit(solution)/shard_map/ppermute | solution.py:362
  35.4 3.0 %collective-permute-start.10 = (f32[80,80]{1,0:T(8,128)S(1)}, f32[80,80]{1,0:T(8,128)S(1)}, u32[]{:S(2)}, u32[]{:S(2)}) collective-permute-start(f32[80,80]{1,0:T(8,128)S(1)} %get-tuple-element.80.refs_2_), channel_id=1, source_target_pairs={{0,0},{1,17},{2,2},{3,19},{4,4},{5,21},{6,6},{7,23},{8,8},{9,25},{... | collective-permute-start | bytes 76808 | tf_op jit(solution)/shard_map/ppermute | solution.py:362
  38.7 7.7 %collective-permute-start.11 = (f32[80,1408]{1,0:T(8,128)S(1)}, f32[80,1408]{1,0:T(8,128)S(1)}, u32[]{:S(2)}, u32[]{:S(2)}) collective-permute-start(f32[80,1408]{1,0:T(8,128)S(1)} %add.7.gram_mine), channel_id=1, source_target_pairs={{0,1},{1,0},{2,3},{3,2},{4,5},{5,4},{6,7},{7,6},{8,9},{9,8},{10,11... | collective-permute-start | bytes 1351688 | tf_op jit(solution)/shard_map/ppermute | solution.py:362
  44.9 1.5 %collective-permute-start.12 = (f32[80,80]{1,0:T(8,128)S(1)}, f32[80,80]{1,0:T(8,128)S(1)}, u32[]{:S(2)}, u32[]{:S(2)}) collective-permute-start(f32[80,80]{1,0:T(8,128)S(1)} %get-tuple-element.86.refs_1_.carry_mine), channel_id=1, source_target_pairs={{0,1},{1,0},{2,3},{3,2},{4,5},{5,4},{6,7},{7,6},{8,9},{9,8},{10,11... | collective-permute-start | bytes 76808 | tf_op jit(solution)/shard_map/ppermute | solution.py:362

commit v6 on v5

--- a/solution.py
+++ b/solution.py
@@ -188,9 +188,17 @@
             copy.wait()
 
 
-def late_gram_kernel(plan, ens, cot, suffixes, early, offset, _, grams, offsets):
-    grams[:, : early.shape[1]] = early[...]
-    offsets[...] = offset[...] + gram_of(plan, PIECES - 1, cot, ens, suffixes, grams)
+def late_gram_kernel(plan, ens, cot, suffixes, early, offset, _, kept, sent, offsets, whole):
+    whole[:, : early.shape[1]] = early[...]
+    offsets[...] = offset[...] + gram_of(plan, PIECES - 1, cot, ens, suffixes, whole)
+    half = plan.members // 2
+    core = lax.rem(lax.axis_index("space"), 2)
+    kept[...] = whole[pl.ds(core * half, half)]
+    sent[...] = whole[pl.ds((1 - core) * half, half)]
+
+
+def sum_kernel(left, right, _, total):
+    total[...] = left[...] + right[...]
 
 
 def chip_kernel(mine, other, _, __, offset, ___):
@@ -211,8 +219,7 @@
     new_before[...] = jnp.where(upper, mul_exact(other[...], before[...]), before[...])
 
 
-def pass_kernel(level, own, other, carry, upper_total, before, *refs):
-    new_own, new_carry = refs[len(refs) // 2 : len(refs) // 2 + 2] if len(refs) > 3 else refs[1:]
+def pass_kernel(level, own, other, carry, upper_total, before, _, new_own, new_carry):
     upper = upper_half(level)
     left = jnp.where(upper, other[...], own[...])
     right = jnp.where(upper, own[...], other[...])
@@ -226,7 +233,7 @@
 
 
 def enter_kernel(level, number, later, other, *refs):
-    values, (_, __, entering, own, ___) = refs[:number], refs[number:]
+    values, (_, entering, own) = refs[:number], refs[number:]
     joined = mul_exact(later[...], other[...])
     entering[...] = jnp.where(upper_half(level), later[...], joined)
     total = values[0][...]
@@ -292,8 +299,9 @@
 
     totals = []
     for at, (start, stop) in enumerate(plan.groups):
-        lanes = plan.lanes(at)
-        tall = jnp.where(first, gram_mine[:, lanes], gram_other[:, lanes]).T
+        mine, other = gram_mine[:, plan.lanes(at)], gram_other[:, plan.lanes(at)]
+        halves = [jnp.where(first, mine, other), jnp.where(first, other, mine)]
+        tall = jnp.concatenate(halves, axis=0).T
         for i in range(stop - start):
             totals.append(tall[i * members : (i + 1) * members])
     totals[0] = totals[0] + carry.T
@@ -352,26 +360,25 @@
         for value in (ensembles, cotangents, transforms)
     )
 
-    def send(value, target, core):
+    def send(value, *targets):
         pairs = []
         for at in range(blocks * lanes):
             block, lane = divmod(at, lanes)
-            if lane % 2 in core:
-                block, lane = target(block, lane)
+            block, lane = targets[lane % 2](block, lane)
             pairs.append((at, block * lanes + lane))
         return lax.ppermute(value, ("tm", "space"), pairs)
 
+    def along_tm(bit):
+        return lambda block, lane: (block ^ bit, lane)
+
+    def along_space(distance):
+        return lambda block, lane: (block, (lane + distance) % lanes)
+
     def exchange(value, bit):
-        return send(value, lambda block, lane: (block ^ bit, lane), (1,))
+        return send(value, along_space(2), along_tm(bit))
 
     def hand_over(value):
-        return send(value, lambda block, lane: (block, lane ^ 1), (0, 1))
-
-    def around(value, *core):
-        return [
-            send(value, lambda block, lane: (block, (lane + 2 * d) % lanes), core)
-            for d in range(1, chips)
-        ]
+        return send(value, along_space(1), along_space(lanes - 1))
 
     def piece_shape(piece):
         first, last = plan.pieces[piece]
@@ -386,7 +393,7 @@
         [HBM] * 3, [VMEM] * 5, [pltpu.SemaphoreType.DMA] + piece_sems(0), 3.5, "transform_chain",
     )(transforms, ensembles, cotangents)
 
-    wide = shape(members, plan.width)
+    wide = shape(members // 2, plan.width)
     later = before = jnp.eye(members, dtype=F32)
     uppers, befores = [], []
 
@@ -412,35 +419,37 @@
     total, later, before = join(0, total, other, later, before, offset)
 
     other = exchange(total, 2)
-    gram, offset = call(
+    gram, gram_sent, offset = call(
         functools.partial(late_gram_kernel, plan),
-        [wide, square], [VMEM] * 5 + [ANY], [VMEM] * 2, [], 1.2, "late_gram",
+        [wide, wide, square], [VMEM] * 5 + [ANY], [VMEM] * 3,
+        [pltpu.VMEM((members, plan.width), F32)], 1.2, "late_gram",
     )(*parts[-1], suffixes, early, offset, total)
     offset_core = hand_over(offset)
     for level in range(1, levels - 1):
         total, later, before = join(level, total, other, later, before, gram)
         other = exchange(total, 2 << level)
     befores.append(before)
-    offset, gram = call(
+    offset, gram_sent = call(
         chip_kernel, [square, wide], [VMEM] * 2 + [ANY] * 2, [VMEM, ANY], [], 0.2, "chip_offset",
         aliases={3: 1},
-    )(offset, offset_core, total, gram)
-    gram_core = hand_over(gram)
-    offsets = [offset] + around(offset, 1)
+    )(offset, offset_core, total, gram_sent)
+    gram_core = hand_over(gram_sent)
+    offsets = [offset] + [send(offset, along_tm(1), along_space(2 * d)) for d in range(1, chips)]
 
     steps = call(
         functools.partial(windows_kernel, plan),
         shape(2, count_steps(count) * members, members, kind=BF16), [VMEM, ANY], VMEM,
         [pltpu.VMEM((count * members, members), F32)], 10, "windows",
     )(kept, offset)
-    entering, own, gram_core = call(
+    entering, own = call(
         functools.partial(enter_kernel, levels - 1, chips),
-        [square] * 2 + [wide], [VMEM] * (2 + chips) + [ANY] * 2, [VMEM] * 2 + [ANY], [], 0.2,
-        "entering", aliases={3 + chips: 2},
-    )(later, other, *offsets, steps, gram_core)
+        [square] * 2, [VMEM] * (2 + chips) + [ANY], [VMEM] * 2, [], 0.2, "entering",
+    )(later, other, *offsets, steps)
+    gram = call(
+        sum_kernel, wide, [VMEM] * 2 + [ANY], VMEM, [], 0.1, "chip_gram",
+    )(gram, gram_core, own)
+    grams = [send(gram, *[along_space(2 * d)] * 2) for d in range(1, chips)]
     other_own = exchange(own, 1)
-    gram = gram + gram_core
-    grams = around(gram, 0)
     entering_core = hand_over(entering)
     size = plan.stack * members
     ens_factors, cot_factors, follow = call(
@@ -449,7 +458,6 @@
         + [shape(2, count * members, members, kind=BF16)],
         [VMEM] * 3 + [ANY], [VMEM] * 3, [], 0.1, "carries",
     )(suffixes, entering, entering_core, own)
-
     def apply(factors, which, pieces, out, after, name, micros):
         first, last = plan.pieces[pieces[0]][0], plan.pieces[pieces[-1]][1]
         number = 2 * sum(len(plan.piece_groups[piece]) for piece in pieces)
@@ -465,14 +473,10 @@
     smoothed, done = apply(ens_factors, 0, rear, (), follow, "smoothed_0", 0.1)
     carry = jnp.zeros((members, members), F32)
     for level in range(levels - 1):
-        waits = level > 0
-        own, carry, *rest = call(
+        own, carry = call(
             functools.partial(pass_kernel, level),
-            [square] * 2 + [wide] * waits,
-            [VMEM] * 5 + [ANY] * (1 + waits), [VMEM] * 2 + [ANY] * waits, [], 0.3, f"pass_{level}",
-            aliases={6: 2} if waits else None,
-        )(own, other_own, carry, uppers[level], befores[level], done, *grams[:waits])
-        grams[:waits] = rest
+            [square] * 2, [VMEM] * 5 + [ANY], [VMEM] * 2, [], 0.3, f"pass_{level}",
+        )(own, other_own, carry, uppers[level], befores[level], done)
         other_own = exchange(own, 2 << level)
         if level == 0:
             smoothed, done = apply(ens_factors, 0, front, (smoothed,), own, "smoothed_1", 2.4)

time: 49 us -> 42.3 us (0.86)
  starting transfers between devices: 25.9 us -> 11.2 us
  waiting for transfers between devices: 0.87 us -> 9.12 us
    ppermute x13, starting transfers between devices: 25.9 us -> 11.2 us  [send(): return lax.ppermute(value, ('tm', 'space'), pairs)]
    ppermute x13, waiting for transfers between devices: 0.87 us -> 9.12 us  [send(): return lax.ppermute(value, ('tm', 'space'), pairs)]
    pallas_call x4 -> x5, Pallas kernels: 1.74 us -> 1.78 us  [the longest x1 1.17 us: shards(): call(functools.partial(late_gram_kernel, plan), [wide, wide, square], [VM...]
  transfers between devices with their start and end apart: 13 -> 13, of which waited for: 2 -> 6; matrix products, arithmetic and copies ran while one was open for 0% -> 0% of each run, Pallas kernels for 30% -> 35%
where the time goes in v6:
time: 42.3 us; the launch traced here: 42.1 us
  Pallas kernels  20.9 us (49%)
  starting transfers between devices  11.2 us (26%)
  waiting for transfers between devices  9.12 us (22%)
  between operations  0.82 us (2%)
    ppermute x13, starting transfers between devices, send(): return lax.ppermute(value, ('tm', 'space'), pairs)  11.2 us
    ppermute x13, waiting for transfers between devices, send(): return lax.ppermute(value, ('tm', 'space'), pairs)  9.12 us
    pallas_call x4, Pallas kernels, apply(): call(functools.partial(apply_kernel, plan, pieces), [shape(count, members...  7.28 us
    pallas_call x1, Pallas kernels, shards(): call(functools.partial(early_gram_kernel, plan), [shape(members, early_wi...  3.85 us
    pallas_call x1, Pallas kernels, shards(): call(functools.partial(chain_kernel, plan), [shape(count * members, membe...  3.22 us
    pallas_call x1, Pallas kernels, shards(): call(functools.partial(final_kernel, plan, scale), shape(count, members,...  2.29 us
    pallas_call x1, Pallas kernels, shards(): call(functools.partial(late_gram_kernel, plan), [wide, wide, square], [VM...  1.17 us
    pallas_call x1, Pallas kernels, shards(): call(functools.partial(windows_kernel, plan), shape(2, count_steps(count)...  0.94 us
  transfers between devices with their start and end apart: 13, of which 6 were waited for; matrix products, arithmetic and copies ran while one was open for 0% of the time, Pallas kernels for 35%

profile of v6, /device:TPU:0, one launch (start us, length us, event | category | flops | bytes accessed | tf_op | source)
XLA Modules:
  0.0 42.1 jit_solution(10655002823425767302)
XLA Ops:
  0.6 3.2 %transform_chain.1 = (f32[1280,80]{1,0:T(8,128)S(1)}, f32[80,80]{1,0:T(8,128)S(1)}, f32[16,80,80]{2,1,0:T(8,128)S(1)}, bf16[6,80,2048]{2,1,0:T(8,128)(2,1)S(1)}, bf16[6,80,2048]{2,1,0:T(8,128)(2,1)S(1)}) custom-call(f32[16,80,80]{2,1,0:T(8,128)} %transforms.1, bf16[16,80,2048]{2,1,0:T(8,128)(2,1)} %ensembles.3, bf16[16,80,2048]{2,1,0:T(8,128)(2,1)} %cotangents.3), custom_call_target="tpu_custom_call" | custom-call | bytes 12600000 | tf_op jit(solution)/shard_map/transform_chain/pallas_call | solution.py:390
  3.9 3.0 %collective-permute-start = (f32[80,80]{1,0:T(8,128)S(1)}, f32[80,80]{1,0:T(8,128)S(1)}, u32[]{:S(2)}, u32[]{:S(2)}) collective-permute-start(f32[80,80]{1,0:T(8,128)S(1)} %get-tuple-element.47.total), channel_id=1, source_target_pairs={{0,2},{1,5},{2,0},{3,7},{4,6},{5,1},{6,4},{7,3},{8,10},{9,13},{10,... | collective-permute-start | bytes 76808 | tf_op jit(solution)/shard_map/ppermute | solution.py:369
  6.9 3.8 %early_gram.1 = (f32[80,1024]{1,0:T(8,128)S(1)}, f32[80,80]{1,0:T(8,128)S(1)}, bf16[6,80,2048]{2,1,0:T(8,128)(2,1)S(1)}, bf16[6,80,2048]{2,1,0:T(8,128)(2,1)S(1)...) custom-call(bf16[16,80,2048]{2,1,0:T(8,128)(2,1)} %ensembles.3, bf16[16,80,2048]{2,1,0:T(8,128)(2,1)} %cotangents.3, ...), custom_call_target="tpu_custom_call" | custom-call | bytes 10800000 | tf_op jit(solution)/shard_map/early_gram/pallas_call | solution.py:411
  10.8 0.0 collective-permute-done.other
  10.8 0.3 join_0.1
  11.0 0.2 collective-permute-start.1
  11.2 1.2 %late_gram.1 = (f32[40,1408]{1,0:T(8,128)S(1)}, f32[40,1408]{1,0:T(8,128)S(1)}, f32[80,80]{1,0:T(8,128)S(1)}) custom-call(bf16[4,80,2048]{2,1,0:T(8,128)(2,1)S(1)} %get-tuple-element.54.ens.refs_0_, bf16[4,80,2048]{2,1,0:T(8,128)(2,1)S(1)} %get-tuple-element.55.cot.refs_0_, f32[1280,80]{1,0:T(8,128)S(1)} %get-tuple-element.46.suffixes, ...), custom_call_target="tpu_custom_call" | custom-call | bytes 4320000 | tf_op jit(solution)/shard_map/late_gram/pallas_call | solution.py:422
  12.4 0.8 %collective-permute-start.3 = (f32[80,80]{1,0:T(8,128)S(1)}, f32[80,80]{1,0:T(8,128)S(1)}, u32[]{:S(2)}, u32[]{:S(2)}) collective-permute-start(f32[80,80]{1,0:T(8,128)S(1)} %get-tuple-element.60.mine), channel_id=1, source_target_pairs={{0,1},{1,0},{2,3},{3,2},{4,5},{5,4},{6,7},{7,6},{8,9},{9,8},{10,11... | collective-permute-start | bytes 76808 | tf_op jit(solution)/shard_map/ppermute | solution.py:369
  13.2 1.9 %collective-permute-done.1.other = f32[80,80]{1,0:T(8,128)S(1)} collective-permute-done((f32[80,80]{1,0:T(8,128)S(1)}, f32[80,80]{1,0:T(8,128)S(1)}, u32[]{:S(2)}, u32[]{:S(2)}) %collective-permute-start.1) | collective-permute-done | bytes 25632 | tf_op jit(solution)/shard_map/ppermute | solution.py:369
  15.1 0.3 join_1.1
  15.4 0.0 collective-permute-done.3.other
  15.4 0.1 collective-permute-start.9
  15.5 0.5 %collective-permute-start.2 = (f32[80,80]{1,0:T(8,128)S(1)}, f32[80,80]{1,0:T(8,128)S(1)}, u32[]{:S(2)}, u32[]{:S(2)}) collective-permute-start(f32[80,80]{1,0:T(8,128)S(1)} %get-tuple-element.59._), channel_id=1, source_target_pairs={{0,2},{1,17},{2,0},{3,19},{4,6},{5,21},{6,4},{7,23},{8,10},{9,25},... | collective-permute-start | bytes 76808 | tf_op jit(solution)/shard_map/ppermute | solution.py:369
  16.0 1.6 %collective-permute-start.4 = (f32[80,80]{1,0:T(8,128)S(1)}, f32[80,80]{1,0:T(8,128)S(1)}, u32[]{:S(2)}, u32[]{:S(2)}) collective-permute-start(f32[80,80]{1,0:T(8,128)S(1)} %get-tuple-element.62._.refs_0_), channel_id=1, source_target_pairs={{0,4},{1,3},{2,6},{3,1},{4,0},{5,7},{6,2},{7,5},{8,12},{9,11},{10,... | collective-permute-start | bytes 76808 | tf_op jit(solution)/shard_map/ppermute | solution.py:369
  17.5 0.9 %windows.1.refs_2_.steps = bf16[2,2560,80]{2,1,0:T(8,128)(2,1)S(1)} custom-call(f32[16,80,80]{2,1,0:T(8,128)S(1)} %get-tuple-element.63.kept, f32[80,80]{1,0:T(8,128)S(1)} %get-tuple-element.62._.refs_0_), custom_call_target="tpu_custom_call" | custom-call | bytes 36000000 | tf_op jit(solution)/shard_map/windows/pallas_call | solution.py:439
  18.5 1.1 %collective-permute-done.2.other = f32[80,80]{1,0:T(8,128)S(1)} collective-permute-done((f32[80,80]{1,0:T(8,128)S(1)}, f32[80,80]{1,0:T(8,128)S(1)}, u32[]{:S(2)}, u32[]{:S(2)}) %collective-permute-start.2) | collective-permute-done | bytes 25632 | tf_op jit(solution)/shard_map/ppermute | solution.py:369
  19.5 0.4 %collective-permute-done.4.refs_1_ = f32[80,80]{1,0:T(8,128)S(1)} collective-permute-done((f32[80,80]{1,0:T(8,128)S(1)}, f32[80,80]{1,0:T(8,128)S(1)}, u32[]{:S(2)}, u32[]{:S(2)}) %collective-permute-start.4) | collective-permute-done | bytes 25632 | tf_op jit(solution)/shard_map/ppermute | solution.py:369
  20.0 0.2 entering.1
  20.1 0.0 collective-permute-done.9.right
  20.2 1.7 %collective-permute-start.10 = (f32[40,1408]{1,0:T(8,128)S(1)}, f32[40,1408]{1,0:T(8,128)S(1)}, u32[]{:S(2)}, u32[]{:S(2)}) collective-permute-start(f32[40,1408]{1,0:T(8,128)S(1)} %chip_gram.1), channel_id=1, source_target_pairs={{0,2},{1,3},{2,0},{3,1},{4,6},{5,7},{6,4},{7,5},{8,10},{9,11},{10,... | collective-permute-start | bytes 675848 | tf_op jit(solution)/shard_map/ppermute | solution.py:369
  21.8 0.0 collective-permute-start.5
  21.9 1.3 %collective-permute-start.6 = (f32[80,80]{1,0:T(8,128)S(1)}, f32[80,80]{1,0:T(8,128)S(1)}, u32[]{:S(2)}, u32[]{:S(2)}) collective-permute-start(f32[80,80]{1,0:T(8,128)S(1)} %get-tuple-element.65._.own), channel_id=1, source_target_pairs={{0,2},{1,5},{2,0},{3,7},{4,6},{5,1},{6,4},{7,3},{8,10},{9,13},{10,... | collective-permute-start | bytes 76808 | tf_op jit(solution)/shard_map/ppermute | solution.py:369
  23.2 0.0 collective-permute-done.5.other
  23.2 0.9 %carries.1 = (bf16[6,240,240]{2,1,0:T(8,128)(2,1)S(1)}, bf16[6,240,240]{2,1,0:T(8,128)(2,1)S(1)}, bf16[2,1280,80]{2,1,0:T(8,128)(2,1)S(1)}) custom-call(f32[1280,80]{1,0:T(8,128)S(1)} %get-tuple-element.46.suffixes, f32[80,80]{1,0:T(8,128)S(1)} %get-tuple-element.64.mine, f32[80,80]{1,0:T(8,128)S(1)} %collective-permute-done.5.other, ...), custom_call_target="tpu_custom_call" | custom-call | bytes 360000 | tf_op jit(solution)/shard_map/carries/pallas_call | solution.py:455
  24.0 1.4 %smoothed_0.1 = (bf16[16,80,2048]{2,1,0:T(8,128)(2,1)}, f32[8,128]{1,0:T(8,128)S(1)}) custom-call(bf16[6,240,240]{2,1,0:T(8,128)(2,1)S(1)} %get-tuple-element.66.factors, bf16[4,80,2048]{2,1,0:T(8,128)(2,1)S(1)} %get-tuple-element.54.ens.refs_0_, bf16[2,1280,80]{2,1,0:T(8,128)(2,1)S(1)} %get-tuple-element.69.refs_1_.follow), custom_call_target="tpu_custom_call" | custom-call | bytes 360000 | tf_op jit(solution)/shard_map/smoothed_0/pallas_call | solution.py:464
  25.4 3.7 %collective-permute-done.6.other = f32[80,80]{1,0:T(8,128)S(1)} collective-permute-done((f32[80,80]{1,0:T(8,128)S(1)}, f32[80,80]{1,0:T(8,128)S(1)}, u32[]{:S(2)}, u32[]{:S(2)}) %collective-permute-start.6) | collective-permute-done | bytes 25632 | tf_op jit(solution)/shard_map/ppermute | solution.py:369
  29.1 0.2 pass_0.1
  29.3 0.8 %collective-permute-start.7 = (f32[80,80]{1,0:T(8,128)S(1)}, f32[80,80]{1,0:T(8,128)S(1)}, u32[]{:S(2)}, u32[]{:S(2)}) collective-permute-start(f32[80,80]{1,0:T(8,128)S(1)} %get-tuple-element.71.refs_2_.own), channel_id=1, source_target_pairs={{0,2},{1,9},{2,0},{3,11},{4,6},{5,13},{6,4},{7,15},{8,10},{9,1},{1... | collective-permute-start | bytes 76808 | tf_op jit(solution)/shard_map/ppermute | solution.py:369
  30.1 2.3 %smoothed_1.1 = (bf16[16,80,2048]{2,1,0:T(8,128)(2,1)}, f32[8,128]{1,0:T(8,128)S(1)}) custom-call(bf16[6,240,240]{2,1,0:T(8,128)(2,1)S(1)} %get-tuple-element.66.factors, bf16[6,80,2048]{2,1,0:T(8,128)(2,1)S(1)} %get-tuple-element.48.ens.refs_0_, bf16[6,80,2048]{2,1,0:T(8,128)(2,1)S(1)} %get-tuple-element.67.refs_1_, ...), custom_call_target="tpu_custom_call", output_to_operand_aliasing={{0}: (4, {})} | custom-call | bytes 8640000 | tf_op jit(solution)/shard_map/smoothed_1/pallas_call | solution.py:464
  32.4 1.0 %collective-permute-done.7.other = f32[80,80]{1,0:T(8,128)S(1)} collective-permute-done((f32[80,80]{1,0:T(8,128)S(1)}, f32[80,80]{1,0:T(8,128)S(1)}, u32[]{:S(2)}, u32[]{:S(2)}) %collective-permute-start.7) | collective-permute-done | bytes 25632 | tf_op jit(solution)/shard_map/ppermute | solution.py:369
  33.4 0.2 pass_1.1
  33.6 0.8 %collective-permute-start.8 = (f32[80,80]{1,0:T(8,128)S(1)}, f32[80,80]{1,0:T(8,128)S(1)}, u32[]{:S(2)}, u32[]{:S(2)}) collective-permute-start(f32[80,80]{1,0:T(8,128)S(1)} %get-tuple-element.78.refs_2_), channel_id=1, source_target_pairs={{0,2},{1,17},{2,0},{3,19},{4,6},{5,21},{6,4},{7,23},{8,10},{9,25},... | collective-permute-start | bytes 76808 | tf_op jit(solution)/shard_map/ppermute | solution.py:369
  34.4 2.3 %ensemble_grad_0.1 = (bf16[16,80,2048]{2,1,0:T(8,128)(2,1)}, f32[8,128]{1,0:T(8,128)S(1)}) custom-call(bf16[6,240,240]{2,1,0:T(8,128)(2,1)S(1)} %get-tuple-element.74.factors, bf16[6,80,2048]{2,1,0:T(8,128)(2,1)S(1)} %get-tuple-element.49.cot.refs_0_, bf16[6,80,2048]{2,1,0:T(8,128)(2,1)S(1)} %get-tuple-element.81.refs_1_, f32[80,80]{1,0:T(8,128)S(1)} %get-tuple-element.78.refs_2_), custom_call_target="tpu_custom_call" | custom-call | bytes 8640000 | tf_op jit(solution)/shard_map/ensemble_grad_0/pallas_call | solution.py:464
  36.7 1.0 %collective-permute-done.8.other = f32[80,80]{1,0:T(8,128)S(1)} collective-permute-done((f32[80,80]{1,0:T(8,128)S(1)}, f32[80,80]{1,0:T(8,128)S(1)}, u32[]{:S(2)}, u32[]{:S(2)}) %collective-permute-start.8) | collective-permute-done | bytes 25632 | tf_op jit(solution)/shard_map/ppermute | solution.py:369
  37.7 0.0 collective-permute-done.10.__
  37.7 0.2 pass_last.1
  37.9 0.1 collective-permute-start.11
  37.9 0.5 %collective-permute-start.12 = (f32[80,80]{1,0:T(8,128)S(1)}, f32[80,80]{1,0:T(8,128)S(1)}, u32[]{:S(2)}, u32[]{:S(2)}) collective-permute-start(f32[80,80]{1,0:T(8,128)S(1)} %get-tuple-element.84.refs_1_.carry_mine), channel_id=1, source_target_pairs={{0,1},{1,0},{2,3},{3,2},{4,5},{5,4},{6,7},{7,6},{8,9},{9,8},{10,11... | collective-permute-start | bytes 76808 | tf_op jit(solution)/shard_map/ppermute | solution.py:369
  38.4 1.4 %ensemble_grad_1.1 = (bf16[16,80,2048]{2,1,0:T(8,128)(2,1)}, f32[8,128]{1,0:T(8,128)S(1)}) custom-call(bf16[6,240,240]{2,1,0:T(8,128)(2,1)S(1)} %get-tuple-element.74.factors, bf16[4,80,2048]{2,1,0:T(8,128)(2,1)S(1)} %get-tuple-element.55.cot.refs_0_, f32[80,80]{1,0:T(8,128)S(1)} %get-tuple-element.84.refs_1_.carry_mine, ...), custom_call_target="tpu_custom_call", output_to_operand_aliasing={{0}: (3, {})} | custom-call | bytes 5040000 | tf_op jit(solution)/shard_map/ensemble_grad_1/pallas_call | solution.py:464
  39.8 0.0 collective-permute-done.12.carry_other
  39.8 0.0 collective-permute-done.11.gram_other
  39.8 2.3 %transform_grad.1 = f32[16,80,80]{2,1,0:T(8,128)} custom-call(f32[40,1408]{1,0:T(8,128)S(1)} %add.3.gram_mine, f32[40,1408]{1,0:T(8,128)S(1)} %collective-permute-done.11.gram_other, f32[80,80]{1,0:T(8,128)S(1)} %get-tuple-element.84.refs_1_.carry_mine, f32[80,80]{1,0:T(8,128)S(1)} %collective-permute-done.12.carry_other, ...), custom_call_target="tpu_custom_call" | custom-call | bytes 9000000 | tf_op jit(solution)/shard_map/transform_grad/pallas_call | solution.py:495
  (5 shorter events, 0.1 us)
Async XLA Ops:
  3.9 6.9 %collective-permute-start = (f32[80,80]{1,0:T(8,128)S(1)}, f32[80,80]{1,0:T(8,128)S(1)}, u32[]{:S(2)}, u32[]{:S(2)}) collective-permute-start(f32[80,80]{1,0:T(8,128)S(1)} %get-tuple-element.47.total), channel_id=1, source_target_pairs={{0,2},{1,5},{2,0},{3,7},{4,6},{5,1},{6,4},{7,3},{8,10},{9,13},{10,... | collective-permute-start | bytes 76808 | tf_op jit(solution)/shard_map/ppermute | solution.py:369
  11.0 4.1 %collective-permute-start.1 = (f32[80,80]{1,0:T(8,128)S(1)}, f32[80,80]{1,0:T(8,128)S(1)}, u32[]{:S(2)}, u32[]{:S(2)}) collective-permute-start(f32[80,80]{1,0:T(8,128)S(1)} %get-tuple-element.51._.total), channel_id=1, source_target_pairs={{0,2},{1,9},{2,0},{3,11},{4,6},{5,13},{6,4},{7,15},{8,10},{9,1},{1... | collective-permute-start | bytes 76808 | tf_op jit(solution)/shard_map/ppermute | solution.py:369
  12.4 3.0 %collective-permute-start.3 = (f32[80,80]{1,0:T(8,128)S(1)}, f32[80,80]{1,0:T(8,128)S(1)}, u32[]{:S(2)}, u32[]{:S(2)}) collective-permute-start(f32[80,80]{1,0:T(8,128)S(1)} %get-tuple-element.60.mine), channel_id=1, source_target_pairs={{0,1},{1,0},{2,3},{3,2},{4,5},{5,4},{6,7},{7,6},{8,9},{9,8},{10,11... | collective-permute-start | bytes 76808 | tf_op jit(solution)/shard_map/ppermute | solution.py:369
  15.4 4.8 %collective-permute-start.9 = (f32[40,1408]{1,0:T(8,128)S(1)}, f32[40,1408]{1,0:T(8,128)S(1)}, u32[]{:S(2)}, u32[]{:S(2)}) collective-permute-start(f32[40,1408]{1,0:T(8,128)S(1)} %get-tuple-element.83), channel_id=1, source_target_pairs={{0,1},{1,0},{2,3},{3,2},{4,5},{5,4},{6,7},{7,6},{8,9},{9,8},{10,11... | collective-permute-start | bytes 675848 | tf_op jit(solution)/shard_map/ppermute | solution.py:369
  15.5 4.1 %collective-permute-start.2 = (f32[80,80]{1,0:T(8,128)S(1)}, f32[80,80]{1,0:T(8,128)S(1)}, u32[]{:S(2)}, u32[]{:S(2)}) collective-permute-start(f32[80,80]{1,0:T(8,128)S(1)} %get-tuple-element.59._), channel_id=1, source_target_pairs={{0,2},{1,17},{2,0},{3,19},{4,6},{5,21},{6,4},{7,23},{8,10},{9,25},... | collective-permute-start | bytes 76808 | tf_op jit(solution)/shard_map/ppermute | solution.py:369
  16.0 4.0 %collective-permute-start.4 = (f32[80,80]{1,0:T(8,128)S(1)}, f32[80,80]{1,0:T(8,128)S(1)}, u32[]{:S(2)}, u32[]{:S(2)}) collective-permute-start(f32[80,80]{1,0:T(8,128)S(1)} %get-tuple-element.62._.refs_0_), channel_id=1, source_target_pairs={{0,4},{1,3},{2,6},{3,1},{4,0},{5,7},{6,2},{7,5},{8,12},{9,11},{10,... | collective-permute-start | bytes 76808 | tf_op jit(solution)/shard_map/ppermute | solution.py:369
  20.2 17.5 %collective-permute-start.10 = (f32[40,1408]{1,0:T(8,128)S(1)}, f32[40,1408]{1,0:T(8,128)S(1)}, u32[]{:S(2)}, u32[]{:S(2)}) collective-permute-start(f32[40,1408]{1,0:T(8,128)S(1)} %chip_gram.1), channel_id=1, source_target_pairs={{0,2},{1,3},{2,0},{3,1},{4,6},{5,7},{6,4},{7,5},{8,10},{9,11},{10,... | collective-permute-start | bytes 675848 | tf_op jit(solution)/shard_map/ppermute | solution.py:369
  21.8 1.3 %collective-permute-start.5 = (f32[80,80]{1,0:T(8,128)S(1)}, f32[80,80]{1,0:T(8,128)S(1)}, u32[]{:S(2)}, u32[]{:S(2)}) collective-permute-start(f32[80,80]{1,0:T(8,128)S(1)} %get-tuple-element.64.mine), channel_id=1, source_target_pairs={{0,1},{1,0},{2,3},{3,2},{4,5},{5,4},{6,7},{7,6},{8,9},{9,8},{10,11... | collective-permute-start | bytes 76808 | tf_op jit(solution)/shard_map/ppermute | solution.py:369
  21.9 7.2 %collective-permute-start.6 = (f32[80,80]{1,0:T(8,128)S(1)}, f32[80,80]{1,0:T(8,128)S(1)}, u32[]{:S(2)}, u32[]{:S(2)}) collective-permute-start(f32[80,80]{1,0:T(8,128)S(1)} %get-tuple-element.65._.own), channel_id=1, source_target_pairs={{0,2},{1,5},{2,0},{3,7},{4,6},{5,1},{6,4},{7,3},{8,10},{9,13},{10,... | collective-permute-start | bytes 76808 | tf_op jit(solution)/shard_map/ppermute | solution.py:369
  29.3 4.1 %collective-permute-start.7 = (f32[80,80]{1,0:T(8,128)S(1)}, f32[80,80]{1,0:T(8,128)S(1)}, u32[]{:S(2)}, u32[]{:S(2)}) collective-permute-start(f32[80,80]{1,0:T(8,128)S(1)} %get-tuple-element.71.refs_2_.own), channel_id=1, source_target_pairs={{0,2},{1,9},{2,0},{3,11},{4,6},{5,13},{6,4},{7,15},{8,10},{9,1},{1... | collective-permute-start | bytes 76808 | tf_op jit(solution)/shard_map/ppermute | solution.py:369
  33.6 4.1 %collective-permute-start.8 = (f32[80,80]{1,0:T(8,128)S(1)}, f32[80,80]{1,0:T(8,128)S(1)}, u32[]{:S(2)}, u32[]{:S(2)}) collective-permute-start(f32[80,80]{1,0:T(8,128)S(1)} %get-tuple-element.78.refs_2_), channel_id=1, source_target_pairs={{0,2},{1,17},{2,0},{3,19},{4,6},{5,21},{6,4},{7,23},{8,10},{9,25},... | collective-permute-start | bytes 76808 | tf_op jit(solution)/shard_map/ppermute | solution.py:369
  37.9 2.0 %collective-permute-start.11 = (f32[40,1408]{1,0:T(8,128)S(1)}, f32[40,1408]{1,0:T(8,128)S(1)}, u32[]{:S(2)}, u32[]{:S(2)}) collective-permute-start(f32[40,1408]{1,0:T(8,128)S(1)} %add.3.gram_mine), channel_id=1, source_target_pairs={{0,1},{1,0},{2,3},{3,2},{4,5},{5,4},{6,7},{7,6},{8,9},{9,8},{10,11... | collective-permute-start | bytes 675848 | tf_op jit(solution)/shard_map/ppermute | solution.py:369
  37.9 1.9 %collective-permute-start.12 = (f32[80,80]{1,0:T(8,128)S(1)}, f32[80,80]{1,0:T(8,128)S(1)}, u32[]{:S(2)}, u32[]{:S(2)}) collective-permute-start(f32[80,80]{1,0:T(8,128)S(1)} %get-tuple-element.84.refs_1_.carry_mine), channel_id=1, source_target_pairs={{0,1},{1,0},{2,3},{3,2},{4,5},{5,4},{6,7},{7,6},{8,9},{9,8},{10,11... | collective-permute-start | bytes 76808 | tf_op jit(solution)/shard_map/ppermute | solution.py:369

commit v7 on v5

--- a/solution.py
+++ b/solution.py
@@ -76,6 +76,12 @@
 
     def rows(self, first, last):
         return slice(first * self.members, last * self.members)
+
+
+def eye(members):
+    rows = lax.broadcasted_iota(jnp.int32, (members, members), 0)
+    columns = lax.broadcasted_iota(jnp.int32, (members, members), 1)
+    return (rows == columns).astype(F32)
 
 
 def on_blocks(members, size):
@@ -193,8 +199,11 @@
     offsets[...] = offset[...] + gram_of(plan, PIECES - 1, cot, ens, suffixes, grams)
 
 
-def chip_kernel(mine, other, _, __, offset, ___):
-    offset[...] = mine[...] + other[...]
+def sum_kernel(number, through, *refs):
+    total = refs[0][...]
+    for ref in refs[1:number]:
+        total = total + ref[...]
+    refs[number + 1 + through][...] = total
 
 
 def upper_half(level):
@@ -211,8 +220,7 @@
     new_before[...] = jnp.where(upper, mul_exact(other[...], before[...]), before[...])
 
 
-def pass_kernel(level, own, other, carry, upper_total, before, *refs):
-    new_own, new_carry = refs[len(refs) // 2 : len(refs) // 2 + 2] if len(refs) > 3 else refs[1:]
+def pass_kernel(level, own, other, carry, upper_total, before, _, new_own, new_carry):
     upper = upper_half(level)
     left = jnp.where(upper, other[...], own[...])
     right = jnp.where(upper, own[...], other[...])
@@ -220,24 +228,22 @@
     new_carry[...] = carry[...] + jnp.where(upper, mul_exact(left, before[...]), 0.0)
 
 
-def last_pass_kernel(level, other, carry, before, _, __, new_carry, ___):
-    added = mul_exact(other[...], before[...])
-    new_carry[...] = carry[...] + jnp.where(upper_half(level), added, 0.0)
-
-
-def enter_kernel(level, number, later, other, *refs):
-    values, (_, __, entering, own, ___) = refs[:number], refs[number:]
-    joined = mul_exact(later[...], other[...])
-    entering[...] = jnp.where(upper_half(level), later[...], joined)
-    total = values[0][...]
-    for ref in values[1:]:
-        total = total + ref[...]
-    own[...] = total
-
-
-def carry_kernel(plan, suffixes, mine, other, _, ens_factors, cot_factors, follow):
+def enter_kernel(level, total, later, before, near, far, cross, entering, upper_total, new_before):
+    place = lax.rem(lax.axis_index("tm") // (1 << level), 4)
+    unit = eye(total.shape[0])
+    odd = lax.rem(place, 2) == 1
+    first = jnp.where(odd, cross[...], near[...])
+    second = far[...]
+    joined = mul_exact(later[...], jnp.where(place == 3, unit, first))
+    rest = jnp.where(place == 0, mul_exact(second, cross[...]), jnp.where(place == 1, second, unit))
+    entering[...] = mul_exact(joined, rest)
+    upper_total[...] = jnp.where(odd, total[...], near[...])
+    new_before[...] = jnp.where(odd, mul_exact(near[...], before[...]), before[...])
+
+
+def carry_kernel(plan, suffixes, later, _, ens_factors, cot_factors, follow):
     count, members = plan.count, plan.members
-    entering = jnp.where(lax.rem(lax.axis_index("space"), 2) == 1, mine[...], other[...])
+    entering = later[...]
     mask = on_blocks(members, plan.stack * members)
     repeated = split(jnp.concatenate([entering] * plan.stack, axis=1))
     for at, (start, stop) in enumerate(plan.groups):
@@ -283,17 +289,18 @@
         copy.wait()
 
 
-def final_kernel(
-    plan, scale, gram_mine, gram_other, carry_mine, carry_other, follow, steps, _, out, buffer, sems
-):
+def final_kernel(plan, level, scale, number, *refs):
+    messages = refs[:number]
+    other, carry, before, follow, steps, _, out, buffer, sems = refs[number:]
     count, members = plan.count, plan.members
-    first = lax.rem(lax.axis_index("space"), 2) == 0
-    carry = jnp.where(first, carry_other[...], carry_mine[...])
-
+    added = mul_exact(other[...], before[...])
+    carry = carry[...] + jnp.where(upper_half(level), added, 0.0)
     totals = []
     for at, (start, stop) in enumerate(plan.groups):
-        lanes = plan.lanes(at)
-        tall = jnp.where(first, gram_mine[:, lanes], gram_other[:, lanes]).T
+        wide = messages[0][:, plan.lanes(at)]
+        for ref in messages[1:]:
+            wide = wide + ref[:, plan.lanes(at)]
+        tall = wide.T
         for i in range(stop - start):
             totals.append(tall[i * members : (i + 1) * members])
     totals[0] = totals[0] + carry.T
@@ -352,24 +359,15 @@
         for value in (ensembles, cotangents, transforms)
     )
 
-    def send(value, target, core):
-        pairs = []
-        for at in range(blocks * lanes):
-            block, lane = divmod(at, lanes)
-            if lane % 2 in core:
-                block, lane = target(block, lane)
-            pairs.append((at, block * lanes + lane))
-        return lax.ppermute(value, ("tm", "space"), pairs)
-
     def exchange(value, bit):
-        return send(value, lambda block, lane: (block ^ bit, lane), (1,))
-
-    def hand_over(value):
-        return send(value, lambda block, lane: (block, lane ^ 1), (0, 1))
-
-    def around(value, *core):
+        return lax.ppermute(value, "tm", [(at, at ^ bit) for at in range(blocks)])
+
+    def swap_cores(value):
+        return lax.ppermute(value, "space", [(at, at ^ 1) for at in range(lanes)])
+
+    def around(value):
         return [
-            send(value, lambda block, lane: (block, (lane + 2 * d) % lanes), core)
+            lax.ppermute(value, "space", [(at, (at + 2 * d) % lanes) for at in range(lanes)])
             for d in range(1, chips)
         ]
 
@@ -394,10 +392,19 @@
         befores.append(before)
         *new, upper = call(
             functools.partial(join_kernel, level),
-            [square] * 4, [VMEM] * 4 + [ANY], [VMEM] * 4, [], 3, f"join_{level}",
+            [square] * 4, [VMEM] * 4 + [ANY], [VMEM] * 4, [], 0.3, f"join_{level}",
         )(total, other, later, before, after)
         uppers.append(upper)
         return new
+
+    def add(values, after, name, *through):
+        number = len(values)
+        return call(
+            functools.partial(sum_kernel, number, len(through)),
+            [shape(*values[0].shape)] + [shape(*value.shape) for value in through],
+            [VMEM] * number + [ANY] * (1 + len(through)), [VMEM] + [ANY] * len(through), [], 0.1, name,
+            aliases={number + 1 + at: 1 + at for at in range(len(through))},
+        )(*values, after, *through)
 
     other = exchange(total, 1)
     early_width = plan.lanes(plan.first_group[-1]).start
@@ -410,45 +417,39 @@
     )(ensembles, cotangents, suffixes, *first_part)
     parts = [first_part] + [loaded[at : at + 2] for at in range(0, len(loaded), 2)]
     total, later, before = join(0, total, other, later, before, offset)
-
-    other = exchange(total, 2)
+    for level in range(1, levels - 2):
+        other = exchange(total, 1 << level)
+        total, later, before = join(level, total, other, later, before, total)
+
+    others = [exchange(total, bit << (levels - 2)) for bit in (1, 2, 3)]
     gram, offset = call(
         functools.partial(late_gram_kernel, plan),
         [wide, square], [VMEM] * 5 + [ANY], [VMEM] * 2, [], 1.2, "late_gram",
     )(*parts[-1], suffixes, early, offset, total)
-    offset_core = hand_over(offset)
-    for level in range(1, levels - 1):
-        total, later, before = join(level, total, other, later, before, gram)
-        other = exchange(total, 2 << level)
+    offset_core = swap_cores(offset)
     befores.append(before)
-    offset, gram = call(
-        chip_kernel, [square, wide], [VMEM] * 2 + [ANY] * 2, [VMEM, ANY], [], 0.2, "chip_offset",
-        aliases={3: 1},
-    )(offset, offset_core, total, gram)
-    gram_core = hand_over(gram)
-    offsets = [offset] + around(offset, 1)
+    entering, upper, before = call(
+        functools.partial(enter_kernel, levels - 2),
+        [square] * 3, [VMEM] * 6, [VMEM] * 3, [], 0.4, "entering",
+    )(total, later, before, *others)
+    uppers.append(upper)
+    befores.append(before)
+    offset, gram = add([offset, offset_core], entering, "chip_offset", gram)
+    gram_core = swap_cores(gram)
+    offsets = [offset] + around(offset)
 
     steps = call(
         functools.partial(windows_kernel, plan),
         shape(2, count_steps(count) * members, members, kind=BF16), [VMEM, ANY], VMEM,
-        [pltpu.VMEM((count * members, members), F32)], 10, "windows",
+        [pltpu.VMEM((count * members, members), F32)], 1.0, "windows",
     )(kept, offset)
-    entering, own, gram_core = call(
-        functools.partial(enter_kernel, levels - 1, chips),
-        [square] * 2 + [wide], [VMEM] * (2 + chips) + [ANY] * 2, [VMEM] * 2 + [ANY], [], 0.2,
-        "entering", aliases={3 + chips: 2},
-    )(later, other, *offsets, steps, gram_core)
-    other_own = exchange(own, 1)
-    gram = gram + gram_core
-    grams = around(gram, 0)
-    entering_core = hand_over(entering)
     size = plan.stack * members
     ens_factors, cot_factors, follow = call(
         functools.partial(carry_kernel, plan),
         [shape(len(plan.groups), size, size, kind=BF16)] * 2
         + [shape(2, count * members, members, kind=BF16)],
-        [VMEM] * 3 + [ANY], [VMEM] * 3, [], 0.1, "carries",
-    )(suffixes, entering, entering_core, own)
+        [VMEM] * 2 + [ANY], [VMEM] * 3, [], 0.9, "carries",
+    )(suffixes, entering, steps)
 
     def apply(factors, which, pieces, out, after, name, micros):
         first, last = plan.pieces[pieces[0]][0], plan.pieces[pieces[-1]][1]
@@ -462,39 +463,31 @@
         )(factors, *(parts[piece][which] for piece in pieces), after, *out)
 
     front, rear = tuple(range(PIECES - 1)), (PIECES - 1,)
-    smoothed, done = apply(ens_factors, 0, rear, (), follow, "smoothed_0", 0.1)
+    smoothed, done = apply(ens_factors, 0, rear, (), follow, "smoothed_0", 1.4)
+    own, gram_core = add(offsets, done, "own_offset", gram_core)
+    gram = gram + gram_core
+    grams = [gram] + around(gram)
     carry = jnp.zeros((members, members), F32)
-    for level in range(levels - 1):
-        waits = level > 0
-        own, carry, *rest = call(
-            functools.partial(pass_kernel, level),
-            [square] * 2 + [wide] * waits,
-            [VMEM] * 5 + [ANY] * (1 + waits), [VMEM] * 2 + [ANY] * waits, [], 0.3, f"pass_{level}",
-            aliases={6: 2} if waits else None,
-        )(own, other_own, carry, uppers[level], befores[level], done, *grams[:waits])
-        grams[:waits] = rest
-        other_own = exchange(own, 2 << level)
+    for level in range(levels):
+        other = exchange(own, 1 << level)
         if level == 0:
-            smoothed, done = apply(ens_factors, 0, front, (smoothed,), own, "smoothed_1", 2.4)
+            smoothed, done = apply(ens_factors, 0, front, (smoothed,), own, "smoothed_1", 2.3)
         if level == 1:
-            ensemble_grad, done = apply(cot_factors, 1, front, (), own, "ensemble_grad_0", 2.4)
-    carry, grams[0] = call(
-        functools.partial(last_pass_kernel, levels - 1),
-        [square, wide], [VMEM] * 3 + [ANY] * 2, [VMEM, ANY], [], 0.2, "pass_last",
-        aliases={4: 1},
-    )(other_own, carry, befores[-1], done, grams[0])
-    for part in grams:
-        gram = gram + part
-    gram_other = hand_over(gram)
-    carry_other = hand_over(carry)
-    ensemble_grad, done = apply(cot_factors, 1, rear, (ensemble_grad,), carry, "ensemble_grad_1", 1.4)
+            ensemble_grad, done = apply(cot_factors, 1, front, (), own, "ensemble_grad_0", 2.3)
+        if level == levels - 1:
+            ensemble_grad, done = apply(cot_factors, 1, rear, (ensemble_grad,), own, "ensemble_grad_1", 1.4)
+        if level < levels - 1:
+            own, carry = call(
+                functools.partial(pass_kernel, level),
+                [square] * 2, [VMEM] * 5 + [ANY], [VMEM] * 2, [], 0.3, f"pass_{level}",
+            )(own, other, carry, uppers[level], befores[level], done)
     transform_grad = call(
-        functools.partial(final_kernel, plan, scale),
+        functools.partial(final_kernel, plan, levels - 1, scale, chips),
         shape(count, members, members),
-        [VMEM] * 6 + [ANY], HBM,
+        [VMEM] * (chips + 5) + [ANY], HBM,
         [pltpu.VMEM((count, members, members), F32), pltpu.SemaphoreType.DMA((count,))],
         2.5, "transform_grad",
-    )(gram, gram_other, carry, carry_other, follow, steps, done)
+    )(*grams, other, carry, befores[-1], follow, steps, done)
     return (smoothed, ensemble_grad, transform_grad)
 
 

time: 49 us -> 43.6 us (0.89)
  starting transfers between devices: 25.9 us -> 10.7 us
  waiting for transfers between devices: 0.87 us -> 10.9 us
    ppermute x13 -> x11, starting transfers between devices: 25.9 us -> 10.7 us  [the longest x7 8.14 us: exchange(): return lax.ppermute(value, 'tm', [(at, at ^ bit) for at in range(blocks)])]
    ppermute x13 -> x11, waiting for transfers between devices: 0.87 us -> 10.9 us  [the longest x7 10.9 us: exchange(): return lax.ppermute(value, 'tm', [(at, at ^ bit) for at in range(blocks)])]
  transfers between devices with their start and end apart: 13 -> 11, of which waited for: 2 -> 5; matrix products, arithmetic and copies ran while one was open for 0% -> 0% of each run, Pallas kernels for 30% -> 34%
where the time goes in v7:
time: 43.6 us; the launch traced here: 43.4 us
  Pallas kernels  20.8 us (48%)
  waiting for transfers between devices  10.9 us (25%)
  starting transfers between devices  10.7 us (25%)
  between operations  0.82 us (2%)
    ppermute x7, waiting for transfers between devices, exchange(): return lax.ppermute(value, 'tm', [(at, at ^ bit) for at in range(blocks)])  10.9 us
    ppermute x7, starting transfers between devices, exchange(): return lax.ppermute(value, 'tm', [(at, at ^ bit) for at in range(blocks)])  8.14 us
    pallas_call x4, Pallas kernels, apply(): call(functools.partial(apply_kernel, plan, pieces), [shape(count, members...  7.29 us
    pallas_call x1, Pallas kernels, shards(): call(functools.partial(early_gram_kernel, plan), [shape(members, early_wi...  3.85 us
    pallas_call x1, Pallas kernels, shards(): call(functools.partial(chain_kernel, plan), [shape(count * members, membe...  3.22 us
    pallas_call x1, Pallas kernels, shards(): call(functools.partial(final_kernel, plan, levels - 1, scale, chips), sha...  2.46 us
    ppermute x2, starting transfers between devices, around(): lax.ppermute(value, 'space', [(at, (at + 2 * d) % lanes) for at in range(...  2.44 us
    pallas_call x1, Pallas kernels, shards(): call(functools.partial(late_gram_kernel, plan), [wide, square], [VMEM] *...  1.14 us
  transfers between devices with their start and end apart: 11, of which 5 were waited for; matrix products, arithmetic and copies ran while one was open for 0% of the time, Pallas kernels for 34%

profile of v7, /device:TPU:0, one launch (start us, length us, event | category | flops | bytes accessed | tf_op | source)
XLA Modules:
  0.0 43.4 jit_solution(16936103286581328659)
XLA Ops:
  0.6 3.2 %transform_chain.1 = (f32[1280,80]{1,0:T(8,128)S(1)}, f32[80,80]{1,0:T(8,128)S(1)}, f32[16,80,80]{2,1,0:T(8,128)S(1)}, bf16[6,80,2048]{2,1,0:T(8,128)(2,1)S(1)}, bf16[6,80,2048]{2,1,0:T(8,128)(2,1)S(1)}) custom-call(f32[16,80,80]{2,1,0:T(8,128)} %transforms.1, bf16[16,80,2048]{2,1,0:T(8,128)(2,1)} %ensembles.3, bf16[16,80,2048]{2,1,0:T(8,128)(2,1)} %cotangents.3), custom_call_target="tpu_custom_call" | custom-call | bytes 12600000 | tf_op jit(solution)/shard_map/transform_chain/pallas_call | solution.py:381
  3.9 3.0 %collective-permute-start = (f32[80,80]{1,0:T(8,128)S(1)}, f32[80,80]{1,0:T(8,128)S(1)}, u32[]{:S(2)}, u32[]{:S(2)}) collective-permute-start(f32[80,80]{1,0:T(8,128)S(1)} %get-tuple-element.43.total), channel_id=1, source_target_pairs={{0,4},{4,0},{8,12},{12,8},{16,20},{20,16},{24,28},{28,24},{1,5},{5... | collective-permute-start | bytes 76808 | tf_op jit(solution)/shard_map/ppermute | solution.py:363
  6.9 3.8 %early_gram.1 = (f32[80,1024]{1,0:T(8,128)S(1)}, f32[80,80]{1,0:T(8,128)S(1)}, bf16[6,80,2048]{2,1,0:T(8,128)(2,1)S(1)}, bf16[6,80,2048]{2,1,0:T(8,128)(2,1)S(1)...) custom-call(bf16[16,80,2048]{2,1,0:T(8,128)(2,1)} %ensembles.3, bf16[16,80,2048]{2,1,0:T(8,128)(2,1)} %cotangents.3, ...), custom_call_target="tpu_custom_call" | custom-call | bytes 10800000 | tf_op jit(solution)/shard_map/early_gram/pallas_call | solution.py:411
  10.7 0.0 collective-permute-done.other
  10.7 0.3 join_0.1
  11.0 1.6 %collective-permute-start.1 = (f32[80,80]{1,0:T(8,128)S(1)}, f32[80,80]{1,0:T(8,128)S(1)}, u32[]{:S(2)}, u32[]{:S(2)}) collective-permute-start(f32[80,80]{1,0:T(8,128)S(1)} %get-tuple-element.47.total._), channel_id=1, source_target_pairs={{0,8},{4,12},{8,0},{12,4},{16,24},{20,28},{24,16},{28,20},{1,9},{5... | collective-permute-start | bytes 76808 | tf_op jit(solution)/shard_map/ppermute | solution.py:363
  12.6 2.6 %collective-permute-start.2 = (f32[80,80]{1,0:T(8,128)S(1)}, f32[80,80]{1,0:T(8,128)S(1)}, u32[]{:S(2)}, u32[]{:S(2)}) collective-permute-start(f32[80,80]{1,0:T(8,128)S(1)} %get-tuple-element.47.total._), channel_id=1, source_target_pairs={{0,16},{4,20},{8,24},{12,28},{16,0},{20,4},{24,8},{28,12},{1,17},{... | collective-permute-start | bytes 76808 | tf_op jit(solution)/shard_map/ppermute | solution.py:363
  15.2 0.2 collective-permute-start.3
  15.5 1.1 %late_gram.1 = (f32[80,1408]{1,0:T(8,128)S(1)}, f32[80,80]{1,0:T(8,128)S(1)}) custom-call(bf16[4,80,2048]{2,1,0:T(8,128)(2,1)S(1)} %get-tuple-element.52.ens.refs_0_, bf16[4,80,2048]{2,1,0:T(8,128)(2,1)S(1)} %get-tuple-element.53.cot.refs_0_, f32[1280,80]{1,0:T(8,128)S(1)} %get-tuple-element.42.suffixes, f32[80,1024]{1,0:T(8,128)S(1)} %get-tuple-element.54.early, ...), custom_call_target="tpu_custom_call" | custom-call | bytes 4320000 | tf_op jit(solution)/shard_map/late_gram/pallas_call | solution.py:425
  16.6 0.1 collective-permute-start.4
  16.7 0.0 collective-permute-done.1.near
  16.7 1.3 %collective-permute-done.2.far = f32[80,80]{1,0:T(8,128)S(1)} collective-permute-done((f32[80,80]{1,0:T(8,128)S(1)}, f32[80,80]{1,0:T(8,128)S(1)}, u32[]{:S(2)}, u32[]{:S(2)}) %collective-permute-start.2) | collective-permute-done | bytes 25632 | tf_op jit(solution)/shard_map/ppermute | solution.py:363
  18.0 3.0 %collective-permute-done.3.cross = f32[80,80]{1,0:T(8,128)S(1)} collective-permute-done((f32[80,80]{1,0:T(8,128)S(1)}, f32[80,80]{1,0:T(8,128)S(1)}, u32[]{:S(2)}, u32[]{:S(2)}) %collective-permute-start.3) | collective-permute-done | bytes 25632 | tf_op jit(solution)/shard_map/ppermute | solution.py:363
  21.0 0.4 entering.1
  21.4 0.0 collective-permute-done.4.refs_1_
  21.4 0.1 collective-permute-start.6
  21.5 1.6 %collective-permute-start.5 = (f32[80,80]{1,0:T(8,128)S(1)}, f32[80,80]{1,0:T(8,128)S(1)}, u32[]{:S(2)}, u32[]{:S(2)}) collective-permute-start(f32[80,80]{1,0:T(8,128)S(1)} %get-tuple-element.57._.refs_0_), channel_id=1, source_target_pairs={{0,2},{1,3},{2,0},{3,1},{4,6},{5,7},{6,4},{7,5},{8,10},{9,11},{10,... | collective-permute-start | bytes 76808 | tf_op jit(solution)/shard_map/ppermute | solution.py:370
  23.1 0.9 %windows.1._.refs_6_ = bf16[2,2560,80]{2,1,0:T(8,128)(2,1)S(1)} custom-call(f32[16,80,80]{2,1,0:T(8,128)S(1)} %get-tuple-element.51.kept, f32[80,80]{1,0:T(8,128)S(1)} %get-tuple-element.57._.refs_0_), custom_call_target="tpu_custom_call" | custom-call | bytes 3600000 | tf_op jit(solution)/shard_map/windows/pallas_call | solution.py:441
  24.1 0.9 %carries.1 = (bf16[6,240,240]{2,1,0:T(8,128)(2,1)S(1)}, bf16[6,240,240]{2,1,0:T(8,128)(2,1)S(1)}, bf16[2,1280,80]{2,1,0:T(8,128)(2,1)S(1)}) custom-call(f32[1280,80]{1,0:T(8,128)S(1)} %get-tuple-element.42.suffixes, f32[80,80]{1,0:T(8,128)S(1)} %get-tuple-element.50.refs_2_.later, bf16[2,2560,80]{2,1,0:T(8,128)(2,1)S(1)} %windows.1._.refs_6_), custom_call_target="tpu_custom_call" | custom-call | bytes 3240000 | tf_op jit(solution)/shard_map/carries/pallas_call | solution.py:447
  24.9 1.4 %smoothed_0.1 = (bf16[16,80,2048]{2,1,0:T(8,128)(2,1)}, f32[8,128]{1,0:T(8,128)S(1)}) custom-call(bf16[6,240,240]{2,1,0:T(8,128)(2,1)S(1)} %get-tuple-element.58.factors, bf16[4,80,2048]{2,1,0:T(8,128)(2,1)S(1)} %get-tuple-element.52.ens.refs_0_, bf16[2,1280,80]{2,1,0:T(8,128)(2,1)S(1)} %get-tuple-element.60.refs_1_.refs_5_), custom_call_target="tpu_custom_call" | custom-call | bytes 5040000 | tf_op jit(solution)/shard_map/smoothed_0/pallas_call | solution.py:457
  26.3 0.0 collective-permute-done.5.refs_1_
  26.3 0.0 collective-permute-done.6.refs_3_
  26.3 0.1 add.3.refs_0_
  26.4 0.9 %collective-permute-start.9 = (f32[80,1408]{1,0:T(8,128)S(1)}, f32[80,1408]{1,0:T(8,128)S(1)}, u32[]{:S(2)}, u32[]{:S(2)}) collective-permute-start(f32[80,1408]{1,0:T(8,128)S(1)} %add.3.refs_0_), channel_id=1, source_target_pairs={{0,2},{1,3},{2,0},{3,1},{4,6},{5,7},{6,4},{7,5},{8,10},{9,11},{10,... | collective-permute-start | bytes 1351688 | tf_op jit(solution)/shard_map/ppermute | solution.py:370
  27.3 0.5 %collective-permute-start.7 = (f32[80,80]{1,0:T(8,128)S(1)}, f32[80,80]{1,0:T(8,128)S(1)}, u32[]{:S(2)}, u32[]{:S(2)}) collective-permute-start(f32[80,80]{1,0:T(8,128)S(1)} %get-tuple-element.63.refs_2_.own), channel_id=1, source_target_pairs={{0,4},{4,0},{8,12},{12,8},{16,20},{20,16},{24,28},{28,24},{1,5},{5... | collective-permute-start | bytes 76808 | tf_op jit(solution)/shard_map/ppermute | solution.py:363
  27.8 2.3 %smoothed_1.1 = (bf16[16,80,2048]{2,1,0:T(8,128)(2,1)}, f32[8,128]{1,0:T(8,128)S(1)}) custom-call(bf16[6,240,240]{2,1,0:T(8,128)(2,1)S(1)} %get-tuple-element.58.factors, bf16[6,80,2048]{2,1,0:T(8,128)(2,1)S(1)} %get-tuple-element.44.ens.refs_0_, bf16[6,80,2048]{2,1,0:T(8,128)(2,1)S(1)} %get-tuple-element.59.refs_1_, ...), custom_call_target="tpu_custom_call", output_to_operand_aliasing={{0}: (4, {})} | custom-call | bytes 8279999 | tf_op jit(solution)/shard_map/smoothed_1/pallas_call | solution.py:457
  30.1 1.2 %collective-permute-done.7.other = f32[80,80]{1,0:T(8,128)S(1)} collective-permute-done((f32[80,80]{1,0:T(8,128)S(1)}, f32[80,80]{1,0:T(8,128)S(1)}, u32[]{:S(2)}, u32[]{:S(2)}) %collective-permute-start.7) | collective-permute-done | bytes 25632 | tf_op jit(solution)/shard_map/ppermute | solution.py:363
  31.3 0.2 pass_0.1
  31.5 0.1 collective-permute-start.8
  31.6 2.3 %ensemble_grad_0.1 = (bf16[16,80,2048]{2,1,0:T(8,128)(2,1)}, f32[8,128]{1,0:T(8,128)S(1)}) custom-call(bf16[6,240,240]{2,1,0:T(8,128)(2,1)S(1)} %get-tuple-element.66.factors, bf16[6,80,2048]{2,1,0:T(8,128)(2,1)S(1)} %get-tuple-element.45.cot.refs_0_, bf16[6,80,2048]{2,1,0:T(8,128)(2,1)S(1)} %get-tuple-element.72.refs_1_, ...), custom_call_target="tpu_custom_call" | custom-call | bytes 8279999 | tf_op jit(solution)/shard_map/ensemble_grad_0/pallas_call | solution.py:457
  33.8 1.7 %collective-permute-done.8.other = f32[80,80]{1,0:T(8,128)S(1)} collective-permute-done((f32[80,80]{1,0:T(8,128)S(1)}, f32[80,80]{1,0:T(8,128)S(1)}, u32[]{:S(2)}, u32[]{:S(2)}) %collective-permute-start.8) | collective-permute-done | bytes 25632 | tf_op jit(solution)/shard_map/ppermute | solution.py:363
  35.5 0.2 pass_1.1
  35.8 0.1 collective-permute-start.10
  35.8 1.4 %ensemble_grad_1.1 = (bf16[16,80,2048]{2,1,0:T(8,128)(2,1)}, f32[8,128]{1,0:T(8,128)S(1)}) custom-call(bf16[6,240,240]{2,1,0:T(8,128)(2,1)S(1)} %get-tuple-element.66.factors, bf16[4,80,2048]{2,1,0:T(8,128)(2,1)S(1)} %get-tuple-element.53.cot.refs_0_, f32[80,80]{1,0:T(8,128)S(1)} %get-tuple-element.74.refs_1_, ...), custom_call_target="tpu_custom_call", output_to_operand_aliasing={{0}: (3, {})} | custom-call | bytes 5040000 | tf_op jit(solution)/shard_map/ensemble_grad_1/pallas_call | solution.py:457
  37.2 3.7 %collective-permute-done.10.refs_2_ = f32[80,80]{1,0:T(8,128)S(1)} collective-permute-done((f32[80,80]{1,0:T(8,128)S(1)}, f32[80,80]{1,0:T(8,128)S(1)}, u32[]{:S(2)}, u32[]{:S(2)}) %collective-permute-start.10) | collective-permute-done | bytes 25632 | tf_op jit(solution)/shard_map/ppermute | solution.py:363
  40.9 0.0 collective-permute-done.9.refs_1_
  40.9 2.5 %transform_grad.1 = f32[16,80,80]{2,1,0:T(8,128)} custom-call(f32[80,1408]{1,0:T(8,128)S(1)} %add.3.refs_0_, f32[80,1408]{1,0:T(8,128)S(1)} %collective-permute-done.9.refs_1_, f32[80,80]{1,0:T(8,128)S(1)} %collective-permute-done.10.refs_2_, f32[80,80]{1,0:T(8,128)S(1)} %get-tuple-element.78.refs_3_, f32[80,80]{1,0:T(8,128)S(1)} %get-tuple-element.79.refs_4_, ...), custom_call_target="tpu_custom_call" | custom-call | bytes 9000000 | tf_op jit(solution)/shard_map/transform_grad/pallas_call | solution.py:484
  (4 shorter events, 0.0 us)
Async XLA Ops:
  3.9 6.9 %collective-permute-start = (f32[80,80]{1,0:T(8,128)S(1)}, f32[80,80]{1,0:T(8,128)S(1)}, u32[]{:S(2)}, u32[]{:S(2)}) collective-permute-start(f32[80,80]{1,0:T(8,128)S(1)} %get-tuple-element.43.total), channel_id=1, source_target_pairs={{0,4},{4,0},{8,12},{12,8},{16,20},{20,16},{24,28},{28,24},{1,5},{5... | collective-permute-start | bytes 76808 | tf_op jit(solution)/shard_map/ppermute | solution.py:363
  11.0 5.7 %collective-permute-start.1 = (f32[80,80]{1,0:T(8,128)S(1)}, f32[80,80]{1,0:T(8,128)S(1)}, u32[]{:S(2)}, u32[]{:S(2)}) collective-permute-start(f32[80,80]{1,0:T(8,128)S(1)} %get-tuple-element.47.total._), channel_id=1, source_target_pairs={{0,8},{4,12},{8,0},{12,4},{16,24},{20,28},{24,16},{28,20},{1,9},{5... | collective-permute-start | bytes 76808 | tf_op jit(solution)/shard_map/ppermute | solution.py:363
  12.6 5.4 %collective-permute-start.2 = (f32[80,80]{1,0:T(8,128)S(1)}, f32[80,80]{1,0:T(8,128)S(1)}, u32[]{:S(2)}, u32[]{:S(2)}) collective-permute-start(f32[80,80]{1,0:T(8,128)S(1)} %get-tuple-element.47.total._), channel_id=1, source_target_pairs={{0,16},{4,20},{8,24},{12,28},{16,0},{20,4},{24,8},{28,12},{1,17},{... | collective-permute-start | bytes 76808 | tf_op jit(solution)/shard_map/ppermute | solution.py:363
  15.2 5.8 %collective-permute-start.3 = (f32[80,80]{1,0:T(8,128)S(1)}, f32[80,80]{1,0:T(8,128)S(1)}, u32[]{:S(2)}, u32[]{:S(2)}) collective-permute-start(f32[80,80]{1,0:T(8,128)S(1)} %get-tuple-element.47.total._), channel_id=1, source_target_pairs={{0,24},{4,28},{8,16},{12,20},{16,8},{20,12},{24,0},{28,4},{1,25},{... | collective-permute-start | bytes 76808 | tf_op jit(solution)/shard_map/ppermute | solution.py:363
  16.6 4.8 %collective-permute-start.4 = (f32[80,80]{1,0:T(8,128)S(1)}, f32[80,80]{1,0:T(8,128)S(1)}, u32[]{:S(2)}, u32[]{:S(2)}) collective-permute-start(f32[80,80]{1,0:T(8,128)S(1)} %get-tuple-element.55.refs_0_), channel_id=1, source_target_pairs={{0,1},{1,0},{2,3},{3,2},{4,5},{5,4},{6,7},{7,6},{8,9},{9,8},{10,11... | collective-permute-start | bytes 76808 | tf_op jit(solution)/shard_map/ppermute | solution.py:366
  21.4 4.9 %collective-permute-start.6 = (f32[80,1408]{1,0:T(8,128)S(1)}, f32[80,1408]{1,0:T(8,128)S(1)}, u32[]{:S(2)}, u32[]{:S(2)}) collective-permute-start(f32[80,1408]{1,0:T(8,128)S(1)} %get-tuple-element.62), channel_id=1, source_target_pairs={{0,1},{1,0},{2,3},{3,2},{4,5},{5,4},{6,7},{7,6},{8,9},{9,8},{10,11... | collective-permute-start | bytes 1351688 | tf_op jit(solution)/shard_map/ppermute | solution.py:366
  21.5 4.8 %collective-permute-start.5 = (f32[80,80]{1,0:T(8,128)S(1)}, f32[80,80]{1,0:T(8,128)S(1)}, u32[]{:S(2)}, u32[]{:S(2)}) collective-permute-start(f32[80,80]{1,0:T(8,128)S(1)} %get-tuple-element.57._.refs_0_), channel_id=1, source_target_pairs={{0,2},{1,3},{2,0},{3,1},{4,6},{5,7},{6,4},{7,5},{8,10},{9,11},{10,... | collective-permute-start | bytes 76808 | tf_op jit(solution)/shard_map/ppermute | solution.py:370
  26.4 14.5 %collective-permute-start.9 = (f32[80,1408]{1,0:T(8,128)S(1)}, f32[80,1408]{1,0:T(8,128)S(1)}, u32[]{:S(2)}, u32[]{:S(2)}) collective-permute-start(f32[80,1408]{1,0:T(8,128)S(1)} %add.3.refs_0_), channel_id=1, source_target_pairs={{0,2},{1,3},{2,0},{3,1},{4,6},{5,7},{6,4},{7,5},{8,10},{9,11},{10,... | collective-permute-start | bytes 1351688 | tf_op jit(solution)/shard_map/ppermute | solution.py:370
  27.3 4.0 %collective-permute-start.7 = (f32[80,80]{1,0:T(8,128)S(1)}, f32[80,80]{1,0:T(8,128)S(1)}, u32[]{:S(2)}, u32[]{:S(2)}) collective-permute-start(f32[80,80]{1,0:T(8,128)S(1)} %get-tuple-element.63.refs_2_.own), channel_id=1, source_target_pairs={{0,4},{4,0},{8,12},{12,8},{16,20},{20,16},{24,28},{28,24},{1,5},{5... | collective-permute-start | bytes 76808 | tf_op jit(solution)/shard_map/ppermute | solution.py:363
  31.5 4.1 %collective-permute-start.8 = (f32[80,80]{1,0:T(8,128)S(1)}, f32[80,80]{1,0:T(8,128)S(1)}, u32[]{:S(2)}, u32[]{:S(2)}) collective-permute-start(f32[80,80]{1,0:T(8,128)S(1)} %get-tuple-element.69.refs_2_.own), channel_id=1, source_target_pairs={{0,8},{4,12},{8,0},{12,4},{16,24},{20,28},{24,16},{28,20},{1,9},{5... | collective-permute-start | bytes 76808 | tf_op jit(solution)/shard_map/ppermute | solution.py:363
  35.8 5.2 %collective-permute-start.10 = (f32[80,80]{1,0:T(8,128)S(1)}, f32[80,80]{1,0:T(8,128)S(1)}, u32[]{:S(2)}, u32[]{:S(2)}) collective-permute-start(f32[80,80]{1,0:T(8,128)S(1)} %get-tuple-element.74.refs_1_), channel_id=1, source_target_pairs={{0,16},{4,20},{8,24},{12,28},{16,0},{20,4},{24,8},{28,12},{1,17},{... | collective-permute-start | bytes 76808 | tf_op jit(solution)/shard_map/ppermute | solution.py:363

commit v8 on v7

--- a/solution.py
+++ b/solution.py
@@ -206,39 +206,15 @@
     refs[number + 1 + through][...] = total
 
 
-def upper_half(level):
-    return lax.rem(lax.axis_index("tm") // (1 << level), 2) == 1
-
-
-def join_kernel(level, total, other, later, before, _, new_total, new_later, new_before, upper_total):
-    upper = upper_half(level)
-    left = jnp.where(upper, other[...], total[...])
-    right = jnp.where(upper, total[...], other[...])
-    new_total[...] = mul_exact(left, right)
-    upper_total[...] = right
-    new_later[...] = jnp.where(upper, later[...], mul_exact(later[...], other[...]))
-    new_before[...] = jnp.where(upper, mul_exact(other[...], before[...]), before[...])
-
-
-def pass_kernel(level, own, other, carry, upper_total, before, _, new_own, new_carry):
-    upper = upper_half(level)
-    left = jnp.where(upper, other[...], own[...])
-    right = jnp.where(upper, own[...], other[...])
-    new_own[...] = mul_exact(left, upper_total[...]) + right
-    new_carry[...] = carry[...] + jnp.where(upper, mul_exact(left, before[...]), 0.0)
-
-
-def enter_kernel(level, total, later, before, near, far, cross, entering, upper_total, new_before):
-    place = lax.rem(lax.axis_index("tm") // (1 << level), 4)
-    unit = eye(total.shape[0])
-    odd = lax.rem(place, 2) == 1
-    first = jnp.where(odd, cross[...], near[...])
-    second = far[...]
-    joined = mul_exact(later[...], jnp.where(place == 3, unit, first))
-    rest = jnp.where(place == 0, mul_exact(second, cross[...]), jnp.where(place == 1, second, unit))
-    entering[...] = mul_exact(joined, rest)
-    upper_total[...] = jnp.where(odd, total[...], near[...])
-    new_before[...] = jnp.where(odd, mul_exact(near[...], before[...]), before[...])
+def enter_kernel(blocks, products, entering, windows):
+    members = entering.shape[0]
+    mine = lax.axis_index("tm")
+    unit = eye(members)
+    factors = [products[at] for at in range(blocks)]
+    entering[...] = product_of([jnp.where(at > mine, factors[at], unit) for at in range(1, blocks)])
+    for at in range(1, blocks):
+        windows[(at - 1) * members : at * members] = jnp.where(at < mine, factors[at], unit)
+    suffix_scan(windows, blocks - 1, members, blocks - 1)
 
 
 def carry_kernel(plan, suffixes, later, _, ens_factors, cot_factors, follow):
@@ -289,12 +265,15 @@
         copy.wait()
 
 
-def final_kernel(plan, level, scale, number, *refs):
+def final_kernel(plan, blocks, scale, number, *refs):
     messages = refs[:number]
-    other, carry, before, follow, steps, _, out, buffer, sems = refs[number:]
+    offsets, windows, follow, steps, _, out, buffer, sems = refs[number:]
     count, members = plan.count, plan.members
-    added = mul_exact(other[...], before[...])
-    carry = carry[...] + jnp.where(upper_half(level), added, 0.0)
+    mine = lax.axis_index("tm")
+    carry = jnp.zeros((members, members), F32)
+    for at in range(blocks - 1):
+        window = windows[at * members : (at + 1) * members]
+        carry = carry + mul_exact(jnp.where(at < mine, offsets[at], 0.0), window)
     totals = []
     for at, (start, stop) in enumerate(plan.groups):
         wide = messages[0][:, plan.lanes(at)]
@@ -352,15 +331,15 @@
     chips = lanes // 2
     scale = 1.0 / math.sqrt(cells * lanes * count * blocks)
     plan = Plan(count, members)
-    levels = blocks.bit_length() - 1
     square = shape(members, members)
     ensembles, cotangents, transforms = (
         pltpu.with_memory_space_constraint(value, pltpu.HBM)
         for value in (ensembles, cotangents, transforms)
     )
 
-    def exchange(value, bit):
-        return lax.ppermute(value, "tm", [(at, at ^ bit) for at in range(blocks)])
+    def to_all(value):
+        copies = jnp.broadcast_to(value[None], (blocks,) + value.shape)
+        return lax.all_to_all(copies, "tm", 0, 0)
 
     def swap_cores(value):
         return lax.ppermute(value, "space", [(at, at ^ 1) for at in range(lanes)])
@@ -385,18 +364,6 @@
     )(transforms, ensembles, cotangents)
 
     wide = shape(members, plan.width)
-    later = before = jnp.eye(members, dtype=F32)
-    uppers, befores = [], []
-
-    def join(level, total, other, later, before, after):
-        befores.append(before)
-        *new, upper = call(
-            functools.partial(join_kernel, level),
-            [square] * 4, [VMEM] * 4 + [ANY], [VMEM] * 4, [], 0.3, f"join_{level}",
-        )(total, other, later, before, after)
-        uppers.append(upper)
-        return new
-
     def add(values, after, name, *through):
         number = len(values)
         return call(
@@ -406,7 +373,7 @@
             aliases={number + 1 + at: 1 + at for at in range(len(through))},
         )(*values, after, *through)
 
-    other = exchange(total, 1)
+    products = to_all(total)
     early_width = plan.lanes(plan.first_group[-1]).start
     early, offset, *loaded = call(
         functools.partial(early_gram_kernel, plan),
@@ -416,27 +383,18 @@
         [sem for piece in range(1, PIECES) for sem in piece_sems(piece)], 3, "early_gram",
     )(ensembles, cotangents, suffixes, *first_part)
     parts = [first_part] + [loaded[at : at + 2] for at in range(0, len(loaded), 2)]
-    total, later, before = join(0, total, other, later, before, offset)
-    for level in range(1, levels - 2):
-        other = exchange(total, 1 << level)
-        total, later, before = join(level, total, other, later, before, total)
-
-    others = [exchange(total, bit << (levels - 2)) for bit in (1, 2, 3)]
     gram, offset = call(
         functools.partial(late_gram_kernel, plan),
         [wide, square], [VMEM] * 5 + [ANY], [VMEM] * 2, [], 1.2, "late_gram",
-    )(*parts[-1], suffixes, early, offset, total)
+    )(*parts[-1], suffixes, early, offset, offset)
     offset_core = swap_cores(offset)
-    befores.append(before)
-    entering, upper, before = call(
-        functools.partial(enter_kernel, levels - 2),
-        [square] * 3, [VMEM] * 6, [VMEM] * 3, [], 0.4, "entering",
-    )(total, later, before, *others)
-    uppers.append(upper)
-    befores.append(before)
-    offset, gram = add([offset, offset_core], entering, "chip_offset", gram)
+    offset, gram = add([offset, offset_core], offset, "chip_offset", gram)
     gram_core = swap_cores(gram)
     offsets = [offset] + around(offset)
+    entering, windows = call(
+        functools.partial(enter_kernel, blocks),
+        [square, shape((blocks - 1) * members, members)], [VMEM], [VMEM] * 2, [], 0.8, "entering",
+    )(products)
 
     steps = call(
         functools.partial(windows_kernel, plan),
@@ -467,27 +425,16 @@
     own, gram_core = add(offsets, done, "own_offset", gram_core)
     gram = gram + gram_core
     grams = [gram] + around(gram)
-    carry = jnp.zeros((members, members), F32)
-    for level in range(levels):
-        other = exchange(own, 1 << level)
-        if level == 0:
-            smoothed, done = apply(ens_factors, 0, front, (smoothed,), own, "smoothed_1", 2.3)
-        if level == 1:
-            ensemble_grad, done = apply(cot_factors, 1, front, (), own, "ensemble_grad_0", 2.3)
-        if level == levels - 1:
-            ensemble_grad, done = apply(cot_factors, 1, rear, (ensemble_grad,), own, "ensemble_grad_1", 1.4)
-        if level < levels - 1:
-            own, carry = call(
-                functools.partial(pass_kernel, level),
-                [square] * 2, [VMEM] * 5 + [ANY], [VMEM] * 2, [], 0.3, f"pass_{level}",
-            )(own, other, carry, uppers[level], befores[level], done)
+    offsets = to_all(own)
+    smoothed, done = apply(ens_factors, 0, front, (smoothed,), own, "smoothed_1", 2.3)
+    ensemble_grad, done = apply(cot_factors, 1, tuple(range(PIECES)), (), done, "ensemble_grad", 2.8)
     transform_grad = call(
-        functools.partial(final_kernel, plan, levels - 1, scale, chips),
+        functools.partial(final_kernel, plan, blocks, scale, chips),
         shape(count, members, members),
-        [VMEM] * (chips + 5) + [ANY], HBM,
+        [VMEM] * (chips + 4) + [ANY], HBM,
         [pltpu.VMEM((count, members, members), F32), pltpu.SemaphoreType.DMA((count,))],
         2.5, "transform_grad",
-    )(*grams, other, carry, befores[-1], follow, steps, done)
+    )(*grams, offsets, windows, follow, steps, done)
     return (smoothed, ensemble_grad, transform_grad)
 
 

time: 43.6 us -> 66.2 us (1.52)
  local copies, waits for them, and re-layouts: 0.01 us -> 14.8 us
  starting transfers between devices: 10.7 us -> 15 us
  Pallas kernels: 20.8 us -> 24.6 us
  waiting for transfers between devices: 10.9 us -> 8.22 us
  other arithmetic: 0.07 us -> 1.96 us
    unnamed x0 -> x44, local copies, waits for them, and re-layouts: none -> 13.3 us
    all_to_all x0 -> x2, starting transfers between devices: none -> 11 us  [to_all(): return lax.all_to_all(copies, 'tm', 0, 0)]
    ppermute x7 -> x0, waiting for transfers between devices: 10.9 us -> none  [exchange(): return lax.ppermute(value, 'tm', [(at, at ^ bit) for at in range(blocks)])]
    ppermute x7 -> x0, starting transfers between devices: 8.14 us -> none  [exchange(): return lax.ppermute(value, 'tm', [(at, at ^ bit) for at in range(blocks)])]
    all_to_all x0 -> x2, waiting for transfers between devices: none -> 7.34 us  [to_all(): return lax.all_to_all(copies, 'tm', 0, 0)]
    pallas_call x5 -> x2, Pallas kernels: 3.53 us -> 6.32 us  [the longest x1 4.27 us: shards(): call(functools.partial(final_kernel, plan, blocks, scale, chips), shape(c...]
    add x1, other arithmetic: 0.06 us -> 1.96 us  [shards(): gram = gram + gram_core]
    broadcast_in_dim x1 -> x2, local copies, waits for them, and re-layouts: 0.01 us -> 1.51 us  [to_all(): copies = jnp.broadcast_to(value[None], (blocks,) + value.shape)]
  transfers between devices with their start and end apart: 11 -> 6, of which waited for: 5 -> 2; matrix products, arithmetic and copies ran while one was open for 0% -> 2% of each run, Pallas kernels for 34% -> 16%
where the time goes in v8:
time: 66.2 us; the launch traced here: 65.5 us
  Pallas kernels  24.6 us (37%)
  starting transfers between devices  15 us (23%)
  local copies, waits for them, and re-layouts  14.8 us (22%)
  waiting for transfers between devices  8.22 us (12%)
  other arithmetic  1.96 us (3%)
  between operations  0.87 us (1%)
    unnamed x44, local copies, waits for them, and re-layouts  13.3 us
    all_to_all x2, starting transfers between devices, to_all(): return lax.all_to_all(copies, 'tm', 0, 0)  11 us
    all_to_all x2, waiting for transfers between devices, to_all(): return lax.all_to_all(copies, 'tm', 0, 0)  7.34 us
    pallas_call x3, Pallas kernels, apply(): call(functools.partial(apply_kernel, plan, pieces), [shape(count, members...  6.5 us
    pallas_call x1, Pallas kernels, shards(): call(functools.partial(early_gram_kernel, plan), [shape(members, early_wi...  4.86 us
    pallas_call x1, Pallas kernels, shards(): call(functools.partial(final_kernel, plan, blocks, scale, chips), shape(c...  4.27 us
    pallas_call x1, Pallas kernels, shards(): call(functools.partial(chain_kernel, plan), [shape(count * members, membe...  3.22 us
    ppermute x2, starting transfers between devices, around(): lax.ppermute(value, 'space', [(at, (at + 2 * d) % lanes) for at in range(...  3.1 us
  transfers between devices with their start and end apart: 6, of which 2 were waited for; matrix products, arithmetic and copies ran while one was open for 2% of the time, Pallas kernels for 16%

profile of v8, /device:TPU:0, one launch (start us, length us, event | category | flops | bytes accessed | tf_op | source)
XLA Modules:
  0.0 65.5 jit_solution(1813464217910690476)
XLA Ops:
  0.6 3.2 %transform_chain.1 = (f32[1280,80]{1,0:T(8,128)S(1)}, f32[80,80]{1,0:T(8,128)S(1)}, f32[16,80,80]{2,1,0:T(8,128)S(1)}, bf16[6,80,2048]{2,1,0:T(8,128)(2,1)S(1)}, bf16[6,80,2048]{2,1,0:T(8,128)(2,1)S(1)}) custom-call(f32[16,80,80]{2,1,0:T(8,128)} %transforms.1, bf16[16,80,2048]{2,1,0:T(8,128)(2,1)} %ensembles.3, bf16[16,80,2048]{2,1,0:T(8,128)(2,1)} %cotangents.3), custom_call_target="tpu_custom_call" | custom-call | bytes 12600000 | tf_op jit(solution)/shard_map/transform_chain/pallas_call | solution.py:360
  3.9 0.0 copy-start
  3.9 0.0 copy-start.18
  3.9 0.0 copy-start.2
  3.9 4.9 %early_gram.1 = (f32[80,1024]{1,0:T(8,128)S(1)}, f32[80,80]{1,0:T(8,128)S(1)}, bf16[6,80,2048]{2,1,0:T(8,128)(2,1)S(1)}, bf16[6,80,2048]{2,1,0:T(8,128)(2,1)S(1)...) custom-call(bf16[16,80,2048]{2,1,0:T(8,128)(2,1)} %ensembles.3, bf16[16,80,2048]{2,1,0:T(8,128)(2,1)} %cotangents.3, ...), custom_call_target="tpu_custom_call" | custom-call | bytes 10800000 | tf_op jit(solution)/shard_map/early_gram/pallas_call | solution.py:378
  8.8 0.0 copy-done
  8.8 0.0 copy-done.18
  8.8 0.0 copy-start.12
  8.8 1.3 %copy-done.12 = bf16[6,80,2048]{2,1,0:T(8,128)(2,1)} copy-done((bf16[6,80,2048]{2,1,0:T(8,128)(2,1)}, bf16[6,80,2048]{2,1,0:T(8,128)(2,1)S(1)}, u32[]{:S(2)}) %copy-start.12) | copy-done | bytes 1966104
  10.1 0.0 copy-start.14
  10.1 1.3 %copy-done.14 = bf16[6,80,2048]{2,1,0:T(8,128)(2,1)} copy-done((bf16[6,80,2048]{2,1,0:T(8,128)(2,1)}, bf16[6,80,2048]{2,1,0:T(8,128)(2,1)S(1)}, u32[]{:S(2)}) %copy-start.14) | copy-done | bytes 1966104
  11.4 0.0 copy-start.4
  11.4 0.0 copy-start.6
  11.4 0.0 copy-done.2
  11.4 1.9 %late_gram.1 = (f32[80,1408]{1,0:T(8,128)}, f32[80,80]{1,0:T(8,128)S(1)}) custom-call(bf16[4,80,2048]{2,1,0:T(8,128)(2,1)S(1)} %get-tuple-element.37.ens.refs_0_, bf16[4,80,2048]{2,1,0:T(8,128)(2,1)S(1)} %get-tuple-element.38.cot.refs_2_, f32[1280,80]{1,0:T(8,128)S(1)} %get-tuple-element.31.suffixes, f32[80,1024]{1,0:T(8,128)S(1)} %get-tuple-element.39.early, ...), custom_call_target="tpu_custom_call" | custom-call | bytes 4320000 | tf_op jit(solution)/shard_map/late_gram/pallas_call | solution.py:386
  13.3 0.5 collective-permute-start
  13.7 0.9 %collective-permute-done.refs_1_ = f32[80,80]{1,0:T(8,128)S(1)} collective-permute-done((f32[80,80]{1,0:T(8,128)S(1)}, f32[80,80]{1,0:T(8,128)S(1)}, u32[]{:S(2)}, u32[]{:S(2)}) %collective-permute-start) | collective-permute-done | bytes 25632 | tf_op jit(solution)/shard_map/ppermute | solution.py:345
  14.6 0.0 copy-done.4
  14.6 0.0 copy-done.6
  14.6 0.4 collective-permute-start.2
  15.0 0.7 %broadcast_in_dim.4 = f32[8,80,80]{2,1,0:T(8,128)} broadcast(f32[80,80]{1,0:T(8,128)S(1)} %get-tuple-element.32), dimensions={1,2} | broadcast | bytes 230400 | tf_op jit(solution)/shard_map/broadcast_in_dim | solution.py:341
  15.8 7.0 %all-to-all-start = ((f32[8,80,80]{2,1,0:T(8,128)}), f32[8,80,80]{2,1,0:T(8,128)}, u32[]{:S(2)}, u32[]{:S(2)}) async-start(f32[8,80,80]{2,1,0:T(8,128)} %broadcast_in_dim.4), calls=%async_computation | async-start | bytes 655360 | tf_op jit(solution)/shard_map/all_to_all | solution.py:342
  22.7 1.5 %collective-permute-start.1 = (f32[80,80]{1,0:T(8,128)S(1)}, f32[80,80]{1,0:T(8,128)S(1)}, u32[]{:S(2)}, u32[]{:S(2)}) collective-permute-start(f32[80,80]{1,0:T(8,128)S(1)} %get-tuple-element.43._.refs_0_), channel_id=1, source_target_pairs={{0,2},{1,3},{2,0},{3,1},{4,6},{5,7},{6,4},{7,5},{8,10},{9,11},{10,... | collective-permute-start | bytes 76808 | tf_op jit(solution)/shard_map/ppermute | solution.py:349
  24.2 0.0 copy-start.19
  24.2 1.1 %copy-done.19 = f32[16,80,80]{2,1,0:T(8,128)S(1)} copy-done((f32[16,80,80]{2,1,0:T(8,128)S(1)}, f32[16,80,80]{2,1,0:T(8,128)}, u32[]{:S(2)}) %copy-start.19) | copy-done | bytes 409624
  25.3 0.9 %windows.1._.refs_5_ = bf16[2,2560,80]{2,1,0:T(8,128)(2,1)S(1)} custom-call(f32[16,80,80]{2,1,0:T(8,128)S(1)} %copy-done.19, f32[80,80]{1,0:T(8,128)S(1)} %get-tuple-element.43._.refs_0_), custom_call_target="tpu_custom_call" | custom-call | bytes 3600000 | tf_op jit(solution)/shard_map/windows/pallas_call | solution.py:399
  26.3 7.3 %all-to-all-done.products = f32[8,80,80]{2,1,0:T(8,128)} async-done(((f32[8,80,80]{2,1,0:T(8,128)}), f32[8,80,80]{2,1,0:T(8,128)}, u32[]{:S(2)}, u32[]{:S(2)}) %all-to-all-start) | async-done | bytes 204832 | tf_op jit(solution)/shard_map/all_to_all | solution.py:342
  33.6 2.1 %entering.1 = (f32[80,80]{1,0:T(8,128)S(1)}, f32[560,80]{1,0:T(8,128)S(1)}) custom-call(f32[8,80,80]{2,1,0:T(8,128)} %all-to-all-done.products), custom_call_target="tpu_custom_call" | custom-call | bytes 2880000 | tf_op jit(solution)/shard_map/entering/pallas_call | solution.py:394
  35.7 0.0 copy-start.20
  35.7 0.7 %copy-done.20 = f32[560,80]{1,0:T(8,128)} copy-done((f32[560,80]{1,0:T(8,128)}, f32[560,80]{1,0:T(8,128)S(1)}, u32[]{:S(2)}) %copy-start.20) | copy-done | bytes 179224
  36.4 0.0 copy-start.3
  36.4 1.1 %copy-done.3 = f32[1280,80]{1,0:T(8,128)S(1)} copy-done((f32[1280,80]{1,0:T(8,128)S(1)}, f32[1280,80]{1,0:T(8,128)}, u32[]{:S(2)}) %copy-start.3) | copy-done | bytes 409624
  37.5 0.0 copy-start.7
  37.5 0.9 %carries.1 = (bf16[6,240,240]{2,1,0:T(8,128)(2,1)S(1)}, bf16[6,240,240]{2,1,0:T(8,128)(2,1)S(1)}, bf16[2,1280,80]{2,1,0:T(8,128)(2,1)S(1)}) custom-call(f32[1280,80]{1,0:T(8,128)S(1)} %copy-done.3, f32[80,80]{1,0:T(8,128)S(1)} %get-tuple-element.33.later, bf16[2,2560,80]{2,1,0:T(8,128)(2,1)S(1)} %windows.1._.refs_5_), custom_call_target="tpu_custom_call" | custom-call | bytes 3240000 | tf_op jit(solution)/shard_map/carries/pallas_call | solution.py:405
  38.3 0.0 copy-start.8
  38.4 0.0 copy-start.10
  38.4 0.0 copy-start.16
  38.4 0.4 copy-done.7
  38.8 1.4 %smoothed_0.1 = (bf16[16,80,2048]{2,1,0:T(8,128)(2,1)}, f32[8,128]{1,0:T(8,128)S(1)}) custom-call(bf16[6,240,240]{2,1,0:T(8,128)(2,1)S(1)} %get-tuple-element.44.factors, bf16[4,80,2048]{2,1,0:T(8,128)(2,1)S(1)} %copy-done.7, bf16[2,1280,80]{2,1,0:T(8,128)(2,1)S(1)} %get-tuple-element.46.refs_1_.refs_4_), custom_call_target="tpu_custom_call" | custom-call | bytes 5040000 | tf_op jit(solution)/shard_map/smoothed_0/pallas_call | solution.py:415
  40.2 0.0 collective-permute-done.1.refs_1_
  40.2 0.0 collective-permute-done.2.refs_3_
  40.3 2.0 %add.3.refs_0_ = f32[80,1408]{1,0:T(8,128)} add(f32[80,1408]{1,0:T(8,128)} %get-tuple-element.48, f32[80,1408]{1,0:T(8,128)} %get-tuple-element.56) | non-fusion elementwise | flops 112640 | bytes 1351680 | tf_op jit(solution)/shard_map/add | solution.py:426
  42.2 0.0 copy-done.8
  42.2 0.0 copy-done.10
  42.2 0.0 copy-done.16
  42.2 1.6 %collective-permute-start.3 = (f32[80,1408]{1,0:T(8,128)}, f32[80,1408]{1,0:T(8,128)}, u32[]{:S(2)}, u32[]{:S(2)}) collective-permute-start(f32[80,1408]{1,0:T(8,128)} %add.3.refs_0_), channel_id=1, source_target_pairs={{0,2},{1,3},{2,0},{3,1},{4,6},{5,7},{6,4},{7,5},{8,10},{9,11},{10,... | collective-permute-start | bytes 1351688 | tf_op jit(solution)/shard_map/ppermute | solution.py:349
  43.8 0.8 %broadcast_in_dim.5 = f32[8,80,80]{2,1,0:T(8,128)} broadcast(f32[80,80]{1,0:T(8,128)S(1)} %get-tuple-element.49.refs_2_), dimensions={1,2} | broadcast | bytes 230400 | tf_op jit(solution)/shard_map/broadcast_in_dim | solution.py:341
  44.6 4.1 %all-to-all-start.1 = ((f32[8,80,80]{2,1,0:T(8,128)}), f32[8,80,80]{2,1,0:T(8,128)}, u32[]{:S(2)}, u32[]{:S(2)}) async-start(f32[8,80,80]{2,1,0:T(8,128)} %broadcast_in_dim.5), calls=%async_computation.1 | async-start | bytes 655360 | tf_op jit(solution)/shard_map/all_to_all | solution.py:342
  48.7 0.0 copy-start.1
  48.7 1.5 %copy-done.1 = bf16[6,80,2048]{2,1,0:T(8,128)(2,1)S(1)} copy-done((bf16[6,80,2048]{2,1,0:T(8,128)(2,1)S(1)}, bf16[6,80,2048]{2,1,0:T(8,128)(2,1)}, u32[]{:S(2)}) %copy-start.1) | copy-done | bytes 1966104
  50.2 0.0 copy-start.9
  50.2 1.1 %copy-done.9 = bf16[6,240,240]{2,1,0:T(8,128)(2,1)S(1)} copy-done((bf16[6,240,240]{2,1,0:T(8,128)(2,1)S(1)}, bf16[6,240,240]{2,1,0:T(8,128)(2,1)}, u32[]{:S(2)}) %copy-start.9) | copy-done | bytes 691224
  51.3 1.5 %copy-done.15 = bf16[6,80,2048]{2,1,0:T(8,128)(2,1)S(1)} copy-done((bf16[6,80,2048]{2,1,0:T(8,128)(2,1)S(1)}, bf16[6,80,2048]{2,1,0:T(8,128)(2,1)}, u32[]{:S(2)}) %copy-start.15) | copy-done | bytes 1966104
  52.9 2.4 %smoothed_1.1 = (bf16[16,80,2048]{2,1,0:T(8,128)(2,1)}, f32[8,128]{1,0:T(8,128)S(1)}) custom-call(bf16[6,240,240]{2,1,0:T(8,128)(2,1)S(1)} %copy-done.9, bf16[6,80,2048]{2,1,0:T(8,128)(2,1)S(1)} %copy-done.1, bf16[6,80,2048]{2,1,0:T(8,128)(2,1)S(1)} %copy-done.15, f32[80,80]{1,0:T(8,128)S(1)} %get-tuple-element.49.refs_2_, ...), custom_call_target="tpu_custom_call", output_to_operand_aliasing={{0}: (4, {})} | custom-call | bytes 8279999 | tf_op jit(solution)/shard_map/smoothed_1/pallas_call | solution.py:415
  55.3 0.0 copy-done.5
  55.3 1.0 %copy-done.13 = bf16[6,80,2048]{2,1,0:T(8,128)(2,1)S(1)} copy-done((bf16[6,80,2048]{2,1,0:T(8,128)(2,1)S(1)}, bf16[6,80,2048]{2,1,0:T(8,128)(2,1)}, u32[]{:S(2)}) %copy-start.13) | copy-done | bytes 1966104
  56.3 0.2 copy-done.17
  56.4 2.7 %ensemble_grad.1 = (bf16[16,80,2048]{2,1,0:T(8,128)(2,1)}, f32[8,128]{1,0:T(8,128)S(1)}) custom-call(bf16[6,240,240]{2,1,0:T(8,128)(2,1)S(1)} %copy-done.17, bf16[6,80,2048]{2,1,0:T(8,128)(2,1)S(1)} %get-tuple-element.36.cot.refs_0_, bf16[6,80,2048]{2,1,0:T(8,128)(2,1)S(1)} %copy-done.13, bf16[4,80,2048]{2,1,0:T(8,128)(2,1)S(1)} %copy-done.5, ...), custom_call_target="tpu_custom_call" | custom-call | bytes 10080000 | tf_op jit(solution)/shard_map/ensemble_grad/pallas_call | solution.py:415
  59.1 0.0 all-to-all-done.1.refs_2_
  59.1 0.0 collective-permute-done.3.refs_1_
  59.2 0.0 copy-start.11
  59.2 1.1 %copy-done.11 = bf16[2,1280,80]{2,1,0:T(8,128)(2,1)S(1)} copy-done((bf16[2,1280,80]{2,1,0:T(8,128)(2,1)S(1)}, bf16[2,1280,80]{2,1,0:T(8,128)(2,1)}, u32[]{:S(2)}) %copy-start.11) | copy-done | bytes 409624
  60.2 1.0 %copy-done.21 = f32[560,80]{1,0:T(8,128)S(1)} copy-done((f32[560,80]{1,0:T(8,128)S(1)}, f32[560,80]{1,0:T(8,128)}, u32[]{:S(2)}) %copy-start.21) | copy-done | bytes 179224
  61.2 4.3 %transform_grad.1 = f32[16,80,80]{2,1,0:T(8,128)} custom-call(f32[80,1408]{1,0:T(8,128)} %add.3.refs_0_, f32[80,1408]{1,0:T(8,128)} %collective-permute-done.3.refs_1_, f32[8,80,80]{2,1,0:T(8,128)} %all-to-all-done.1.refs_2_, f32[560,80]{1,0:T(8,128)S(1)} %copy-done.21, bf16[2,1280,80]{2,1,0:T(8,128)(2,1)S(1)} %copy-done.11, ...), custom_call_target="tpu_custom_call" | custom-call | bytes 9000000 | tf_op jit(solution)/shard_map/transform_grad/pallas_call | solution.py:431
  (7 shorter events, 0.0 us)
Async XLA Ops:
  3.9 4.9 %copy-start = (bf16[6,80,2048]{2,1,0:T(8,128)(2,1)}, bf16[6,80,2048]{2,1,0:T(8,128)(2,1)S(1)}, u32[]{:S(2)}) copy-start(bf16[6,80,2048]{2,1,0:T(8,128)(2,1)S(1)} %get-tuple-element.35.ens.refs_0_) | copy-start | bytes 5898244
  3.9 4.9 %copy-start.18 = (f32[16,80,80]{2,1,0:T(8,128)}, f32[16,80,80]{2,1,0:T(8,128)S(1)}, u32[]{:S(2)}) copy-start(f32[16,80,80]{2,1,0:T(8,128)S(1)} %get-tuple-element.34.kept) | copy-start | bytes 1228804
  3.9 7.5 %copy-start.2 = (f32[1280,80]{1,0:T(8,128)}, f32[1280,80]{1,0:T(8,128)S(1)}, u32[]{:S(2)}) copy-start(f32[1280,80]{1,0:T(8,128)S(1)} %get-tuple-element.31.suffixes) | copy-start | bytes 1228804
  8.8 1.3 %copy-start.12 = (bf16[6,80,2048]{2,1,0:T(8,128)(2,1)}, bf16[6,80,2048]{2,1,0:T(8,128)(2,1)S(1)}, u32[]{:S(2)}) copy-start(bf16[6,80,2048]{2,1,0:T(8,128)(2,1)S(1)} %get-tuple-element.53.refs_1_) | copy-start | bytes 5898244
  10.1 1.3 %copy-start.14 = (bf16[6,80,2048]{2,1,0:T(8,128)(2,1)}, bf16[6,80,2048]{2,1,0:T(8,128)(2,1)S(1)}, u32[]{:S(2)}) copy-start(bf16[6,80,2048]{2,1,0:T(8,128)(2,1)S(1)} %get-tuple-element.45.refs_1_) | copy-start | bytes 5898244
  11.4 3.2 %copy-start.4 = (bf16[4,80,2048]{2,1,0:T(8,128)(2,1)}, bf16[4,80,2048]{2,1,0:T(8,128)(2,1)S(1)}, u32[]{:S(2)}) copy-start(bf16[4,80,2048]{2,1,0:T(8,128)(2,1)S(1)} %get-tuple-element.38.cot.refs_2_) | copy-start | bytes 3932164
  11.4 3.2 %copy-start.6 = (bf16[4,80,2048]{2,1,0:T(8,128)(2,1)}, bf16[4,80,2048]{2,1,0:T(8,128)(2,1)S(1)}, u32[]{:S(2)}) copy-start(bf16[4,80,2048]{2,1,0:T(8,128)(2,1)S(1)} %get-tuple-element.37.ens.refs_0_) | copy-start | bytes 3932164
  13.3 1.3 %collective-permute-start = (f32[80,80]{1,0:T(8,128)S(1)}, f32[80,80]{1,0:T(8,128)S(1)}, u32[]{:S(2)}, u32[]{:S(2)}) collective-permute-start(f32[80,80]{1,0:T(8,128)S(1)} %get-tuple-element.41.refs_0_.refs_2_), channel_id=1, source_target_pairs={{0,1},{1,0},{2,3},{3,2},{4,5},{5,4},{6,7},{7,6},{8,9},{9,8},{10,11... | collective-permute-start | bytes 76808 | tf_op jit(solution)/shard_map/ppermute | solution.py:345
  14.6 25.6 %collective-permute-start.2 = (f32[80,1408]{1,0:T(8,128)}, f32[80,1408]{1,0:T(8,128)}, u32[]{:S(2)}, u32[]{:S(2)}) collective-permute-start(f32[80,1408]{1,0:T(8,128)} %get-tuple-element.48), channel_id=1, source_target_pairs={{0,1},{1,0},{2,3},{3,2},{4,5},{5,4},{6,7},{7,6},{8,9},{9,8},{10,11... | collective-permute-start | bytes 1351688 | tf_op jit(solution)/shard_map/ppermute | solution.py:345
  15.8 17.9 %all-to-all-start = ((f32[8,80,80]{2,1,0:T(8,128)}), f32[8,80,80]{2,1,0:T(8,128)}, u32[]{:S(2)}, u32[]{:S(2)}) async-start(f32[8,80,80]{2,1,0:T(8,128)} %broadcast_in_dim.4), calls=%async_computation | async-start | bytes 655360 | tf_op jit(solution)/shard_map/all_to_all | solution.py:342
  22.7 17.5 %collective-permute-start.1 = (f32[80,80]{1,0:T(8,128)S(1)}, f32[80,80]{1,0:T(8,128)S(1)}, u32[]{:S(2)}, u32[]{:S(2)}) collective-permute-start(f32[80,80]{1,0:T(8,128)S(1)} %get-tuple-element.43._.refs_0_), channel_id=1, source_target_pairs={{0,2},{1,3},{2,0},{3,1},{4,6},{5,7},{6,4},{7,5},{8,10},{9,11},{10,... | collective-permute-start | bytes 76808 | tf_op jit(solution)/shard_map/ppermute | solution.py:349
  24.2 1.1 %copy-start.19 = (f32[16,80,80]{2,1,0:T(8,128)S(1)}, f32[16,80,80]{2,1,0:T(8,128)}, u32[]{:S(2)}) copy-start(f32[16,80,80]{2,1,0:T(8,128)} %copy-done.18) | copy-start | bytes 1228804
  35.7 0.7 %copy-start.20 = (f32[560,80]{1,0:T(8,128)}, f32[560,80]{1,0:T(8,128)S(1)}, u32[]{:S(2)}) copy-start(f32[560,80]{1,0:T(8,128)S(1)} %get-tuple-element.57.refs_3_) | copy-start | bytes 537604
  36.4 1.1 %copy-start.3 = (f32[1280,80]{1,0:T(8,128)S(1)}, f32[1280,80]{1,0:T(8,128)}, u32[]{:S(2)}) copy-start(f32[1280,80]{1,0:T(8,128)} %copy-done.2) | copy-start | bytes 1228804
  37.5 1.3 %copy-start.7 = (bf16[4,80,2048]{2,1,0:T(8,128)(2,1)S(1)}, bf16[4,80,2048]{2,1,0:T(8,128)(2,1)}, u32[]{:S(2)}) copy-start(bf16[4,80,2048]{2,1,0:T(8,128)(2,1)} %copy-done.6) | copy-start | bytes 3932164
  38.3 3.9 %copy-start.8 = (bf16[6,240,240]{2,1,0:T(8,128)(2,1)}, bf16[6,240,240]{2,1,0:T(8,128)(2,1)S(1)}, u32[]{:S(2)}) copy-start(bf16[6,240,240]{2,1,0:T(8,128)(2,1)S(1)} %get-tuple-element.44.factors) | copy-start | bytes 2073604
  38.4 3.9 %copy-start.10 = (bf16[2,1280,80]{2,1,0:T(8,128)(2,1)}, bf16[2,1280,80]{2,1,0:T(8,128)(2,1)S(1)}, u32[]{:S(2)}) copy-start(bf16[2,1280,80]{2,1,0:T(8,128)(2,1)S(1)} %get-tuple-element.46.refs_1_.refs_4_) | copy-start | bytes 1228804
  38.4 3.9 %copy-start.16 = (bf16[6,240,240]{2,1,0:T(8,128)(2,1)}, bf16[6,240,240]{2,1,0:T(8,128)(2,1)S(1)}, u32[]{:S(2)}) copy-start(bf16[6,240,240]{2,1,0:T(8,128)(2,1)S(1)} %get-tuple-element.52.factors) | copy-start | bytes 2073604
  42.2 16.9 %collective-permute-start.3 = (f32[80,1408]{1,0:T(8,128)}, f32[80,1408]{1,0:T(8,128)}, u32[]{:S(2)}, u32[]{:S(2)}) collective-permute-start(f32[80,1408]{1,0:T(8,128)} %add.3.refs_0_), channel_id=1, source_target_pairs={{0,2},{1,3},{2,0},{3,1},{4,6},{5,7},{6,4},{7,5},{8,10},{9,11},{10,... | collective-permute-start | bytes 1351688 | tf_op jit(solution)/shard_map/ppermute | solution.py:349
  44.6 14.5 %all-to-all-start.1 = ((f32[8,80,80]{2,1,0:T(8,128)}), f32[8,80,80]{2,1,0:T(8,128)}, u32[]{:S(2)}, u32[]{:S(2)}) async-start(f32[8,80,80]{2,1,0:T(8,128)} %broadcast_in_dim.5), calls=%async_computation.1 | async-start | bytes 655360 | tf_op jit(solution)/shard_map/all_to_all | solution.py:342
  48.7 1.5 %copy-start.1 = (bf16[6,80,2048]{2,1,0:T(8,128)(2,1)S(1)}, bf16[6,80,2048]{2,1,0:T(8,128)(2,1)}, u32[]{:S(2)}) copy-start(bf16[6,80,2048]{2,1,0:T(8,128)(2,1)} %copy-done) | copy-start | bytes 5898244
  50.2 1.1 %copy-start.9 = (bf16[6,240,240]{2,1,0:T(8,128)(2,1)S(1)}, bf16[6,240,240]{2,1,0:T(8,128)(2,1)}, u32[]{:S(2)}) copy-start(bf16[6,240,240]{2,1,0:T(8,128)(2,1)} %copy-done.8) | copy-start | bytes 2073604
  51.3 1.5 %copy-start.15 = (bf16[6,80,2048]{2,1,0:T(8,128)(2,1)S(1)}, bf16[6,80,2048]{2,1,0:T(8,128)(2,1)}, u32[]{:S(2)}) copy-start(bf16[6,80,2048]{2,1,0:T(8,128)(2,1)} %copy-done.14) | copy-start | bytes 5898244
  52.9 2.4 %copy-start.5 = (bf16[4,80,2048]{2,1,0:T(8,128)(2,1)S(1)}, bf16[4,80,2048]{2,1,0:T(8,128)(2,1)}, u32[]{:S(2)}) copy-start(bf16[4,80,2048]{2,1,0:T(8,128)(2,1)} %copy-done.4) | copy-start | bytes 3932164
  52.9 3.4 %copy-start.13 = (bf16[6,80,2048]{2,1,0:T(8,128)(2,1)S(1)}, bf16[6,80,2048]{2,1,0:T(8,128)(2,1)}, u32[]{:S(2)}) copy-start(bf16[6,80,2048]{2,1,0:T(8,128)(2,1)} %copy-done.12) | copy-start | bytes 5898244
  52.9 3.5 %copy-start.17 = (bf16[6,240,240]{2,1,0:T(8,128)(2,1)S(1)}, bf16[6,240,240]{2,1,0:T(8,128)(2,1)}, u32[]{:S(2)}) copy-start(bf16[6,240,240]{2,1,0:T(8,128)(2,1)} %copy-done.16) | copy-start | bytes 2073604
  59.2 1.1 %copy-start.11 = (bf16[2,1280,80]{2,1,0:T(8,128)(2,1)S(1)}, bf16[2,1280,80]{2,1,0:T(8,128)(2,1)}, u32[]{:S(2)}) copy-start(bf16[2,1280,80]{2,1,0:T(8,128)(2,1)} %copy-done.10) | copy-start | bytes 1228804
  60.2 1.0 %copy-start.21 = (f32[560,80]{1,0:T(8,128)S(1)}, f32[560,80]{1,0:T(8,128)}, u32[]{:S(2)}) copy-start(f32[560,80]{1,0:T(8,128)} %copy-done.20) | copy-start | bytes 537604

commit v9 on v3

--- a/solution.py
+++ b/solution.py
@@ -188,20 +188,13 @@
             copy.wait()
 
 
-def late_gram_kernel(
-    plan, ens, cot, suffixes, early, offset, _,
-    gram_kept, gram_sent, offset_kept, offset_sent, whole, offsets,
-):
-    members = plan.members
+def late_gram_kernel(plan, ens, cot, suffixes, early, offset, _, kept, sent, offsets, whole):
     whole[:, : early.shape[1]] = early[...]
     offsets[...] = offset[...] + gram_of(plan, PIECES - 1, cot, ens, suffixes, whole)
-    half = members // 2
+    half = plan.members // 2
     core = lax.rem(lax.axis_index("space"), 2)
-    mine, other = pl.ds(core * half, half), pl.ds((1 - core) * half, half)
-    gram_kept[...] = whole[mine]
-    gram_sent[...] = whole[other]
-    offset_kept[...] = offsets[mine]
-    offset_sent[...] = offsets[other]
+    kept[...] = whole[pl.ds(core * half, half)]
+    sent[...] = whole[pl.ds((1 - core) * half, half)]
 
 
 def upper_half(level):
@@ -218,15 +211,12 @@
     new_before[...] = jnp.where(upper, mul_exact(other[...], before[...]), before[...])
 
 
-def sum_kernel(number, out, *refs):
-    total = refs[0][...]
-    for ref in refs[1:number]:
-        total = total + ref[...]
-    refs[out][...] = total
-
-
-def pass_kernel(level, last, own, other, carry, upper_total, before, *refs):
-    new_own, new_carry = refs[2:4] if last else refs[1:3]
+def sum_kernel(left, right, _, __, total, ___):
+    total[...] = left[...] + right[...]
+
+
+def pass_kernel(level, own, other, carry, upper_total, before, _, *refs):
+    new_own, new_carry = refs[len(refs) // 2 - 1 : len(refs) // 2 + 1]
     upper = upper_half(level)
     left = jnp.where(upper, other[...], own[...])
     right = jnp.where(upper, own[...], other[...])
@@ -239,10 +229,14 @@
     new_carry[...] = carry[...] + jnp.where(upper_half(level), added, 0.0)
 
 
-def carry_kernel(plan, level, suffixes, later, other, _, ens_factors, cot_factors, follow):
+def enter_kernel(level, later, other, _, entering):
+    joined = mul_exact(later[...], other[...])
+    entering[...] = jnp.where(upper_half(level), later[...], joined)
+
+
+def carry_kernel(plan, suffixes, later, ens_factors, cot_factors, follow):
     count, members = plan.count, plan.members
     entering = later[...]
-    entering = jnp.where(upper_half(level), entering, mul_exact(entering, other[...]))
     mask = on_blocks(members, plan.stack * members)
     repeated = split(jnp.concatenate([entering] * plan.stack, axis=1))
     for at, (start, stop) in enumerate(plan.groups):
@@ -288,9 +282,11 @@
         copy.wait()
 
 
-def final_kernel(
-    plan, scale, gram_mine, gram_other, carry_mine, carry_other, follow, steps, _, out, buffer, sems
-):
+def final_kernel(plan, scale, gram_mine, gram_other, follow, steps, _, *refs):
+    carries, (out, buffer, sems) = refs[:-3], refs[-3:]
+    carry = carries[0][...]
+    for ref in carries[1:]:
+        carry = carry + ref[...]
     count, members = plan.count, plan.members
     first = lax.rem(lax.axis_index("space"), 2) == 0
 
@@ -303,7 +299,7 @@
         tall = whole(gram_mine[:, lanes], gram_other[:, lanes]).T
         for i in range(stop - start):
             totals.append(tall[i * members : (i + 1) * members])
-    totals[0] = totals[0] + whole(carry_mine[...], carry_other[...]).T
+    totals[0] = totals[0] + carry.T
     number = 0
     width = 1
     while width < count:
@@ -381,7 +377,7 @@
         [HBM] * 3, [VMEM] * 5, [pltpu.SemaphoreType.DMA] + piece_sems(0), 3.5, "transform_chain",
     )(transforms, ensembles, cotangents)
 
-    half = members // 2
+    wide = shape(members // 2, plan.width)
     later = before = jnp.eye(members, dtype=F32)
     uppers, befores = [], []
 
@@ -393,15 +389,6 @@
         )(total, other, later, before, after)
         uppers.append(upper)
         return new
-
-    def add(values, after, name, *through):
-        number = len(values)
-        return call(
-            functools.partial(sum_kernel, number, number + 1 + len(through)),
-            [shape(*values[0].shape)] + [shape(*value.shape) for value in through],
-            [VMEM] * number + [ANY] * (1 + len(through)), [VMEM] + [ANY] * len(through), [], 0.1, name,
-            aliases={number + 1 + at: 1 + at for at in range(len(through))},
-        )(*values, after, *through)
 
     other = exchange(total, "tm", blocks, 1)
     early_width = plan.lanes(plan.first_group[-1]).start
@@ -416,39 +403,52 @@
     total, later, before = join(0, total, other, later, before, offset)
 
     other = exchange(total, "tm", blocks, 2)
-    gram, gram_sent, offset, offset_sent = call(
+    gram, gram_sent, own = call(
         functools.partial(late_gram_kernel, plan),
-        [shape(half, plan.width)] * 2 + [shape(half, members)] * 2,
-        [VMEM] * 5 + [ANY], [VMEM] * 4,
-        [pltpu.VMEM((members, plan.width), F32), pltpu.VMEM((members, members), F32)],
-        1.2, "late_gram",
+        [wide, wide, square], [VMEM] * 5 + [ANY], [VMEM] * 3,
+        [pltpu.VMEM((members, plan.width), F32)], 1.2, "late_gram",
     )(*parts[-1], suffixes, early, offset, total)
-    offset_core = exchange(offset_sent, "space", lanes, 1)
+    other_own = exchange(own, "tm", blocks, 1)
     for level in range(1, levels - 1):
-        total, later, before = join(level, total, other, later, before, offset)
+        total, later, before = join(level, total, other, later, before, own)
         other = exchange(total, "tm", blocks, 2 << level)
     befores.append(before)
-
-    offset, gram_sent = add([offset, offset_core], total, "chip_offset", gram_sent)
-    gram_core = exchange(gram_sent, "space", lanes, 1)
-    offsets = [offset] + around(offset)
     steps = call(
         functools.partial(windows_kernel, plan),
         shape(2, count_steps(count) * members, members, kind=BF16), [VMEM, ANY], VMEM,
-        [pltpu.VMEM((count * members, members), F32)], 1.5, "windows",
-    )(kept, offset)
-    own, gram_core, other = add(offsets, steps, "own_offset", gram_core, other)
-
-    other_own = exchange(own, "tm", blocks, 1)
+        [pltpu.VMEM((count * members, members), F32)], 1.0, "windows",
+    )(kept, total)
+
+    def pass_on(level, carry, after, *through):
+        more = [shape(*value.shape) for value in through]
+        return call(
+            functools.partial(pass_kernel, level),
+            [square] * 2 + more, [VMEM] * 5 + [ANY] * (1 + len(more)), [VMEM] * 2 + [ANY] * len(more),
+            [], 0.3, f"pass_{level}", aliases={6 + at: 2 + at for at in range(len(more))},
+        )(own, other_own, carry, uppers[level], befores[level], after, *through)
+
+    carry = jnp.zeros((members, members), F32)
+    own, carry, gram_sent = pass_on(0, carry, steps, gram_sent)
+    other_own = exchange(own, "tm", blocks, 2)
+    gram_core = exchange(gram_sent, "space", lanes, 1)
+    for level in range(1, levels - 2):
+        own, carry = pass_on(level, carry, own)
+        other_own = exchange(own, "tm", blocks, 2 << level)
+    own, carry, gram_core, other = pass_on(levels - 2, carry, own, gram_core, other)
+    other_own = exchange(own, "tm", blocks, blocks // 2)
     gram = gram + gram_core
     grams = around(gram)
+    entering = call(
+        functools.partial(enter_kernel, levels - 1),
+        square, [VMEM] * 2 + [ANY], VMEM, [], 0.2, "entering",
+    )(later, other, own)
     size = plan.stack * members
     ens_factors, cot_factors, follow = call(
-        functools.partial(carry_kernel, plan, levels - 1),
+        functools.partial(carry_kernel, plan),
         [shape(len(plan.groups), size, size, kind=BF16)] * 2
         + [shape(2, count * members, members, kind=BF16)],
-        [VMEM] * 3 + [ANY], [VMEM] * 3, [], 1.0, "carries",
-    )(suffixes, later, other, own)
+        [VMEM] * 2, [VMEM] * 3, [], 0.9, "carries",
+    )(suffixes, entering)
 
     def apply(factors, which, pieces, out, after, name):
         first, last = plan.pieces[pieces[0]][0], plan.pieces[pieces[-1]][1]
@@ -462,38 +462,29 @@
         )(factors, *(parts[piece][which] for piece in pieces), after, *out)
 
     front, rear = tuple(range(PIECES - 1)), (PIECES - 1,)
-    smoothed, done = apply(ens_factors, 0, front, (), follow, "smoothed_0")
-    carry = jnp.zeros((half, members), F32)
-    for level in range(levels - 1):
-        last = level == levels - 2
-        own, carry, *rest = call(
-            functools.partial(pass_kernel, level, last),
-            [shape(half, members)] * 2 + [shape(half, plan.width)] * last,
-            [VMEM] * 5 + [ANY] * (1 + last), [VMEM] * 2 + [ANY] * last, [], 0.3, f"pass_{level}",
-            aliases={6: 2} if last else None,
-        )(own, other_own, carry, uppers[level], befores[level], done, *grams[:last])
-        other_own = exchange(own, "tm", blocks, 2 << level)
-        if level == 0:
-            smoothed, done = apply(ens_factors, 0, rear, (smoothed,), own, "smoothed_1")
-        if level == 1:
-            ensemble_grad, done = apply(cot_factors, 1, front, (), own, "ensemble_grad_0")
-    grams[0] = rest[0]
+    smoothed, done = apply(ens_factors, 0, front + rear, (), follow, "smoothed")
+    carry = call(
+        functools.partial(last_pass_kernel, levels - 1),
+        square, [VMEM] * 3 + [ANY], VMEM, [], 0.2, "pass_last",
+    )(other_own, carry, befores[-1], done)
+    carry_core = exchange(carry, "space", lanes, 1)
+    ensemble_grad, done = apply(cot_factors, 1, rear, (), carry, "ensemble_grad_0")
+    carry, grams[0] = call(
+        sum_kernel, [square, wide], [VMEM] * 2 + [ANY] * 2, [VMEM, ANY], [], 0.1, "chip_carry",
+        aliases={3: 1},
+    )(carry, carry_core, done, grams[0])
+    carries = [carry] + around(carry)
     for part in grams:
         gram = gram + part
     gram_other = exchange(gram, "space", lanes, 1)
-    carry = call(
-        functools.partial(last_pass_kernel, levels - 1),
-        shape(half, members), [VMEM] * 3 + [ANY], VMEM, [], 0.2, "pass_last",
-    )(other_own, carry, befores[-1], done)
-    carry_other = exchange(carry, "space", lanes, 1)
-    ensemble_grad, done = apply(cot_factors, 1, rear, (ensemble_grad,), carry, "ensemble_grad_1")
+    ensemble_grad, done = apply(cot_factors, 1, front, (ensemble_grad,), carry, "ensemble_grad_1")
     transform_grad = call(
         functools.partial(final_kernel, plan, scale),
         shape(count, members, members),
-        [VMEM] * 6 + [ANY], HBM,
+        [VMEM] * 4 + [ANY] + [VMEM] * chips, HBM,
         [pltpu.VMEM((count, members, members), F32), pltpu.SemaphoreType.DMA((count,))],
         2.5, "transform_grad",
-    )(gram, gram_other, carry, carry_other, follow, steps, done)
+    )(gram, gram_other, follow, steps, done, *carries)
     return (smoothed, ensemble_grad, transform_grad)
 
 

time: 40.7 us -> 40.8 us (level)
  waiting for transfers between devices: 4.36 us -> 7.35 us
  starting transfers between devices: 14.3 us -> 12.4 us
  Pallas kernels: 20.9 us -> 20 us
    ppermute x10 -> x9, waiting for transfers between devices: 3.06 us -> 6.14 us  [exchange(): return lax.ppermute(value, axis, [(at, at ^ bit) for at in range(size)])]
    ppermute x2, starting transfers between devices: 3.12 us -> 2.09 us  [around(): lax.ppermute(value, 'space', [(at, (at + 2 * d) % lanes) for at in range(...]
    pallas_call x4 -> x3, Pallas kernels: 7.3 us -> 6.37 us  [apply(): call(functools.partial(apply_kernel, plan, pieces), [shape(count, members...]
    ppermute x10 -> x9, starting transfers between devices: 11.2 us -> 10.3 us  [exchange(): return lax.ppermute(value, axis, [(at, at ^ bit) for at in range(size)])]
  transfers between devices with their start and end apart: 12 -> 11, of which waited for: 4 -> 6; matrix products, arithmetic and copies ran while one was open for 0% -> 0% of each run, Pallas kernels for 37% -> 34%
where the time goes in v9:
time: 40.8 us; the launch traced here: 40.6 us
  Pallas kernels  20 us (49%)
  starting transfers between devices  12.4 us (30%)
  waiting for transfers between devices  7.35 us (18%)
  between operations  0.8 us (2%)
    ppermute x9, starting transfers between devices, exchange(): return lax.ppermute(value, axis, [(at, at ^ bit) for at in range(size)])  10.3 us
    pallas_call x3, Pallas kernels, apply(): call(functools.partial(apply_kernel, plan, pieces), [shape(count, members...  6.37 us
    ppermute x9, waiting for transfers between devices, exchange(): return lax.ppermute(value, axis, [(at, at ^ bit) for at in range(size)])  6.14 us
    pallas_call x1, Pallas kernels, shards(): call(functools.partial(early_gram_kernel, plan), [shape(members, early_wi...  3.85 us
    pallas_call x1, Pallas kernels, shards(): call(functools.partial(chain_kernel, plan), [shape(count * members, membe...  3.22 us
    pallas_call x1, Pallas kernels, shards(): call(functools.partial(final_kernel, plan, scale), shape(count, members,...  2.29 us
    ppermute x2, starting transfers between devices, around(): lax.ppermute(value, 'space', [(at, (at + 2 * d) % lanes) for at in range(...  2.09 us
    ppermute x2, waiting for transfers between devices, around(): lax.ppermute(value, 'space', [(at, (at + 2 * d) % lanes) for at in range(...  1.21 us
  transfers between devices with their start and end apart: 11, of which 6 were waited for; matrix products, arithmetic and copies ran while one was open for 0% of the time, Pallas kernels for 34%

profile of v9, /device:TPU:0, one launch (start us, length us, event | category | flops | bytes accessed | tf_op | source)
XLA Modules:
  0.0 40.6 jit_solution(1765854092640761580)
XLA Ops:
  0.6 3.2 %transform_chain.1 = (f32[1280,80]{1,0:T(8,128)S(1)}, f32[80,80]{1,0:T(8,128)S(1)}, f32[16,80,80]{2,1,0:T(8,128)S(1)}, bf16[6,80,2048]{2,1,0:T(8,128)(2,1)S(1)}, bf16[6,80,2048]{2,1,0:T(8,128)(2,1)S(1)}) custom-call(f32[16,80,80]{2,1,0:T(8,128)} %transforms.1, bf16[16,80,2048]{2,1,0:T(8,128)(2,1)} %ensembles.3, bf16[16,80,2048]{2,1,0:T(8,128)(2,1)} %cotangents.3), custom_call_target="tpu_custom_call" | custom-call | bytes 12600000 | tf_op jit(solution)/shard_map/transform_chain/pallas_call | solution.py:374
  3.9 3.0 %collective-permute-start = (f32[80,80]{1,0:T(8,128)S(1)}, f32[80,80]{1,0:T(8,128)S(1)}, u32[]{:S(2)}, u32[]{:S(2)}) collective-permute-start(f32[80,80]{1,0:T(8,128)S(1)} %get-tuple-element.44.total), channel_id=1, source_target_pairs={{0,4},{4,0},{8,12},{12,8},{16,20},{20,16},{24,28},{28,24},{1,5},{5... | collective-permute-start | bytes 76808 | tf_op jit(solution)/shard_map/ppermute | solution.py:359
  6.9 3.8 %early_gram.1 = (f32[80,1024]{1,0:T(8,128)S(1)}, f32[80,80]{1,0:T(8,128)S(1)}, bf16[6,80,2048]{2,1,0:T(8,128)(2,1)S(1)}, bf16[6,80,2048]{2,1,0:T(8,128)(2,1)S(1)...) custom-call(bf16[16,80,2048]{2,1,0:T(8,128)(2,1)} %ensembles.3, bf16[16,80,2048]{2,1,0:T(8,128)(2,1)} %cotangents.3, ...), custom_call_target="tpu_custom_call" | custom-call | bytes 10800000 | tf_op jit(solution)/shard_map/early_gram/pallas_call | solution.py:395
  10.7 0.0 collective-permute-done.other
  10.7 0.3 join_0.1
  11.0 1.6 %collective-permute-start.1 = (f32[80,80]{1,0:T(8,128)S(1)}, f32[80,80]{1,0:T(8,128)S(1)}, u32[]{:S(2)}, u32[]{:S(2)}) collective-permute-start(f32[80,80]{1,0:T(8,128)S(1)} %get-tuple-element.48._.total), channel_id=1, source_target_pairs={{0,8},{4,12},{8,0},{12,4},{16,24},{20,28},{24,16},{28,20},{1,9},{5... | collective-permute-start | bytes 76808 | tf_op jit(solution)/shard_map/ppermute | solution.py:359
  12.6 1.2 %late_gram.1 = (f32[40,1408]{1,0:T(8,128)S(1)}, f32[40,1408]{1,0:T(8,128)S(1)}, f32[80,80]{1,0:T(8,128)S(1)}) custom-call(bf16[4,80,2048]{2,1,0:T(8,128)(2,1)S(1)} %get-tuple-element.51.ens.refs_2_, bf16[4,80,2048]{2,1,0:T(8,128)(2,1)S(1)} %get-tuple-element.52.cot.refs_0_, f32[1280,80]{1,0:T(8,128)S(1)} %get-tuple-element.43.suffixes, ...), custom_call_target="tpu_custom_call" | custom-call | bytes 4320000 | tf_op jit(solution)/shard_map/late_gram/pallas_call | solution.py:406
  13.8 0.6 %collective-permute-start.2 = (f32[80,80]{1,0:T(8,128)S(1)}, f32[80,80]{1,0:T(8,128)S(1)}, u32[]{:S(2)}, u32[]{:S(2)}) collective-permute-start(f32[80,80]{1,0:T(8,128)S(1)} %get-tuple-element.54._.own), channel_id=1, source_target_pairs={{0,4},{4,0},{8,12},{12,8},{16,20},{20,16},{24,28},{28,24},{1,5},{5... | collective-permute-start | bytes 76808 | tf_op jit(solution)/shard_map/ppermute | solution.py:359
  14.4 0.7 %collective-permute-done.1.other = f32[80,80]{1,0:T(8,128)S(1)} collective-permute-done((f32[80,80]{1,0:T(8,128)S(1)}, f32[80,80]{1,0:T(8,128)S(1)}, u32[]{:S(2)}, u32[]{:S(2)}) %collective-permute-start.1) | collective-permute-done | bytes 25632 | tf_op jit(solution)/shard_map/ppermute | solution.py:359
  15.1 0.2 join_1.1
  15.3 0.9 %windows.1._.steps = bf16[2,2560,80]{2,1,0:T(8,128)(2,1)S(1)} custom-call(f32[16,80,80]{2,1,0:T(8,128)S(1)} %get-tuple-element.57.kept, f32[80,80]{1,0:T(8,128)S(1)} %get-tuple-element.58._), custom_call_target="tpu_custom_call" | custom-call | bytes 3600000 | tf_op jit(solution)/shard_map/windows/pallas_call | solution.py:416
  16.3 1.6 %collective-permute-done.2.other = f32[80,80]{1,0:T(8,128)S(1)} collective-permute-done((f32[80,80]{1,0:T(8,128)S(1)}, f32[80,80]{1,0:T(8,128)S(1)}, u32[]{:S(2)}, u32[]{:S(2)}) %collective-permute-start.2) | collective-permute-done | bytes 25632 | tf_op jit(solution)/shard_map/ppermute | solution.py:359
  17.9 0.2 pass_0.1
  18.1 0.1 collective-permute-start.4
  18.2 2.7 %collective-permute-start.5 = (f32[80,80]{1,0:T(8,128)S(1)}, f32[80,80]{1,0:T(8,128)S(1)}, u32[]{:S(2)}, u32[]{:S(2)}) collective-permute-start(f32[80,80]{1,0:T(8,128)S(1)} %get-tuple-element.58._), channel_id=1, source_target_pairs={{0,16},{4,20},{8,24},{12,28},{16,0},{20,4},{24,8},{28,12},{1,17},{... | collective-permute-start | bytes 76808 | tf_op jit(solution)/shard_map/ppermute | solution.py:359
  20.8 0.4 %collective-permute-start.3 = (f32[80,80]{1,0:T(8,128)S(1)}, f32[80,80]{1,0:T(8,128)S(1)}, u32[]{:S(2)}, u32[]{:S(2)}) collective-permute-start(f32[80,80]{1,0:T(8,128)S(1)} %get-tuple-element.60.own._), channel_id=1, source_target_pairs={{0,8},{4,12},{8,0},{12,4},{16,24},{20,28},{24,16},{28,20},{1,9},{5... | collective-permute-start | bytes 76808 | tf_op jit(solution)/shard_map/ppermute | solution.py:359
  21.3 2.6 %collective-permute-done.5.refs_1_ = f32[80,80]{1,0:T(8,128)S(1)} collective-permute-done((f32[80,80]{1,0:T(8,128)S(1)}, f32[80,80]{1,0:T(8,128)S(1)}, u32[]{:S(2)}, u32[]{:S(2)}) %collective-permute-start.5) | collective-permute-done | bytes 25632 | tf_op jit(solution)/shard_map/ppermute | solution.py:359
  23.9 1.0 %collective-permute-done.3.other = f32[80,80]{1,0:T(8,128)S(1)} collective-permute-done((f32[80,80]{1,0:T(8,128)S(1)}, f32[80,80]{1,0:T(8,128)S(1)}, u32[]{:S(2)}, u32[]{:S(2)}) %collective-permute-start.3) | collective-permute-done | bytes 25632 | tf_op jit(solution)/shard_map/ppermute | solution.py:359
  24.8 0.0 collective-permute-done.4.refs_0_
  24.8 0.2 pass_1.1
  25.1 1.6 %collective-permute-start.8 = (f32[40,1408]{1,0:T(8,128)S(1)}, f32[40,1408]{1,0:T(8,128)S(1)}, u32[]{:S(2)}, u32[]{:S(2)}) collective-permute-start(f32[40,1408]{1,0:T(8,128)S(1)} %add.6), channel_id=1, source_target_pairs={{0,2},{1,3},{2,0},{3,1},{4,6},{5,7},{6,4},{7,5},{8,10},{9,11},{10,... | collective-permute-start | bytes 675848 | tf_op jit(solution)/shard_map/ppermute | solution.py:363
  26.7 1.3 %collective-permute-start.6 = (f32[80,80]{1,0:T(8,128)S(1)}, f32[80,80]{1,0:T(8,128)S(1)}, u32[]{:S(2)}, u32[]{:S(2)}) collective-permute-start(f32[80,80]{1,0:T(8,128)S(1)} %get-tuple-element.65._), channel_id=1, source_target_pairs={{0,16},{4,20},{8,24},{12,28},{16,0},{20,4},{24,8},{28,12},{1,17},{... | collective-permute-start | bytes 76808 | tf_op jit(solution)/shard_map/ppermute | solution.py:359
  27.9 0.2 entering.1.later
  28.1 0.9 %carries.1 = (bf16[6,240,240]{2,1,0:T(8,128)(2,1)S(1)}, bf16[6,240,240]{2,1,0:T(8,128)(2,1)S(1)}, bf16[2,1280,80]{2,1,0:T(8,128)(2,1)S(1)}) custom-call(f32[1280,80]{1,0:T(8,128)S(1)} %get-tuple-element.43.suffixes, f32[80,80]{1,0:T(8,128)S(1)} %entering.1.later), custom_call_target="tpu_custom_call" | custom-call | bytes 3240000 | tf_op jit(solution)/shard_map/carries/pallas_call | solution.py:446
  29.0 2.7 %smoothed.1 = (bf16[16,80,2048]{2,1,0:T(8,128)(2,1)}, f32[8,128]{1,0:T(8,128)S(1)}) custom-call(bf16[6,240,240]{2,1,0:T(8,128)(2,1)S(1)} %get-tuple-element.66.factors, bf16[6,80,2048]{2,1,0:T(8,128)(2,1)S(1)} %get-tuple-element.45.ens.refs_0_, bf16[6,80,2048]{2,1,0:T(8,128)(2,1)S(1)} %get-tuple-element.67.refs_1_, ...), custom_call_target="tpu_custom_call" | custom-call | bytes 6480000 | tf_op jit(solution)/shard_map/smoothed/pallas_call | solution.py:456
  31.7 0.3 collective-permute-done.6.other
  32.0 0.2 pass_last.1.refs_1_.left
  32.2 0.1 collective-permute-start.7
  32.3 1.4 %ensemble_grad_0.1 = (bf16[16,80,2048]{2,1,0:T(8,128)(2,1)}, f32[8,128]{1,0:T(8,128)S(1)}) custom-call(bf16[6,240,240]{2,1,0:T(8,128)(2,1)S(1)} %get-tuple-element.70.factors, bf16[4,80,2048]{2,1,0:T(8,128)(2,1)S(1)} %get-tuple-element.52.cot.refs_0_, f32[80,80]{1,0:T(8,128)S(1)} %pass_last.1.refs_1_.left), custom_call_target="tpu_custom_call" | custom-call | bytes 6480000 | tf_op jit(solution)/shard_map/ensemble_grad_0/pallas_call | solution.py:456
  33.7 0.0 collective-permute-done.7.right
  33.7 0.0 collective-permute-done.8.__
  33.7 0.6 %collective-permute-start.9 = (f32[40,1408]{1,0:T(8,128)S(1)}, f32[40,1408]{1,0:T(8,128)S(1)}, u32[]{:S(2)}, u32[]{:S(2)}) collective-permute-start(f32[40,1408]{1,0:T(8,128)S(1)} %add.7.gram_mine), channel_id=1, source_target_pairs={{0,1},{1,0},{2,3},{3,2},{4,5},{5,4},{6,7},{7,6},{8,9},{9,8},{10,11... | collective-permute-start | bytes 675848 | tf_op jit(solution)/shard_map/ppermute | solution.py:359
  34.3 0.5 %collective-permute-start.10 = (f32[80,80]{1,0:T(8,128)S(1)}, f32[80,80]{1,0:T(8,128)S(1)}, u32[]{:S(2)}, u32[]{:S(2)}) collective-permute-start(f32[80,80]{1,0:T(8,128)S(1)} %get-tuple-element.78.refs_2_.refs_0_), channel_id=1, source_target_pairs={{0,2},{1,3},{2,0},{3,1},{4,6},{5,7},{6,4},{7,5},{8,10},{9,11},{10,... | collective-permute-start | bytes 76808 | tf_op jit(solution)/shard_map/ppermute | solution.py:363
  34.8 2.3 %ensemble_grad_1.1 = (bf16[16,80,2048]{2,1,0:T(8,128)(2,1)}, f32[8,128]{1,0:T(8,128)S(1)}) custom-call(bf16[6,240,240]{2,1,0:T(8,128)(2,1)S(1)} %get-tuple-element.70.factors, bf16[6,80,2048]{2,1,0:T(8,128)(2,1)S(1)} %get-tuple-element.46.cot.refs_0_, bf16[6,80,2048]{2,1,0:T(8,128)(2,1)S(1)} %get-tuple-element.71.refs_1_, ...), custom_call_target="tpu_custom_call", output_to_operand_aliasing={{0}: (4, {})} | custom-call | bytes 6480000 | tf_op jit(solution)/shard_map/ensemble_grad_1/pallas_call | solution.py:456
  37.1 1.2 %collective-permute-done.10.refs_1_ = f32[80,80]{1,0:T(8,128)S(1)} collective-permute-done((f32[80,80]{1,0:T(8,128)S(1)}, f32[80,80]{1,0:T(8,128)S(1)}, u32[]{:S(2)}, u32[]{:S(2)}) %collective-permute-start.10) | collective-permute-done | bytes 25632 | tf_op jit(solution)/shard_map/ppermute | solution.py:363
  38.3 0.0 collective-permute-done.9.gram_other
  38.3 2.3 %transform_grad.1 = f32[16,80,80]{2,1,0:T(8,128)} custom-call(f32[40,1408]{1,0:T(8,128)S(1)} %add.7.gram_mine, f32[40,1408]{1,0:T(8,128)S(1)} %collective-permute-done.9.gram_other, bf16[2,1280,80]{2,1,0:T(8,128)(2,1)S(1)} %get-tuple-element.68.refs_3_.follow, bf16[2,2560,80]{2,1,0:T(8,128)(2,1)S(1)} %windows.1._.steps, f32[8,128]{1,0:T(8,128)S(1)} %get-tuple-element.82._, ...), custom_call_target="tpu_custom_call" | custom-call | bytes 9000000 | tf_op jit(solution)/shard_map/transform_grad/pallas_call | solution.py:481
  (5 shorter events, 0.1 us)
Async XLA Ops:
  3.9 6.9 %collective-permute-start = (f32[80,80]{1,0:T(8,128)S(1)}, f32[80,80]{1,0:T(8,128)S(1)}, u32[]{:S(2)}, u32[]{:S(2)}) collective-permute-start(f32[80,80]{1,0:T(8,128)S(1)} %get-tuple-element.44.total), channel_id=1, source_target_pairs={{0,4},{4,0},{8,12},{12,8},{16,20},{20,16},{24,28},{28,24},{1,5},{5... | collective-permute-start | bytes 76808 | tf_op jit(solution)/shard_map/ppermute | solution.py:359
  11.0 4.1 %collective-permute-start.1 = (f32[80,80]{1,0:T(8,128)S(1)}, f32[80,80]{1,0:T(8,128)S(1)}, u32[]{:S(2)}, u32[]{:S(2)}) collective-permute-start(f32[80,80]{1,0:T(8,128)S(1)} %get-tuple-element.48._.total), channel_id=1, source_target_pairs={{0,8},{4,12},{8,0},{12,4},{16,24},{20,28},{24,16},{28,20},{1,9},{5... | collective-permute-start | bytes 76808 | tf_op jit(solution)/shard_map/ppermute | solution.py:359
  13.8 4.1 %collective-permute-start.2 = (f32[80,80]{1,0:T(8,128)S(1)}, f32[80,80]{1,0:T(8,128)S(1)}, u32[]{:S(2)}, u32[]{:S(2)}) collective-permute-start(f32[80,80]{1,0:T(8,128)S(1)} %get-tuple-element.54._.own), channel_id=1, source_target_pairs={{0,4},{4,0},{8,12},{12,8},{16,20},{20,16},{24,28},{28,24},{1,5},{5... | collective-permute-start | bytes 76808 | tf_op jit(solution)/shard_map/ppermute | solution.py:359
  18.1 6.7 %collective-permute-start.4 = (f32[40,1408]{1,0:T(8,128)S(1)}, f32[40,1408]{1,0:T(8,128)S(1)}, u32[]{:S(2)}, u32[]{:S(2)}) collective-permute-start(f32[40,1408]{1,0:T(8,128)S(1)} %get-tuple-element.63), channel_id=1, source_target_pairs={{0,1},{1,0},{2,3},{3,2},{4,5},{5,4},{6,7},{7,6},{8,9},{9,8},{10,11... | collective-permute-start | bytes 675848 | tf_op jit(solution)/shard_map/ppermute | solution.py:359
  18.2 5.7 %collective-permute-start.5 = (f32[80,80]{1,0:T(8,128)S(1)}, f32[80,80]{1,0:T(8,128)S(1)}, u32[]{:S(2)}, u32[]{:S(2)}) collective-permute-start(f32[80,80]{1,0:T(8,128)S(1)} %get-tuple-element.58._), channel_id=1, source_target_pairs={{0,16},{4,20},{8,24},{12,28},{16,0},{20,4},{24,8},{28,12},{1,17},{... | collective-permute-start | bytes 76808 | tf_op jit(solution)/shard_map/ppermute | solution.py:359
  20.8 4.0 %collective-permute-start.3 = (f32[80,80]{1,0:T(8,128)S(1)}, f32[80,80]{1,0:T(8,128)S(1)}, u32[]{:S(2)}, u32[]{:S(2)}) collective-permute-start(f32[80,80]{1,0:T(8,128)S(1)} %get-tuple-element.60.own._), channel_id=1, source_target_pairs={{0,8},{4,12},{8,0},{12,4},{16,24},{20,28},{24,16},{28,20},{1,9},{5... | collective-permute-start | bytes 76808 | tf_op jit(solution)/shard_map/ppermute | solution.py:359
  25.1 8.6 %collective-permute-start.8 = (f32[40,1408]{1,0:T(8,128)S(1)}, f32[40,1408]{1,0:T(8,128)S(1)}, u32[]{:S(2)}, u32[]{:S(2)}) collective-permute-start(f32[40,1408]{1,0:T(8,128)S(1)} %add.6), channel_id=1, source_target_pairs={{0,2},{1,3},{2,0},{3,1},{4,6},{5,7},{6,4},{7,5},{8,10},{9,11},{10,... | collective-permute-start | bytes 675848 | tf_op jit(solution)/shard_map/ppermute | solution.py:363
  26.7 5.3 %collective-permute-start.6 = (f32[80,80]{1,0:T(8,128)S(1)}, f32[80,80]{1,0:T(8,128)S(1)}, u32[]{:S(2)}, u32[]{:S(2)}) collective-permute-start(f32[80,80]{1,0:T(8,128)S(1)} %get-tuple-element.65._), channel_id=1, source_target_pairs={{0,16},{4,20},{8,24},{12,28},{16,0},{20,4},{24,8},{28,12},{1,17},{... | collective-permute-start | bytes 76808 | tf_op jit(solution)/shard_map/ppermute | solution.py:359
  32.2 1.5 %collective-permute-start.7 = (f32[80,80]{1,0:T(8,128)S(1)}, f32[80,80]{1,0:T(8,128)S(1)}, u32[]{:S(2)}, u32[]{:S(2)}) collective-permute-start(f32[80,80]{1,0:T(8,128)S(1)} %pass_last.1.refs_1_.left), channel_id=1, source_target_pairs={{0,1},{1,0},{2,3},{3,2},{4,5},{5,4},{6,7},{7,6},{8,9},{9,8},{10,11... | collective-permute-start | bytes 76808 | tf_op jit(solution)/shard_map/ppermute | solution.py:359
  33.7 4.6 %collective-permute-start.9 = (f32[40,1408]{1,0:T(8,128)S(1)}, f32[40,1408]{1,0:T(8,128)S(1)}, u32[]{:S(2)}, u32[]{:S(2)}) collective-permute-start(f32[40,1408]{1,0:T(8,128)S(1)} %add.7.gram_mine), channel_id=1, source_target_pairs={{0,1},{1,0},{2,3},{3,2},{4,5},{5,4},{6,7},{7,6},{8,9},{9,8},{10,11... | collective-permute-start | bytes 675848 | tf_op jit(solution)/shard_map/ppermute | solution.py:359
  34.3 4.0 %collective-permute-start.10 = (f32[80,80]{1,0:T(8,128)S(1)}, f32[80,80]{1,0:T(8,128)S(1)}, u32[]{:S(2)}, u32[]{:S(2)}) collective-permute-start(f32[80,80]{1,0:T(8,128)S(1)} %get-tuple-element.78.refs_2_.refs_0_), channel_id=1, source_target_pairs={{0,2},{1,3},{2,0},{3,1},{4,6},{5,7},{6,4},{7,5},{8,10},{9,11},{10,... | collective-permute-start | bytes 76808 | tf_op jit(solution)/shard_map/ppermute | solution.py:363

commit v10 on v9

--- a/solution.py
+++ b/solution.py
@@ -188,20 +188,17 @@
             copy.wait()
 
 
-def late_gram_kernel(plan, ens, cot, suffixes, early, offset, _, kept, sent, offsets, whole):
-    whole[:, : early.shape[1]] = early[...]
-    offsets[...] = offset[...] + gram_of(plan, PIECES - 1, cot, ens, suffixes, whole)
-    half = plan.members // 2
-    core = lax.rem(lax.axis_index("space"), 2)
-    kept[...] = whole[pl.ds(core * half, half)]
-    sent[...] = whole[pl.ds((1 - core) * half, half)]
+def late_gram_kernel(plan, ens, cot, suffixes, early, offset, _, grams, offsets):
+    grams[:, : early.shape[1]] = early[...]
+    offsets[...] = offset[...] + gram_of(plan, PIECES - 1, cot, ens, suffixes, grams)
 
 
 def upper_half(level):
     return lax.rem(lax.axis_index("tm") // (1 << level), 2) == 1
 
 
-def join_kernel(level, total, other, later, before, _, new_total, new_later, new_before, upper_total):
+def join_kernel(level, total, other, later, before, _, *refs):
+    new_total, new_later, new_before, upper_total = refs[len(refs) // 2 - 2 : len(refs) // 2 + 2]
     upper = upper_half(level)
     left = jnp.where(upper, other[...], total[...])
     right = jnp.where(upper, total[...], other[...])
@@ -211,7 +208,7 @@
     new_before[...] = jnp.where(upper, mul_exact(other[...], before[...]), before[...])
 
 
-def sum_kernel(left, right, _, __, total, ___):
+def sum_kernel(left, right, _, total):
     total[...] = left[...] + right[...]
 
 
@@ -224,7 +221,7 @@
     new_carry[...] = carry[...] + jnp.where(upper, mul_exact(left, before[...]), 0.0)
 
 
-def last_pass_kernel(level, other, carry, before, _, new_carry):
+def last_pass_kernel(level, other, carry, before, _, __, new_carry, ___):
     added = mul_exact(other[...], before[...])
     new_carry[...] = carry[...] + jnp.where(upper_half(level), added, 0.0)
 
@@ -282,21 +279,15 @@
         copy.wait()
 
 
-def final_kernel(plan, scale, gram_mine, gram_other, follow, steps, _, *refs):
+def final_kernel(plan, scale, gram, gram_core, follow, steps, _, *refs):
     carries, (out, buffer, sems) = refs[:-3], refs[-3:]
     carry = carries[0][...]
     for ref in carries[1:]:
         carry = carry + ref[...]
     count, members = plan.count, plan.members
-    first = lax.rem(lax.axis_index("space"), 2) == 0
-
-    def whole(mine, other):
-        return jnp.concatenate([jnp.where(first, mine, other), jnp.where(first, other, mine)], axis=0)
-
     totals = []
     for at, (start, stop) in enumerate(plan.groups):
-        lanes = plan.lanes(at)
-        tall = whole(gram_mine[:, lanes], gram_other[:, lanes]).T
+        tall = (gram[:, plan.lanes(at)] + gram_core[:, plan.lanes(at)]).T
         for i in range(stop - start):
             totals.append(tall[i * members : (i + 1) * members])
     totals[0] = totals[0] + carry.T
@@ -377,18 +368,20 @@
         [HBM] * 3, [VMEM] * 5, [pltpu.SemaphoreType.DMA] + piece_sems(0), 3.5, "transform_chain",
     )(transforms, ensembles, cotangents)
 
-    wide = shape(members // 2, plan.width)
+    wide = shape(members, plan.width)
     later = before = jnp.eye(members, dtype=F32)
     uppers, befores = [], []
 
-    def join(level, total, other, later, before, after):
+    def join(level, total, other, later, before, after, *through):
+        more = [shape(*value.shape) for value in through]
         befores.append(before)
-        *new, upper = call(
+        total, later, before, upper, *through = call(
             functools.partial(join_kernel, level),
-            [square] * 4, [VMEM] * 4 + [ANY], [VMEM] * 4, [], 0.3, f"join_{level}",
-        )(total, other, later, before, after)
+            [square] * 4 + more, [VMEM] * 4 + [ANY] * (1 + len(more)), [VMEM] * 4 + [ANY] * len(more),
+            [], 0.3, f"join_{level}", aliases={5 + at: 4 + at for at in range(len(more))},
+        )(total, other, later, before, after, *through)
         uppers.append(upper)
-        return new
+        return total, later, before, *through
 
     other = exchange(total, "tm", blocks, 1)
     early_width = plan.lanes(plan.first_group[-1]).start
@@ -403,10 +396,9 @@
     total, later, before = join(0, total, other, later, before, offset)
 
     other = exchange(total, "tm", blocks, 2)
-    gram, gram_sent, own = call(
+    gram, own = call(
         functools.partial(late_gram_kernel, plan),
-        [wide, wide, square], [VMEM] * 5 + [ANY], [VMEM] * 3,
-        [pltpu.VMEM((members, plan.width), F32)], 1.2, "late_gram",
+        [wide, square], [VMEM] * 5 + [ANY], [VMEM] * 2, [], 1.2, "late_gram",
     )(*parts[-1], suffixes, early, offset, total)
     other_own = exchange(own, "tm", blocks, 1)
     for level in range(1, levels - 1):
@@ -428,15 +420,12 @@
         )(own, other_own, carry, uppers[level], befores[level], after, *through)
 
     carry = jnp.zeros((members, members), F32)
-    own, carry, gram_sent = pass_on(0, carry, steps, gram_sent)
-    other_own = exchange(own, "tm", blocks, 2)
-    gram_core = exchange(gram_sent, "space", lanes, 1)
-    for level in range(1, levels - 2):
-        own, carry = pass_on(level, carry, own)
+    for level in range(levels - 2):
+        if level == levels - 3:
+            own, carry, gram, other = pass_on(level, carry, steps, gram, other)
+        else:
+            own, carry = pass_on(level, carry, steps)
         other_own = exchange(own, "tm", blocks, 2 << level)
-    own, carry, gram_core, other = pass_on(levels - 2, carry, own, gram_core, other)
-    other_own = exchange(own, "tm", blocks, blocks // 2)
-    gram = gram + gram_core
     grams = around(gram)
     entering = call(
         functools.partial(enter_kernel, levels - 1),
@@ -449,6 +438,8 @@
         + [shape(2, count * members, members, kind=BF16)],
         [VMEM] * 2, [VMEM] * 3, [], 0.9, "carries",
     )(suffixes, entering)
+    own, carry = pass_on(levels - 2, carry, follow)
+    other_own = exchange(own, "tm", blocks, blocks // 2)
 
     def apply(factors, which, pieces, out, after, name):
         first, last = plan.pieces[pieces[0]][0], plan.pieces[pieces[-1]][1]
@@ -462,21 +453,20 @@
         )(factors, *(parts[piece][which] for piece in pieces), after, *out)
 
     front, rear = tuple(range(PIECES - 1)), (PIECES - 1,)
-    smoothed, done = apply(ens_factors, 0, front + rear, (), follow, "smoothed")
-    carry = call(
+    smoothed, done = apply(ens_factors, 0, front + rear, (), own, "smoothed")
+    carry, grams[0] = call(
         functools.partial(last_pass_kernel, levels - 1),
-        square, [VMEM] * 3 + [ANY], VMEM, [], 0.2, "pass_last",
-    )(other_own, carry, befores[-1], done)
+        [square, wide], [VMEM] * 3 + [ANY] * 2, [VMEM, ANY], [], 0.2, "pass_last", aliases={4: 1},
+    )(other_own, carry, befores[-1], done, grams[0])
     carry_core = exchange(carry, "space", lanes, 1)
-    ensemble_grad, done = apply(cot_factors, 1, rear, (), carry, "ensemble_grad_0")
-    carry, grams[0] = call(
-        sum_kernel, [square, wide], [VMEM] * 2 + [ANY] * 2, [VMEM, ANY], [], 0.1, "chip_carry",
-        aliases={3: 1},
-    )(carry, carry_core, done, grams[0])
-    carries = [carry] + around(carry)
     for part in grams:
         gram = gram + part
-    gram_other = exchange(gram, "space", lanes, 1)
+    gram_core = exchange(gram, "space", lanes, 1)
+    ensemble_grad, done = apply(cot_factors, 1, rear, (), carry, "ensemble_grad_0")
+    carry = call(
+        sum_kernel, square, [VMEM] * 2 + [ANY], VMEM, [], 0.1, "chip_carry",
+    )(carry, carry_core, done)
+    carries = [carry] + around(carry)
     ensemble_grad, done = apply(cot_factors, 1, front, (ensemble_grad,), carry, "ensemble_grad_1")
     transform_grad = call(
         functools.partial(final_kernel, plan, scale),
@@ -484,7 +474,7 @@
         [VMEM] * 4 + [ANY] + [VMEM] * chips, HBM,
         [pltpu.VMEM((count, members, members), F32), pltpu.SemaphoreType.DMA((count,))],
         2.5, "transform_grad",
-    )(gram, gram_other, follow, steps, done, *carries)
+    )(gram, gram_core, follow, steps, done, *carries)
     return (smoothed, ensemble_grad, transform_grad)
 
 

time: 40.8 us -> 40.5 us (level)
  waiting for transfers between devices: 7.35 us -> 5.09 us
  starting transfers between devices: 12.4 us -> 14.4 us
    ppermute x9 -> x8, waiting for transfers between devices: 6.14 us -> 3.87 us  [exchange(): return lax.ppermute(value, axis, [(at, at ^ bit) for at in range(size)])]
    ppermute x9 -> x8, starting transfers between devices: 10.3 us -> 12.3 us  [exchange(): return lax.ppermute(value, axis, [(at, at ^ bit) for at in range(size)])]
  transfers between devices with their start and end apart: 11 -> 10, of which waited for: 6 -> 4; matrix products, arithmetic and copies ran while one was open for 0% -> 0% of each run, Pallas kernels for 34% -> 34%
where the time goes in v10:
time: 40.5 us; the launch traced here: 40.3 us
  Pallas kernels  19.9 us (49%)
  starting transfers between devices  14.4 us (36%)
  waiting for transfers between devices  5.09 us (13%)
  between operations  0.8 us (2%)
    ppermute x8, starting transfers between devices, exchange(): return lax.ppermute(value, axis, [(at, at ^ bit) for at in range(size)])  12.3 us
    pallas_call x3, Pallas kernels, apply(): call(functools.partial(apply_kernel, plan, pieces), [shape(count, members...  6.35 us
    ppermute x8, waiting for transfers between devices, exchange(): return lax.ppermute(value, axis, [(at, at ^ bit) for at in range(size)])  3.87 us
    pallas_call x1, Pallas kernels, shards(): call(functools.partial(early_gram_kernel, plan), [shape(members, early_wi...  3.85 us
    pallas_call x1, Pallas kernels, shards(): call(functools.partial(chain_kernel, plan), [shape(count * members, membe...  3.22 us
    pallas_call x1, Pallas kernels, shards(): call(functools.partial(final_kernel, plan, scale), shape(count, members,...  2.28 us
    ppermute x2, starting transfers between devices, around(): lax.ppermute(value, 'space', [(at, (at + 2 * d) % lanes) for at in range(...  2.14 us
    ppermute x2, waiting for transfers between devices, around(): lax.ppermute(value, 'space', [(at, (at + 2 * d) % lanes) for at in range(...  1.22 us
  transfers between devices with their start and end apart: 10, of which 4 were waited for; matrix products, arithmetic and copies ran while one was open for 0% of the time, Pallas kernels for 34%

profile of v10, /device:TPU:0, one launch (start us, length us, event | category | flops | bytes accessed | tf_op | source)
XLA Modules:
  0.0 40.3 jit_solution(16197362890072935285)
XLA Ops:
  0.6 3.2 %transform_chain.1 = (f32[1280,80]{1,0:T(8,128)S(1)}, f32[80,80]{1,0:T(8,128)S(1)}, f32[16,80,80]{2,1,0:T(8,128)S(1)}, bf16[6,80,2048]{2,1,0:T(8,128)(2,1)S(1)}, bf16[6,80,2048]{2,1,0:T(8,128)(2,1)S(1)}) custom-call(f32[16,80,80]{2,1,0:T(8,128)} %transforms.1, bf16[16,80,2048]{2,1,0:T(8,128)(2,1)} %ensembles.3, bf16[16,80,2048]{2,1,0:T(8,128)(2,1)} %cotangents.3), custom_call_target="tpu_custom_call" | custom-call | bytes 12600000 | tf_op jit(solution)/shard_map/transform_chain/pallas_call | solution.py:365
  3.9 3.0 %collective-permute-start = (f32[80,80]{1,0:T(8,128)S(1)}, f32[80,80]{1,0:T(8,128)S(1)}, u32[]{:S(2)}, u32[]{:S(2)}) collective-permute-start(f32[80,80]{1,0:T(8,128)S(1)} %get-tuple-element.42.total), channel_id=1, source_target_pairs={{0,4},{4,0},{8,12},{12,8},{16,20},{20,16},{24,28},{28,24},{1,5},{5... | collective-permute-start | bytes 76808 | tf_op jit(solution)/shard_map/ppermute | solution.py:350
  6.9 3.8 %early_gram.1 = (f32[80,1024]{1,0:T(8,128)S(1)}, f32[80,80]{1,0:T(8,128)S(1)}, bf16[6,80,2048]{2,1,0:T(8,128)(2,1)S(1)}, bf16[6,80,2048]{2,1,0:T(8,128)(2,1)S(1)...) custom-call(bf16[16,80,2048]{2,1,0:T(8,128)(2,1)} %ensembles.3, bf16[16,80,2048]{2,1,0:T(8,128)(2,1)} %cotangents.3, ...), custom_call_target="tpu_custom_call" | custom-call | bytes 10800000 | tf_op jit(solution)/shard_map/early_gram/pallas_call | solution.py:388
  10.7 0.0 collective-permute-done.other
  10.7 0.3 join_0.1
  11.0 1.6 %collective-permute-start.1 = (f32[80,80]{1,0:T(8,128)S(1)}, f32[80,80]{1,0:T(8,128)S(1)}, u32[]{:S(2)}, u32[]{:S(2)}) collective-permute-start(f32[80,80]{1,0:T(8,128)S(1)} %get-tuple-element.46._.total), channel_id=1, source_target_pairs={{0,8},{4,12},{8,0},{12,4},{16,24},{20,28},{24,16},{28,20},{1,9},{5... | collective-permute-start | bytes 76808 | tf_op jit(solution)/shard_map/ppermute | solution.py:350
  12.6 1.1 %late_gram.1 = (f32[80,1408]{1,0:T(8,128)S(1)}, f32[80,80]{1,0:T(8,128)S(1)}) custom-call(bf16[4,80,2048]{2,1,0:T(8,128)(2,1)S(1)} %get-tuple-element.49.ens.refs_2_, bf16[4,80,2048]{2,1,0:T(8,128)(2,1)S(1)} %get-tuple-element.50.cot.refs_0_, f32[1280,80]{1,0:T(8,128)S(1)} %get-tuple-element.41.suffixes, f32[80,1024]{1,0:T(8,128)S(1)} %get-tuple-element.51.early, ...), custom_call_target="tpu_custom_call" | custom-call | bytes 4320000 | tf_op jit(solution)/shard_map/late_gram/pallas_call | solution.py:399
  13.8 0.6 %collective-permute-start.2 = (f32[80,80]{1,0:T(8,128)S(1)}, f32[80,80]{1,0:T(8,128)S(1)}, u32[]{:S(2)}, u32[]{:S(2)}) collective-permute-start(f32[80,80]{1,0:T(8,128)S(1)} %get-tuple-element.52._.own), channel_id=1, source_target_pairs={{0,4},{4,0},{8,12},{12,8},{16,20},{20,16},{24,28},{28,24},{1,5},{5... | collective-permute-start | bytes 76808 | tf_op jit(solution)/shard_map/ppermute | solution.py:350
  14.4 0.7 %collective-permute-done.1.other = f32[80,80]{1,0:T(8,128)S(1)} collective-permute-done((f32[80,80]{1,0:T(8,128)S(1)}, f32[80,80]{1,0:T(8,128)S(1)}, u32[]{:S(2)}, u32[]{:S(2)}) %collective-permute-start.1) | collective-permute-done | bytes 25632 | tf_op jit(solution)/shard_map/ppermute | solution.py:350
  15.1 0.2 join_1.1
  15.3 2.6 %collective-permute-start.3 = (f32[80,80]{1,0:T(8,128)S(1)}, f32[80,80]{1,0:T(8,128)S(1)}, u32[]{:S(2)}, u32[]{:S(2)}) collective-permute-start(f32[80,80]{1,0:T(8,128)S(1)} %get-tuple-element.56._), channel_id=1, source_target_pairs={{0,16},{4,20},{8,24},{12,28},{16,0},{20,4},{24,8},{28,12},{1,17},{... | collective-permute-start | bytes 76808 | tf_op jit(solution)/shard_map/ppermute | solution.py:350
  18.0 0.9 %windows.1._.steps = bf16[2,2560,80]{2,1,0:T(8,128)(2,1)S(1)} custom-call(f32[16,80,80]{2,1,0:T(8,128)S(1)} %get-tuple-element.55.kept, f32[80,80]{1,0:T(8,128)S(1)} %get-tuple-element.56._), custom_call_target="tpu_custom_call" | custom-call | bytes 3600000 | tf_op jit(solution)/shard_map/windows/pallas_call | solution.py:408
  18.9 0.0 collective-permute-done.2.other
  18.9 1.4 %collective-permute-done.3.refs_1_ = f32[80,80]{1,0:T(8,128)S(1)} collective-permute-done((f32[80,80]{1,0:T(8,128)S(1)}, f32[80,80]{1,0:T(8,128)S(1)}, u32[]{:S(2)}, u32[]{:S(2)}) %collective-permute-start.3) | collective-permute-done | bytes 25632 | tf_op jit(solution)/shard_map/ppermute | solution.py:350
  20.3 0.2 pass_0.1
  20.5 1.6 %collective-permute-start.6 = (f32[80,1408]{1,0:T(8,128)S(1)}, f32[80,1408]{1,0:T(8,128)S(1)}, u32[]{:S(2)}, u32[]{:S(2)}) collective-permute-start(f32[80,1408]{1,0:T(8,128)S(1)} %get-tuple-element.72), channel_id=1, source_target_pairs={{0,2},{1,3},{2,0},{3,1},{4,6},{5,7},{6,4},{7,5},{8,10},{9,11},{10,... | collective-permute-start | bytes 1351688 | tf_op jit(solution)/shard_map/ppermute | solution.py:354
  22.1 1.6 %collective-permute-start.4 = (f32[80,80]{1,0:T(8,128)S(1)}, f32[80,80]{1,0:T(8,128)S(1)}, u32[]{:S(2)}, u32[]{:S(2)}) collective-permute-start(f32[80,80]{1,0:T(8,128)S(1)} %get-tuple-element.59._.own), channel_id=1, source_target_pairs={{0,8},{4,12},{8,0},{12,4},{16,24},{20,28},{24,16},{28,20},{1,9},{5... | collective-permute-start | bytes 76808 | tf_op jit(solution)/shard_map/ppermute | solution.py:350
  23.7 0.2 entering.1.later
  23.9 0.9 %carries.1 = (bf16[6,240,240]{2,1,0:T(8,128)(2,1)S(1)}, bf16[6,240,240]{2,1,0:T(8,128)(2,1)S(1)}, bf16[2,1280,80]{2,1,0:T(8,128)(2,1)S(1)}) custom-call(f32[1280,80]{1,0:T(8,128)S(1)} %get-tuple-element.41.suffixes, f32[80,80]{1,0:T(8,128)S(1)} %entering.1.later), custom_call_target="tpu_custom_call" | custom-call | bytes 3240000 | tf_op jit(solution)/shard_map/carries/pallas_call | solution.py:435
  24.7 1.8 %collective-permute-done.4.other = f32[80,80]{1,0:T(8,128)S(1)} collective-permute-done((f32[80,80]{1,0:T(8,128)S(1)}, f32[80,80]{1,0:T(8,128)S(1)}, u32[]{:S(2)}, u32[]{:S(2)}) %collective-permute-start.4) | collective-permute-done | bytes 25632 | tf_op jit(solution)/shard_map/ppermute | solution.py:350
  26.5 0.2 pass_1.1
  26.8 2.3 %collective-permute-start.5 = (f32[80,80]{1,0:T(8,128)S(1)}, f32[80,80]{1,0:T(8,128)S(1)}, u32[]{:S(2)}, u32[]{:S(2)}) collective-permute-start(f32[80,80]{1,0:T(8,128)S(1)} %get-tuple-element.65.refs_3_), channel_id=1, source_target_pairs={{0,16},{4,20},{8,24},{12,28},{16,0},{20,4},{24,8},{28,12},{1,17},{... | collective-permute-start | bytes 76808 | tf_op jit(solution)/shard_map/ppermute | solution.py:350
  29.0 2.7 %smoothed.1 = (bf16[16,80,2048]{2,1,0:T(8,128)(2,1)}, f32[8,128]{1,0:T(8,128)S(1)}) custom-call(bf16[6,240,240]{2,1,0:T(8,128)(2,1)S(1)} %get-tuple-element.60.factors, bf16[6,80,2048]{2,1,0:T(8,128)(2,1)S(1)} %get-tuple-element.43.ens.refs_0_, bf16[6,80,2048]{2,1,0:T(8,128)(2,1)S(1)} %get-tuple-element.61.refs_1_, ...), custom_call_target="tpu_custom_call" | custom-call | bytes 6480000 | tf_op jit(solution)/shard_map/smoothed/pallas_call | solution.py:447
  31.7 0.0 collective-permute-done.5.other
  31.7 0.0 collective-permute-done.6.__
  31.7 0.2 pass_last.1
  31.9 0.1 add.3.gram
  32.0 0.1 collective-permute-start.8
  32.1 0.5 %collective-permute-start.7 = (f32[80,80]{1,0:T(8,128)S(1)}, f32[80,80]{1,0:T(8,128)S(1)}, u32[]{:S(2)}, u32[]{:S(2)}) collective-permute-start(f32[80,80]{1,0:T(8,128)S(1)} %get-tuple-element.73.refs_1_.left), channel_id=1, source_target_pairs={{0,1},{1,0},{2,3},{3,2},{4,5},{5,4},{6,7},{7,6},{8,9},{9,8},{10,11... | collective-permute-start | bytes 76808 | tf_op jit(solution)/shard_map/ppermute | solution.py:350
  32.6 1.4 %ensemble_grad_0.1 = (bf16[16,80,2048]{2,1,0:T(8,128)(2,1)}, f32[8,128]{1,0:T(8,128)S(1)}) custom-call(bf16[6,240,240]{2,1,0:T(8,128)(2,1)S(1)} %get-tuple-element.67.factors, bf16[4,80,2048]{2,1,0:T(8,128)(2,1)S(1)} %get-tuple-element.50.cot.refs_0_, f32[80,80]{1,0:T(8,128)S(1)} %get-tuple-element.73.refs_1_.left), custom_call_target="tpu_custom_call" | custom-call | bytes 6480000 | tf_op jit(solution)/shard_map/ensemble_grad_0/pallas_call | solution.py:447
  33.9 0.0 collective-permute-done.7.right
  34.0 0.6 %collective-permute-start.9 = (f32[80,80]{1,0:T(8,128)S(1)}, f32[80,80]{1,0:T(8,128)S(1)}, u32[]{:S(2)}, u32[]{:S(2)}) collective-permute-start(f32[80,80]{1,0:T(8,128)S(1)} %chip_carry.1.refs_2_.refs_0_), channel_id=1, source_target_pairs={{0,2},{1,3},{2,0},{3,1},{4,6},{5,7},{6,4},{7,5},{8,10},{9,11},{10,... | collective-permute-start | bytes 76808 | tf_op jit(solution)/shard_map/ppermute | solution.py:354
  34.5 2.3 %ensemble_grad_1.1 = (bf16[16,80,2048]{2,1,0:T(8,128)(2,1)}, f32[8,128]{1,0:T(8,128)S(1)}) custom-call(bf16[6,240,240]{2,1,0:T(8,128)(2,1)S(1)} %get-tuple-element.67.factors, bf16[6,80,2048]{2,1,0:T(8,128)(2,1)S(1)} %get-tuple-element.44.cot.refs_0_, bf16[6,80,2048]{2,1,0:T(8,128)(2,1)S(1)} %get-tuple-element.68.refs_1_, ...), custom_call_target="tpu_custom_call", output_to_operand_aliasing={{0}: (4, {})} | custom-call | bytes 6480000 | tf_op jit(solution)/shard_map/ensemble_grad_1/pallas_call | solution.py:447
  36.8 1.2 %collective-permute-done.9.refs_1_ = f32[80,80]{1,0:T(8,128)S(1)} collective-permute-done((f32[80,80]{1,0:T(8,128)S(1)}, f32[80,80]{1,0:T(8,128)S(1)}, u32[]{:S(2)}, u32[]{:S(2)}) %collective-permute-start.9) | collective-permute-done | bytes 25632 | tf_op jit(solution)/shard_map/ppermute | solution.py:354
  38.0 0.0 collective-permute-done.8.gram_core
  38.0 2.3 %transform_grad.1 = f32[16,80,80]{2,1,0:T(8,128)} custom-call(f32[80,1408]{1,0:T(8,128)S(1)} %add.3.gram, f32[80,1408]{1,0:T(8,128)S(1)} %collective-permute-done.8.gram_core, bf16[2,1280,80]{2,1,0:T(8,128)(2,1)S(1)} %get-tuple-element.64._.follow, bf16[2,2560,80]{2,1,0:T(8,128)(2,1)S(1)} %windows.1._.steps, f32[8,128]{1,0:T(8,128)S(1)} %get-tuple-element.78._, ...), custom_call_target="tpu_custom_call" | custom-call | bytes 9000000 | tf_op jit(solution)/shard_map/transform_grad/pallas_call | solution.py:471
  (3 shorter events, 0.0 us)
Async XLA Ops:
  3.9 6.9 %collective-permute-start = (f32[80,80]{1,0:T(8,128)S(1)}, f32[80,80]{1,0:T(8,128)S(1)}, u32[]{:S(2)}, u32[]{:S(2)}) collective-permute-start(f32[80,80]{1,0:T(8,128)S(1)} %get-tuple-element.42.total), channel_id=1, source_target_pairs={{0,4},{4,0},{8,12},{12,8},{16,20},{20,16},{24,28},{28,24},{1,5},{5... | collective-permute-start | bytes 76808 | tf_op jit(solution)/shard_map/ppermute | solution.py:350
  11.0 4.1 %collective-permute-start.1 = (f32[80,80]{1,0:T(8,128)S(1)}, f32[80,80]{1,0:T(8,128)S(1)}, u32[]{:S(2)}, u32[]{:S(2)}) collective-permute-start(f32[80,80]{1,0:T(8,128)S(1)} %get-tuple-element.46._.total), channel_id=1, source_target_pairs={{0,8},{4,12},{8,0},{12,4},{16,24},{20,28},{24,16},{28,20},{1,9},{5... | collective-permute-start | bytes 76808 | tf_op jit(solution)/shard_map/ppermute | solution.py:350
  13.8 5.1 %collective-permute-start.2 = (f32[80,80]{1,0:T(8,128)S(1)}, f32[80,80]{1,0:T(8,128)S(1)}, u32[]{:S(2)}, u32[]{:S(2)}) collective-permute-start(f32[80,80]{1,0:T(8,128)S(1)} %get-tuple-element.52._.own), channel_id=1, source_target_pairs={{0,4},{4,0},{8,12},{12,8},{16,20},{20,16},{24,28},{28,24},{1,5},{5... | collective-permute-start | bytes 76808 | tf_op jit(solution)/shard_map/ppermute | solution.py:350
  15.3 5.0 %collective-permute-start.3 = (f32[80,80]{1,0:T(8,128)S(1)}, f32[80,80]{1,0:T(8,128)S(1)}, u32[]{:S(2)}, u32[]{:S(2)}) collective-permute-start(f32[80,80]{1,0:T(8,128)S(1)} %get-tuple-element.56._), channel_id=1, source_target_pairs={{0,16},{4,20},{8,24},{12,28},{16,0},{20,4},{24,8},{28,12},{1,17},{... | collective-permute-start | bytes 76808 | tf_op jit(solution)/shard_map/ppermute | solution.py:350
  20.5 11.2 %collective-permute-start.6 = (f32[80,1408]{1,0:T(8,128)S(1)}, f32[80,1408]{1,0:T(8,128)S(1)}, u32[]{:S(2)}, u32[]{:S(2)}) collective-permute-start(f32[80,1408]{1,0:T(8,128)S(1)} %get-tuple-element.72), channel_id=1, source_target_pairs={{0,2},{1,3},{2,0},{3,1},{4,6},{5,7},{6,4},{7,5},{8,10},{9,11},{10,... | collective-permute-start | bytes 1351688 | tf_op jit(solution)/shard_map/ppermute | solution.py:354
  22.1 4.4 %collective-permute-start.4 = (f32[80,80]{1,0:T(8,128)S(1)}, f32[80,80]{1,0:T(8,128)S(1)}, u32[]{:S(2)}, u32[]{:S(2)}) collective-permute-start(f32[80,80]{1,0:T(8,128)S(1)} %get-tuple-element.59._.own), channel_id=1, source_target_pairs={{0,8},{4,12},{8,0},{12,4},{16,24},{20,28},{24,16},{28,20},{1,9},{5... | collective-permute-start | bytes 76808 | tf_op jit(solution)/shard_map/ppermute | solution.py:350
  26.8 5.0 %collective-permute-start.5 = (f32[80,80]{1,0:T(8,128)S(1)}, f32[80,80]{1,0:T(8,128)S(1)}, u32[]{:S(2)}, u32[]{:S(2)}) collective-permute-start(f32[80,80]{1,0:T(8,128)S(1)} %get-tuple-element.65.refs_3_), channel_id=1, source_target_pairs={{0,16},{4,20},{8,24},{12,28},{16,0},{20,4},{24,8},{28,12},{1,17},{... | collective-permute-start | bytes 76808 | tf_op jit(solution)/shard_map/ppermute | solution.py:350
  32.0 6.0 %collective-permute-start.8 = (f32[80,1408]{1,0:T(8,128)S(1)}, f32[80,1408]{1,0:T(8,128)S(1)}, u32[]{:S(2)}, u32[]{:S(2)}) collective-permute-start(f32[80,1408]{1,0:T(8,128)S(1)} %add.3.gram), channel_id=1, source_target_pairs={{0,1},{1,0},{2,3},{3,2},{4,5},{5,4},{6,7},{7,6},{8,9},{9,8},{10,11... | collective-permute-start | bytes 1351688 | tf_op jit(solution)/shard_map/ppermute | solution.py:350
  32.1 1.9 %collective-permute-start.7 = (f32[80,80]{1,0:T(8,128)S(1)}, f32[80,80]{1,0:T(8,128)S(1)}, u32[]{:S(2)}, u32[]{:S(2)}) collective-permute-start(f32[80,80]{1,0:T(8,128)S(1)} %get-tuple-element.73.refs_1_.left), channel_id=1, source_target_pairs={{0,1},{1,0},{2,3},{3,2},{4,5},{5,4},{6,7},{7,6},{8,9},{9,8},{10,11... | collective-permute-start | bytes 76808 | tf_op jit(solution)/shard_map/ppermute | solution.py:350
  34.0 4.1 %collective-permute-start.9 = (f32[80,80]{1,0:T(8,128)S(1)}, f32[80,80]{1,0:T(8,128)S(1)}, u32[]{:S(2)}, u32[]{:S(2)}) collective-permute-start(f32[80,80]{1,0:T(8,128)S(1)} %chip_carry.1.refs_2_.refs_0_), channel_id=1, source_target_pairs={{0,2},{1,3},{2,0},{3,1},{4,6},{5,7},{6,4},{7,5},{8,10},{9,11},{10,... | collective-permute-start | bytes 76808 | tf_op jit(solution)/shard_map/ppermute | solution.py:354

commit v11 on v10

--- a/solution.py
+++ b/solution.py
@@ -323,7 +323,7 @@
         input_output_aliases=aliases or {},
         compiler_params=pltpu.CompilerParams(vmem_limit_bytes=limit << 20),
         cost_estimate=pl.CostEstimate(
-            flops=0, bytes_accessed=int(micros * 3.6e6), transcendentals=0
+            flops=int(micros * 1e9), bytes_accessed=int(micros * 3e6), transcendentals=0
         ),
         name=name,
     )
@@ -401,6 +401,7 @@
         [wide, square], [VMEM] * 5 + [ANY], [VMEM] * 2, [], 1.2, "late_gram",
     )(*parts[-1], suffixes, early, offset, total)
     other_own = exchange(own, "tm", blocks, 1)
+    grams = around(gram)
     for level in range(1, levels - 1):
         total, later, before = join(level, total, other, later, before, own)
         other = exchange(total, "tm", blocks, 2 << level)
@@ -421,12 +422,8 @@
 
     carry = jnp.zeros((members, members), F32)
     for level in range(levels - 2):
-        if level == levels - 3:
-            own, carry, gram, other = pass_on(level, carry, steps, gram, other)
-        else:
-            own, carry = pass_on(level, carry, steps)
+        own, carry = pass_on(level, carry, steps)
         other_own = exchange(own, "tm", blocks, 2 << level)
-    grams = around(gram)
     entering = call(
         functools.partial(enter_kernel, levels - 1),
         square, [VMEM] * 2 + [ANY], VMEM, [], 0.2, "entering",
@@ -449,7 +446,7 @@
             [shape(count, members, cells, kind=BF16), shape(8, 128)],
             [VMEM] * (1 + len(pieces)) + [ANY] + [HBM] * len(out), [HBM, VMEM],
             [pltpu.VMEM((last - first, members, cells), BF16), pltpu.SemaphoreType.DMA((number,))],
-            1.8, name, aliases={2 + len(pieces): 0} if out else None,
+            0.15 * (last - first) + 0.6, name, aliases={2 + len(pieces): 0} if out else None,
         )(factors, *(parts[piece][which] for piece in pieces), after, *out)
 
     front, rear = tuple(range(PIECES - 1)), (PIECES - 1,)

time: 40.5 us -> 38.5 us (0.951)
  starting transfers between devices: 14.4 us -> 11.8 us
  waiting for transfers between devices: 5.09 us -> 5.7 us
    ppermute x8, starting transfers between devices: 12.3 us -> 10 us  [exchange(): return lax.ppermute(value, axis, [(at, at ^ bit) for at in range(size)])]
  transfers between devices with their start and end apart: 10 -> 10, of which waited for: 4 -> 4; matrix products, arithmetic and copies ran while one was open for 0% -> 0% of each run, Pallas kernels for 34% -> 37%
where the time goes in v11:
time: 38.5 us; the launch traced here: 38.3 us
  Pallas kernels  19.9 us (52%)
  starting transfers between devices  11.8 us (31%)
  waiting for transfers between devices  5.7 us (15%)
  between operations  0.8 us (2%)
    ppermute x8, starting transfers between devices, exchange(): return lax.ppermute(value, axis, [(at, at ^ bit) for at in range(size)])  10 us
    pallas_call x3, Pallas kernels, apply(): call(functools.partial(apply_kernel, plan, pieces), [shape(count, members...  6.36 us
    ppermute x8, waiting for transfers between devices, exchange(): return lax.ppermute(value, axis, [(at, at ^ bit) for at in range(size)])  4.19 us
    pallas_call x1, Pallas kernels, shards(): call(functools.partial(early_gram_kernel, plan), [shape(members, early_wi...  3.85 us
    pallas_call x1, Pallas kernels, shards(): call(functools.partial(chain_kernel, plan), [shape(count * members, membe...  3.22 us
    pallas_call x1, Pallas kernels, shards(): call(functools.partial(final_kernel, plan, scale), shape(count, members,...  2.28 us
    ppermute x2, starting transfers between devices, around(): lax.ppermute(value, 'space', [(at, (at + 2 * d) % lanes) for at in range(...  1.8 us
    ppermute x2, waiting for transfers between devices, around(): lax.ppermute(value, 'space', [(at, (at + 2 * d) % lanes) for at in range(...  1.51 us
  transfers between devices with their start and end apart: 10, of which 4 were waited for; matrix products, arithmetic and copies ran while one was open for 0% of the time, Pallas kernels for 37%

profile of v11, /device:TPU:0, one launch (start us, length us, event | category | flops | bytes accessed | tf_op | source)
XLA Modules:
  0.0 38.3 jit_solution(1995005279311219238)
XLA Ops:
  0.6 3.2 %transform_chain.1 = (f32[1280,80]{1,0:T(8,128)S(1)}, f32[80,80]{1,0:T(8,128)S(1)}, f32[16,80,80]{2,1,0:T(8,128)S(1)}, bf16[6,80,2048]{2,1,0:T(8,128)(2,1)S(1)}, bf16[6,80,2048]{2,1,0:T(8,128)(2,1)S(1)}) custom-call(f32[16,80,80]{2,1,0:T(8,128)} %transforms.1, bf16[16,80,2048]{2,1,0:T(8,128)(2,1)} %ensembles.3, bf16[16,80,2048]{2,1,0:T(8,128)(2,1)} %cotangents.3), custom_call_target="tpu_custom_call" | custom-call | flops 3500000000 | bytes 10500000 | tf_op jit(solution)/shard_map/transform_chain/pallas_call | solution.py:365
  3.9 3.0 %collective-permute-start = (f32[80,80]{1,0:T(8,128)S(1)}, f32[80,80]{1,0:T(8,128)S(1)}, u32[]{:S(2)}, u32[]{:S(2)}) collective-permute-start(f32[80,80]{1,0:T(8,128)S(1)} %get-tuple-element.40.total), channel_id=1, source_target_pairs={{0,4},{4,0},{8,12},{12,8},{16,20},{20,16},{24,28},{28,24},{1,5},{5... | collective-permute-start | bytes 76808 | tf_op jit(solution)/shard_map/ppermute | solution.py:350
  6.9 3.8 %early_gram.1 = (f32[80,1024]{1,0:T(8,128)S(1)}, f32[80,80]{1,0:T(8,128)S(1)}, bf16[6,80,2048]{2,1,0:T(8,128)(2,1)S(1)}, bf16[6,80,2048]{2,1,0:T(8,128)(2,1)S(1)...) custom-call(bf16[16,80,2048]{2,1,0:T(8,128)(2,1)} %ensembles.3, bf16[16,80,2048]{2,1,0:T(8,128)(2,1)} %cotangents.3, ...), custom_call_target="tpu_custom_call" | custom-call | flops 3000000000 | bytes 9000000 | tf_op jit(solution)/shard_map/early_gram/pallas_call | solution.py:388
  10.7 0.0 collective-permute-done.other
  10.7 0.3 join_0.1
  11.0 1.6 %collective-permute-start.1 = (f32[80,80]{1,0:T(8,128)S(1)}, f32[80,80]{1,0:T(8,128)S(1)}, u32[]{:S(2)}, u32[]{:S(2)}) collective-permute-start(f32[80,80]{1,0:T(8,128)S(1)} %get-tuple-element.44._.total), channel_id=1, source_target_pairs={{0,8},{4,12},{8,0},{12,4},{16,24},{20,28},{24,16},{28,20},{1,9},{5... | collective-permute-start | bytes 76808 | tf_op jit(solution)/shard_map/ppermute | solution.py:350
  12.7 1.1 %late_gram.1 = (f32[80,1408]{1,0:T(8,128)S(1)}, f32[80,80]{1,0:T(8,128)S(1)}) custom-call(bf16[4,80,2048]{2,1,0:T(8,128)(2,1)S(1)} %get-tuple-element.47.ens.refs_2_, bf16[4,80,2048]{2,1,0:T(8,128)(2,1)S(1)} %get-tuple-element.48.cot.refs_0_, f32[1280,80]{1,0:T(8,128)S(1)} %get-tuple-element.39.suffixes, f32[80,1024]{1,0:T(8,128)S(1)} %get-tuple-element.49.early, ...), custom_call_target="tpu_custom_call" | custom-call | flops 1200000000 | bytes 3600000 | tf_op jit(solution)/shard_map/late_gram/pallas_call | solution.py:399
  13.8 0.6 %collective-permute-start.3 = (f32[80,80]{1,0:T(8,128)S(1)}, f32[80,80]{1,0:T(8,128)S(1)}, u32[]{:S(2)}, u32[]{:S(2)}) collective-permute-start(f32[80,80]{1,0:T(8,128)S(1)} %get-tuple-element.50._.own), channel_id=1, source_target_pairs={{0,4},{4,0},{8,12},{12,8},{16,20},{20,16},{24,28},{28,24},{1,5},{5... | collective-permute-start | bytes 76808 | tf_op jit(solution)/shard_map/ppermute | solution.py:350
  14.4 1.5 %collective-permute-start.6 = (f32[80,1408]{1,0:T(8,128)S(1)}, f32[80,1408]{1,0:T(8,128)S(1)}, u32[]{:S(2)}, u32[]{:S(2)}) collective-permute-start(f32[80,1408]{1,0:T(8,128)S(1)} %get-tuple-element.68), channel_id=1, source_target_pairs={{0,2},{1,3},{2,0},{3,1},{4,6},{5,7},{6,4},{7,5},{8,10},{9,11},{10,... | collective-permute-start | bytes 1351688 | tf_op jit(solution)/shard_map/ppermute | solution.py:354
  15.9 0.0 collective-permute-done.1.other
  15.9 0.3 join_1.1
  16.2 2.7 %collective-permute-start.2 = (f32[80,80]{1,0:T(8,128)S(1)}, f32[80,80]{1,0:T(8,128)S(1)}, u32[]{:S(2)}, u32[]{:S(2)}) collective-permute-start(f32[80,80]{1,0:T(8,128)S(1)} %get-tuple-element.52._), channel_id=1, source_target_pairs={{0,16},{4,20},{8,24},{12,28},{16,0},{20,4},{24,8},{28,12},{1,17},{... | collective-permute-start | bytes 76808 | tf_op jit(solution)/shard_map/ppermute | solution.py:350
  18.9 0.9 %windows.1._.steps = bf16[2,2560,80]{2,1,0:T(8,128)(2,1)S(1)} custom-call(f32[16,80,80]{2,1,0:T(8,128)S(1)} %get-tuple-element.54.kept, f32[80,80]{1,0:T(8,128)S(1)} %get-tuple-element.52._), custom_call_target="tpu_custom_call" | custom-call | flops 1000000000 | bytes 3000000 | tf_op jit(solution)/shard_map/windows/pallas_call | solution.py:409
  19.8 0.0 collective-permute-done.3.other
  19.8 0.2 pass_0.1
  20.0 0.8 %collective-permute-start.4 = (f32[80,80]{1,0:T(8,128)S(1)}, f32[80,80]{1,0:T(8,128)S(1)}, u32[]{:S(2)}, u32[]{:S(2)}) collective-permute-start(f32[80,80]{1,0:T(8,128)S(1)} %get-tuple-element.55._.own), channel_id=1, source_target_pairs={{0,8},{4,12},{8,0},{12,4},{16,24},{20,28},{24,16},{28,20},{1,9},{5... | collective-permute-start | bytes 76808 | tf_op jit(solution)/shard_map/ppermute | solution.py:350
  20.8 0.7 %collective-permute-done.2.other = f32[80,80]{1,0:T(8,128)S(1)} collective-permute-done((f32[80,80]{1,0:T(8,128)S(1)}, f32[80,80]{1,0:T(8,128)S(1)}, u32[]{:S(2)}, u32[]{:S(2)}) %collective-permute-start.2) | collective-permute-done | bytes 25632 | tf_op jit(solution)/shard_map/ppermute | solution.py:350
  21.5 0.2 entering.1.later
  21.7 0.9 %carries.1 = (bf16[6,240,240]{2,1,0:T(8,128)(2,1)S(1)}, bf16[6,240,240]{2,1,0:T(8,128)(2,1)S(1)}, bf16[2,1280,80]{2,1,0:T(8,128)(2,1)S(1)}) custom-call(f32[1280,80]{1,0:T(8,128)S(1)} %get-tuple-element.39.suffixes, f32[80,80]{1,0:T(8,128)S(1)} %entering.1.later), custom_call_target="tpu_custom_call" | custom-call | flops 900000000 | bytes 2700000 | tf_op jit(solution)/shard_map/carries/pallas_call | solution.py:432
  22.5 1.6 %collective-permute-done.4.other = f32[80,80]{1,0:T(8,128)S(1)} collective-permute-done((f32[80,80]{1,0:T(8,128)S(1)}, f32[80,80]{1,0:T(8,128)S(1)}, u32[]{:S(2)}, u32[]{:S(2)}) %collective-permute-start.4) | collective-permute-done | bytes 25632 | tf_op jit(solution)/shard_map/ppermute | solution.py:350
  24.1 0.2 pass_1.1
  24.3 0.8 %collective-permute-start.5 = (f32[80,80]{1,0:T(8,128)S(1)}, f32[80,80]{1,0:T(8,128)S(1)}, u32[]{:S(2)}, u32[]{:S(2)}) collective-permute-start(f32[80,80]{1,0:T(8,128)S(1)} %get-tuple-element.61.refs_3_), channel_id=1, source_target_pairs={{0,16},{4,20},{8,24},{12,28},{16,0},{20,4},{24,8},{28,12},{1,17},{... | collective-permute-start | bytes 76808 | tf_op jit(solution)/shard_map/ppermute | solution.py:350
  25.1 2.7 %smoothed.1 = (bf16[16,80,2048]{2,1,0:T(8,128)(2,1)}, f32[8,128]{1,0:T(8,128)S(1)}) custom-call(bf16[6,240,240]{2,1,0:T(8,128)(2,1)S(1)} %get-tuple-element.56.factors, bf16[6,80,2048]{2,1,0:T(8,128)(2,1)S(1)} %get-tuple-element.41.ens.refs_0_, bf16[6,80,2048]{2,1,0:T(8,128)(2,1)S(1)} %get-tuple-element.57.refs_1_, ...), custom_call_target="tpu_custom_call" | custom-call | flops 3000000000 | bytes 9000000 | tf_op jit(solution)/shard_map/smoothed/pallas_call | solution.py:444
  27.8 1.9 %collective-permute-done.5.other = f32[80,80]{1,0:T(8,128)S(1)} collective-permute-done((f32[80,80]{1,0:T(8,128)S(1)}, f32[80,80]{1,0:T(8,128)S(1)}, u32[]{:S(2)}, u32[]{:S(2)}) %collective-permute-start.5) | collective-permute-done | bytes 25632 | tf_op jit(solution)/shard_map/ppermute | solution.py:350
  29.7 0.0 collective-permute-done.6.__
  29.7 0.2 pass_last.1
  29.9 0.1 add.3.gram
  30.0 0.1 collective-permute-start.8
  30.1 0.5 %collective-permute-start.7 = (f32[80,80]{1,0:T(8,128)S(1)}, f32[80,80]{1,0:T(8,128)S(1)}, u32[]{:S(2)}, u32[]{:S(2)}) collective-permute-start(f32[80,80]{1,0:T(8,128)S(1)} %get-tuple-element.69.refs_1_.left), channel_id=1, source_target_pairs={{0,1},{1,0},{2,3},{3,2},{4,5},{5,4},{6,7},{7,6},{8,9},{9,8},{10,11... | collective-permute-start | bytes 76808 | tf_op jit(solution)/shard_map/ppermute | solution.py:350
  30.6 1.4 %ensemble_grad_0.1 = (bf16[16,80,2048]{2,1,0:T(8,128)(2,1)}, f32[8,128]{1,0:T(8,128)S(1)}) custom-call(bf16[6,240,240]{2,1,0:T(8,128)(2,1)S(1)} %get-tuple-element.63.factors, bf16[4,80,2048]{2,1,0:T(8,128)(2,1)S(1)} %get-tuple-element.48.cot.refs_0_, f32[80,80]{1,0:T(8,128)S(1)} %get-tuple-element.69.refs_1_.left), custom_call_target="tpu_custom_call" | custom-call | flops 1200000000 | bytes 3600000 | tf_op jit(solution)/shard_map/ensemble_grad_0/pallas_call | solution.py:444
  31.9 0.0 collective-permute-done.7.right
  32.0 0.3 collective-permute-start.9
  32.2 2.3 %ensemble_grad_1.1 = (bf16[16,80,2048]{2,1,0:T(8,128)(2,1)}, f32[8,128]{1,0:T(8,128)S(1)}) custom-call(bf16[6,240,240]{2,1,0:T(8,128)(2,1)S(1)} %get-tuple-element.63.factors, bf16[6,80,2048]{2,1,0:T(8,128)(2,1)S(1)} %get-tuple-element.42.cot.refs_0_, bf16[6,80,2048]{2,1,0:T(8,128)(2,1)S(1)} %get-tuple-element.64.refs_1_, ...), custom_call_target="tpu_custom_call", output_to_operand_aliasing={{0}: (4, {})} | custom-call | flops 2400000000 | bytes 7200000 | tf_op jit(solution)/shard_map/ensemble_grad_1/pallas_call | solution.py:444
  34.5 1.5 %collective-permute-done.9.refs_1_ = f32[80,80]{1,0:T(8,128)S(1)} collective-permute-done((f32[80,80]{1,0:T(8,128)S(1)}, f32[80,80]{1,0:T(8,128)S(1)}, u32[]{:S(2)}, u32[]{:S(2)}) %collective-permute-start.9) | collective-permute-done | bytes 25632 | tf_op jit(solution)/shard_map/ppermute | solution.py:354
  36.0 0.0 collective-permute-done.8.gram_core
  36.0 2.3 %transform_grad.1 = f32[16,80,80]{2,1,0:T(8,128)} custom-call(f32[80,1408]{1,0:T(8,128)S(1)} %add.3.gram, f32[80,1408]{1,0:T(8,128)S(1)} %collective-permute-done.8.gram_core, bf16[2,1280,80]{2,1,0:T(8,128)(2,1)S(1)} %get-tuple-element.60._.follow, bf16[2,2560,80]{2,1,0:T(8,128)(2,1)S(1)} %windows.1._.steps, f32[8,128]{1,0:T(8,128)S(1)} %get-tuple-element.74._, ...), custom_call_target="tpu_custom_call" | custom-call | flops 2500000000 | bytes 7500000 | tf_op jit(solution)/shard_map/transform_grad/pallas_call | solution.py:468
  (3 shorter events, 0.0 us)
Async XLA Ops:
  3.9 6.9 %collective-permute-start = (f32[80,80]{1,0:T(8,128)S(1)}, f32[80,80]{1,0:T(8,128)S(1)}, u32[]{:S(2)}, u32[]{:S(2)}) collective-permute-start(f32[80,80]{1,0:T(8,128)S(1)} %get-tuple-element.40.total), channel_id=1, source_target_pairs={{0,4},{4,0},{8,12},{12,8},{16,20},{20,16},{24,28},{28,24},{1,5},{5... | collective-permute-start | bytes 76808 | tf_op jit(solution)/shard_map/ppermute | solution.py:350
  11.0 4.9 %collective-permute-start.1 = (f32[80,80]{1,0:T(8,128)S(1)}, f32[80,80]{1,0:T(8,128)S(1)}, u32[]{:S(2)}, u32[]{:S(2)}) collective-permute-start(f32[80,80]{1,0:T(8,128)S(1)} %get-tuple-element.44._.total), channel_id=1, source_target_pairs={{0,8},{4,12},{8,0},{12,4},{16,24},{20,28},{24,16},{28,20},{1,9},{5... | collective-permute-start | bytes 76808 | tf_op jit(solution)/shard_map/ppermute | solution.py:350
  13.8 6.0 %collective-permute-start.3 = (f32[80,80]{1,0:T(8,128)S(1)}, f32[80,80]{1,0:T(8,128)S(1)}, u32[]{:S(2)}, u32[]{:S(2)}) collective-permute-start(f32[80,80]{1,0:T(8,128)S(1)} %get-tuple-element.50._.own), channel_id=1, source_target_pairs={{0,4},{4,0},{8,12},{12,8},{16,20},{20,16},{24,28},{28,24},{1,5},{5... | collective-permute-start | bytes 76808 | tf_op jit(solution)/shard_map/ppermute | solution.py:350
  14.4 15.3 %collective-permute-start.6 = (f32[80,1408]{1,0:T(8,128)S(1)}, f32[80,1408]{1,0:T(8,128)S(1)}, u32[]{:S(2)}, u32[]{:S(2)}) collective-permute-start(f32[80,1408]{1,0:T(8,128)S(1)} %get-tuple-element.68), channel_id=1, source_target_pairs={{0,2},{1,3},{2,0},{3,1},{4,6},{5,7},{6,4},{7,5},{8,10},{9,11},{10,... | collective-permute-start | bytes 1351688 | tf_op jit(solution)/shard_map/ppermute | solution.py:354
  16.2 5.3 %collective-permute-start.2 = (f32[80,80]{1,0:T(8,128)S(1)}, f32[80,80]{1,0:T(8,128)S(1)}, u32[]{:S(2)}, u32[]{:S(2)}) collective-permute-start(f32[80,80]{1,0:T(8,128)S(1)} %get-tuple-element.52._), channel_id=1, source_target_pairs={{0,16},{4,20},{8,24},{12,28},{16,0},{20,4},{24,8},{28,12},{1,17},{... | collective-permute-start | bytes 76808 | tf_op jit(solution)/shard_map/ppermute | solution.py:350
  20.0 4.1 %collective-permute-start.4 = (f32[80,80]{1,0:T(8,128)S(1)}, f32[80,80]{1,0:T(8,128)S(1)}, u32[]{:S(2)}, u32[]{:S(2)}) collective-permute-start(f32[80,80]{1,0:T(8,128)S(1)} %get-tuple-element.55._.own), channel_id=1, source_target_pairs={{0,8},{4,12},{8,0},{12,4},{16,24},{20,28},{24,16},{28,20},{1,9},{5... | collective-permute-start | bytes 76808 | tf_op jit(solution)/shard_map/ppermute | solution.py:350
  24.3 5.4 %collective-permute-start.5 = (f32[80,80]{1,0:T(8,128)S(1)}, f32[80,80]{1,0:T(8,128)S(1)}, u32[]{:S(2)}, u32[]{:S(2)}) collective-permute-start(f32[80,80]{1,0:T(8,128)S(1)} %get-tuple-element.61.refs_3_), channel_id=1, source_target_pairs={{0,16},{4,20},{8,24},{12,28},{16,0},{20,4},{24,8},{28,12},{1,17},{... | collective-permute-start | bytes 76808 | tf_op jit(solution)/shard_map/ppermute | solution.py:350
  30.0 6.1 %collective-permute-start.8 = (f32[80,1408]{1,0:T(8,128)S(1)}, f32[80,1408]{1,0:T(8,128)S(1)}, u32[]{:S(2)}, u32[]{:S(2)}) collective-permute-start(f32[80,1408]{1,0:T(8,128)S(1)} %add.3.gram), channel_id=1, source_target_pairs={{0,1},{1,0},{2,3},{3,2},{4,5},{5,4},{6,7},{7,6},{8,9},{9,8},{10,11... | collective-permute-start | bytes 1351688 | tf_op jit(solution)/shard_map/ppermute | solution.py:350
  30.1 1.9 %collective-permute-start.7 = (f32[80,80]{1,0:T(8,128)S(1)}, f32[80,80]{1,0:T(8,128)S(1)}, u32[]{:S(2)}, u32[]{:S(2)}) collective-permute-start(f32[80,80]{1,0:T(8,128)S(1)} %get-tuple-element.69.refs_1_.left), channel_id=1, source_target_pairs={{0,1},{1,0},{2,3},{3,2},{4,5},{5,4},{6,7},{7,6},{8,9},{9,8},{10,11... | collective-permute-start | bytes 76808 | tf_op jit(solution)/shard_map/ppermute | solution.py:350
  32.0 4.1 %collective-permute-start.9 = (f32[80,80]{1,0:T(8,128)S(1)}, f32[80,80]{1,0:T(8,128)S(1)}, u32[]{:S(2)}, u32[]{:S(2)}) collective-permute-start(f32[80,80]{1,0:T(8,128)S(1)} %chip_carry.1.refs_2_.refs_0_), channel_id=1, source_target_pairs={{0,2},{1,3},{2,0},{3,1},{4,6},{5,7},{6,4},{7,5},{8,10},{9,11},{10,... | collective-permute-start | bytes 76808 | tf_op jit(solution)/shard_map/ppermute | solution.py:354

commit v12 on v11

--- a/solution.py
+++ b/solution.py
@@ -111,7 +111,7 @@
         copy.wait()
 
 
-def windows_kernel(plan, kept, _, steps, runs):
+def windows_kernel(plan, kept, _, __, steps, ___, runs):
     count = plan.count
     for at in range(count - 1):
         runs[plan.rows(at + 1, at + 2)] = kept[at].T
@@ -188,9 +188,13 @@
             copy.wait()
 
 
-def late_gram_kernel(plan, ens, cot, suffixes, early, offset, _, grams, offsets):
-    grams[:, : early.shape[1]] = early[...]
-    offsets[...] = offset[...] + gram_of(plan, PIECES - 1, cot, ens, suffixes, grams)
+def late_gram_kernel(plan, ens, cot, suffixes, early, offset, _, kept, sent, offsets, whole):
+    whole[:, : early.shape[1]] = early[...]
+    offsets[...] = offset[...] + gram_of(plan, PIECES - 1, cot, ens, suffixes, whole)
+    half = plan.members // 2
+    core = lax.rem(lax.axis_index("space"), 2)
+    kept[...] = whole[pl.ds(core * half, half)]
+    sent[...] = whole[pl.ds((1 - core) * half, half)]
 
 
 def upper_half(level):
@@ -286,8 +290,11 @@
         carry = carry + ref[...]
     count, members = plan.count, plan.members
     totals = []
+    first = lax.rem(lax.axis_index("space"), 2) == 0
     for at, (start, stop) in enumerate(plan.groups):
-        tall = (gram[:, plan.lanes(at)] + gram_core[:, plan.lanes(at)]).T
+        mine, other = gram[:, plan.lanes(at)], gram_core[:, plan.lanes(at)]
+        halves = [jnp.where(first, mine, other), jnp.where(first, other, mine)]
+        tall = jnp.concatenate(halves, axis=0).T
         for i in range(stop - start):
             totals.append(tall[i * members : (i + 1) * members])
     totals[0] = totals[0] + carry.T
@@ -368,7 +375,7 @@
         [HBM] * 3, [VMEM] * 5, [pltpu.SemaphoreType.DMA] + piece_sems(0), 3.5, "transform_chain",
     )(transforms, ensembles, cotangents)
 
-    wide = shape(members, plan.width)
+    wide = shape(members // 2, plan.width)
     later = before = jnp.eye(members, dtype=F32)
     uppers, befores = [], []
 
@@ -378,7 +385,7 @@
         total, later, before, upper, *through = call(
             functools.partial(join_kernel, level),
             [square] * 4 + more, [VMEM] * 4 + [ANY] * (1 + len(more)), [VMEM] * 4 + [ANY] * len(more),
-            [], 0.3, f"join_{level}", aliases={5 + at: 4 + at for at in range(len(more))},
+            [], 3, f"join_{level}", aliases={5 + at: 4 + at for at in range(len(more))},
         )(total, other, later, before, after, *through)
         uppers.append(upper)
         return total, later, before, *through
@@ -396,38 +403,42 @@
     total, later, before = join(0, total, other, later, before, offset)
 
     other = exchange(total, "tm", blocks, 2)
-    gram, own = call(
+    gram, gram_sent, own = call(
         functools.partial(late_gram_kernel, plan),
-        [wide, square], [VMEM] * 5 + [ANY], [VMEM] * 2, [], 1.2, "late_gram",
+        [wide, wide, square], [VMEM] * 5 + [ANY], [VMEM] * 3,
+        [pltpu.VMEM((members, plan.width), F32)], 1.2, "late_gram",
     )(*parts[-1], suffixes, early, offset, total)
     other_own = exchange(own, "tm", blocks, 1)
-    grams = around(gram)
+    gram_core = exchange(gram_sent, "space", lanes, 1)
     for level in range(1, levels - 1):
         total, later, before = join(level, total, other, later, before, own)
         other = exchange(total, "tm", blocks, 2 << level)
     befores.append(before)
-    steps = call(
-        functools.partial(windows_kernel, plan),
-        shape(2, count_steps(count) * members, members, kind=BF16), [VMEM, ANY], VMEM,
-        [pltpu.VMEM((count * members, members), F32)], 1.0, "windows",
-    )(kept, total)
 
     def pass_on(level, carry, after, *through):
         more = [shape(*value.shape) for value in through]
         return call(
             functools.partial(pass_kernel, level),
             [square] * 2 + more, [VMEM] * 5 + [ANY] * (1 + len(more)), [VMEM] * 2 + [ANY] * len(more),
-            [], 0.3, f"pass_{level}", aliases={6 + at: 2 + at for at in range(len(more))},
+            [], 3, f"pass_{level}", aliases={6 + at: 2 + at for at in range(len(more))},
         )(own, other_own, carry, uppers[level], befores[level], after, *through)
 
     carry = jnp.zeros((members, members), F32)
     for level in range(levels - 2):
-        own, carry = pass_on(level, carry, steps)
+        own, carry = pass_on(level, carry, total)
         other_own = exchange(own, "tm", blocks, 2 << level)
+    steps, gram_core = call(
+        functools.partial(windows_kernel, plan),
+        [shape(2, count_steps(count) * members, members, kind=BF16), wide],
+        [VMEM, ANY, ANY], [VMEM, ANY], [pltpu.VMEM((count * members, members), F32)], 1.0, "windows",
+        aliases={2: 1},
+    )(kept, own, gram_core)
+    gram = gram + gram_core
+    grams = around(gram)
     entering = call(
         functools.partial(enter_kernel, levels - 1),
         square, [VMEM] * 2 + [ANY], VMEM, [], 0.2, "entering",
-    )(later, other, own)
+    )(later, other, steps)
     size = plan.stack * members
     ens_factors, cot_factors, follow = call(
         functools.partial(carry_kernel, plan),

time: 38.5 us -> 37.7 us (0.979)
  waiting for transfers between devices: 5.7 us -> 3.2 us
  starting transfers between devices: 11.8 us -> 13.5 us
    ppermute x8 -> x9, waiting for transfers between devices: 4.19 us -> 1.8 us  [exchange(): return lax.ppermute(value, axis, [(at, at ^ bit) for at in range(size)])]
    ppermute x8 -> x9, starting transfers between devices: 10 us -> 11.5 us  [exchange(): return lax.ppermute(value, axis, [(at, at ^ bit) for at in range(size)])]
  transfers between devices with their start and end apart: 10 -> 11, of which waited for: 4 -> 3; matrix products, arithmetic and copies ran while one was open for 0% -> 0% of each run, Pallas kernels for 37% -> 37%
where the time goes in v12:
time: 37.7 us; the launch traced here: 37.6 us
  Pallas kernels  20 us (53%)
  starting transfers between devices  13.5 us (36%)
  waiting for transfers between devices  3.2 us (8%)
  between operations  0.8 us (2%)
    ppermute x9, starting transfers between devices, exchange(): return lax.ppermute(value, axis, [(at, at ^ bit) for at in range(size)])  11.5 us
    pallas_call x3, Pallas kernels, apply(): call(functools.partial(apply_kernel, plan, pieces), [shape(count, members...  6.36 us
    pallas_call x1, Pallas kernels, shards(): call(functools.partial(early_gram_kernel, plan), [shape(members, early_wi...  3.85 us
    pallas_call x1, Pallas kernels, shards(): call(functools.partial(chain_kernel, plan), [shape(count * members, membe...  3.22 us
    pallas_call x1, Pallas kernels, shards(): call(functools.partial(final_kernel, plan, scale), shape(count, members,...  2.29 us
    ppermute x2, starting transfers between devices, around(): lax.ppermute(value, 'space', [(at, (at + 2 * d) % lanes) for at in range(...  1.98 us
    ppermute x9, waiting for transfers between devices, exchange(): return lax.ppermute(value, axis, [(at, at ^ bit) for at in range(size)])  1.8 us
    ppermute x2, waiting for transfers between devices, around(): lax.ppermute(value, 'space', [(at, (at + 2 * d) % lanes) for at in range(...  1.4 us
  transfers between devices with their start and end apart: 11, of which 3 were waited for; matrix products, arithmetic and copies ran while one was open for 0% of the time, Pallas kernels for 37%

profile of v12, /device:TPU:0, one launch (start us, length us, event | category | flops | bytes accessed | tf_op | source)
XLA Modules:
  0.0 37.6 jit_solution(1836486209138770729)
XLA Ops:
  0.6 3.2 %transform_chain.1 = (f32[1280,80]{1,0:T(8,128)S(1)}, f32[80,80]{1,0:T(8,128)S(1)}, f32[16,80,80]{2,1,0:T(8,128)S(1)}, bf16[6,80,2048]{2,1,0:T(8,128)(2,1)S(1)}, bf16[6,80,2048]{2,1,0:T(8,128)(2,1)S(1)}) custom-call(f32[16,80,80]{2,1,0:T(8,128)} %transforms.1, bf16[16,80,2048]{2,1,0:T(8,128)(2,1)} %ensembles.3, bf16[16,80,2048]{2,1,0:T(8,128)(2,1)} %cotangents.3), custom_call_target="tpu_custom_call" | custom-call | flops 3500000000 | bytes 10500000 | tf_op jit(solution)/shard_map/transform_chain/pallas_call | solution.py:372
  3.9 3.0 %collective-permute-start = (f32[80,80]{1,0:T(8,128)S(1)}, f32[80,80]{1,0:T(8,128)S(1)}, u32[]{:S(2)}, u32[]{:S(2)}) collective-permute-start(f32[80,80]{1,0:T(8,128)S(1)} %get-tuple-element.43.total), channel_id=1, source_target_pairs={{0,4},{4,0},{8,12},{12,8},{16,20},{20,16},{24,28},{28,24},{1,5},{5... | collective-permute-start | bytes 76808 | tf_op jit(solution)/shard_map/ppermute | solution.py:357
  6.9 3.8 %early_gram.1 = (f32[80,1024]{1,0:T(8,128)S(1)}, f32[80,80]{1,0:T(8,128)S(1)}, bf16[6,80,2048]{2,1,0:T(8,128)(2,1)S(1)}, bf16[6,80,2048]{2,1,0:T(8,128)(2,1)S(1)...) custom-call(bf16[16,80,2048]{2,1,0:T(8,128)(2,1)} %ensembles.3, bf16[16,80,2048]{2,1,0:T(8,128)(2,1)} %cotangents.3, ...), custom_call_target="tpu_custom_call" | custom-call | flops 3000000000 | bytes 9000000 | tf_op jit(solution)/shard_map/early_gram/pallas_call | solution.py:395
  10.7 0.0 collective-permute-done.other
  10.7 0.3 join_0.1
  11.0 1.6 %collective-permute-start.1 = (f32[80,80]{1,0:T(8,128)S(1)}, f32[80,80]{1,0:T(8,128)S(1)}, u32[]{:S(2)}, u32[]{:S(2)}) collective-permute-start(f32[80,80]{1,0:T(8,128)S(1)} %get-tuple-element.47._.total), channel_id=1, source_target_pairs={{0,8},{4,12},{8,0},{12,4},{16,24},{20,28},{24,16},{28,20},{1,9},{5... | collective-permute-start | bytes 76808 | tf_op jit(solution)/shard_map/ppermute | solution.py:357
  12.7 1.2 %late_gram.1 = (f32[40,1408]{1,0:T(8,128)S(1)}, f32[40,1408]{1,0:T(8,128)S(1)}, f32[80,80]{1,0:T(8,128)S(1)}) custom-call(bf16[4,80,2048]{2,1,0:T(8,128)(2,1)S(1)} %get-tuple-element.50.ens.refs_2_, bf16[4,80,2048]{2,1,0:T(8,128)(2,1)S(1)} %get-tuple-element.51.cot.refs_0_, f32[1280,80]{1,0:T(8,128)S(1)} %get-tuple-element.42.suffixes, ...), custom_call_target="tpu_custom_call" | custom-call | flops 1200000000 | bytes 3600000 | tf_op jit(solution)/shard_map/late_gram/pallas_call | solution.py:406
  13.8 0.6 %collective-permute-start.3 = (f32[80,80]{1,0:T(8,128)S(1)}, f32[80,80]{1,0:T(8,128)S(1)}, u32[]{:S(2)}, u32[]{:S(2)}) collective-permute-start(f32[80,80]{1,0:T(8,128)S(1)} %get-tuple-element.53._.own), channel_id=1, source_target_pairs={{0,4},{4,0},{8,12},{12,8},{16,20},{20,16},{24,28},{28,24},{1,5},{5... | collective-permute-start | bytes 76808 | tf_op jit(solution)/shard_map/ppermute | solution.py:357
  14.4 0.0 collective-permute-start.4
  14.4 0.6 %collective-permute-done.1.other = f32[80,80]{1,0:T(8,128)S(1)} collective-permute-done((f32[80,80]{1,0:T(8,128)S(1)}, f32[80,80]{1,0:T(8,128)S(1)}, u32[]{:S(2)}, u32[]{:S(2)}) %collective-permute-start.1) | collective-permute-done | bytes 25632 | tf_op jit(solution)/shard_map/ppermute | solution.py:357
  15.1 0.3 join_1.1
  15.3 2.7 %collective-permute-start.2 = (f32[80,80]{1,0:T(8,128)S(1)}, f32[80,80]{1,0:T(8,128)S(1)}, u32[]{:S(2)}, u32[]{:S(2)}) collective-permute-start(f32[80,80]{1,0:T(8,128)S(1)} %get-tuple-element.55._), channel_id=1, source_target_pairs={{0,16},{4,20},{8,24},{12,28},{16,0},{20,4},{24,8},{28,12},{1,17},{... | collective-permute-start | bytes 76808 | tf_op jit(solution)/shard_map/ppermute | solution.py:357
  18.0 0.0 collective-permute-done.3.other
  18.0 0.2 pass_0.1
  18.2 1.6 %collective-permute-start.5 = (f32[80,80]{1,0:T(8,128)S(1)}, f32[80,80]{1,0:T(8,128)S(1)}, u32[]{:S(2)}, u32[]{:S(2)}) collective-permute-start(f32[80,80]{1,0:T(8,128)S(1)} %get-tuple-element.58._.own), channel_id=1, source_target_pairs={{0,8},{4,12},{8,0},{12,4},{16,24},{20,28},{24,16},{28,20},{1,9},{5... | collective-permute-start | bytes 76808 | tf_op jit(solution)/shard_map/ppermute | solution.py:357
  19.9 0.0 collective-permute-done.4.__
  19.9 0.9 %windows.1 = (bf16[2,2560,80]{2,1,0:T(8,128)(2,1)S(1)}, f32[40,1408]{1,0:T(8,128)S(1)}) custom-call(f32[16,80,80]{2,1,0:T(8,128)S(1)} %get-tuple-element.56.kept, f32[80,80]{1,0:T(8,128)S(1)} %get-tuple-element.58._.own, f32[40,1408]{1,0:T(8,128)S(1)} %collective-permute-done.4.__), custom_call_target="tpu_custom_call", output_to_operand_aliasing={{1}: (2, {})} | custom-call | flops 1000000000 | bytes 3000000 | tf_op jit(solution)/shard_map/windows/pallas_call | solution.py:430
  20.8 1.6 %collective-permute-start.7 = (f32[40,1408]{1,0:T(8,128)S(1)}, f32[40,1408]{1,0:T(8,128)S(1)}, u32[]{:S(2)}, u32[]{:S(2)}) collective-permute-start(f32[40,1408]{1,0:T(8,128)S(1)} %add.6), channel_id=1, source_target_pairs={{0,2},{1,3},{2,0},{3,1},{4,6},{5,7},{6,4},{7,5},{8,10},{9,11},{10,... | collective-permute-start | bytes 675848 | tf_op jit(solution)/shard_map/ppermute | solution.py:361
  22.4 0.0 collective-permute-done.2.other
  22.4 0.2 entering.1.later
  22.6 0.9 %carries.1 = (bf16[6,240,240]{2,1,0:T(8,128)(2,1)S(1)}, bf16[6,240,240]{2,1,0:T(8,128)(2,1)S(1)}, bf16[2,1280,80]{2,1,0:T(8,128)(2,1)S(1)}) custom-call(f32[1280,80]{1,0:T(8,128)S(1)} %get-tuple-element.42.suffixes, f32[80,80]{1,0:T(8,128)S(1)} %entering.1.later), custom_call_target="tpu_custom_call" | custom-call | flops 900000000 | bytes 2700000 | tf_op jit(solution)/shard_map/carries/pallas_call | solution.py:443
  23.5 0.0 collective-permute-done.5.other
  23.5 0.2 pass_1.1
  23.7 1.4 %collective-permute-start.6 = (f32[80,80]{1,0:T(8,128)S(1)}, f32[80,80]{1,0:T(8,128)S(1)}, u32[]{:S(2)}, u32[]{:S(2)}) collective-permute-start(f32[80,80]{1,0:T(8,128)S(1)} %get-tuple-element.66.refs_3_), channel_id=1, source_target_pairs={{0,16},{4,20},{8,24},{12,28},{16,0},{20,4},{24,8},{28,12},{1,17},{... | collective-permute-start | bytes 76808 | tf_op jit(solution)/shard_map/ppermute | solution.py:357
  25.1 2.7 %smoothed.1 = (bf16[16,80,2048]{2,1,0:T(8,128)(2,1)}, f32[8,128]{1,0:T(8,128)S(1)}) custom-call(bf16[6,240,240]{2,1,0:T(8,128)(2,1)S(1)} %get-tuple-element.61.factors, bf16[6,80,2048]{2,1,0:T(8,128)(2,1)S(1)} %get-tuple-element.44.ens.refs_0_, bf16[6,80,2048]{2,1,0:T(8,128)(2,1)S(1)} %get-tuple-element.62.refs_1_, ...), custom_call_target="tpu_custom_call" | custom-call | flops 3000000000 | bytes 9000000 | tf_op jit(solution)/shard_map/smoothed/pallas_call | solution.py:455
  27.9 1.1 %collective-permute-done.6.other = f32[80,80]{1,0:T(8,128)S(1)} collective-permute-done((f32[80,80]{1,0:T(8,128)S(1)}, f32[80,80]{1,0:T(8,128)S(1)}, u32[]{:S(2)}, u32[]{:S(2)}) %collective-permute-start.6) | collective-permute-done | bytes 25632 | tf_op jit(solution)/shard_map/ppermute | solution.py:357
  29.0 0.0 collective-permute-done.7.__
  29.0 0.2 pass_last.1
  29.2 0.1 collective-permute-start.8
  29.3 0.5 %collective-permute-start.9 = (f32[40,1408]{1,0:T(8,128)S(1)}, f32[40,1408]{1,0:T(8,128)S(1)}, u32[]{:S(2)}, u32[]{:S(2)}) collective-permute-start(f32[40,1408]{1,0:T(8,128)S(1)} %add.7.gram), channel_id=1, source_target_pairs={{0,1},{1,0},{2,3},{3,2},{4,5},{5,4},{6,7},{7,6},{8,9},{9,8},{10,11... | collective-permute-start | bytes 675848 | tf_op jit(solution)/shard_map/ppermute | solution.py:357
  29.8 1.4 %ensemble_grad_0.1 = (bf16[16,80,2048]{2,1,0:T(8,128)(2,1)}, f32[8,128]{1,0:T(8,128)S(1)}) custom-call(bf16[6,240,240]{2,1,0:T(8,128)(2,1)S(1)} %get-tuple-element.68.factors, bf16[4,80,2048]{2,1,0:T(8,128)(2,1)S(1)} %get-tuple-element.51.cot.refs_0_, f32[80,80]{1,0:T(8,128)S(1)} %get-tuple-element.75.refs_1_.left), custom_call_target="tpu_custom_call" | custom-call | flops 1200000000 | bytes 3600000 | tf_op jit(solution)/shard_map/ensemble_grad_0/pallas_call | solution.py:455
  31.2 0.0 collective-permute-done.8.right
  31.2 0.4 %collective-permute-start.10 = (f32[80,80]{1,0:T(8,128)S(1)}, f32[80,80]{1,0:T(8,128)S(1)}, u32[]{:S(2)}, u32[]{:S(2)}) collective-permute-start(f32[80,80]{1,0:T(8,128)S(1)} %chip_carry.1.refs_2_.refs_0_), channel_id=1, source_target_pairs={{0,2},{1,3},{2,0},{3,1},{4,6},{5,7},{6,4},{7,5},{8,10},{9,11},{10,... | collective-permute-start | bytes 76808 | tf_op jit(solution)/shard_map/ppermute | solution.py:361
  31.6 2.3 %ensemble_grad_1.1 = (bf16[16,80,2048]{2,1,0:T(8,128)(2,1)}, f32[8,128]{1,0:T(8,128)S(1)}) custom-call(bf16[6,240,240]{2,1,0:T(8,128)(2,1)S(1)} %get-tuple-element.68.factors, bf16[6,80,2048]{2,1,0:T(8,128)(2,1)S(1)} %get-tuple-element.45.cot.refs_0_, bf16[6,80,2048]{2,1,0:T(8,128)(2,1)S(1)} %get-tuple-element.69.refs_1_, ...), custom_call_target="tpu_custom_call", output_to_operand_aliasing={{0}: (4, {})} | custom-call | flops 2400000000 | bytes 7200000 | tf_op jit(solution)/shard_map/ensemble_grad_1/pallas_call | solution.py:455
  33.9 1.4 %collective-permute-done.10.refs_1_ = f32[80,80]{1,0:T(8,128)S(1)} collective-permute-done((f32[80,80]{1,0:T(8,128)S(1)}, f32[80,80]{1,0:T(8,128)S(1)}, u32[]{:S(2)}, u32[]{:S(2)}) %collective-permute-start.10) | collective-permute-done | bytes 25632 | tf_op jit(solution)/shard_map/ppermute | solution.py:361
  35.3 0.0 collective-permute-done.9.gram_core
  35.3 2.3 %transform_grad.1 = f32[16,80,80]{2,1,0:T(8,128)} custom-call(f32[40,1408]{1,0:T(8,128)S(1)} %add.7.gram, f32[40,1408]{1,0:T(8,128)S(1)} %collective-permute-done.9.gram_core, bf16[2,1280,80]{2,1,0:T(8,128)(2,1)S(1)} %get-tuple-element.65._.follow, bf16[2,2560,80]{2,1,0:T(8,128)(2,1)S(1)} %get-tuple-element.60._.steps, f32[8,128]{1,0:T(8,128)S(1)} %get-tuple-element.80._, ...), custom_call_target="tpu_custom_call" | custom-call | flops 2500000000 | bytes 7500000 | tf_op jit(solution)/shard_map/transform_grad/pallas_call | solution.py:479
  (5 shorter events, 0.1 us)
Async XLA Ops:
  3.9 6.9 %collective-permute-start = (f32[80,80]{1,0:T(8,128)S(1)}, f32[80,80]{1,0:T(8,128)S(1)}, u32[]{:S(2)}, u32[]{:S(2)}) collective-permute-start(f32[80,80]{1,0:T(8,128)S(1)} %get-tuple-element.43.total), channel_id=1, source_target_pairs={{0,4},{4,0},{8,12},{12,8},{16,20},{20,16},{24,28},{28,24},{1,5},{5... | collective-permute-start | bytes 76808 | tf_op jit(solution)/shard_map/ppermute | solution.py:357
  11.0 4.1 %collective-permute-start.1 = (f32[80,80]{1,0:T(8,128)S(1)}, f32[80,80]{1,0:T(8,128)S(1)}, u32[]{:S(2)}, u32[]{:S(2)}) collective-permute-start(f32[80,80]{1,0:T(8,128)S(1)} %get-tuple-element.47._.total), channel_id=1, source_target_pairs={{0,8},{4,12},{8,0},{12,4},{16,24},{20,28},{24,16},{28,20},{1,9},{5... | collective-permute-start | bytes 76808 | tf_op jit(solution)/shard_map/ppermute | solution.py:357
  13.8 4.2 %collective-permute-start.3 = (f32[80,80]{1,0:T(8,128)S(1)}, f32[80,80]{1,0:T(8,128)S(1)}, u32[]{:S(2)}, u32[]{:S(2)}) collective-permute-start(f32[80,80]{1,0:T(8,128)S(1)} %get-tuple-element.53._.own), channel_id=1, source_target_pairs={{0,4},{4,0},{8,12},{12,8},{16,20},{20,16},{24,28},{28,24},{1,5},{5... | collective-permute-start | bytes 76808 | tf_op jit(solution)/shard_map/ppermute | solution.py:357
  14.4 5.4 %collective-permute-start.4 = (f32[40,1408]{1,0:T(8,128)S(1)}, f32[40,1408]{1,0:T(8,128)S(1)}, u32[]{:S(2)}, u32[]{:S(2)}) collective-permute-start(f32[40,1408]{1,0:T(8,128)S(1)} %get-tuple-element.59), channel_id=1, source_target_pairs={{0,1},{1,0},{2,3},{3,2},{4,5},{5,4},{6,7},{7,6},{8,9},{9,8},{10,11... | collective-permute-start | bytes 675848 | tf_op jit(solution)/shard_map/ppermute | solution.py:357
  15.3 7.1 %collective-permute-start.2 = (f32[80,80]{1,0:T(8,128)S(1)}, f32[80,80]{1,0:T(8,128)S(1)}, u32[]{:S(2)}, u32[]{:S(2)}) collective-permute-start(f32[80,80]{1,0:T(8,128)S(1)} %get-tuple-element.55._), channel_id=1, source_target_pairs={{0,16},{4,20},{8,24},{12,28},{16,0},{20,4},{24,8},{28,12},{1,17},{... | collective-permute-start | bytes 76808 | tf_op jit(solution)/shard_map/ppermute | solution.py:357
  18.2 5.3 %collective-permute-start.5 = (f32[80,80]{1,0:T(8,128)S(1)}, f32[80,80]{1,0:T(8,128)S(1)}, u32[]{:S(2)}, u32[]{:S(2)}) collective-permute-start(f32[80,80]{1,0:T(8,128)S(1)} %get-tuple-element.58._.own), channel_id=1, source_target_pairs={{0,8},{4,12},{8,0},{12,4},{16,24},{20,28},{24,16},{28,20},{1,9},{5... | collective-permute-start | bytes 76808 | tf_op jit(solution)/shard_map/ppermute | solution.py:357
  20.8 8.2 %collective-permute-start.7 = (f32[40,1408]{1,0:T(8,128)S(1)}, f32[40,1408]{1,0:T(8,128)S(1)}, u32[]{:S(2)}, u32[]{:S(2)}) collective-permute-start(f32[40,1408]{1,0:T(8,128)S(1)} %add.6), channel_id=1, source_target_pairs={{0,2},{1,3},{2,0},{3,1},{4,6},{5,7},{6,4},{7,5},{8,10},{9,11},{10,... | collective-permute-start | bytes 675848 | tf_op jit(solution)/shard_map/ppermute | solution.py:361
  23.7 5.3 %collective-permute-start.6 = (f32[80,80]{1,0:T(8,128)S(1)}, f32[80,80]{1,0:T(8,128)S(1)}, u32[]{:S(2)}, u32[]{:S(2)}) collective-permute-start(f32[80,80]{1,0:T(8,128)S(1)} %get-tuple-element.66.refs_3_), channel_id=1, source_target_pairs={{0,16},{4,20},{8,24},{12,28},{16,0},{20,4},{24,8},{28,12},{1,17},{... | collective-permute-start | bytes 76808 | tf_op jit(solution)/shard_map/ppermute | solution.py:357
  29.2 2.0 %collective-permute-start.8 = (f32[80,80]{1,0:T(8,128)S(1)}, f32[80,80]{1,0:T(8,128)S(1)}, u32[]{:S(2)}, u32[]{:S(2)}) collective-permute-start(f32[80,80]{1,0:T(8,128)S(1)} %get-tuple-element.75.refs_1_.left), channel_id=1, source_target_pairs={{0,1},{1,0},{2,3},{3,2},{4,5},{5,4},{6,7},{7,6},{8,9},{9,8},{10,11... | collective-permute-start | bytes 76808 | tf_op jit(solution)/shard_map/ppermute | solution.py:357
  29.3 6.0 %collective-permute-start.9 = (f32[40,1408]{1,0:T(8,128)S(1)}, f32[40,1408]{1,0:T(8,128)S(1)}, u32[]{:S(2)}, u32[]{:S(2)}) collective-permute-start(f32[40,1408]{1,0:T(8,128)S(1)} %add.7.gram), channel_id=1, source_target_pairs={{0,1},{1,0},{2,3},{3,2},{4,5},{5,4},{6,7},{7,6},{8,9},{9,8},{10,11... | collective-permute-start | bytes 675848 | tf_op jit(solution)/shard_map/ppermute | solution.py:357
  31.2 4.1 %collective-permute-start.10 = (f32[80,80]{1,0:T(8,128)S(1)}, f32[80,80]{1,0:T(8,128)S(1)}, u32[]{:S(2)}, u32[]{:S(2)}) collective-permute-start(f32[80,80]{1,0:T(8,128)S(1)} %chip_carry.1.refs_2_.refs_0_), channel_id=1, source_target_pairs={{0,2},{1,3},{2,0},{3,1},{4,6},{5,7},{6,4},{7,5},{8,10},{9,11},{10,... | collective-permute-start | bytes 76808 | tf_op jit(solution)/shard_map/ppermute | solution.py:361

commit v13 on v12

--- a/solution.py
+++ b/solution.py
@@ -111,7 +111,7 @@
         copy.wait()
 
 
-def windows_kernel(plan, kept, _, __, steps, ___, runs):
+def windows_kernel(plan, kept, _, steps, runs):
     count = plan.count
     for at in range(count - 1):
         runs[plan.rows(at + 1, at + 2)] = kept[at].T
@@ -235,7 +235,7 @@
     entering[...] = jnp.where(upper_half(level), later[...], joined)
 
 
-def carry_kernel(plan, suffixes, later, ens_factors, cot_factors, follow):
+def carry_kernel(plan, suffixes, later, _, ens_factors, cot_factors, follow):
     count, members = plan.count, plan.members
     entering = later[...]
     mask = on_blocks(members, plan.stack * members)
@@ -254,14 +254,13 @@
         follow[side, plan.rows(count - 1, count)] = value
 
 
-def apply_kernel(plan, pieces, factors, *refs):
+def apply_kernel(plan, factors, *refs):
     out, marker, out_buf, out_sem = refs[-4:]
     members = plan.members
     marker[...] = jnp.zeros_like(marker)
-    base = plan.pieces[pieces[0]][0]
     chunk = out_buf.shape[2] // 2
     writes = []
-    for values, piece in zip(refs, pieces):
+    for piece, values in enumerate(refs[:PIECES]):
         first = plan.pieces[piece][0]
         for at, (start, stop) in enumerate(plan.piece_groups[piece]):
             size = (stop - start) * members
@@ -269,11 +268,11 @@
                 columns = slice(side * chunk, (side + 1) * chunk)
                 stacked = values[start - first : stop - first, :, columns].reshape(size, chunk)
                 result = mul(factors[plan.first_group[piece] + at, :size, :size], stacked)
-                out_buf[start - base : stop - base, :, columns] = result.astype(BF16).reshape(
+                out_buf[start:stop, :, columns] = result.astype(BF16).reshape(
                     stop - start, members, chunk
                 )
                 copy = pltpu.make_async_copy(
-                    out_buf.at[start - base : stop - base, :, columns],
+                    out_buf.at[start:stop, :, columns],
                     out.at[start:stop, :, columns],
                     out_sem.at[len(writes)],
                 )
@@ -427,41 +426,32 @@
     for level in range(levels - 2):
         own, carry = pass_on(level, carry, total)
         other_own = exchange(own, "tm", blocks, 2 << level)
-    steps, gram_core = call(
-        functools.partial(windows_kernel, plan),
-        [shape(2, count_steps(count) * members, members, kind=BF16), wide],
-        [VMEM, ANY, ANY], [VMEM, ANY], [pltpu.VMEM((count * members, members), F32)], 1.0, "windows",
-        aliases={2: 1},
-    )(kept, own, gram_core)
-    gram = gram + gram_core
+    gram = call(sum_kernel, wide, [VMEM] * 2 + [ANY], VMEM, [], 0.1, "chip_gram")(gram, gram_core, own)
     grams = around(gram)
     entering = call(
         functools.partial(enter_kernel, levels - 1),
         square, [VMEM] * 2 + [ANY], VMEM, [], 0.2, "entering",
-    )(later, other, steps)
+    )(later, other, gram)
+    own, carry = pass_on(levels - 2, carry, entering)
+    other_own = exchange(own, "tm", blocks, blocks // 2)
     size = plan.stack * members
     ens_factors, cot_factors, follow = call(
         functools.partial(carry_kernel, plan),
         [shape(len(plan.groups), size, size, kind=BF16)] * 2
         + [shape(2, count * members, members, kind=BF16)],
-        [VMEM] * 2, [VMEM] * 3, [], 0.9, "carries",
-    )(suffixes, entering)
-    own, carry = pass_on(levels - 2, carry, follow)
-    other_own = exchange(own, "tm", blocks, blocks // 2)
-
-    def apply(factors, which, pieces, out, after, name):
-        first, last = plan.pieces[pieces[0]][0], plan.pieces[pieces[-1]][1]
-        number = 2 * sum(len(plan.piece_groups[piece]) for piece in pieces)
+        [VMEM] * 2 + [ANY], [VMEM] * 3, [], 0.9, "carries",
+    )(suffixes, entering, own)
+    def apply(factors, which, after, name):
         return call(
-            functools.partial(apply_kernel, plan, pieces),
+            functools.partial(apply_kernel, plan),
             [shape(count, members, cells, kind=BF16), shape(8, 128)],
-            [VMEM] * (1 + len(pieces)) + [ANY] + [HBM] * len(out), [HBM, VMEM],
-            [pltpu.VMEM((last - first, members, cells), BF16), pltpu.SemaphoreType.DMA((number,))],
-            0.15 * (last - first) + 0.6, name, aliases={2 + len(pieces): 0} if out else None,
-        )(factors, *(parts[piece][which] for piece in pieces), after, *out)
-
-    front, rear = tuple(range(PIECES - 1)), (PIECES - 1,)
-    smoothed, done = apply(ens_factors, 0, front + rear, (), own, "smoothed")
+            [VMEM] * (1 + PIECES) + [ANY], [HBM, VMEM],
+            [pltpu.VMEM((count, members, cells), BF16),
+             pltpu.SemaphoreType.DMA((2 * len(plan.groups),))],
+            2.7, name,
+        )(factors, *(part[which] for part in parts), after)
+
+    smoothed, done = apply(ens_factors, 0, follow, "smoothed")
     carry, grams[0] = call(
         functools.partial(last_pass_kernel, levels - 1),
         [square, wide], [VMEM] * 3 + [ANY] * 2, [VMEM, ANY], [], 0.2, "pass_last", aliases={4: 1},
@@ -470,12 +460,16 @@
     for part in grams:
         gram = gram + part
     gram_core = exchange(gram, "space", lanes, 1)
-    ensemble_grad, done = apply(cot_factors, 1, rear, (), carry, "ensemble_grad_0")
+    steps = call(
+        functools.partial(windows_kernel, plan),
+        shape(2, count_steps(count) * members, members, kind=BF16), [VMEM, ANY], VMEM,
+        [pltpu.VMEM((count * members, members), F32)], 1.0, "windows",
+    )(kept, carry)
     carry = call(
         sum_kernel, square, [VMEM] * 2 + [ANY], VMEM, [], 0.1, "chip_carry",
-    )(carry, carry_core, done)
+    )(carry, carry_core, steps)
     carries = [carry] + around(carry)
-    ensemble_grad, done = apply(cot_factors, 1, front, (ensemble_grad,), carry, "ensemble_grad_1")
+    ensemble_grad, done = apply(cot_factors, 1, carry, "ensemble_grad")
     transform_grad = call(
         functools.partial(final_kernel, plan, scale),
         shape(count, members, members),

time: 37.7 us -> 37.3 us (0.989)
  starting transfers between devices: 13.5 us -> 15.8 us
  waiting for transfers between devices: 3.2 us -> 1.37 us
  Pallas kernels: 20 us -> 19.1 us
    ppermute x2, waiting for transfers between devices: 1.4 us -> 0.01 us  [around(): lax.ppermute(value, 'space', [(at, (at + 2 * d) % lanes) for at in range(...]
    ppermute x2, starting transfers between devices: 1.98 us -> 3.17 us  [around(): lax.ppermute(value, 'space', [(at, (at + 2 * d) % lanes) for at in range(...]
    ppermute x9, starting transfers between devices: 11.5 us -> 12.7 us  [exchange(): return lax.ppermute(value, axis, [(at, at ^ bit) for at in range(size)])]
    pallas_call x4, Pallas kernels: 7.3 us -> 6.4 us  [the longest x2 5.43 us: apply(): call(functools.partial(apply_kernel, plan), [shape(count, members, cells,...]
    ppermute x9, waiting for transfers between devices: 1.8 us -> 1.37 us  [exchange(): return lax.ppermute(value, axis, [(at, at ^ bit) for at in range(size)])]
  transfers between devices with their start and end apart: 11 -> 11, of which waited for: 3 -> 3; matrix products, arithmetic and copies ran while one was open for 0% -> 0% of each run, Pallas kernels for 37% -> 35%
where the time goes in v13:
time: 37.3 us; the launch traced here: 37.1 us
  Pallas kernels  19.1 us (51%)
  starting transfers between devices  15.8 us (42%)
  waiting for transfers between devices  1.37 us (4%)
  between operations  0.79 us (2%)
    ppermute x9, starting transfers between devices, exchange(): return lax.ppermute(value, axis, [(at, at ^ bit) for at in range(size)])  12.7 us
    pallas_call x2, Pallas kernels, apply(): call(functools.partial(apply_kernel, plan), [shape(count, members, cells,...  5.43 us
    pallas_call x1, Pallas kernels, shards(): call(functools.partial(early_gram_kernel, plan), [shape(members, early_wi...  3.85 us
    pallas_call x1, Pallas kernels, shards(): call(functools.partial(chain_kernel, plan), [shape(count * members, membe...  3.22 us
    ppermute x2, starting transfers between devices, around(): lax.ppermute(value, 'space', [(at, (at + 2 * d) % lanes) for at in range(...  3.17 us
    pallas_call x1, Pallas kernels, shards(): call(functools.partial(final_kernel, plan, scale), shape(count, members,...  2.29 us
    ppermute x9, waiting for transfers between devices, exchange(): return lax.ppermute(value, axis, [(at, at ^ bit) for at in range(size)])  1.37 us
    pallas_call x1, Pallas kernels, shards(): call(functools.partial(late_gram_kernel, plan), [wide, wide, square], [VM...  1.17 us
  transfers between devices with their start and end apart: 11, of which 3 were waited for; matrix products, arithmetic and copies ran while one was open for 0% of the time, Pallas kernels for 35%

profile of v13, /device:TPU:0, one launch (start us, length us, event | category | flops | bytes accessed | tf_op | source)
XLA Modules:
  0.0 37.1 jit_solution(18286264190601599036)
XLA Ops:
  0.6 3.2 %transform_chain.1 = (f32[1280,80]{1,0:T(8,128)S(1)}, f32[80,80]{1,0:T(8,128)S(1)}, f32[16,80,80]{2,1,0:T(8,128)S(1)}, bf16[6,80,2048]{2,1,0:T(8,128)(2,1)S(1)}, bf16[6,80,2048]{2,1,0:T(8,128)(2,1)S(1)}) custom-call(f32[16,80,80]{2,1,0:T(8,128)} %transforms.1, bf16[16,80,2048]{2,1,0:T(8,128)(2,1)} %ensembles.3, bf16[16,80,2048]{2,1,0:T(8,128)(2,1)} %cotangents.3), custom_call_target="tpu_custom_call" | custom-call | flops 3500000000 | bytes 10500000 | tf_op jit(solution)/shard_map/transform_chain/pallas_call | solution.py:371
  3.9 3.0 %collective-permute-start = (f32[80,80]{1,0:T(8,128)S(1)}, f32[80,80]{1,0:T(8,128)S(1)}, u32[]{:S(2)}, u32[]{:S(2)}) collective-permute-start(f32[80,80]{1,0:T(8,128)S(1)} %get-tuple-element.39.total), channel_id=1, source_target_pairs={{0,4},{4,0},{8,12},{12,8},{16,20},{20,16},{24,28},{28,24},{1,5},{5... | collective-permute-start | bytes 76808 | tf_op jit(solution)/shard_map/ppermute | solution.py:356
  6.9 3.8 %early_gram.1 = (f32[80,1024]{1,0:T(8,128)S(1)}, f32[80,80]{1,0:T(8,128)S(1)}, bf16[6,80,2048]{2,1,0:T(8,128)(2,1)S(1)}, bf16[6,80,2048]{2,1,0:T(8,128)(2,1)S(1)...) custom-call(bf16[16,80,2048]{2,1,0:T(8,128)(2,1)} %ensembles.3, bf16[16,80,2048]{2,1,0:T(8,128)(2,1)} %cotangents.3, ...), custom_call_target="tpu_custom_call" | custom-call | flops 3000000000 | bytes 9000000 | tf_op jit(solution)/shard_map/early_gram/pallas_call | solution.py:394
  10.7 0.0 collective-permute-done.other
  10.7 0.3 join_0.1
  11.0 1.6 %collective-permute-start.1 = (f32[80,80]{1,0:T(8,128)S(1)}, f32[80,80]{1,0:T(8,128)S(1)}, u32[]{:S(2)}, u32[]{:S(2)}) collective-permute-start(f32[80,80]{1,0:T(8,128)S(1)} %get-tuple-element.43._.total), channel_id=1, source_target_pairs={{0,8},{4,12},{8,0},{12,4},{16,24},{20,28},{24,16},{28,20},{1,9},{5... | collective-permute-start | bytes 76808 | tf_op jit(solution)/shard_map/ppermute | solution.py:356
  12.7 1.2 %late_gram.1 = (f32[40,1408]{1,0:T(8,128)S(1)}, f32[40,1408]{1,0:T(8,128)S(1)}, f32[80,80]{1,0:T(8,128)S(1)}) custom-call(bf16[4,80,2048]{2,1,0:T(8,128)(2,1)S(1)} %get-tuple-element.46.ens.refs_2_, bf16[4,80,2048]{2,1,0:T(8,128)(2,1)S(1)} %get-tuple-element.47.cot.refs_2_, f32[1280,80]{1,0:T(8,128)S(1)} %get-tuple-element.38.suffixes, ...), custom_call_target="tpu_custom_call" | custom-call | flops 1200000000 | bytes 3600000 | tf_op jit(solution)/shard_map/late_gram/pallas_call | solution.py:405
  13.8 0.6 %collective-permute-start.4 = (f32[80,80]{1,0:T(8,128)S(1)}, f32[80,80]{1,0:T(8,128)S(1)}, u32[]{:S(2)}, u32[]{:S(2)}) collective-permute-start(f32[80,80]{1,0:T(8,128)S(1)} %get-tuple-element.49._.own), channel_id=1, source_target_pairs={{0,4},{4,0},{8,12},{12,8},{16,20},{20,16},{24,28},{28,24},{1,5},{5... | collective-permute-start | bytes 76808 | tf_op jit(solution)/shard_map/ppermute | solution.py:356
  14.4 0.0 collective-permute-start.3
  14.4 0.6 %collective-permute-done.1.other = f32[80,80]{1,0:T(8,128)S(1)} collective-permute-done((f32[80,80]{1,0:T(8,128)S(1)}, f32[80,80]{1,0:T(8,128)S(1)}, u32[]{:S(2)}, u32[]{:S(2)}) %collective-permute-start.1) | collective-permute-done | bytes 25632 | tf_op jit(solution)/shard_map/ppermute | solution.py:356
  15.1 0.3 join_1.1
  15.3 2.7 %collective-permute-start.2 = (f32[80,80]{1,0:T(8,128)S(1)}, f32[80,80]{1,0:T(8,128)S(1)}, u32[]{:S(2)}, u32[]{:S(2)}) collective-permute-start(f32[80,80]{1,0:T(8,128)S(1)} %get-tuple-element.51._), channel_id=1, source_target_pairs={{0,16},{4,20},{8,24},{12,28},{16,0},{20,4},{24,8},{28,12},{1,17},{... | collective-permute-start | bytes 76808 | tf_op jit(solution)/shard_map/ppermute | solution.py:356
  18.0 0.0 collective-permute-done.4.other
  18.0 0.2 pass_0.1
  18.2 1.6 %collective-permute-start.5 = (f32[80,80]{1,0:T(8,128)S(1)}, f32[80,80]{1,0:T(8,128)S(1)}, u32[]{:S(2)}, u32[]{:S(2)}) collective-permute-start(f32[80,80]{1,0:T(8,128)S(1)} %get-tuple-element.55._.own), channel_id=1, source_target_pairs={{0,8},{4,12},{8,0},{12,4},{16,24},{20,28},{24,16},{28,20},{1,9},{5... | collective-permute-start | bytes 76808 | tf_op jit(solution)/shard_map/ppermute | solution.py:356
  19.9 0.0 collective-permute-done.3.right
  19.9 1.6 %collective-permute-start.7 = (f32[40,1408]{1,0:T(8,128)S(1)}, f32[40,1408]{1,0:T(8,128)S(1)}, u32[]{:S(2)}, u32[]{:S(2)}) collective-permute-start(f32[40,1408]{1,0:T(8,128)S(1)} %chip_gram.1._), channel_id=1, source_target_pairs={{0,2},{1,3},{2,0},{3,1},{4,6},{5,7},{6,4},{7,5},{8,10},{9,11},{10,... | collective-permute-start | bytes 675848 | tf_op jit(solution)/shard_map/ppermute | solution.py:360
  21.5 0.0 collective-permute-done.2.other
  21.5 0.2 entering.1._.later
  21.7 0.6 %collective-permute-done.5.other = f32[80,80]{1,0:T(8,128)S(1)} collective-permute-done((f32[80,80]{1,0:T(8,128)S(1)}, f32[80,80]{1,0:T(8,128)S(1)}, u32[]{:S(2)}, u32[]{:S(2)}) %collective-permute-start.5) | collective-permute-done | bytes 25632 | tf_op jit(solution)/shard_map/ppermute | solution.py:356
  22.3 0.2 pass_1.1
  22.5 0.9 %carries.1 = (bf16[6,240,240]{2,1,0:T(8,128)(2,1)S(1)}, bf16[6,240,240]{2,1,0:T(8,128)(2,1)S(1)}, bf16[2,1280,80]{2,1,0:T(8,128)(2,1)S(1)}) custom-call(f32[1280,80]{1,0:T(8,128)S(1)} %get-tuple-element.38.suffixes, f32[80,80]{1,0:T(8,128)S(1)} %entering.1._.later, f32[80,80]{1,0:T(8,128)S(1)} %get-tuple-element.58._), custom_call_target="tpu_custom_call" | custom-call | flops 900000000 | bytes 2700000 | tf_op jit(solution)/shard_map/carries/pallas_call | solution.py:438
  23.4 2.6 %collective-permute-start.6 = (f32[80,80]{1,0:T(8,128)S(1)}, f32[80,80]{1,0:T(8,128)S(1)}, u32[]{:S(2)}, u32[]{:S(2)}) collective-permute-start(f32[80,80]{1,0:T(8,128)S(1)} %get-tuple-element.58._), channel_id=1, source_target_pairs={{0,16},{4,20},{8,24},{12,28},{16,0},{20,4},{24,8},{28,12},{1,17},{... | collective-permute-start | bytes 76808 | tf_op jit(solution)/shard_map/ppermute | solution.py:356
  25.9 2.7 %smoothed.1 = (bf16[16,80,2048]{2,1,0:T(8,128)(2,1)}, f32[8,128]{1,0:T(8,128)S(1)}) custom-call(bf16[6,240,240]{2,1,0:T(8,128)(2,1)S(1)} %get-tuple-element.59.factors, bf16[6,80,2048]{2,1,0:T(8,128)(2,1)S(1)} %get-tuple-element.40.ens.refs_0_, bf16[6,80,2048]{2,1,0:T(8,128)(2,1)S(1)} %get-tuple-element.60.refs_1_, ...), custom_call_target="tpu_custom_call" | custom-call | flops 2700000000 | bytes 8100000 | tf_op jit(solution)/shard_map/smoothed/pallas_call | solution.py:445
  28.6 0.0 collective-permute-done.6.other
  28.6 0.0 collective-permute-done.7.__
  28.7 0.2 pass_last.1
  28.9 0.1 collective-permute-start.9
  29.0 0.5 %collective-permute-start.8 = (f32[80,80]{1,0:T(8,128)S(1)}, f32[80,80]{1,0:T(8,128)S(1)}, u32[]{:S(2)}, u32[]{:S(2)}) collective-permute-start(f32[80,80]{1,0:T(8,128)S(1)} %get-tuple-element.68._.left), channel_id=1, source_target_pairs={{0,1},{1,0},{2,3},{3,2},{4,5},{5,4},{6,7},{7,6},{8,9},{9,8},{10,11... | collective-permute-start | bytes 76808 | tf_op jit(solution)/shard_map/ppermute | solution.py:356
  29.4 0.9 %windows.1._.steps = bf16[2,2560,80]{2,1,0:T(8,128)(2,1)S(1)} custom-call(f32[16,80,80]{2,1,0:T(8,128)S(1)} %get-tuple-element.69.kept, f32[80,80]{1,0:T(8,128)S(1)} %get-tuple-element.68._.left), custom_call_target="tpu_custom_call" | custom-call | flops 1000000000 | bytes 3000000 | tf_op jit(solution)/shard_map/windows/pallas_call | solution.py:463
  30.4 0.1 collective-permute-done.8.right
  30.5 1.6 %collective-permute-start.10 = (f32[80,80]{1,0:T(8,128)S(1)}, f32[80,80]{1,0:T(8,128)S(1)}, u32[]{:S(2)}, u32[]{:S(2)}) collective-permute-start(f32[80,80]{1,0:T(8,128)S(1)} %chip_carry.1.refs_3_.refs_0_), channel_id=1, source_target_pairs={{0,2},{1,3},{2,0},{3,1},{4,6},{5,7},{6,4},{7,5},{8,10},{9,11},{10,... | collective-permute-start | bytes 76808 | tf_op jit(solution)/shard_map/ppermute | solution.py:360
  32.1 2.7 %ensemble_grad.1 = (bf16[16,80,2048]{2,1,0:T(8,128)(2,1)}, f32[8,128]{1,0:T(8,128)S(1)}) custom-call(bf16[6,240,240]{2,1,0:T(8,128)(2,1)S(1)} %get-tuple-element.63.factors, bf16[6,80,2048]{2,1,0:T(8,128)(2,1)S(1)} %get-tuple-element.41.cot.refs_0_, bf16[6,80,2048]{2,1,0:T(8,128)(2,1)S(1)} %get-tuple-element.64.refs_1_, ...), custom_call_target="tpu_custom_call" | custom-call | flops 2700000000 | bytes 8100000 | tf_op jit(solution)/shard_map/ensemble_grad/pallas_call | solution.py:445
  34.8 0.0 collective-permute-done.10.refs_1_
  34.8 0.0 collective-permute-done.9.gram_core
  34.8 2.3 %transform_grad.1 = f32[16,80,80]{2,1,0:T(8,128)} custom-call(f32[40,1408]{1,0:T(8,128)S(1)} %add.3.gram, f32[40,1408]{1,0:T(8,128)S(1)} %collective-permute-done.9.gram_core, bf16[2,1280,80]{2,1,0:T(8,128)(2,1)S(1)} %get-tuple-element.61.refs_3_.follow, bf16[2,2560,80]{2,1,0:T(8,128)(2,1)S(1)} %windows.1._.steps, f32[8,128]{1,0:T(8,128)S(1)} %get-tuple-element.72._, ...), custom_call_target="tpu_custom_call" | custom-call | flops 2500000000 | bytes 7500000 | tf_op jit(solution)/shard_map/transform_grad/pallas_call | solution.py:473
  (5 shorter events, 0.1 us)
Async XLA Ops:
  3.9 6.9 %collective-permute-start = (f32[80,80]{1,0:T(8,128)S(1)}, f32[80,80]{1,0:T(8,128)S(1)}, u32[]{:S(2)}, u32[]{:S(2)}) collective-permute-start(f32[80,80]{1,0:T(8,128)S(1)} %get-tuple-element.39.total), channel_id=1, source_target_pairs={{0,4},{4,0},{8,12},{12,8},{16,20},{20,16},{24,28},{28,24},{1,5},{5... | collective-permute-start | bytes 76808 | tf_op jit(solution)/shard_map/ppermute | solution.py:356
  11.0 4.1 %collective-permute-start.1 = (f32[80,80]{1,0:T(8,128)S(1)}, f32[80,80]{1,0:T(8,128)S(1)}, u32[]{:S(2)}, u32[]{:S(2)}) collective-permute-start(f32[80,80]{1,0:T(8,128)S(1)} %get-tuple-element.43._.total), channel_id=1, source_target_pairs={{0,8},{4,12},{8,0},{12,4},{16,24},{20,28},{24,16},{28,20},{1,9},{5... | collective-permute-start | bytes 76808 | tf_op jit(solution)/shard_map/ppermute | solution.py:356
  13.8 4.2 %collective-permute-start.4 = (f32[80,80]{1,0:T(8,128)S(1)}, f32[80,80]{1,0:T(8,128)S(1)}, u32[]{:S(2)}, u32[]{:S(2)}) collective-permute-start(f32[80,80]{1,0:T(8,128)S(1)} %get-tuple-element.49._.own), channel_id=1, source_target_pairs={{0,4},{4,0},{8,12},{12,8},{16,20},{20,16},{24,28},{28,24},{1,5},{5... | collective-permute-start | bytes 76808 | tf_op jit(solution)/shard_map/ppermute | solution.py:356
  14.4 5.4 %collective-permute-start.3 = (f32[40,1408]{1,0:T(8,128)S(1)}, f32[40,1408]{1,0:T(8,128)S(1)}, u32[]{:S(2)}, u32[]{:S(2)}) collective-permute-start(f32[40,1408]{1,0:T(8,128)S(1)} %get-tuple-element.53), channel_id=1, source_target_pairs={{0,1},{1,0},{2,3},{3,2},{4,5},{5,4},{6,7},{7,6},{8,9},{9,8},{10,11... | collective-permute-start | bytes 675848 | tf_op jit(solution)/shard_map/ppermute | solution.py:356
  15.3 6.1 %collective-permute-start.2 = (f32[80,80]{1,0:T(8,128)S(1)}, f32[80,80]{1,0:T(8,128)S(1)}, u32[]{:S(2)}, u32[]{:S(2)}) collective-permute-start(f32[80,80]{1,0:T(8,128)S(1)} %get-tuple-element.51._), channel_id=1, source_target_pairs={{0,16},{4,20},{8,24},{12,28},{16,0},{20,4},{24,8},{28,12},{1,17},{... | collective-permute-start | bytes 76808 | tf_op jit(solution)/shard_map/ppermute | solution.py:356
  18.2 4.1 %collective-permute-start.5 = (f32[80,80]{1,0:T(8,128)S(1)}, f32[80,80]{1,0:T(8,128)S(1)}, u32[]{:S(2)}, u32[]{:S(2)}) collective-permute-start(f32[80,80]{1,0:T(8,128)S(1)} %get-tuple-element.55._.own), channel_id=1, source_target_pairs={{0,8},{4,12},{8,0},{12,4},{16,24},{20,28},{24,16},{28,20},{1,9},{5... | collective-permute-start | bytes 76808 | tf_op jit(solution)/shard_map/ppermute | solution.py:356
  19.9 8.8 %collective-permute-start.7 = (f32[40,1408]{1,0:T(8,128)S(1)}, f32[40,1408]{1,0:T(8,128)S(1)}, u32[]{:S(2)}, u32[]{:S(2)}) collective-permute-start(f32[40,1408]{1,0:T(8,128)S(1)} %chip_gram.1._), channel_id=1, source_target_pairs={{0,2},{1,3},{2,0},{3,1},{4,6},{5,7},{6,4},{7,5},{8,10},{9,11},{10,... | collective-permute-start | bytes 675848 | tf_op jit(solution)/shard_map/ppermute | solution.py:360
  23.4 5.3 %collective-permute-start.6 = (f32[80,80]{1,0:T(8,128)S(1)}, f32[80,80]{1,0:T(8,128)S(1)}, u32[]{:S(2)}, u32[]{:S(2)}) collective-permute-start(f32[80,80]{1,0:T(8,128)S(1)} %get-tuple-element.58._), channel_id=1, source_target_pairs={{0,16},{4,20},{8,24},{12,28},{16,0},{20,4},{24,8},{28,12},{1,17},{... | collective-permute-start | bytes 76808 | tf_op jit(solution)/shard_map/ppermute | solution.py:356
  28.9 5.9 %collective-permute-start.9 = (f32[40,1408]{1,0:T(8,128)S(1)}, f32[40,1408]{1,0:T(8,128)S(1)}, u32[]{:S(2)}, u32[]{:S(2)}) collective-permute-start(f32[40,1408]{1,0:T(8,128)S(1)} %add.3.gram), channel_id=1, source_target_pairs={{0,1},{1,0},{2,3},{3,2},{4,5},{5,4},{6,7},{7,6},{8,9},{9,8},{10,11... | collective-permute-start | bytes 675848 | tf_op jit(solution)/shard_map/ppermute | solution.py:356
  29.0 1.5 %collective-permute-start.8 = (f32[80,80]{1,0:T(8,128)S(1)}, f32[80,80]{1,0:T(8,128)S(1)}, u32[]{:S(2)}, u32[]{:S(2)}) collective-permute-start(f32[80,80]{1,0:T(8,128)S(1)} %get-tuple-element.68._.left), channel_id=1, source_target_pairs={{0,1},{1,0},{2,3},{3,2},{4,5},{5,4},{6,7},{7,6},{8,9},{9,8},{10,11... | collective-permute-start | bytes 76808 | tf_op jit(solution)/shard_map/ppermute | solution.py:356
  30.5 4.3 %collective-permute-start.10 = (f32[80,80]{1,0:T(8,128)S(1)}, f32[80,80]{1,0:T(8,128)S(1)}, u32[]{:S(2)}, u32[]{:S(2)}) collective-permute-start(f32[80,80]{1,0:T(8,128)S(1)} %chip_carry.1.refs_3_.refs_0_), channel_id=1, source_target_pairs={{0,2},{1,3},{2,0},{3,1},{4,6},{5,7},{6,4},{7,5},{8,10},{9,11},{10,... | collective-permute-start | bytes 76808 | tf_op jit(solution)/shard_map/ppermute | solution.py:360

commit v14 on v13

--- a/solution.py
+++ b/solution.py
@@ -14,7 +14,7 @@
 HBM = pl.BlockSpec(memory_space=pltpu.HBM)
 ANY = pl.BlockSpec(memory_space=pl.ANY)
 DEPTH = 256
-PIECES = 3
+PIECES = 2
 NORMAL = (((1,), (0,)), ((), ()))
 ROWS = (((1,), (1,)), ((), ()))
 
@@ -84,12 +84,12 @@
     return rows == columns
 
 
-def loads(plan, piece, values, buffer, sems):
+def loads(plan, piece, values, buffer, sems, which=slice(None)):
     base = plan.pieces[piece][0]
     copies = [
         pltpu.make_async_copy(values.at[start:stop], buffer.at[start - base : stop - base], sems.at[at])
         for at, (start, stop) in enumerate(plan.piece_groups[piece])
-    ]
+    ][which]
     for copy in copies:
         copy.start()
     return copies
@@ -101,8 +101,11 @@
     count, members = plan.count, plan.members
     read = pltpu.make_async_copy(transforms, kept, sem)
     read.start()
+    more = loads(plan, 0, ensembles, ens, ens_sem, slice(1))
+    more += loads(plan, 0, cotangents, cot, cot_sem, slice(1))
     read.wait()
-    more = loads(plan, 0, ensembles, ens, ens_sem) + loads(plan, 0, cotangents, cot, cot_sem)
+    more += loads(plan, 0, ensembles, ens, ens_sem, slice(1, None))
+    more += loads(plan, 0, cotangents, cot, cot_sem, slice(1, None))
     for at in range(count):
         suffixes[plan.rows(at, at + 1)] = kept[at]
     suffix_scan(suffixes, count, members, count)
@@ -162,35 +165,20 @@
     return offset
 
 
-def early_gram_kernel(plan, ensembles, cotangents, suffixes, ens, cot, whole, offset, *refs):
-    buffers, sems = refs[: 2 * (PIECES - 1)], refs[2 * (PIECES - 1) :]
-    copies = []
-    for piece in range(1, PIECES):
-        pair = buffers[2 * piece - 2 : 2 * piece]
-        own = sems[2 * piece - 2 : 2 * piece]
-        copies.append(list(zip(
-            loads(plan, piece, ensembles, pair[0], own[0]),
-            loads(plan, piece, cotangents, pair[1], own[1]),
-        )))
+def gram_kernel(
+    plan, ensembles, cotangents, suffixes, ens, cot,
+    kept, sent, offsets, next_ens, next_cot, whole, ens_sem, cot_sem,
+):
+    waiting = iter(list(zip(
+        loads(plan, 1, ensembles, next_ens, ens_sem), loads(plan, 1, cotangents, next_cot, cot_sem)
+    )))
+
+    def ready():
+        for copy in next(waiting):
+            copy.wait()
+
     total = gram_of(plan, 0, cot, ens, suffixes, whole)
-    for piece in range(1, PIECES - 1):
-        waiting = iter(copies[piece - 1])
-
-        def ready():
-            for copy in next(waiting):
-                copy.wait()
-
-        ens, cot = buffers[2 * piece - 2 : 2 * piece]
-        total = total + gram_of(plan, piece, cot, ens, suffixes, whole, ready)
-    offset[...] = total
-    for pair in copies[-1]:
-        for copy in pair:
-            copy.wait()
-
-
-def late_gram_kernel(plan, ens, cot, suffixes, early, offset, _, kept, sent, offsets, whole):
-    whole[:, : early.shape[1]] = early[...]
-    offsets[...] = offset[...] + gram_of(plan, PIECES - 1, cot, ens, suffixes, whole)
+    offsets[...] = total + gram_of(plan, 1, next_cot, next_ens, suffixes, whole, ready)
     half = plan.members // 2
     core = lax.rem(lax.axis_index("space"), 2)
     kept[...] = whole[pl.ds(core * half, half)]
@@ -390,29 +378,19 @@
         return total, later, before, *through
 
     other = exchange(total, "tm", blocks, 1)
-    early_width = plan.lanes(plan.first_group[-1]).start
-    early, offset, *loaded = call(
-        functools.partial(early_gram_kernel, plan),
-        [shape(members, early_width), square]
-        + [piece_shape(piece) for piece in range(1, PIECES) for _ in range(2)],
-        [HBM] * 2 + [VMEM] * 3, [VMEM] * (2 * PIECES),
-        [sem for piece in range(1, PIECES) for sem in piece_sems(piece)], 3, "early_gram",
+    gram, gram_sent, own, *second_part = call(
+        functools.partial(gram_kernel, plan),
+        [wide, wide, square] + [piece_shape(1)] * 2,
+        [HBM] * 2 + [VMEM] * 3, [VMEM] * 5,
+        [pltpu.VMEM((members, plan.width), F32)] + piece_sems(1), 4.5, "gram",
     )(ensembles, cotangents, suffixes, *first_part)
-    parts = [first_part] + [loaded[at : at + 2] for at in range(0, len(loaded), 2)]
-    total, later, before = join(0, total, other, later, before, offset)
-
-    other = exchange(total, "tm", blocks, 2)
-    gram, gram_sent, own = call(
-        functools.partial(late_gram_kernel, plan),
-        [wide, wide, square], [VMEM] * 5 + [ANY], [VMEM] * 3,
-        [pltpu.VMEM((members, plan.width), F32)], 1.2, "late_gram",
-    )(*parts[-1], suffixes, early, offset, total)
+    parts = [first_part, second_part]
     other_own = exchange(own, "tm", blocks, 1)
     gram_core = exchange(gram_sent, "space", lanes, 1)
-    for level in range(1, levels - 1):
-        total, later, before = join(level, total, other, later, before, own)
-        other = exchange(total, "tm", blocks, 2 << level)
-    befores.append(before)
+    total, later, before = join(0, total, other, later, before, own)
+    other = exchange(total, "tm", blocks, 2)
+    gram = call(sum_kernel, wide, [VMEM] * 2 + [ANY], VMEM, [], 0.1, "chip_gram")(gram, gram_core, total)
+    grams = around(gram)
 
     def pass_on(level, carry, after, *through):
         more = [shape(*value.shape) for value in through]
@@ -423,17 +401,20 @@
         )(own, other_own, carry, uppers[level], befores[level], after, *through)
 
     carry = jnp.zeros((members, members), F32)
+    after = gram
     for level in range(levels - 2):
-        own, carry = pass_on(level, carry, total)
+        own, carry = pass_on(level, carry, after)
         other_own = exchange(own, "tm", blocks, 2 << level)
-    gram = call(sum_kernel, wide, [VMEM] * 2 + [ANY], VMEM, [], 0.1, "chip_gram")(gram, gram_core, own)
-    grams = around(gram)
+        total, later, before = join(level + 1, total, other, later, before, own)
+        other = exchange(total, "tm", blocks, 4 << level)
+        after = total
+    befores.append(before)
+    own, carry = pass_on(levels - 2, carry, total)
+    other_own = exchange(own, "tm", blocks, blocks // 2)
     entering = call(
         functools.partial(enter_kernel, levels - 1),
         square, [VMEM] * 2 + [ANY], VMEM, [], 0.2, "entering",
-    )(later, other, gram)
-    own, carry = pass_on(levels - 2, carry, entering)
-    other_own = exchange(own, "tm", blocks, blocks // 2)
+    )(later, other, own)
     size = plan.stack * members
     ens_factors, cot_factors, follow = call(
         functools.partial(carry_kernel, plan),
@@ -448,7 +429,7 @@
             [VMEM] * (1 + PIECES) + [ANY], [HBM, VMEM],
             [pltpu.VMEM((count, members, cells), BF16),
              pltpu.SemaphoreType.DMA((2 * len(plan.groups),))],
-            2.7, name,
+            0.5, name,
         )(factors, *(part[which] for part in parts), after)
 
     smoothed, done = apply(ens_factors, 0, follow, "smoothed")

time: 37.3 us -> 35.7 us (0.957)
  Pallas kernels: 19.1 us -> 18 us
    pallas_call x2 -> x1, Pallas kernels: 5.02 us -> 3.87 us  [shards(): call(functools.partial(gram_kernel, plan), [wide, wide, square] + [piece_...]
  transfers between devices with their start and end apart: 11 -> 11, of which waited for: 3 -> 2; matrix products, arithmetic and copies ran while one was open for 0% -> 0% of each run, Pallas kernels for 35% -> 34%
where the time goes in v14:
time: 35.7 us; the launch traced here: 35.5 us
  Pallas kernels  18 us (50%)
  starting transfers between devices  15.5 us (43%)
  waiting for transfers between devices  1.08 us (3%)
  between operations  0.79 us (2%)
    ppermute x9, starting transfers between devices, exchange(): return lax.ppermute(value, axis, [(at, at ^ bit) for at in range(size)])  12.3 us
    pallas_call x2, Pallas kernels, apply(): call(functools.partial(apply_kernel, plan), [shape(count, members, cells,...  5.44 us
    pallas_call x1, Pallas kernels, shards(): call(functools.partial(gram_kernel, plan), [wide, wide, square] + [piece_...  3.87 us
    pallas_call x1, Pallas kernels, shards(): call(functools.partial(chain_kernel, plan), [shape(count * members, membe...  3.36 us
    ppermute x2, starting transfers between devices, around(): lax.ppermute(value, 'space', [(at, (at + 2 * d) % lanes) for at in range(...  3.18 us
    pallas_call x1, Pallas kernels, shards(): call(functools.partial(final_kernel, plan, scale), shape(count, members,...  2.29 us
    ppermute x9, waiting for transfers between devices, exchange(): return lax.ppermute(value, axis, [(at, at ^ bit) for at in range(size)])  1.08 us
    pallas_call x1, Pallas kernels, shards(): call(functools.partial(windows_kernel, plan), shape(2, count_steps(count)...  0.94 us
  transfers between devices with their start and end apart: 11, of which 2 were waited for; matrix products, arithmetic and copies ran while one was open for 0% of the time, Pallas kernels for 34%

profile of v14, /device:TPU:0, one launch (start us, length us, event | category | flops | bytes accessed | tf_op | source)
XLA Modules:
  0.0 35.5 jit_solution(5229154635206325924)
XLA Ops:
  0.6 3.4 %transform_chain.1 = (f32[1280,80]{1,0:T(8,128)S(1)}, f32[80,80]{1,0:T(8,128)S(1)}, f32[16,80,80]{2,1,0:T(8,128)S(1)}, bf16[9,80,2048]{2,1,0:T(8,128)(2,1)S(1)}, bf16[9,80,2048]{2,1,0:T(8,128)(2,1)S(1)}) custom-call(f32[16,80,80]{2,1,0:T(8,128)} %transforms.1, bf16[16,80,2048]{2,1,0:T(8,128)(2,1)} %ensembles.3, bf16[16,80,2048]{2,1,0:T(8,128)(2,1)} %cotangents.3), custom_call_target="tpu_custom_call" | custom-call | flops 3500000000 | bytes 10500000 | tf_op jit(solution)/shard_map/transform_chain/pallas_call | solution.py:359
  4.0 3.0 %collective-permute-start = (f32[80,80]{1,0:T(8,128)S(1)}, f32[80,80]{1,0:T(8,128)S(1)}, u32[]{:S(2)}, u32[]{:S(2)}) collective-permute-start(f32[80,80]{1,0:T(8,128)S(1)} %get-tuple-element.35.total), channel_id=1, source_target_pairs={{0,4},{4,0},{8,12},{12,8},{16,20},{20,16},{24,28},{28,24},{1,5},{5... | collective-permute-start | bytes 76808 | tf_op jit(solution)/shard_map/ppermute | solution.py:344
  7.0 3.9 %gram.1 = (f32[40,1408]{1,0:T(8,128)S(1)}, f32[40,1408]{1,0:T(8,128)S(1)}, f32[80,80]{1,0:T(8,128)S(1)}, bf16[7,80,2048]{2,1,0:T(8,128)(2,1)S(1)}, bf16[7,80,2048]{2,1,0:T(8,128)(2,1)S(1)}) custom-call(bf16[16,80,2048]{2,1,0:T(8,128)(2,1)} %ensembles.3, bf16[16,80,2048]{2,1,0:T(8,128)(2,1)} %cotangents.3, f32[1280,80]{1,0:T(8,128)S(1)} %get-tuple-element.34.suffixes, ...), custom_call_target="tpu_custom_call" | custom-call | flops 4499999744 | bytes 13500000 | tf_op jit(solution)/shard_map/gram/pallas_call | solution.py:381
  10.9 0.1 collective-permute-start.3
  11.0 0.1 collective-permute-start.2
  11.1 0.0 collective-permute-done.other
  11.1 0.3 join_0.1
  11.3 2.1 %collective-permute-start.1 = (f32[80,80]{1,0:T(8,128)S(1)}, f32[80,80]{1,0:T(8,128)S(1)}, u32[]{:S(2)}, u32[]{:S(2)}) collective-permute-start(f32[80,80]{1,0:T(8,128)S(1)} %get-tuple-element.39._.total), channel_id=1, source_target_pairs={{0,8},{4,12},{8,0},{12,4},{16,24},{20,28},{24,16},{28,20},{1,9},{5... | collective-permute-start | bytes 76808 | tf_op jit(solution)/shard_map/ppermute | solution.py:344
  13.5 0.0 collective-permute-done.3.right
  13.5 1.6 %collective-permute-start.7 = (f32[40,1408]{1,0:T(8,128)S(1)}, f32[40,1408]{1,0:T(8,128)S(1)}, u32[]{:S(2)}, u32[]{:S(2)}) collective-permute-start(f32[40,1408]{1,0:T(8,128)S(1)} %chip_gram.1._), channel_id=1, source_target_pairs={{0,2},{1,3},{2,0},{3,1},{4,6},{5,7},{6,4},{7,5},{8,10},{9,11},{10,... | collective-permute-start | bytes 675848 | tf_op jit(solution)/shard_map/ppermute | solution.py:348
  15.1 0.0 collective-permute-done.2.other
  15.1 0.2 pass_0.1
  15.3 1.6 %collective-permute-start.5 = (f32[80,80]{1,0:T(8,128)S(1)}, f32[80,80]{1,0:T(8,128)S(1)}, u32[]{:S(2)}, u32[]{:S(2)}) collective-permute-start(f32[80,80]{1,0:T(8,128)S(1)} %get-tuple-element.45._.own), channel_id=1, source_target_pairs={{0,8},{4,12},{8,0},{12,4},{16,24},{20,28},{24,16},{28,20},{1,9},{5... | collective-permute-start | bytes 76808 | tf_op jit(solution)/shard_map/ppermute | solution.py:344
  16.9 0.0 collective-permute-done.1.other
  16.9 0.3 join_1.1
  17.2 2.7 %collective-permute-start.4 = (f32[80,80]{1,0:T(8,128)S(1)}, f32[80,80]{1,0:T(8,128)S(1)}, u32[]{:S(2)}, u32[]{:S(2)}) collective-permute-start(f32[80,80]{1,0:T(8,128)S(1)} %get-tuple-element.47._), channel_id=1, source_target_pairs={{0,16},{4,20},{8,24},{12,28},{16,0},{20,4},{24,8},{28,12},{1,17},{... | collective-permute-start | bytes 76808 | tf_op jit(solution)/shard_map/ppermute | solution.py:344
  19.8 0.0 collective-permute-done.5.other
  19.8 0.2 pass_1.1
  20.0 2.2 %collective-permute-start.6 = (f32[80,80]{1,0:T(8,128)S(1)}, f32[80,80]{1,0:T(8,128)S(1)}, u32[]{:S(2)}, u32[]{:S(2)}) collective-permute-start(f32[80,80]{1,0:T(8,128)S(1)} %get-tuple-element.50._), channel_id=1, source_target_pairs={{0,16},{4,20},{8,24},{12,28},{16,0},{20,4},{24,8},{28,12},{1,17},{... | collective-permute-start | bytes 76808 | tf_op jit(solution)/shard_map/ppermute | solution.py:344
  22.2 1.0 %collective-permute-done.4.other = f32[80,80]{1,0:T(8,128)S(1)} collective-permute-done((f32[80,80]{1,0:T(8,128)S(1)}, f32[80,80]{1,0:T(8,128)S(1)}, u32[]{:S(2)}, u32[]{:S(2)}) %collective-permute-start.4) | collective-permute-done | bytes 25632 | tf_op jit(solution)/shard_map/ppermute | solution.py:344
  23.2 0.2 entering.1.later
  23.4 0.8 %carries.1 = (bf16[6,240,240]{2,1,0:T(8,128)(2,1)S(1)}, bf16[6,240,240]{2,1,0:T(8,128)(2,1)S(1)}, bf16[2,1280,80]{2,1,0:T(8,128)(2,1)S(1)}) custom-call(f32[1280,80]{1,0:T(8,128)S(1)} %get-tuple-element.34.suffixes, f32[80,80]{1,0:T(8,128)S(1)} %entering.1.later, f32[80,80]{1,0:T(8,128)S(1)} %get-tuple-element.50._), custom_call_target="tpu_custom_call" | custom-call | flops 900000000 | bytes 2700000 | tf_op jit(solution)/shard_map/carries/pallas_call | solution.py:419
  24.3 2.7 %smoothed.1 = (bf16[16,80,2048]{2,1,0:T(8,128)(2,1)}, f32[8,128]{1,0:T(8,128)S(1)}) custom-call(bf16[6,240,240]{2,1,0:T(8,128)(2,1)S(1)} %get-tuple-element.51.factors, bf16[9,80,2048]{2,1,0:T(8,128)(2,1)S(1)} %get-tuple-element.36.ens.refs_0_, bf16[7,80,2048]{2,1,0:T(8,128)(2,1)S(1)} %get-tuple-element.52.refs_1_, ...), custom_call_target="tpu_custom_call" | custom-call | flops 500000000 | bytes 1500000 | tf_op jit(solution)/shard_map/smoothed/pallas_call | solution.py:426
  27.0 0.0 collective-permute-done.6.other
  27.0 0.0 collective-permute-done.7.__
  27.0 0.2 pass_last.1
  27.2 0.1 collective-permute-start.9
  27.3 0.5 %collective-permute-start.8 = (f32[80,80]{1,0:T(8,128)S(1)}, f32[80,80]{1,0:T(8,128)S(1)}, u32[]{:S(2)}, u32[]{:S(2)}) collective-permute-start(f32[80,80]{1,0:T(8,128)S(1)} %get-tuple-element.60._.left), channel_id=1, source_target_pairs={{0,1},{1,0},{2,3},{3,2},{4,5},{5,4},{6,7},{7,6},{8,9},{9,8},{10,11... | collective-permute-start | bytes 76808 | tf_op jit(solution)/shard_map/ppermute | solution.py:344
  27.8 0.9 %windows.1._.steps = bf16[2,2560,80]{2,1,0:T(8,128)(2,1)S(1)} custom-call(f32[16,80,80]{2,1,0:T(8,128)S(1)} %get-tuple-element.61.kept, f32[80,80]{1,0:T(8,128)S(1)} %get-tuple-element.60._.left), custom_call_target="tpu_custom_call" | custom-call | flops 1000000000 | bytes 3000000 | tf_op jit(solution)/shard_map/windows/pallas_call | solution.py:444
  28.7 0.1 collective-permute-done.8.right
  28.8 1.6 %collective-permute-start.10 = (f32[80,80]{1,0:T(8,128)S(1)}, f32[80,80]{1,0:T(8,128)S(1)}, u32[]{:S(2)}, u32[]{:S(2)}) collective-permute-start(f32[80,80]{1,0:T(8,128)S(1)} %chip_carry.1.refs_2_.refs_0_), channel_id=1, source_target_pairs={{0,2},{1,3},{2,0},{3,1},{4,6},{5,7},{6,4},{7,5},{8,10},{9,11},{10,... | collective-permute-start | bytes 76808 | tf_op jit(solution)/shard_map/ppermute | solution.py:348
  30.4 2.7 %ensemble_grad.1 = (bf16[16,80,2048]{2,1,0:T(8,128)(2,1)}, f32[8,128]{1,0:T(8,128)S(1)}) custom-call(bf16[6,240,240]{2,1,0:T(8,128)(2,1)S(1)} %get-tuple-element.55.factors, bf16[9,80,2048]{2,1,0:T(8,128)(2,1)S(1)} %get-tuple-element.37.cot.refs_0_, bf16[7,80,2048]{2,1,0:T(8,128)(2,1)S(1)} %get-tuple-element.56.refs_1_, f32[80,80]{1,0:T(8,128)S(1)} %chip_carry.1.refs_2_.refs_0_), custom_call_target="tpu_custom_call" | custom-call | flops 500000000 | bytes 1500000 | tf_op jit(solution)/shard_map/ensemble_grad/pallas_call | solution.py:426
  33.2 0.0 collective-permute-done.10.refs_1_
  33.2 0.0 collective-permute-done.9.gram_core
  33.2 2.3 %transform_grad.1 = f32[16,80,80]{2,1,0:T(8,128)} custom-call(f32[40,1408]{1,0:T(8,128)S(1)} %add.3.gram, f32[40,1408]{1,0:T(8,128)S(1)} %collective-permute-done.9.gram_core, bf16[2,1280,80]{2,1,0:T(8,128)(2,1)S(1)} %get-tuple-element.53.refs_2_.follow, bf16[2,2560,80]{2,1,0:T(8,128)(2,1)S(1)} %windows.1._.steps, f32[8,128]{1,0:T(8,128)S(1)} %get-tuple-element.64._, ...), custom_call_target="tpu_custom_call" | custom-call | flops 2500000000 | bytes 7500000 | tf_op jit(solution)/shard_map/transform_grad/pallas_call | solution.py:454
  (5 shorter events, 0.1 us)
Async XLA Ops:
  4.0 7.1 %collective-permute-start = (f32[80,80]{1,0:T(8,128)S(1)}, f32[80,80]{1,0:T(8,128)S(1)}, u32[]{:S(2)}, u32[]{:S(2)}) collective-permute-start(f32[80,80]{1,0:T(8,128)S(1)} %get-tuple-element.35.total), channel_id=1, source_target_pairs={{0,4},{4,0},{8,12},{12,8},{16,20},{20,16},{24,28},{28,24},{1,5},{5... | collective-permute-start | bytes 76808 | tf_op jit(solution)/shard_map/ppermute | solution.py:344
  10.9 2.6 %collective-permute-start.3 = (f32[40,1408]{1,0:T(8,128)S(1)}, f32[40,1408]{1,0:T(8,128)S(1)}, u32[]{:S(2)}, u32[]{:S(2)}) collective-permute-start(f32[40,1408]{1,0:T(8,128)S(1)} %get-tuple-element.44), channel_id=1, source_target_pairs={{0,1},{1,0},{2,3},{3,2},{4,5},{5,4},{6,7},{7,6},{8,9},{9,8},{10,11... | collective-permute-start | bytes 675848 | tf_op jit(solution)/shard_map/ppermute | solution.py:344
  11.0 4.1 %collective-permute-start.2 = (f32[80,80]{1,0:T(8,128)S(1)}, f32[80,80]{1,0:T(8,128)S(1)}, u32[]{:S(2)}, u32[]{:S(2)}) collective-permute-start(f32[80,80]{1,0:T(8,128)S(1)} %get-tuple-element.38._.own), channel_id=1, source_target_pairs={{0,4},{4,0},{8,12},{12,8},{16,20},{20,16},{24,28},{28,24},{1,5},{5... | collective-permute-start | bytes 76808 | tf_op jit(solution)/shard_map/ppermute | solution.py:344
  11.3 5.6 %collective-permute-start.1 = (f32[80,80]{1,0:T(8,128)S(1)}, f32[80,80]{1,0:T(8,128)S(1)}, u32[]{:S(2)}, u32[]{:S(2)}) collective-permute-start(f32[80,80]{1,0:T(8,128)S(1)} %get-tuple-element.39._.total), channel_id=1, source_target_pairs={{0,8},{4,12},{8,0},{12,4},{16,24},{20,28},{24,16},{28,20},{1,9},{5... | collective-permute-start | bytes 76808 | tf_op jit(solution)/shard_map/ppermute | solution.py:344
  13.5 13.5 %collective-permute-start.7 = (f32[40,1408]{1,0:T(8,128)S(1)}, f32[40,1408]{1,0:T(8,128)S(1)}, u32[]{:S(2)}, u32[]{:S(2)}) collective-permute-start(f32[40,1408]{1,0:T(8,128)S(1)} %chip_gram.1._), channel_id=1, source_target_pairs={{0,2},{1,3},{2,0},{3,1},{4,6},{5,7},{6,4},{7,5},{8,10},{9,11},{10,... | collective-permute-start | bytes 675848 | tf_op jit(solution)/shard_map/ppermute | solution.py:348
  15.3 4.5 %collective-permute-start.5 = (f32[80,80]{1,0:T(8,128)S(1)}, f32[80,80]{1,0:T(8,128)S(1)}, u32[]{:S(2)}, u32[]{:S(2)}) collective-permute-start(f32[80,80]{1,0:T(8,128)S(1)} %get-tuple-element.45._.own), channel_id=1, source_target_pairs={{0,8},{4,12},{8,0},{12,4},{16,24},{20,28},{24,16},{28,20},{1,9},{5... | collective-permute-start | bytes 76808 | tf_op jit(solution)/shard_map/ppermute | solution.py:344
  17.2 6.1 %collective-permute-start.4 = (f32[80,80]{1,0:T(8,128)S(1)}, f32[80,80]{1,0:T(8,128)S(1)}, u32[]{:S(2)}, u32[]{:S(2)}) collective-permute-start(f32[80,80]{1,0:T(8,128)S(1)} %get-tuple-element.47._), channel_id=1, source_target_pairs={{0,16},{4,20},{8,24},{12,28},{16,0},{20,4},{24,8},{28,12},{1,17},{... | collective-permute-start | bytes 76808 | tf_op jit(solution)/shard_map/ppermute | solution.py:344
  20.0 7.0 %collective-permute-start.6 = (f32[80,80]{1,0:T(8,128)S(1)}, f32[80,80]{1,0:T(8,128)S(1)}, u32[]{:S(2)}, u32[]{:S(2)}) collective-permute-start(f32[80,80]{1,0:T(8,128)S(1)} %get-tuple-element.50._), channel_id=1, source_target_pairs={{0,16},{4,20},{8,24},{12,28},{16,0},{20,4},{24,8},{28,12},{1,17},{... | collective-permute-start | bytes 76808 | tf_op jit(solution)/shard_map/ppermute | solution.py:344
  27.2 5.9 %collective-permute-start.9 = (f32[40,1408]{1,0:T(8,128)S(1)}, f32[40,1408]{1,0:T(8,128)S(1)}, u32[]{:S(2)}, u32[]{:S(2)}) collective-permute-start(f32[40,1408]{1,0:T(8,128)S(1)} %add.3.gram), channel_id=1, source_target_pairs={{0,1},{1,0},{2,3},{3,2},{4,5},{5,4},{6,7},{7,6},{8,9},{9,8},{10,11... | collective-permute-start | bytes 675848 | tf_op jit(solution)/shard_map/ppermute | solution.py:344
  27.3 1.5 %collective-permute-start.8 = (f32[80,80]{1,0:T(8,128)S(1)}, f32[80,80]{1,0:T(8,128)S(1)}, u32[]{:S(2)}, u32[]{:S(2)}) collective-permute-start(f32[80,80]{1,0:T(8,128)S(1)} %get-tuple-element.60._.left), channel_id=1, source_target_pairs={{0,1},{1,0},{2,3},{3,2},{4,5},{5,4},{6,7},{7,6},{8,9},{9,8},{10,11... | collective-permute-start | bytes 76808 | tf_op jit(solution)/shard_map/ppermute | solution.py:344
  28.8 4.3 %collective-permute-start.10 = (f32[80,80]{1,0:T(8,128)S(1)}, f32[80,80]{1,0:T(8,128)S(1)}, u32[]{:S(2)}, u32[]{:S(2)}) collective-permute-start(f32[80,80]{1,0:T(8,128)S(1)} %chip_carry.1.refs_2_.refs_0_), channel_id=1, source_target_pairs={{0,2},{1,3},{2,0},{3,1},{4,6},{5,7},{6,4},{7,5},{8,10},{9,11},{10,... | collective-permute-start | bytes 76808 | tf_op jit(solution)/shard_map/ppermute | solution.py:348

commit v15 on v14

--- a/solution.py
+++ b/solution.py
@@ -114,7 +114,7 @@
         copy.wait()
 
 
-def windows_kernel(plan, kept, _, steps, runs):
+def windows_kernel(plan, kept, _, steps, prefixes, runs):
     count = plan.count
     for at in range(count - 1):
         runs[plan.rows(at + 1, at + 2)] = kept[at].T
@@ -126,11 +126,13 @@
             for side, part in enumerate(split(runs[plan.rows(middle, middle + size)])):
                 steps[side, plan.rows(number, number + size)] = part
             number += size
-        for start in range(2 * width, count, 2 * width):
-            if start + width < count:
+        for start in range(0, count, 2 * width):
+            if start + width < count and (start or width > 1):
                 rows = plan.rows(start + width, min(start + 2 * width, count))
                 runs[rows] = mul_exact(runs[rows], runs[plan.rows(start + width - 1, start + width)])
         width *= 2
+    for side, part in enumerate(split(runs[plan.rows(1, count)])):
+        prefixes[side] = part
 
 
 def count_steps(count):
@@ -204,8 +206,7 @@
     total[...] = left[...] + right[...]
 
 
-def pass_kernel(level, own, other, carry, upper_total, before, _, *refs):
-    new_own, new_carry = refs[len(refs) // 2 - 1 : len(refs) // 2 + 1]
+def pass_kernel(level, own, other, carry, upper_total, before, _, new_own, new_carry):
     upper = upper_half(level)
     left = jnp.where(upper, other[...], own[...])
     right = jnp.where(upper, own[...], other[...])
@@ -213,14 +214,19 @@
     new_carry[...] = carry[...] + jnp.where(upper, mul_exact(left, before[...]), 0.0)
 
 
-def last_pass_kernel(level, other, carry, before, _, __, new_carry, ___):
-    added = mul_exact(other[...], before[...])
-    new_carry[...] = carry[...] + jnp.where(upper_half(level), added, 0.0)
-
-
-def enter_kernel(level, later, other, _, entering):
-    joined = mul_exact(later[...], other[...])
-    entering[...] = jnp.where(upper_half(level), later[...], joined)
+def last_pass_kernel(
+    level, own, other, carry, upper_total, before, total, _, __, message, new_carry, ___
+):
+    pass_kernel(level, own, other, carry, upper_total, before, _, message, new_carry)
+    message[...] = jnp.where(upper_half(level + 1), total[...], message[...])
+
+
+def enter_kernel(level, later, carry, before, message, _, entering, new_carry):
+    upper = upper_half(level)
+    joined = mul_exact(later[...], message[...])
+    added = mul_exact(message[...], before[...])
+    entering[...] = jnp.where(upper, later[...], joined)
+    new_carry[...] = carry[...] + jnp.where(upper, added, 0.0)
 
 
 def carry_kernel(plan, suffixes, later, _, ens_factors, cot_factors, follow):
@@ -270,21 +276,16 @@
         copy.wait()
 
 
-def final_kernel(plan, scale, gram, gram_core, follow, steps, _, *refs):
-    carries, (out, buffer, sems) = refs[:-3], refs[-3:]
-    carry = carries[0][...]
-    for ref in carries[1:]:
-        carry = carry + ref[...]
+def scan_kernel(plan, gram, gram_core, steps, out):
     count, members = plan.count, plan.members
+    first = lax.rem(lax.axis_index("space"), 2) == 0
     totals = []
-    first = lax.rem(lax.axis_index("space"), 2) == 0
     for at, (start, stop) in enumerate(plan.groups):
         mine, other = gram[:, plan.lanes(at)], gram_core[:, plan.lanes(at)]
         halves = [jnp.where(first, mine, other), jnp.where(first, other, mine)]
         tall = jnp.concatenate(halves, axis=0).T
         for i in range(stop - start):
             totals.append(tall[i * members : (i + 1) * members])
-    totals[0] = totals[0] + carry.T
     number = 0
     width = 1
     while width < count:
@@ -296,10 +297,23 @@
                 totals[start + at] = totals[start + at] + added[at * members : (at + 1) * members]
             number += size
         width *= 2
+    for at in range(count):
+        out[at] = totals[at]
+
+
+def final_kernel(plan, scale, totals, prefixes, follow, _, *refs):
+    carries, (out, buffer, sems) = refs[:-3], refs[-3:]
+    count, members = plan.count, plan.members
+    carry = carries[0][...]
+    for ref in carries[1:]:
+        carry = carry + ref[...]
+    carry = carry.T
+    added = mul_pairs((prefixes[0], prefixes[1]), split(carry))
     copies = []
     for at in range(count):
         rows = plan.rows(at, at + 1)
-        buffer[at] = mul_pairs(split(totals[at]), (follow[0, rows], follow[1, rows]), ROWS) * scale
+        total = totals[at] + (added[plan.rows(at - 1, at)] if at else carry)
+        buffer[at] = mul_pairs(split(total), (follow[0, rows], follow[1, rows]), ROWS) * scale
         copy = pltpu.make_async_copy(buffer.at[at], out.at[at], sems.at[at])
         copy.start()
         copies.append(copy)
@@ -392,36 +406,52 @@
     gram = call(sum_kernel, wide, [VMEM] * 2 + [ANY], VMEM, [], 0.1, "chip_gram")(gram, gram_core, total)
     grams = around(gram)
 
-    def pass_on(level, carry, after, *through):
-        more = [shape(*value.shape) for value in through]
-        return call(
-            functools.partial(pass_kernel, level),
-            [square] * 2 + more, [VMEM] * 5 + [ANY] * (1 + len(more)), [VMEM] * 2 + [ANY] * len(more),
-            [], 3, f"pass_{level}", aliases={6 + at: 2 + at for at in range(len(more))},
-        )(own, other_own, carry, uppers[level], befores[level], after, *through)
-
     carry = jnp.zeros((members, members), F32)
     after = gram
     for level in range(levels - 2):
-        own, carry = pass_on(level, carry, after)
+        own, carry = call(
+            functools.partial(pass_kernel, level),
+            [square] * 2, [VMEM] * 5 + [ANY], [VMEM] * 2, [], 3, f"pass_{level}",
+        )(own, other_own, carry, uppers[level], befores[level], after)
         other_own = exchange(own, "tm", blocks, 2 << level)
         total, later, before = join(level + 1, total, other, later, before, own)
-        other = exchange(total, "tm", blocks, 4 << level)
+        if level < levels - 3:
+            other = exchange(total, "tm", blocks, 4 << level)
         after = total
     befores.append(before)
-    own, carry = pass_on(levels - 2, carry, total)
-    other_own = exchange(own, "tm", blocks, blocks // 2)
-    entering = call(
+    level = levels - 2
+    message, carry, grams[0] = call(
+        functools.partial(last_pass_kernel, level),
+        [square] * 2 + [wide], [VMEM] * 6 + [ANY] * 2, [VMEM] * 2 + [ANY], [], 3, f"pass_{level}",
+        aliases={7: 2},
+    )(own, other_own, carry, uppers[level], befores[level], total, total, grams[0])
+    message_other = exchange(message, "tm", blocks, blocks // 2)
+    for part in grams:
+        gram = gram + part
+    gram_core = exchange(gram, "space", lanes, 1)
+    steps, prefixes = call(
+        functools.partial(windows_kernel, plan),
+        [shape(2, count_steps(count) * members, members, kind=BF16),
+         shape(2, (count - 1) * members, members, kind=BF16)],
+        [VMEM, ANY], [VMEM] * 2,
+        [pltpu.VMEM((count * members, members), F32)], 1.3, "windows",
+    )(kept, message)
+    totals = call(
+        functools.partial(scan_kernel, plan),
+        shape(count, members, members), [VMEM] * 3, VMEM, [], 1.2, "scan",
+    )(gram, gram_core, steps)
+    entering, carry = call(
         functools.partial(enter_kernel, levels - 1),
-        square, [VMEM] * 2 + [ANY], VMEM, [], 0.2, "entering",
-    )(later, other, own)
+        [square] * 2, [VMEM] * 4 + [ANY], [VMEM] * 2, [], 0.3, "entering",
+    )(later, carry, befores[-1], message_other, totals)
+    carry_core = exchange(carry, "space", lanes, 1)
     size = plan.stack * members
     ens_factors, cot_factors, follow = call(
         functools.partial(carry_kernel, plan),
         [shape(len(plan.groups), size, size, kind=BF16)] * 2
         + [shape(2, count * members, members, kind=BF16)],
         [VMEM] * 2 + [ANY], [VMEM] * 3, [], 0.9, "carries",
-    )(suffixes, entering, own)
+    )(suffixes, entering, carry)
     def apply(factors, which, after, name):
         return call(
             functools.partial(apply_kernel, plan),
@@ -432,32 +462,19 @@
             0.5, name,
         )(factors, *(part[which] for part in parts), after)
 
-    smoothed, done = apply(ens_factors, 0, follow, "smoothed")
-    carry, grams[0] = call(
-        functools.partial(last_pass_kernel, levels - 1),
-        [square, wide], [VMEM] * 3 + [ANY] * 2, [VMEM, ANY], [], 0.2, "pass_last", aliases={4: 1},
-    )(other_own, carry, befores[-1], done, grams[0])
-    carry_core = exchange(carry, "space", lanes, 1)
-    for part in grams:
-        gram = gram + part
-    gram_core = exchange(gram, "space", lanes, 1)
-    steps = call(
-        functools.partial(windows_kernel, plan),
-        shape(2, count_steps(count) * members, members, kind=BF16), [VMEM, ANY], VMEM,
-        [pltpu.VMEM((count * members, members), F32)], 1.0, "windows",
-    )(kept, carry)
     carry = call(
         sum_kernel, square, [VMEM] * 2 + [ANY], VMEM, [], 0.1, "chip_carry",
-    )(carry, carry_core, steps)
+    )(carry, carry_core, follow)
     carries = [carry] + around(carry)
-    ensemble_grad, done = apply(cot_factors, 1, carry, "ensemble_grad")
+    smoothed, done = apply(ens_factors, 0, carry, "smoothed")
+    ensemble_grad, done = apply(cot_factors, 1, done, "ensemble_grad")
     transform_grad = call(
         functools.partial(final_kernel, plan, scale),
         shape(count, members, members),
-        [VMEM] * 4 + [ANY] + [VMEM] * chips, HBM,
+        [VMEM] * 3 + [ANY] + [VMEM] * chips, HBM,
         [pltpu.VMEM((count, members, members), F32), pltpu.SemaphoreType.DMA((count,))],
-        2.5, "transform_grad",
-    )(gram, gram_core, follow, steps, done, *carries)
+        1.5, "transform_grad",
+    )(totals, prefixes, follow, done, *carries)
     return (smoothed, ensemble_grad, transform_grad)
 
 

time: 35.7 us -> 38 us (1.064)
  waiting for transfers between devices: 1.08 us -> 5.1 us
  starting transfers between devices: 15.5 us -> 12.8 us
  Pallas kernels: 18 us -> 19.1 us
    ppermute x9 -> x8, starting transfers between devices: 12.3 us -> 9.59 us  [exchange(): return lax.ppermute(value, axis, [(at, at ^ bit) for at in range(size)])]
    ppermute x9 -> x8, waiting for transfers between devices: 1.08 us -> 3.27 us  [exchange(): return lax.ppermute(value, axis, [(at, at ^ bit) for at in range(size)])]
    ppermute x2, waiting for transfers between devices: 0.01 us -> 1.83 us  [around(): lax.ppermute(value, 'space', [(at, (at + 2 * d) % lanes) for at in range(...]
    pallas_call x5, Pallas kernels: 1.7 us -> 3.08 us  [the longest x1 1.27 us: shards(): call(functools.partial(windows_kernel, plan), [shape(2, count_steps(count...]
  transfers between devices with their start and end apart: 11 -> 10, of which waited for: 2 -> 4; matrix products, arithmetic and copies ran while one was open for 0% -> 0% of each run, Pallas kernels for 34% -> 35%
where the time goes in v15:
time: 38 us; the launch traced here: 37.8 us
  Pallas kernels  19.1 us (50%)
  starting transfers between devices  12.8 us (34%)
  waiting for transfers between devices  5.1 us (13%)
  between operations  0.78 us (2%)
    ppermute x8, starting transfers between devices, exchange(): return lax.ppermute(value, axis, [(at, at ^ bit) for at in range(size)])  9.59 us
    pallas_call x2, Pallas kernels, apply(): call(functools.partial(apply_kernel, plan), [shape(count, members, cells,...  5.44 us
    pallas_call x1, Pallas kernels, shards(): call(functools.partial(gram_kernel, plan), [wide, wide, square] + [piece_...  3.87 us
    pallas_call x1, Pallas kernels, shards(): call(functools.partial(chain_kernel, plan), [shape(count * members, membe...  3.36 us
    ppermute x8, waiting for transfers between devices, exchange(): return lax.ppermute(value, axis, [(at, at ^ bit) for at in range(size)])  3.27 us
    ppermute x2, starting transfers between devices, around(): lax.ppermute(value, 'space', [(at, (at + 2 * d) % lanes) for at in range(...  3.17 us
    pallas_call x1, Pallas kernels, shards(): call(functools.partial(final_kernel, plan, scale), shape(count, members,...  1.99 us
    ppermute x2, waiting for transfers between devices, around(): lax.ppermute(value, 'space', [(at, (at + 2 * d) % lanes) for at in range(...  1.83 us
  transfers between devices with their start and end apart: 10, of which 4 were waited for; matrix products, arithmetic and copies ran while one was open for 0% of the time, Pallas kernels for 35%

profile of v15, /device:TPU:0, one launch (start us, length us, event | category | flops | bytes accessed | tf_op | source)
XLA Modules:
  0.0 37.8 jit_solution(13966269694300229073)
XLA Ops:
  0.6 3.4 %transform_chain.1 = (f32[1280,80]{1,0:T(8,128)S(1)}, f32[80,80]{1,0:T(8,128)S(1)}, f32[16,80,80]{2,1,0:T(8,128)S(1)}, bf16[9,80,2048]{2,1,0:T(8,128)(2,1)S(1)}, bf16[9,80,2048]{2,1,0:T(8,128)(2,1)S(1)}) custom-call(f32[16,80,80]{2,1,0:T(8,128)} %transforms.1, bf16[16,80,2048]{2,1,0:T(8,128)(2,1)} %ensembles.3, bf16[16,80,2048]{2,1,0:T(8,128)(2,1)} %cotangents.3), custom_call_target="tpu_custom_call" | custom-call | flops 3500000000 | bytes 10500000 | tf_op jit(solution)/shard_map/transform_chain/pallas_call | solution.py:373
  4.0 3.0 %collective-permute-start = (f32[80,80]{1,0:T(8,128)S(1)}, f32[80,80]{1,0:T(8,128)S(1)}, u32[]{:S(2)}, u32[]{:S(2)}) collective-permute-start(f32[80,80]{1,0:T(8,128)S(1)} %get-tuple-element.38.total), channel_id=1, source_target_pairs={{0,4},{4,0},{8,12},{12,8},{16,20},{20,16},{24,28},{28,24},{1,5},{5... | collective-permute-start | bytes 76808 | tf_op jit(solution)/shard_map/ppermute | solution.py:358
  7.0 3.9 %gram.1 = (f32[40,1408]{1,0:T(8,128)S(1)}, f32[40,1408]{1,0:T(8,128)S(1)}, f32[80,80]{1,0:T(8,128)S(1)}, bf16[7,80,2048]{2,1,0:T(8,128)(2,1)S(1)}, bf16[7,80,2048]{2,1,0:T(8,128)(2,1)S(1)}) custom-call(bf16[16,80,2048]{2,1,0:T(8,128)(2,1)} %ensembles.3, bf16[16,80,2048]{2,1,0:T(8,128)(2,1)} %cotangents.3, f32[1280,80]{1,0:T(8,128)S(1)} %get-tuple-element.37.suffixes, ...), custom_call_target="tpu_custom_call" | custom-call | flops 4499999744 | bytes 13500000 | tf_op jit(solution)/shard_map/gram/pallas_call | solution.py:395
  10.9 0.1 collective-permute-start.2
  11.0 0.1 collective-permute-start.3
  11.1 0.0 collective-permute-done.other
  11.1 0.3 join_0.1
  11.3 2.1 %collective-permute-start.1 = (f32[80,80]{1,0:T(8,128)S(1)}, f32[80,80]{1,0:T(8,128)S(1)}, u32[]{:S(2)}, u32[]{:S(2)}) collective-permute-start(f32[80,80]{1,0:T(8,128)S(1)} %get-tuple-element.42._.total), channel_id=1, source_target_pairs={{0,8},{4,12},{8,0},{12,4},{16,24},{20,28},{24,16},{28,20},{1,9},{5... | collective-permute-start | bytes 76808 | tf_op jit(solution)/shard_map/ppermute | solution.py:358
  13.4 0.0 collective-permute-done.3.right
  13.4 1.6 %collective-permute-start.5 = (f32[40,1408]{1,0:T(8,128)S(1)}, f32[40,1408]{1,0:T(8,128)S(1)}, u32[]{:S(2)}, u32[]{:S(2)}) collective-permute-start(f32[40,1408]{1,0:T(8,128)S(1)} %chip_gram.1._), channel_id=1, source_target_pairs={{0,2},{1,3},{2,0},{3,1},{4,6},{5,7},{6,4},{7,5},{8,10},{9,11},{10,... | collective-permute-start | bytes 675848 | tf_op jit(solution)/shard_map/ppermute | solution.py:362
  15.0 0.0 collective-permute-done.2.other
  15.0 0.2 pass_0.1
  15.3 1.6 %collective-permute-start.4 = (f32[80,80]{1,0:T(8,128)S(1)}, f32[80,80]{1,0:T(8,128)S(1)}, u32[]{:S(2)}, u32[]{:S(2)}) collective-permute-start(f32[80,80]{1,0:T(8,128)S(1)} %get-tuple-element.48._.own), channel_id=1, source_target_pairs={{0,8},{4,12},{8,0},{12,4},{16,24},{20,28},{24,16},{28,20},{1,9},{5... | collective-permute-start | bytes 76808 | tf_op jit(solution)/shard_map/ppermute | solution.py:358
  16.8 0.0 collective-permute-done.1.other
  16.8 0.3 join_1.1
  17.1 2.2 %collective-permute-done.4.other = f32[80,80]{1,0:T(8,128)S(1)} collective-permute-done((f32[80,80]{1,0:T(8,128)S(1)}, f32[80,80]{1,0:T(8,128)S(1)}, u32[]{:S(2)}, u32[]{:S(2)}) %collective-permute-start.4) | collective-permute-done | bytes 25632 | tf_op jit(solution)/shard_map/ppermute | solution.py:358
  19.3 1.8 %collective-permute-done.5.__ = f32[40,1408]{1,0:T(8,128)S(1)} collective-permute-done((f32[40,1408]{1,0:T(8,128)S(1)}, f32[40,1408]{1,0:T(8,128)S(1)}, u32[]{:S(2)}, u32[]{:S(2)}) %collective-permute-start.5) | collective-permute-done | bytes 225312 | tf_op jit(solution)/shard_map/ppermute | solution.py:362
  21.1 0.2 pass_1.1
  21.4 0.1 collective-permute-start.7
  21.5 2.7 %collective-permute-start.6 = (f32[80,80]{1,0:T(8,128)S(1)}, f32[80,80]{1,0:T(8,128)S(1)}, u32[]{:S(2)}, u32[]{:S(2)}) collective-permute-start(f32[80,80]{1,0:T(8,128)S(1)} %get-tuple-element.55._), channel_id=1, source_target_pairs={{0,16},{4,20},{8,24},{12,28},{16,0},{20,4},{24,8},{28,12},{1,17},{... | collective-permute-start | bytes 76808 | tf_op jit(solution)/shard_map/ppermute | solution.py:358
  24.1 1.3 %windows.1 = (bf16[2,2560,80]{2,1,0:T(8,128)(2,1)S(1)}, bf16[2,1200,80]{2,1,0:T(8,128)(2,1)S(1)}) custom-call(f32[16,80,80]{2,1,0:T(8,128)S(1)} %get-tuple-element.57.kept, f32[80,80]{1,0:T(8,128)S(1)} %get-tuple-element.55._), custom_call_target="tpu_custom_call" | custom-call | flops 1300000000 | bytes 3900000 | tf_op jit(solution)/shard_map/windows/pallas_call | solution.py:432
  25.4 0.0 collective-permute-done.7.gram_core
  25.4 1.2 %scan.1._.totals = f32[16,80,80]{2,1,0:T(8,128)S(1)} custom-call(f32[40,1408]{1,0:T(8,128)S(1)} %add.3.gram, f32[40,1408]{1,0:T(8,128)S(1)} %collective-permute-done.7.gram_core, bf16[2,2560,80]{2,1,0:T(8,128)(2,1)S(1)} %get-tuple-element.58.steps), custom_call_target="tpu_custom_call" | custom-call | flops 1200000000 | bytes 3600000 | tf_op jit(solution)/shard_map/scan/pallas_call | solution.py:439
  26.6 0.7 %collective-permute-done.6.message = f32[80,80]{1,0:T(8,128)S(1)} collective-permute-done((f32[80,80]{1,0:T(8,128)S(1)}, f32[80,80]{1,0:T(8,128)S(1)}, u32[]{:S(2)}, u32[]{:S(2)}) %collective-permute-start.6) | collective-permute-done | bytes 25632 | tf_op jit(solution)/shard_map/ppermute | solution.py:358
  27.3 0.2 entering.1
  27.5 0.1 collective-permute-start.8
  27.6 0.8 %carries.1 = (bf16[6,240,240]{2,1,0:T(8,128)(2,1)S(1)}, bf16[6,240,240]{2,1,0:T(8,128)(2,1)S(1)}, bf16[2,1280,80]{2,1,0:T(8,128)(2,1)S(1)}) custom-call(f32[1280,80]{1,0:T(8,128)S(1)} %get-tuple-element.37.suffixes, f32[80,80]{1,0:T(8,128)S(1)} %get-tuple-element.59.later, f32[80,80]{1,0:T(8,128)S(1)} %get-tuple-element.60._.left), custom_call_target="tpu_custom_call" | custom-call | flops 900000000 | bytes 2700000 | tf_op jit(solution)/shard_map/carries/pallas_call | solution.py:449
  28.4 0.4 collective-permute-done.8.right
  28.8 1.6 %collective-permute-start.9 = (f32[80,80]{1,0:T(8,128)S(1)}, f32[80,80]{1,0:T(8,128)S(1)}, u32[]{:S(2)}, u32[]{:S(2)}) collective-permute-start(f32[80,80]{1,0:T(8,128)S(1)} %chip_carry.1.refs_2_.refs_0_), channel_id=1, source_target_pairs={{0,2},{1,3},{2,0},{3,1},{4,6},{5,7},{6,4},{7,5},{8,10},{9,11},{10,... | collective-permute-start | bytes 76808 | tf_op jit(solution)/shard_map/ppermute | solution.py:362
  30.4 2.7 %smoothed.1 = (bf16[16,80,2048]{2,1,0:T(8,128)(2,1)}, f32[8,128]{1,0:T(8,128)S(1)}) custom-call(bf16[6,240,240]{2,1,0:T(8,128)(2,1)S(1)} %get-tuple-element.61.factors, bf16[9,80,2048]{2,1,0:T(8,128)(2,1)S(1)} %get-tuple-element.39.ens.refs_0_, bf16[7,80,2048]{2,1,0:T(8,128)(2,1)S(1)} %get-tuple-element.62.refs_1_, f32[80,80]{1,0:T(8,128)S(1)} %chip_carry.1.refs_2_.refs_0_), custom_call_target="tpu_custom_call" | custom-call | flops 500000000 | bytes 1500000 | tf_op jit(solution)/shard_map/smoothed/pallas_call | solution.py:456
  33.1 2.7 %ensemble_grad.1 = (bf16[16,80,2048]{2,1,0:T(8,128)(2,1)}, f32[8,128]{1,0:T(8,128)S(1)}) custom-call(bf16[6,240,240]{2,1,0:T(8,128)(2,1)S(1)} %get-tuple-element.65.factors, bf16[9,80,2048]{2,1,0:T(8,128)(2,1)S(1)} %get-tuple-element.40.cot.refs_0_, bf16[7,80,2048]{2,1,0:T(8,128)(2,1)S(1)} %get-tuple-element.66.refs_1_, f32[8,128]{1,0:T(8,128)S(1)} %get-tuple-element.67.refs_2_), custom_call_target="tpu_custom_call" | custom-call | flops 500000000 | bytes 1500000 | tf_op jit(solution)/shard_map/ensemble_grad/pallas_call | solution.py:456
  35.8 0.0 collective-permute-done.9.refs_1_
  35.8 2.0 %transform_grad.1 = f32[16,80,80]{2,1,0:T(8,128)} custom-call(f32[16,80,80]{2,1,0:T(8,128)S(1)} %scan.1._.totals, bf16[2,1200,80]{2,1,0:T(8,128)(2,1)S(1)} %get-tuple-element.69.prefixes, bf16[2,1280,80]{2,1,0:T(8,128)(2,1)S(1)} %get-tuple-element.63._.follow, f32[8,128]{1,0:T(8,128)S(1)} %get-tuple-element.70._, f32[80,80]{1,0:T(8,128)S(1)} %chip_carry.1.refs_2_.refs_0_, ...), custom_call_target="tpu_custom_call" | custom-call | flops 1500000000 | bytes 4500000 | tf_op jit(solution)/shard_map/transform_grad/pallas_call | solution.py:471
  (5 shorter events, 0.1 us)
Async XLA Ops:
  4.0 7.1 %collective-permute-start = (f32[80,80]{1,0:T(8,128)S(1)}, f32[80,80]{1,0:T(8,128)S(1)}, u32[]{:S(2)}, u32[]{:S(2)}) collective-permute-start(f32[80,80]{1,0:T(8,128)S(1)} %get-tuple-element.38.total), channel_id=1, source_target_pairs={{0,4},{4,0},{8,12},{12,8},{16,20},{20,16},{24,28},{28,24},{1,5},{5... | collective-permute-start | bytes 76808 | tf_op jit(solution)/shard_map/ppermute | solution.py:358
  10.9 4.1 %collective-permute-start.2 = (f32[80,80]{1,0:T(8,128)S(1)}, f32[80,80]{1,0:T(8,128)S(1)}, u32[]{:S(2)}, u32[]{:S(2)}) collective-permute-start(f32[80,80]{1,0:T(8,128)S(1)} %get-tuple-element.41._.own), channel_id=1, source_target_pairs={{0,4},{4,0},{8,12},{12,8},{16,20},{20,16},{24,28},{28,24},{1,5},{5... | collective-permute-start | bytes 76808 | tf_op jit(solution)/shard_map/ppermute | solution.py:358
  11.0 2.5 %collective-permute-start.3 = (f32[40,1408]{1,0:T(8,128)S(1)}, f32[40,1408]{1,0:T(8,128)S(1)}, u32[]{:S(2)}, u32[]{:S(2)}) collective-permute-start(f32[40,1408]{1,0:T(8,128)S(1)} %get-tuple-element.47), channel_id=1, source_target_pairs={{0,1},{1,0},{2,3},{3,2},{4,5},{5,4},{6,7},{7,6},{8,9},{9,8},{10,11... | collective-permute-start | bytes 675848 | tf_op jit(solution)/shard_map/ppermute | solution.py:358
  11.3 5.5 %collective-permute-start.1 = (f32[80,80]{1,0:T(8,128)S(1)}, f32[80,80]{1,0:T(8,128)S(1)}, u32[]{:S(2)}, u32[]{:S(2)}) collective-permute-start(f32[80,80]{1,0:T(8,128)S(1)} %get-tuple-element.42._.total), channel_id=1, source_target_pairs={{0,8},{4,12},{8,0},{12,4},{16,24},{20,28},{24,16},{28,20},{1,9},{5... | collective-permute-start | bytes 76808 | tf_op jit(solution)/shard_map/ppermute | solution.py:358
  13.4 7.7 %collective-permute-start.5 = (f32[40,1408]{1,0:T(8,128)S(1)}, f32[40,1408]{1,0:T(8,128)S(1)}, u32[]{:S(2)}, u32[]{:S(2)}) collective-permute-start(f32[40,1408]{1,0:T(8,128)S(1)} %chip_gram.1._), channel_id=1, source_target_pairs={{0,2},{1,3},{2,0},{3,1},{4,6},{5,7},{6,4},{7,5},{8,10},{9,11},{10,... | collective-permute-start | bytes 675848 | tf_op jit(solution)/shard_map/ppermute | solution.py:362
  15.3 4.1 %collective-permute-start.4 = (f32[80,80]{1,0:T(8,128)S(1)}, f32[80,80]{1,0:T(8,128)S(1)}, u32[]{:S(2)}, u32[]{:S(2)}) collective-permute-start(f32[80,80]{1,0:T(8,128)S(1)} %get-tuple-element.48._.own), channel_id=1, source_target_pairs={{0,8},{4,12},{8,0},{12,4},{16,24},{20,28},{24,16},{28,20},{1,9},{5... | collective-permute-start | bytes 76808 | tf_op jit(solution)/shard_map/ppermute | solution.py:358
  21.4 4.0 %collective-permute-start.7 = (f32[40,1408]{1,0:T(8,128)S(1)}, f32[40,1408]{1,0:T(8,128)S(1)}, u32[]{:S(2)}, u32[]{:S(2)}) collective-permute-start(f32[40,1408]{1,0:T(8,128)S(1)} %add.3.gram), channel_id=1, source_target_pairs={{0,1},{1,0},{2,3},{3,2},{4,5},{5,4},{6,7},{7,6},{8,9},{9,8},{10,11... | collective-permute-start | bytes 675848 | tf_op jit(solution)/shard_map/ppermute | solution.py:358
  21.5 5.8 %collective-permute-start.6 = (f32[80,80]{1,0:T(8,128)S(1)}, f32[80,80]{1,0:T(8,128)S(1)}, u32[]{:S(2)}, u32[]{:S(2)}) collective-permute-start(f32[80,80]{1,0:T(8,128)S(1)} %get-tuple-element.55._), channel_id=1, source_target_pairs={{0,16},{4,20},{8,24},{12,28},{16,0},{20,4},{24,8},{28,12},{1,17},{... | collective-permute-start | bytes 76808 | tf_op jit(solution)/shard_map/ppermute | solution.py:358
  27.5 1.3 %collective-permute-start.8 = (f32[80,80]{1,0:T(8,128)S(1)}, f32[80,80]{1,0:T(8,128)S(1)}, u32[]{:S(2)}, u32[]{:S(2)}) collective-permute-start(f32[80,80]{1,0:T(8,128)S(1)} %get-tuple-element.60._.left), channel_id=1, source_target_pairs={{0,1},{1,0},{2,3},{3,2},{4,5},{5,4},{6,7},{7,6},{8,9},{9,8},{10,11... | collective-permute-start | bytes 76808 | tf_op jit(solution)/shard_map/ppermute | solution.py:358
  28.8 7.0 %collective-permute-start.9 = (f32[80,80]{1,0:T(8,128)S(1)}, f32[80,80]{1,0:T(8,128)S(1)}, u32[]{:S(2)}, u32[]{:S(2)}) collective-permute-start(f32[80,80]{1,0:T(8,128)S(1)} %chip_carry.1.refs_2_.refs_0_), channel_id=1, source_target_pairs={{0,2},{1,3},{2,0},{3,1},{4,6},{5,7},{6,4},{7,5},{8,10},{9,11},{10,... | collective-permute-start | bytes 76808 | tf_op jit(solution)/shard_map/ppermute | solution.py:362

commit v16 on v14

--- a/solution.py
+++ b/solution.py
@@ -63,7 +63,7 @@
         self.groups = [
             (start, min(start + self.stack, count)) for start in range(0, count, self.stack)
         ]
-        bounds = [len(self.groups) * at // PIECES for at in range(PIECES + 1)]
+        bounds = [0, len(self.groups) // 3, len(self.groups)]
         self.piece_groups = [self.groups[a:b] for a, b in zip(bounds, bounds[1:])]
         self.pieces = [(part[0][0], part[-1][1]) for part in self.piece_groups]
         self.first_group = bounds[:-1]
@@ -76,6 +76,29 @@
 
     def rows(self, first, last):
         return slice(first * self.members, last * self.members)
+
+
+def packing(members):
+    spare = 128 - members
+    strips = -(-members // spare)
+    rest = members // (strips + 1) // 8 * 8
+    return spare, strips, rest, members - rest
+
+
+def pack(value):
+    members = value.shape[0]
+    spare, strips, rest, rows = packing(members)
+    side = [value[rows:, at * spare : (at + 1) * spare] for at in range(strips)]
+    side = [jnp.pad(part, ((0, 0), (0, spare - part.shape[1]))) for part in side]
+    side.append(jnp.zeros((rows - strips * rest, spare), value.dtype))
+    return jnp.concatenate([value[:rows], jnp.concatenate(side, axis=0)], axis=1)
+
+
+def unpack(value, members):
+    spare, strips, rest, rows = packing(members)
+    side = [value[at * rest : (at + 1) * rest, members:] for at in range(strips)]
+    last = jnp.concatenate(side, axis=1)[:, :members]
+    return jnp.concatenate([value[:, :members], last], axis=0)
 
 
 def on_blocks(members, size):
@@ -189,12 +212,12 @@
     return lax.rem(lax.axis_index("tm") // (1 << level), 2) == 1
 
 
-def join_kernel(level, total, other, later, before, _, *refs):
-    new_total, new_later, new_before, upper_total = refs[len(refs) // 2 - 2 : len(refs) // 2 + 2]
+def join_kernel(level, last, total, other, later, before, _, new_total, new_later, new_before, upper_total):
     upper = upper_half(level)
     left = jnp.where(upper, other[...], total[...])
     right = jnp.where(upper, total[...], other[...])
-    new_total[...] = mul_exact(left, right)
+    joined = mul_exact(left, right)
+    new_total[...] = pack(joined) if last else joined
     upper_total[...] = right
     new_later[...] = jnp.where(upper, later[...], mul_exact(later[...], other[...]))
     new_before[...] = jnp.where(upper, mul_exact(other[...], before[...]), before[...])
@@ -204,22 +227,22 @@
     total[...] = left[...] + right[...]
 
 
-def pass_kernel(level, own, other, carry, upper_total, before, _, *refs):
-    new_own, new_carry = refs[len(refs) // 2 - 1 : len(refs) // 2 + 1]
+def pass_kernel(level, last, own, other, carry, upper_total, before, _, new_own, new_carry):
     upper = upper_half(level)
     left = jnp.where(upper, other[...], own[...])
     right = jnp.where(upper, own[...], other[...])
-    new_own[...] = mul_exact(left, upper_total[...]) + right
+    passed = mul_exact(left, upper_total[...]) + right
+    new_own[...] = pack(passed) if last else passed
     new_carry[...] = carry[...] + jnp.where(upper, mul_exact(left, before[...]), 0.0)
 
 
 def last_pass_kernel(level, other, carry, before, _, __, new_carry, ___):
-    added = mul_exact(other[...], before[...])
+    added = mul_exact(unpack(other[...], before.shape[0]), before[...])
     new_carry[...] = carry[...] + jnp.where(upper_half(level), added, 0.0)
 
 
 def enter_kernel(level, later, other, _, entering):
-    joined = mul_exact(later[...], other[...])
+    joined = mul_exact(later[...], unpack(other[...], later.shape[0]))
     entering[...] = jnp.where(upper_half(level), later[...], joined)
 
 
@@ -366,16 +389,18 @@
     later = before = jnp.eye(members, dtype=F32)
     uppers, befores = [], []
 
-    def join(level, total, other, later, before, after, *through):
-        more = [shape(*value.shape) for value in through]
+    packed = shape(packing(members)[3], 128)
+
+    def join(level, total, other, later, before, after):
         befores.append(before)
-        total, later, before, upper, *through = call(
-            functools.partial(join_kernel, level),
-            [square] * 4 + more, [VMEM] * 4 + [ANY] * (1 + len(more)), [VMEM] * 4 + [ANY] * len(more),
-            [], 3, f"join_{level}", aliases={5 + at: 4 + at for at in range(len(more))},
-        )(total, other, later, before, after, *through)
+        last = level == levels - 2
+        total, later, before, upper = call(
+            functools.partial(join_kernel, level, last),
+            [packed if last else square] + [square] * 3, [VMEM] * 4 + [ANY], [VMEM] * 4,
+            [], 3, f"join_{level}",
+        )(total, other, later, before, after)
         uppers.append(upper)
-        return total, later, before, *through
+        return total, later, before
 
     other = exchange(total, "tm", blocks, 1)
     gram, gram_sent, own, *second_part = call(
@@ -392,13 +417,12 @@
     gram = call(sum_kernel, wide, [VMEM] * 2 + [ANY], VMEM, [], 0.1, "chip_gram")(gram, gram_core, total)
     grams = around(gram)
 
-    def pass_on(level, carry, after, *through):
-        more = [shape(*value.shape) for value in through]
+    def pass_on(level, carry, after):
+        last = level == levels - 2
         return call(
-            functools.partial(pass_kernel, level),
-            [square] * 2 + more, [VMEM] * 5 + [ANY] * (1 + len(more)), [VMEM] * 2 + [ANY] * len(more),
-            [], 3, f"pass_{level}", aliases={6 + at: 2 + at for at in range(len(more))},
-        )(own, other_own, carry, uppers[level], befores[level], after, *through)
+            functools.partial(pass_kernel, level, last),
+            [packed if last else square, square], [VMEM] * 5 + [ANY], [VMEM] * 2, [], 3, f"pass_{level}",
+        )(own, other_own, carry, uppers[level], befores[level], after)
 
     carry = jnp.zeros((members, members), F32)
     after = gram

time: 35.7 us -> 34.7 us (0.972)
  waiting for transfers between devices: 1.08 us -> 0.11 us
    ppermute x9, waiting for transfers between devices: 1.08 us -> 0.1 us  [exchange(): return lax.ppermute(value, axis, [(at, at ^ bit) for at in range(size)])]
    pallas_call x1, Pallas kernels: 3.36 us -> 2.78 us  [shards(): call(functools.partial(chain_kernel, plan), [shape(count * members, membe...]
    pallas_call x1, Pallas kernels: 3.87 us -> 4.32 us  [shards(): call(functools.partial(gram_kernel, plan), [wide, wide, square] + [piece_...]
  transfers between devices with their start and end apart: 11 -> 11, of which waited for: 2 -> 1; matrix products, arithmetic and copies ran while one was open for 0% -> 0% of each run, Pallas kernels for 34% -> 38%
where the time goes in v16:
time: 34.7 us; the launch traced here: 34.5 us
  Pallas kernels  18.2 us (52%)
  starting transfers between devices  15.4 us (44%)
  between operations  0.78 us (2%)
    ppermute x9, starting transfers between devices, exchange(): return lax.ppermute(value, axis, [(at, at ^ bit) for at in range(size)])  12.2 us
    pallas_call x2, Pallas kernels, apply(): call(functools.partial(apply_kernel, plan), [shape(count, members, cells,...  5.43 us
    pallas_call x1, Pallas kernels, shards(): call(functools.partial(gram_kernel, plan), [wide, wide, square] + [piece_...  4.32 us
    ppermute x2, starting transfers between devices, around(): lax.ppermute(value, 'space', [(at, (at + 2 * d) % lanes) for at in range(...  3.15 us
    pallas_call x1, Pallas kernels, shards(): call(functools.partial(chain_kernel, plan), [shape(count * members, membe...  2.78 us
    pallas_call x1, Pallas kernels, shards(): call(functools.partial(final_kernel, plan, scale), shape(count, members,...  2.29 us
    pallas_call x1, Pallas kernels, shards(): call(functools.partial(windows_kernel, plan), shape(2, count_steps(count)...  0.94 us
    pallas_call x1, Pallas kernels, shards(): call(functools.partial(carry_kernel, plan), [shape(len(plan.groups), size...  0.86 us
  transfers between devices with their start and end apart: 11, of which 1 were waited for; matrix products, arithmetic and copies ran while one was open for 0% of the time, Pallas kernels for 38%

profile of v16, /device:TPU:0, one launch (start us, length us, event | category | flops | bytes accessed | tf_op | source)
XLA Modules:
  0.0 34.5 jit_solution(11303349742659587984)
XLA Ops:
  0.6 2.8 %transform_chain.1 = (f32[1280,80]{1,0:T(8,128)S(1)}, f32[80,80]{1,0:T(8,128)S(1)}, f32[16,80,80]{2,1,0:T(8,128)S(1)}, bf16[6,80,2048]{2,1,0:T(8,128)(2,1)S(1)}, bf16[6,80,2048]{2,1,0:T(8,128)(2,1)S(1)}) custom-call(f32[16,80,80]{2,1,0:T(8,128)} %transforms.1, bf16[16,80,2048]{2,1,0:T(8,128)(2,1)} %ensembles.3, bf16[16,80,2048]{2,1,0:T(8,128)(2,1)} %cotangents.3), custom_call_target="tpu_custom_call" | custom-call | flops 3500000000 | bytes 10500000 | tf_op jit(solution)/shard_map/transform_chain/pallas_call | solution.py:382
  3.4 3.0 %collective-permute-start = (f32[80,80]{1,0:T(8,128)S(1)}, f32[80,80]{1,0:T(8,128)S(1)}, u32[]{:S(2)}, u32[]{:S(2)}) collective-permute-start(f32[80,80]{1,0:T(8,128)S(1)} %get-tuple-element.35.total), channel_id=1, source_target_pairs={{0,4},{4,0},{8,12},{12,8},{16,20},{20,16},{24,28},{28,24},{1,5},{5... | collective-permute-start | bytes 76808 | tf_op jit(solution)/shard_map/ppermute | solution.py:367
  6.4 4.3 %gram.1 = (f32[40,1408]{1,0:T(8,128)S(1)}, f32[40,1408]{1,0:T(8,128)S(1)}, f32[80,80]{1,0:T(8,128)S(1)}, bf16[10,80,2048]{2,1,0:T(8,128)(2,1)S(1)}, bf16[10,80,2048]{2,1,0:T(8,128)(2,1)S(1)}) custom-call(bf16[16,80,2048]{2,1,0:T(8,128)(2,1)} %ensembles.3, bf16[16,80,2048]{2,1,0:T(8,128)(2,1)} %cotangents.3, f32[1280,80]{1,0:T(8,128)S(1)} %get-tuple-element.34.suffixes, ...), custom_call_target="tpu_custom_call" | custom-call | flops 4499999744 | bytes 13500000 | tf_op jit(solution)/shard_map/gram/pallas_call | solution.py:406
  10.7 0.1 collective-permute-start.3
  10.8 0.1 collective-permute-start.2
  10.9 0.0 collective-permute-done.other
  10.9 0.3 join_0.1
  11.2 2.2 %collective-permute-start.1 = (f32[80,80]{1,0:T(8,128)S(1)}, f32[80,80]{1,0:T(8,128)S(1)}, u32[]{:S(2)}, u32[]{:S(2)}) collective-permute-start(f32[80,80]{1,0:T(8,128)S(1)} %get-tuple-element.39._.total), channel_id=1, source_target_pairs={{0,8},{4,12},{8,0},{12,4},{16,24},{20,28},{24,16},{28,20},{1,9},{5... | collective-permute-start | bytes 76808 | tf_op jit(solution)/shard_map/ppermute | solution.py:367
  13.3 0.0 collective-permute-done.3.right
  13.4 1.6 %collective-permute-start.7 = (f32[40,1408]{1,0:T(8,128)S(1)}, f32[40,1408]{1,0:T(8,128)S(1)}, u32[]{:S(2)}, u32[]{:S(2)}) collective-permute-start(f32[40,1408]{1,0:T(8,128)S(1)} %chip_gram.1._), channel_id=1, source_target_pairs={{0,2},{1,3},{2,0},{3,1},{4,6},{5,7},{6,4},{7,5},{8,10},{9,11},{10,... | collective-permute-start | bytes 675848 | tf_op jit(solution)/shard_map/ppermute | solution.py:371
  15.0 0.0 collective-permute-done.2.other
  15.0 0.2 pass_0.1
  15.2 1.6 %collective-permute-start.5 = (f32[80,80]{1,0:T(8,128)S(1)}, f32[80,80]{1,0:T(8,128)S(1)}, u32[]{:S(2)}, u32[]{:S(2)}) collective-permute-start(f32[80,80]{1,0:T(8,128)S(1)} %get-tuple-element.45._.own), channel_id=1, source_target_pairs={{0,8},{4,12},{8,0},{12,4},{16,24},{20,28},{24,16},{28,20},{1,9},{5... | collective-permute-start | bytes 76808 | tf_op jit(solution)/shard_map/ppermute | solution.py:367
  16.8 0.0 collective-permute-done.1.other
  16.8 0.3 join_1.1
  17.1 2.6 %collective-permute-start.4 = (f32[56,128]{1,0:T(8,128)S(1)}, f32[56,128]{1,0:T(8,128)S(1)}, u32[]{:S(2)}, u32[]{:S(2)}) collective-permute-start(f32[56,128]{1,0:T(8,128)S(1)} %get-tuple-element.47._), channel_id=1, source_target_pairs={{0,16},{4,20},{8,24},{12,28},{16,0},{20,4},{24,8},{28,12},{1,17},{... | collective-permute-start | bytes 86024 | tf_op jit(solution)/shard_map/ppermute | solution.py:367
  19.7 0.0 collective-permute-done.5.other
  19.7 0.3 pass_1.1
  20.0 2.2 %collective-permute-start.6 = (f32[56,128]{1,0:T(8,128)S(1)}, f32[56,128]{1,0:T(8,128)S(1)}, u32[]{:S(2)}, u32[]{:S(2)}) collective-permute-start(f32[56,128]{1,0:T(8,128)S(1)} %get-tuple-element.50._), channel_id=1, source_target_pairs={{0,16},{4,20},{8,24},{12,28},{16,0},{20,4},{24,8},{28,12},{1,17},{... | collective-permute-start | bytes 86024 | tf_op jit(solution)/shard_map/ppermute | solution.py:367
  22.2 0.0 collective-permute-done.4.other
  22.2 0.2 entering.1.later
  22.4 0.9 %carries.1 = (bf16[6,240,240]{2,1,0:T(8,128)(2,1)S(1)}, bf16[6,240,240]{2,1,0:T(8,128)(2,1)S(1)}, bf16[2,1280,80]{2,1,0:T(8,128)(2,1)S(1)}) custom-call(f32[1280,80]{1,0:T(8,128)S(1)} %get-tuple-element.34.suffixes, f32[80,80]{1,0:T(8,128)S(1)} %entering.1.later, f32[56,128]{1,0:T(8,128)S(1)} %get-tuple-element.50._), custom_call_target="tpu_custom_call" | custom-call | flops 900000000 | bytes 2700000 | tf_op jit(solution)/shard_map/carries/pallas_call | solution.py:443
  23.3 2.7 %smoothed.1 = (bf16[16,80,2048]{2,1,0:T(8,128)(2,1)}, f32[8,128]{1,0:T(8,128)S(1)}) custom-call(bf16[6,240,240]{2,1,0:T(8,128)(2,1)S(1)} %get-tuple-element.51.factors, bf16[6,80,2048]{2,1,0:T(8,128)(2,1)S(1)} %get-tuple-element.36.ens.refs_0_, bf16[10,80,2048]{2,1,0:T(8,128)(2,1)S(1)} %get-tuple-element.52.refs_1_, ...), custom_call_target="tpu_custom_call" | custom-call | flops 500000000 | bytes 1500000 | tf_op jit(solution)/shard_map/smoothed/pallas_call | solution.py:450
  26.0 0.0 collective-permute-done.6.other
  26.0 0.0 collective-permute-done.7.__
  26.0 0.2 pass_last.1
  26.3 0.1 collective-permute-start.9
  26.4 0.5 %collective-permute-start.8 = (f32[80,80]{1,0:T(8,128)S(1)}, f32[80,80]{1,0:T(8,128)S(1)}, u32[]{:S(2)}, u32[]{:S(2)}) collective-permute-start(f32[80,80]{1,0:T(8,128)S(1)} %get-tuple-element.60._.left), channel_id=1, source_target_pairs={{0,1},{1,0},{2,3},{3,2},{4,5},{5,4},{6,7},{7,6},{8,9},{9,8},{10,11... | collective-permute-start | bytes 76808 | tf_op jit(solution)/shard_map/ppermute | solution.py:367
  26.9 0.9 %windows.1._.steps = bf16[2,2560,80]{2,1,0:T(8,128)(2,1)S(1)} custom-call(f32[16,80,80]{2,1,0:T(8,128)S(1)} %get-tuple-element.61.kept, f32[80,80]{1,0:T(8,128)S(1)} %get-tuple-element.60._.left), custom_call_target="tpu_custom_call" | custom-call | flops 1000000000 | bytes 3000000 | tf_op jit(solution)/shard_map/windows/pallas_call | solution.py:468
  27.8 0.1 collective-permute-done.8.right
  27.9 1.6 %collective-permute-start.10 = (f32[80,80]{1,0:T(8,128)S(1)}, f32[80,80]{1,0:T(8,128)S(1)}, u32[]{:S(2)}, u32[]{:S(2)}) collective-permute-start(f32[80,80]{1,0:T(8,128)S(1)} %chip_carry.1.refs_2_.refs_0_), channel_id=1, source_target_pairs={{0,2},{1,3},{2,0},{3,1},{4,6},{5,7},{6,4},{7,5},{8,10},{9,11},{10,... | collective-permute-start | bytes 76808 | tf_op jit(solution)/shard_map/ppermute | solution.py:371
  29.5 2.7 %ensemble_grad.1 = (bf16[16,80,2048]{2,1,0:T(8,128)(2,1)}, f32[8,128]{1,0:T(8,128)S(1)}) custom-call(bf16[6,240,240]{2,1,0:T(8,128)(2,1)S(1)} %get-tuple-element.55.factors, bf16[6,80,2048]{2,1,0:T(8,128)(2,1)S(1)} %get-tuple-element.37.cot.refs_0_, bf16[10,80,2048]{2,1,0:T(8,128)(2,1)S(1)} %get-tuple-element.56.refs_1_, f32[80,80]{1,0:T(8,128)S(1)} %chip_carry.1.refs_2_.refs_0_), custom_call_target="tpu_custom_call" | custom-call | flops 500000000 | bytes 1500000 | tf_op jit(solution)/shard_map/ensemble_grad/pallas_call | solution.py:450
  32.2 0.0 collective-permute-done.10.refs_1_
  32.2 0.0 collective-permute-done.9.gram_core
  32.2 2.3 %transform_grad.1 = f32[16,80,80]{2,1,0:T(8,128)} custom-call(f32[40,1408]{1,0:T(8,128)S(1)} %add.3.gram, f32[40,1408]{1,0:T(8,128)S(1)} %collective-permute-done.9.gram_core, bf16[2,1280,80]{2,1,0:T(8,128)(2,1)S(1)} %get-tuple-element.53.refs_2_.follow, bf16[2,2560,80]{2,1,0:T(8,128)(2,1)S(1)} %windows.1._.steps, f32[8,128]{1,0:T(8,128)S(1)} %get-tuple-element.64._, ...), custom_call_target="tpu_custom_call" | custom-call | flops 2500000000 | bytes 7500000 | tf_op jit(solution)/shard_map/transform_grad/pallas_call | solution.py:478
  (5 shorter events, 0.1 us)
Async XLA Ops:
  3.4 7.5 %collective-permute-start = (f32[80,80]{1,0:T(8,128)S(1)}, f32[80,80]{1,0:T(8,128)S(1)}, u32[]{:S(2)}, u32[]{:S(2)}) collective-permute-start(f32[80,80]{1,0:T(8,128)S(1)} %get-tuple-element.35.total), channel_id=1, source_target_pairs={{0,4},{4,0},{8,12},{12,8},{16,20},{20,16},{24,28},{28,24},{1,5},{5... | collective-permute-start | bytes 76808 | tf_op jit(solution)/shard_map/ppermute | solution.py:367
  10.7 2.6 %collective-permute-start.3 = (f32[40,1408]{1,0:T(8,128)S(1)}, f32[40,1408]{1,0:T(8,128)S(1)}, u32[]{:S(2)}, u32[]{:S(2)}) collective-permute-start(f32[40,1408]{1,0:T(8,128)S(1)} %get-tuple-element.44), channel_id=1, source_target_pairs={{0,1},{1,0},{2,3},{3,2},{4,5},{5,4},{6,7},{7,6},{8,9},{9,8},{10,11... | collective-permute-start | bytes 675848 | tf_op jit(solution)/shard_map/ppermute | solution.py:367
  10.8 4.1 %collective-permute-start.2 = (f32[80,80]{1,0:T(8,128)S(1)}, f32[80,80]{1,0:T(8,128)S(1)}, u32[]{:S(2)}, u32[]{:S(2)}) collective-permute-start(f32[80,80]{1,0:T(8,128)S(1)} %get-tuple-element.38._.own), channel_id=1, source_target_pairs={{0,4},{4,0},{8,12},{12,8},{16,20},{20,16},{24,28},{28,24},{1,5},{5... | collective-permute-start | bytes 76808 | tf_op jit(solution)/shard_map/ppermute | solution.py:367
  11.2 5.6 %collective-permute-start.1 = (f32[80,80]{1,0:T(8,128)S(1)}, f32[80,80]{1,0:T(8,128)S(1)}, u32[]{:S(2)}, u32[]{:S(2)}) collective-permute-start(f32[80,80]{1,0:T(8,128)S(1)} %get-tuple-element.39._.total), channel_id=1, source_target_pairs={{0,8},{4,12},{8,0},{12,4},{16,24},{20,28},{24,16},{28,20},{1,9},{5... | collective-permute-start | bytes 76808 | tf_op jit(solution)/shard_map/ppermute | solution.py:367
  13.4 12.7 %collective-permute-start.7 = (f32[40,1408]{1,0:T(8,128)S(1)}, f32[40,1408]{1,0:T(8,128)S(1)}, u32[]{:S(2)}, u32[]{:S(2)}) collective-permute-start(f32[40,1408]{1,0:T(8,128)S(1)} %chip_gram.1._), channel_id=1, source_target_pairs={{0,2},{1,3},{2,0},{3,1},{4,6},{5,7},{6,4},{7,5},{8,10},{9,11},{10,... | collective-permute-start | bytes 675848 | tf_op jit(solution)/shard_map/ppermute | solution.py:371
  15.2 4.5 %collective-permute-start.5 = (f32[80,80]{1,0:T(8,128)S(1)}, f32[80,80]{1,0:T(8,128)S(1)}, u32[]{:S(2)}, u32[]{:S(2)}) collective-permute-start(f32[80,80]{1,0:T(8,128)S(1)} %get-tuple-element.45._.own), channel_id=1, source_target_pairs={{0,8},{4,12},{8,0},{12,4},{16,24},{20,28},{24,16},{28,20},{1,9},{5... | collective-permute-start | bytes 76808 | tf_op jit(solution)/shard_map/ppermute | solution.py:367
  17.1 5.1 %collective-permute-start.4 = (f32[56,128]{1,0:T(8,128)S(1)}, f32[56,128]{1,0:T(8,128)S(1)}, u32[]{:S(2)}, u32[]{:S(2)}) collective-permute-start(f32[56,128]{1,0:T(8,128)S(1)} %get-tuple-element.47._), channel_id=1, source_target_pairs={{0,16},{4,20},{8,24},{12,28},{16,0},{20,4},{24,8},{28,12},{1,17},{... | collective-permute-start | bytes 86024 | tf_op jit(solution)/shard_map/ppermute | solution.py:367
  20.0 6.0 %collective-permute-start.6 = (f32[56,128]{1,0:T(8,128)S(1)}, f32[56,128]{1,0:T(8,128)S(1)}, u32[]{:S(2)}, u32[]{:S(2)}) collective-permute-start(f32[56,128]{1,0:T(8,128)S(1)} %get-tuple-element.50._), channel_id=1, source_target_pairs={{0,16},{4,20},{8,24},{12,28},{16,0},{20,4},{24,8},{28,12},{1,17},{... | collective-permute-start | bytes 86024 | tf_op jit(solution)/shard_map/ppermute | solution.py:367
  26.3 5.9 %collective-permute-start.9 = (f32[40,1408]{1,0:T(8,128)S(1)}, f32[40,1408]{1,0:T(8,128)S(1)}, u32[]{:S(2)}, u32[]{:S(2)}) collective-permute-start(f32[40,1408]{1,0:T(8,128)S(1)} %add.3.gram), channel_id=1, source_target_pairs={{0,1},{1,0},{2,3},{3,2},{4,5},{5,4},{6,7},{7,6},{8,9},{9,8},{10,11... | collective-permute-start | bytes 675848 | tf_op jit(solution)/shard_map/ppermute | solution.py:367
  26.4 1.5 %collective-permute-start.8 = (f32[80,80]{1,0:T(8,128)S(1)}, f32[80,80]{1,0:T(8,128)S(1)}, u32[]{:S(2)}, u32[]{:S(2)}) collective-permute-start(f32[80,80]{1,0:T(8,128)S(1)} %get-tuple-element.60._.left), channel_id=1, source_target_pairs={{0,1},{1,0},{2,3},{3,2},{4,5},{5,4},{6,7},{7,6},{8,9},{9,8},{10,11... | collective-permute-start | bytes 76808 | tf_op jit(solution)/shard_map/ppermute | solution.py:367
  27.9 4.3 %collective-permute-start.10 = (f32[80,80]{1,0:T(8,128)S(1)}, f32[80,80]{1,0:T(8,128)S(1)}, u32[]{:S(2)}, u32[]{:S(2)}) collective-permute-start(f32[80,80]{1,0:T(8,128)S(1)} %chip_carry.1.refs_2_.refs_0_), channel_id=1, source_target_pairs={{0,2},{1,3},{2,0},{3,1},{4,6},{5,7},{6,4},{7,5},{8,10},{9,11},{10,... | collective-permute-start | bytes 76808 | tf_op jit(solution)/shard_map/ppermute | solution.py:371

commit v17 on v16

--- a/solution.py
+++ b/solution.py
@@ -29,9 +29,9 @@
 
 
 def mul_pairs(left, right, dims=NORMAL):
-    return mul(left[0], right[0], dims) + (
-        mul(left[0], right[1], dims) + mul(left[1], right[0], dims)
-    )
+    rows = left[0].shape[0]
+    both = mul(jnp.concatenate(left, axis=0), right[0], dims)
+    return both[:rows] + (both[rows:] + mul(left[0], right[1], dims))
 
 
 def mul_exact(left, right, dims=NORMAL):

time: 34.7 us -> 35.7 us (1.029)
  Pallas kernels: 18.2 us -> 19.1 us
    pallas_call x1, Pallas kernels: 2.78 us -> 3.39 us  [shards(): call(functools.partial(chain_kernel, plan), [shape(count * members, membe...]
    pallas_call x1, Pallas kernels: 4.32 us -> 4.83 us  [shards(): call(functools.partial(gram_kernel, plan), [wide, wide, square] + [piece_...]
  transfers between devices with their start and end apart: 11 -> 11, of which waited for: 1 -> 1; matrix products, arithmetic and copies ran while one was open for 0% -> 0% of each run, Pallas kernels for 38% -> 37%
where the time goes in v17:
time: 35.7 us; the launch traced here: 35.5 us
  Pallas kernels  19.1 us (54%)
  starting transfers between devices  15.4 us (43%)
  between operations  0.78 us (2%)
    ppermute x9, starting transfers between devices, exchange(): return lax.ppermute(value, axis, [(at, at ^ bit) for at in range(size)])  12.2 us
    pallas_call x2, Pallas kernels, apply(): call(functools.partial(apply_kernel, plan), [shape(count, members, cells,...  5.43 us
    pallas_call x1, Pallas kernels, shards(): call(functools.partial(gram_kernel, plan), [wide, wide, square] + [piece_...  4.83 us
    pallas_call x1, Pallas kernels, shards(): call(functools.partial(chain_kernel, plan), [shape(count * members, membe...  3.39 us
    ppermute x2, starting transfers between devices, around(): lax.ppermute(value, 'space', [(at, (at + 2 * d) % lanes) for at in range(...  3.16 us
    pallas_call x1, Pallas kernels, shards(): call(functools.partial(final_kernel, plan, scale), shape(count, members,...  2.21 us
    pallas_call x1, Pallas kernels, shards(): call(functools.partial(windows_kernel, plan), shape(2, count_steps(count)...  0.87 us
    pallas_call x1, Pallas kernels, shards(): call(functools.partial(carry_kernel, plan), [shape(len(plan.groups), size...  0.86 us
  transfers between devices with their start and end apart: 11, of which 1 were waited for; matrix products, arithmetic and copies ran while one was open for 0% of the time, Pallas kernels for 37%

profile of v17, /device:TPU:0, one launch (start us, length us, event | category | flops | bytes accessed | tf_op | source)
XLA Modules:
  0.0 35.5 jit_solution(14494357382940908872)
XLA Ops:
  0.6 3.4 %transform_chain.1 = (f32[1280,80]{1,0:T(8,128)S(1)}, f32[80,80]{1,0:T(8,128)S(1)}, f32[16,80,80]{2,1,0:T(8,128)S(1)}, bf16[6,80,2048]{2,1,0:T(8,128)(2,1)S(1)}, bf16[6,80,2048]{2,1,0:T(8,128)(2,1)S(1)}) custom-call(f32[16,80,80]{2,1,0:T(8,128)} %transforms.1, bf16[16,80,2048]{2,1,0:T(8,128)(2,1)} %ensembles.3, bf16[16,80,2048]{2,1,0:T(8,128)(2,1)} %cotangents.3), custom_call_target="tpu_custom_call" | custom-call | flops 3500000000 | bytes 10500000 | tf_op jit(solution)/shard_map/transform_chain/pallas_call | solution.py:382
  4.0 3.0 %collective-permute-start = (f32[80,80]{1,0:T(8,128)S(1)}, f32[80,80]{1,0:T(8,128)S(1)}, u32[]{:S(2)}, u32[]{:S(2)}) collective-permute-start(f32[80,80]{1,0:T(8,128)S(1)} %get-tuple-element.35.total), channel_id=1, source_target_pairs={{0,4},{4,0},{8,12},{12,8},{16,20},{20,16},{24,28},{28,24},{1,5},{5... | collective-permute-start | bytes 76808 | tf_op jit(solution)/shard_map/ppermute | solution.py:367
  7.0 4.8 %gram.1 = (f32[40,1408]{1,0:T(8,128)S(1)}, f32[40,1408]{1,0:T(8,128)S(1)}, f32[80,80]{1,0:T(8,128)S(1)}, bf16[10,80,2048]{2,1,0:T(8,128)(2,1)S(1)}, bf16[10,80,2048]{2,1,0:T(8,128)(2,1)S(1)}) custom-call(bf16[16,80,2048]{2,1,0:T(8,128)(2,1)} %ensembles.3, bf16[16,80,2048]{2,1,0:T(8,128)(2,1)} %cotangents.3, f32[1280,80]{1,0:T(8,128)S(1)} %get-tuple-element.34.suffixes, ...), custom_call_target="tpu_custom_call" | custom-call | flops 4499999744 | bytes 13500000 | tf_op jit(solution)/shard_map/gram/pallas_call | solution.py:406
  11.9 0.1 collective-permute-start.3
  11.9 0.1 collective-permute-start.2
  12.0 0.0 collective-permute-done.other
  12.0 0.2 join_0.1
  12.3 2.2 %collective-permute-start.1 = (f32[80,80]{1,0:T(8,128)S(1)}, f32[80,80]{1,0:T(8,128)S(1)}, u32[]{:S(2)}, u32[]{:S(2)}) collective-permute-start(f32[80,80]{1,0:T(8,128)S(1)} %get-tuple-element.39._.total), channel_id=1, source_target_pairs={{0,8},{4,12},{8,0},{12,4},{16,24},{20,28},{24,16},{28,20},{1,9},{5... | collective-permute-start | bytes 76808 | tf_op jit(solution)/shard_map/ppermute | solution.py:367
  14.4 0.0 collective-permute-done.3.right
  14.5 1.6 %collective-permute-start.7 = (f32[40,1408]{1,0:T(8,128)S(1)}, f32[40,1408]{1,0:T(8,128)S(1)}, u32[]{:S(2)}, u32[]{:S(2)}) collective-permute-start(f32[40,1408]{1,0:T(8,128)S(1)} %chip_gram.1._), channel_id=1, source_target_pairs={{0,2},{1,3},{2,0},{3,1},{4,6},{5,7},{6,4},{7,5},{8,10},{9,11},{10,... | collective-permute-start | bytes 675848 | tf_op jit(solution)/shard_map/ppermute | solution.py:371
  16.1 0.0 collective-permute-done.2.other
  16.1 0.2 pass_0.1
  16.3 1.6 %collective-permute-start.5 = (f32[80,80]{1,0:T(8,128)S(1)}, f32[80,80]{1,0:T(8,128)S(1)}, u32[]{:S(2)}, u32[]{:S(2)}) collective-permute-start(f32[80,80]{1,0:T(8,128)S(1)} %get-tuple-element.45._.own), channel_id=1, source_target_pairs={{0,8},{4,12},{8,0},{12,4},{16,24},{20,28},{24,16},{28,20},{1,9},{5... | collective-permute-start | bytes 76808 | tf_op jit(solution)/shard_map/ppermute | solution.py:367
  17.9 0.0 collective-permute-done.1.other
  17.9 0.3 join_1.1
  18.2 2.6 %collective-permute-start.4 = (f32[56,128]{1,0:T(8,128)S(1)}, f32[56,128]{1,0:T(8,128)S(1)}, u32[]{:S(2)}, u32[]{:S(2)}) collective-permute-start(f32[56,128]{1,0:T(8,128)S(1)} %get-tuple-element.47._), channel_id=1, source_target_pairs={{0,16},{4,20},{8,24},{12,28},{16,0},{20,4},{24,8},{28,12},{1,17},{... | collective-permute-start | bytes 86024 | tf_op jit(solution)/shard_map/ppermute | solution.py:367
  20.8 0.0 collective-permute-done.5.other
  20.8 0.3 pass_1.1
  21.1 2.2 %collective-permute-start.6 = (f32[56,128]{1,0:T(8,128)S(1)}, f32[56,128]{1,0:T(8,128)S(1)}, u32[]{:S(2)}, u32[]{:S(2)}) collective-permute-start(f32[56,128]{1,0:T(8,128)S(1)} %get-tuple-element.50._), channel_id=1, source_target_pairs={{0,16},{4,20},{8,24},{12,28},{16,0},{20,4},{24,8},{28,12},{1,17},{... | collective-permute-start | bytes 86024 | tf_op jit(solution)/shard_map/ppermute | solution.py:367
  23.2 0.0 collective-permute-done.4.other
  23.2 0.2 entering.1.later
  23.5 0.9 %carries.1 = (bf16[6,240,240]{2,1,0:T(8,128)(2,1)S(1)}, bf16[6,240,240]{2,1,0:T(8,128)(2,1)S(1)}, bf16[2,1280,80]{2,1,0:T(8,128)(2,1)S(1)}) custom-call(f32[1280,80]{1,0:T(8,128)S(1)} %get-tuple-element.34.suffixes, f32[80,80]{1,0:T(8,128)S(1)} %entering.1.later, f32[56,128]{1,0:T(8,128)S(1)} %get-tuple-element.50._), custom_call_target="tpu_custom_call" | custom-call | flops 900000000 | bytes 2700000 | tf_op jit(solution)/shard_map/carries/pallas_call | solution.py:443
  24.3 2.7 %smoothed.1 = (bf16[16,80,2048]{2,1,0:T(8,128)(2,1)}, f32[8,128]{1,0:T(8,128)S(1)}) custom-call(bf16[6,240,240]{2,1,0:T(8,128)(2,1)S(1)} %get-tuple-element.51.factors, bf16[6,80,2048]{2,1,0:T(8,128)(2,1)S(1)} %get-tuple-element.36.ens.refs_0_, bf16[10,80,2048]{2,1,0:T(8,128)(2,1)S(1)} %get-tuple-element.52.refs_1_, ...), custom_call_target="tpu_custom_call" | custom-call | flops 500000000 | bytes 1500000 | tf_op jit(solution)/shard_map/smoothed/pallas_call | solution.py:450
  27.1 0.0 collective-permute-done.6.other
  27.1 0.0 collective-permute-done.7.__
  27.1 0.2 pass_last.1
  27.3 0.1 collective-permute-start.9
  27.4 0.5 %collective-permute-start.8 = (f32[80,80]{1,0:T(8,128)S(1)}, f32[80,80]{1,0:T(8,128)S(1)}, u32[]{:S(2)}, u32[]{:S(2)}) collective-permute-start(f32[80,80]{1,0:T(8,128)S(1)} %get-tuple-element.60._.left), channel_id=1, source_target_pairs={{0,1},{1,0},{2,3},{3,2},{4,5},{5,4},{6,7},{7,6},{8,9},{9,8},{10,11... | collective-permute-start | bytes 76808 | tf_op jit(solution)/shard_map/ppermute | solution.py:367
  27.9 0.9 %windows.1._.steps = bf16[2,2560,80]{2,1,0:T(8,128)(2,1)S(1)} custom-call(f32[16,80,80]{2,1,0:T(8,128)S(1)} %get-tuple-element.61.kept, f32[80,80]{1,0:T(8,128)S(1)} %get-tuple-element.60._.left), custom_call_target="tpu_custom_call" | custom-call | flops 1000000000 | bytes 3000000 | tf_op jit(solution)/shard_map/windows/pallas_call | solution.py:468
  28.8 0.2 collective-permute-done.8.right
  28.9 1.6 %collective-permute-start.10 = (f32[80,80]{1,0:T(8,128)S(1)}, f32[80,80]{1,0:T(8,128)S(1)}, u32[]{:S(2)}, u32[]{:S(2)}) collective-permute-start(f32[80,80]{1,0:T(8,128)S(1)} %chip_carry.1.refs_2_.refs_0_), channel_id=1, source_target_pairs={{0,2},{1,3},{2,0},{3,1},{4,6},{5,7},{6,4},{7,5},{8,10},{9,11},{10,... | collective-permute-start | bytes 76808 | tf_op jit(solution)/shard_map/ppermute | solution.py:371
  30.5 2.7 %ensemble_grad.1 = (bf16[16,80,2048]{2,1,0:T(8,128)(2,1)}, f32[8,128]{1,0:T(8,128)S(1)}) custom-call(bf16[6,240,240]{2,1,0:T(8,128)(2,1)S(1)} %get-tuple-element.55.factors, bf16[6,80,2048]{2,1,0:T(8,128)(2,1)S(1)} %get-tuple-element.37.cot.refs_0_, bf16[10,80,2048]{2,1,0:T(8,128)(2,1)S(1)} %get-tuple-element.56.refs_1_, f32[80,80]{1,0:T(8,128)S(1)} %chip_carry.1.refs_2_.refs_0_), custom_call_target="tpu_custom_call" | custom-call | flops 500000000 | bytes 1500000 | tf_op jit(solution)/shard_map/ensemble_grad/pallas_call | solution.py:450
  33.2 0.0 collective-permute-done.10.refs_1_
  33.3 0.0 collective-permute-done.9.gram_core
  33.3 2.2 %transform_grad.1 = f32[16,80,80]{2,1,0:T(8,128)} custom-call(f32[40,1408]{1,0:T(8,128)S(1)} %add.3.gram, f32[40,1408]{1,0:T(8,128)S(1)} %collective-permute-done.9.gram_core, bf16[2,1280,80]{2,1,0:T(8,128)(2,1)S(1)} %get-tuple-element.53.refs_2_.follow, bf16[2,2560,80]{2,1,0:T(8,128)(2,1)S(1)} %windows.1._.steps, f32[8,128]{1,0:T(8,128)S(1)} %get-tuple-element.64._, ...), custom_call_target="tpu_custom_call" | custom-call | flops 2500000000 | bytes 7500000 | tf_op jit(solution)/shard_map/transform_grad/pallas_call | solution.py:478
  (5 shorter events, 0.1 us)
Async XLA Ops:
  4.0 8.0 %collective-permute-start = (f32[80,80]{1,0:T(8,128)S(1)}, f32[80,80]{1,0:T(8,128)S(1)}, u32[]{:S(2)}, u32[]{:S(2)}) collective-permute-start(f32[80,80]{1,0:T(8,128)S(1)} %get-tuple-element.35.total), channel_id=1, source_target_pairs={{0,4},{4,0},{8,12},{12,8},{16,20},{20,16},{24,28},{28,24},{1,5},{5... | collective-permute-start | bytes 76808 | tf_op jit(solution)/shard_map/ppermute | solution.py:367
  11.9 2.6 %collective-permute-start.3 = (f32[40,1408]{1,0:T(8,128)S(1)}, f32[40,1408]{1,0:T(8,128)S(1)}, u32[]{:S(2)}, u32[]{:S(2)}) collective-permute-start(f32[40,1408]{1,0:T(8,128)S(1)} %get-tuple-element.44), channel_id=1, source_target_pairs={{0,1},{1,0},{2,3},{3,2},{4,5},{5,4},{6,7},{7,6},{8,9},{9,8},{10,11... | collective-permute-start | bytes 675848 | tf_op jit(solution)/shard_map/ppermute | solution.py:367
  11.9 4.1 %collective-permute-start.2 = (f32[80,80]{1,0:T(8,128)S(1)}, f32[80,80]{1,0:T(8,128)S(1)}, u32[]{:S(2)}, u32[]{:S(2)}) collective-permute-start(f32[80,80]{1,0:T(8,128)S(1)} %get-tuple-element.38._.own), channel_id=1, source_target_pairs={{0,4},{4,0},{8,12},{12,8},{16,20},{20,16},{24,28},{28,24},{1,5},{5... | collective-permute-start | bytes 76808 | tf_op jit(solution)/shard_map/ppermute | solution.py:367
  12.3 5.6 %collective-permute-start.1 = (f32[80,80]{1,0:T(8,128)S(1)}, f32[80,80]{1,0:T(8,128)S(1)}, u32[]{:S(2)}, u32[]{:S(2)}) collective-permute-start(f32[80,80]{1,0:T(8,128)S(1)} %get-tuple-element.39._.total), channel_id=1, source_target_pairs={{0,8},{4,12},{8,0},{12,4},{16,24},{20,28},{24,16},{28,20},{1,9},{5... | collective-permute-start | bytes 76808 | tf_op jit(solution)/shard_map/ppermute | solution.py:367
  14.5 12.6 %collective-permute-start.7 = (f32[40,1408]{1,0:T(8,128)S(1)}, f32[40,1408]{1,0:T(8,128)S(1)}, u32[]{:S(2)}, u32[]{:S(2)}) collective-permute-start(f32[40,1408]{1,0:T(8,128)S(1)} %chip_gram.1._), channel_id=1, source_target_pairs={{0,2},{1,3},{2,0},{3,1},{4,6},{5,7},{6,4},{7,5},{8,10},{9,11},{10,... | collective-permute-start | bytes 675848 | tf_op jit(solution)/shard_map/ppermute | solution.py:371
  16.3 4.5 %collective-permute-start.5 = (f32[80,80]{1,0:T(8,128)S(1)}, f32[80,80]{1,0:T(8,128)S(1)}, u32[]{:S(2)}, u32[]{:S(2)}) collective-permute-start(f32[80,80]{1,0:T(8,128)S(1)} %get-tuple-element.45._.own), channel_id=1, source_target_pairs={{0,8},{4,12},{8,0},{12,4},{16,24},{20,28},{24,16},{28,20},{1,9},{5... | collective-permute-start | bytes 76808 | tf_op jit(solution)/shard_map/ppermute | solution.py:367
  18.2 5.1 %collective-permute-start.4 = (f32[56,128]{1,0:T(8,128)S(1)}, f32[56,128]{1,0:T(8,128)S(1)}, u32[]{:S(2)}, u32[]{:S(2)}) collective-permute-start(f32[56,128]{1,0:T(8,128)S(1)} %get-tuple-element.47._), channel_id=1, source_target_pairs={{0,16},{4,20},{8,24},{12,28},{16,0},{20,4},{24,8},{28,12},{1,17},{... | collective-permute-start | bytes 86024 | tf_op jit(solution)/shard_map/ppermute | solution.py:367
  21.1 6.0 %collective-permute-start.6 = (f32[56,128]{1,0:T(8,128)S(1)}, f32[56,128]{1,0:T(8,128)S(1)}, u32[]{:S(2)}, u32[]{:S(2)}) collective-permute-start(f32[56,128]{1,0:T(8,128)S(1)} %get-tuple-element.50._), channel_id=1, source_target_pairs={{0,16},{4,20},{8,24},{12,28},{16,0},{20,4},{24,8},{28,12},{1,17},{... | collective-permute-start | bytes 86024 | tf_op jit(solution)/shard_map/ppermute | solution.py:367
  27.3 5.9 %collective-permute-start.9 = (f32[40,1408]{1,0:T(8,128)S(1)}, f32[40,1408]{1,0:T(8,128)S(1)}, u32[]{:S(2)}, u32[]{:S(2)}) collective-permute-start(f32[40,1408]{1,0:T(8,128)S(1)} %add.3.gram), channel_id=1, source_target_pairs={{0,1},{1,0},{2,3},{3,2},{4,5},{5,4},{6,7},{7,6},{8,9},{9,8},{10,11... | collective-permute-start | bytes 675848 | tf_op jit(solution)/shard_map/ppermute | solution.py:367
  27.4 1.5 %collective-permute-start.8 = (f32[80,80]{1,0:T(8,128)S(1)}, f32[80,80]{1,0:T(8,128)S(1)}, u32[]{:S(2)}, u32[]{:S(2)}) collective-permute-start(f32[80,80]{1,0:T(8,128)S(1)} %get-tuple-element.60._.left), channel_id=1, source_target_pairs={{0,1},{1,0},{2,3},{3,2},{4,5},{5,4},{6,7},{7,6},{8,9},{9,8},{10,11... | collective-permute-start | bytes 76808 | tf_op jit(solution)/shard_map/ppermute | solution.py:367
  28.9 4.3 %collective-permute-start.10 = (f32[80,80]{1,0:T(8,128)S(1)}, f32[80,80]{1,0:T(8,128)S(1)}, u32[]{:S(2)}, u32[]{:S(2)}) collective-permute-start(f32[80,80]{1,0:T(8,128)S(1)} %chip_carry.1.refs_2_.refs_0_), channel_id=1, source_target_pairs={{0,2},{1,3},{2,0},{3,1},{4,6},{5,7},{6,4},{7,5},{8,10},{9,11},{10,... | collective-permute-start | bytes 76808 | tf_op jit(solution)/shard_map/ppermute | solution.py:371

commit v18 on v16

--- a/solution.py
+++ b/solution.py
@@ -36,6 +36,16 @@
 
 def mul_exact(left, right, dims=NORMAL):
     return mul_pairs(split(left), split(right), dims)
+
+
+def mul_stacked(left, right, dims=NORMAL):
+    rows = left[0].shape[0]
+    both = mul(jnp.concatenate(left, axis=0), right[0], dims)
+    return both[:rows] + (both[rows:] + mul(left[0], right[1], dims))
+
+
+def mul_small(left, right):
+    return mul_stacked(split(left), split(right))
 
 
 def product_of(factors):
@@ -131,8 +141,9 @@
     more += loads(plan, 0, cotangents, cot, cot_sem, slice(1, None))
     for at in range(count):
         suffixes[plan.rows(at, at + 1)] = kept[at]
-    suffix_scan(suffixes, count, members, count)
-    total[...] = suffixes[plan.rows(0, 1)]
+    suffix_scan(suffixes, count, members, count // 2)
+    middle = suffixes[plan.rows(count // 2, count // 2 + 1)]
+    total[...] = mul_exact(suffixes[plan.rows(0, 1)], middle)
     for copy in more:
         copy.wait()
 
@@ -152,7 +163,7 @@
         for start in range(2 * width, count, 2 * width):
             if start + width < count:
                 rows = plan.rows(start + width, min(start + 2 * width, count))
-                runs[rows] = mul_exact(runs[rows], runs[plan.rows(start + width - 1, start + width)])
+                runs[rows] = mul_small(runs[rows], runs[plan.rows(start + width - 1, start + width)])
         width *= 2
 
 
@@ -189,8 +200,8 @@
 
 
 def gram_kernel(
-    plan, ensembles, cotangents, suffixes, ens, cot,
-    kept, sent, offsets, next_ens, next_cot, whole, ens_sem, cot_sem,
+    plan, ensembles, cotangents, halves, ens, cot,
+    kept, sent, offsets, suffixes, next_ens, next_cot, whole, ens_sem, cot_sem,
 ):
     waiting = iter(list(zip(
         loads(plan, 1, ensembles, next_ens, ens_sem), loads(plan, 1, cotangents, next_cot, cot_sem)
@@ -200,6 +211,10 @@
         for copy in next(waiting):
             copy.wait()
 
+    count, middle = plan.count, plan.count // 2
+    first, last = plan.rows(0, middle), plan.rows(middle, count)
+    suffixes[first] = mul_exact(halves[first], halves[plan.rows(middle, middle + 1)])
+    suffixes[last] = halves[last]
     total = gram_of(plan, 0, cot, ens, suffixes, whole)
     offsets[...] = total + gram_of(plan, 1, next_cot, next_ens, suffixes, whole, ready)
     half = plan.members // 2
@@ -216,11 +231,11 @@
     upper = upper_half(level)
     left = jnp.where(upper, other[...], total[...])
     right = jnp.where(upper, total[...], other[...])
-    joined = mul_exact(left, right)
+    joined = mul_small(left, right)
     new_total[...] = pack(joined) if last else joined
     upper_total[...] = right
-    new_later[...] = jnp.where(upper, later[...], mul_exact(later[...], other[...]))
-    new_before[...] = jnp.where(upper, mul_exact(other[...], before[...]), before[...])
+    new_later[...] = jnp.where(upper, later[...], mul_small(later[...], other[...]))
+    new_before[...] = jnp.where(upper, mul_small(other[...], before[...]), before[...])
 
 
 def sum_kernel(left, right, _, total):
@@ -231,18 +246,18 @@
     upper = upper_half(level)
     left = jnp.where(upper, other[...], own[...])
     right = jnp.where(upper, own[...], other[...])
-    passed = mul_exact(left, upper_total[...]) + right
+    passed = mul_small(left, upper_total[...]) + right
     new_own[...] = pack(passed) if last else passed
-    new_carry[...] = carry[...] + jnp.where(upper, mul_exact(left, before[...]), 0.0)
+    new_carry[...] = carry[...] + jnp.where(upper, mul_small(left, before[...]), 0.0)
 
 
 def last_pass_kernel(level, other, carry, before, _, __, new_carry, ___):
-    added = mul_exact(unpack(other[...], before.shape[0]), before[...])
+    added = mul_small(unpack(other[...], before.shape[0]), before[...])
     new_carry[...] = carry[...] + jnp.where(upper_half(level), added, 0.0)
 
 
 def enter_kernel(level, later, other, _, entering):
-    joined = mul_exact(later[...], unpack(other[...], later.shape[0]))
+    joined = mul_small(later[...], unpack(other[...], later.shape[0]))
     entering[...] = jnp.where(upper_half(level), later[...], joined)
 
 
@@ -314,7 +329,7 @@
         for start in range(width, count, 2 * width):
             size = min(width, count - start)
             rows = plan.rows(number, number + size)
-            added = mul_pairs((steps[0, rows], steps[1, rows]), split(totals[start - 1]))
+            added = mul_stacked((steps[0, rows], steps[1, rows]), split(totals[start - 1]))
             for at in range(size):
                 totals[start + at] = totals[start + at] + added[at * members : (at + 1) * members]
             number += size
@@ -322,7 +337,7 @@
     copies = []
     for at in range(count):
         rows = plan.rows(at, at + 1)
-        buffer[at] = mul_pairs(split(totals[at]), (follow[0, rows], follow[1, rows]), ROWS) * scale
+        buffer[at] = mul_stacked(split(totals[at]), (follow[0, rows], follow[1, rows]), ROWS) * scale
         copy = pltpu.make_async_copy(buffer.at[at], out.at[at], sems.at[at])
         copy.start()
         copies.append(copy)
@@ -403,10 +418,10 @@
         return total, later, before
 
     other = exchange(total, "tm", blocks, 1)
-    gram, gram_sent, own, *second_part = call(
+    gram, gram_sent, own, suffixes, *second_part = call(
         functools.partial(gram_kernel, plan),
-        [wide, wide, square] + [piece_shape(1)] * 2,
-        [HBM] * 2 + [VMEM] * 3, [VMEM] * 5,
+        [wide, wide, square, shape(count * members, members)] + [piece_shape(1)] * 2,
+        [HBM] * 2 + [VMEM] * 3, [VMEM] * 6,
         [pltpu.VMEM((members, plan.width), F32)] + piece_sems(1), 4.5, "gram",
     )(ensembles, cotangents, suffixes, *first_part)
     parts = [first_part, second_part]

time: 34.7 us -> 35.6 us (1.026)
  Pallas kernels: 18.2 us -> 19 us
    pallas_call x1, Pallas kernels: 4.32 us -> 5.39 us  [shards(): call(functools.partial(gram_kernel, plan), [wide, wide, square, shape(cou...]
  transfers between devices with their start and end apart: 11 -> 11, of which waited for: 1 -> 1; matrix products, arithmetic and copies ran while one was open for 0% -> 0% of each run, Pallas kernels for 38% -> 39%
where the time goes in v18:
time: 35.6 us; the launch traced here: 35.4 us
  Pallas kernels  19 us (53%)
  starting transfers between devices  15.4 us (43%)
  between operations  0.79 us (2%)
    ppermute x9, starting transfers between devices, exchange(): return lax.ppermute(value, axis, [(at, at ^ bit) for at in range(size)])  12.2 us
    pallas_call x2, Pallas kernels, apply(): call(functools.partial(apply_kernel, plan), [shape(count, members, cells,...  5.43 us
    pallas_call x1, Pallas kernels, shards(): call(functools.partial(gram_kernel, plan), [wide, wide, square, shape(cou...  5.39 us
    ppermute x2, starting transfers between devices, around(): lax.ppermute(value, 'space', [(at, (at + 2 * d) % lanes) for at in range(...  3.16 us
    pallas_call x1, Pallas kernels, shards(): call(functools.partial(chain_kernel, plan), [shape(count * members, membe...  2.78 us
    pallas_call x1, Pallas kernels, shards(): call(functools.partial(final_kernel, plan, scale), shape(count, members,...  2.22 us
    pallas_call x1, Pallas kernels, shards(): call(functools.partial(windows_kernel, plan), shape(2, count_steps(count)...  0.87 us
    pallas_call x1, Pallas kernels, shards(): call(functools.partial(carry_kernel, plan), [shape(len(plan.groups), size...  0.86 us
  transfers between devices with their start and end apart: 11, of which 1 were waited for; matrix products, arithmetic and copies ran while one was open for 0% of the time, Pallas kernels for 39%

profile of v18, /device:TPU:0, one launch (start us, length us, event | category | flops | bytes accessed | tf_op | source)
XLA Modules:
  0.0 35.4 jit_solution(13461484436841520882)
XLA Ops:
  0.6 2.8 %transform_chain.1 = (f32[1280,80]{1,0:T(8,128)S(1)}, f32[80,80]{1,0:T(8,128)S(1)}, f32[16,80,80]{2,1,0:T(8,128)S(1)}, bf16[6,80,2048]{2,1,0:T(8,128)(2,1)S(1)}, bf16[6,80,2048]{2,1,0:T(8,128)(2,1)S(1)}) custom-call(f32[16,80,80]{2,1,0:T(8,128)} %transforms.1, bf16[16,80,2048]{2,1,0:T(8,128)(2,1)} %ensembles.3, bf16[16,80,2048]{2,1,0:T(8,128)(2,1)} %cotangents.3), custom_call_target="tpu_custom_call" | custom-call | flops 3500000000 | bytes 10500000 | tf_op jit(solution)/shard_map/transform_chain/pallas_call | solution.py:397
  3.4 3.0 %collective-permute-start = (f32[80,80]{1,0:T(8,128)S(1)}, f32[80,80]{1,0:T(8,128)S(1)}, u32[]{:S(2)}, u32[]{:S(2)}) collective-permute-start(f32[80,80]{1,0:T(8,128)S(1)} %get-tuple-element.39.total), channel_id=1, source_target_pairs={{0,4},{4,0},{8,12},{12,8},{16,20},{20,16},{24,28},{28,24},{1,5},{5... | collective-permute-start | bytes 76808 | tf_op jit(solution)/shard_map/ppermute | solution.py:382
  6.4 5.4 %gram.1 = (f32[40,1408]{1,0:T(8,128)S(1)}, f32[40,1408]{1,0:T(8,128)S(1)}, f32[80,80]{1,0:T(8,128)S(1)}, f32[1280,80]{1,0:T(8,128)S(1)}, bf16[10,80,2048]{2,1,0:...) custom-call(bf16[16,80,2048]{2,1,0:T(8,128)(2,1)} %ensembles.3, bf16[16,80,2048]{2,1,0:T(8,128)(2,1)} %cotangents.3, ...), custom_call_target="tpu_custom_call" | custom-call | flops 4499999744 | bytes 13500000 | tf_op jit(solution)/shard_map/gram/pallas_call | solution.py:421
  11.8 0.1 collective-permute-start.3
  11.9 0.1 collective-permute-start.2
  12.0 0.0 collective-permute-done.other
  12.0 0.2 join_0.1
  12.2 2.2 %collective-permute-start.1 = (f32[80,80]{1,0:T(8,128)S(1)}, f32[80,80]{1,0:T(8,128)S(1)}, u32[]{:S(2)}, u32[]{:S(2)}) collective-permute-start(f32[80,80]{1,0:T(8,128)S(1)} %get-tuple-element.41._.total), channel_id=1, source_target_pairs={{0,8},{4,12},{8,0},{12,4},{16,24},{20,28},{24,16},{28,20},{1,9},{5... | collective-permute-start | bytes 76808 | tf_op jit(solution)/shard_map/ppermute | solution.py:382
  14.4 0.0 collective-permute-done.3.right
  14.4 1.6 %collective-permute-start.7 = (f32[40,1408]{1,0:T(8,128)S(1)}, f32[40,1408]{1,0:T(8,128)S(1)}, u32[]{:S(2)}, u32[]{:S(2)}) collective-permute-start(f32[40,1408]{1,0:T(8,128)S(1)} %chip_gram.1._), channel_id=1, source_target_pairs={{0,2},{1,3},{2,0},{3,1},{4,6},{5,7},{6,4},{7,5},{8,10},{9,11},{10,... | collective-permute-start | bytes 675848 | tf_op jit(solution)/shard_map/ppermute | solution.py:386
  16.0 0.0 collective-permute-done.2.other
  16.0 0.2 pass_0.1
  16.2 1.6 %collective-permute-start.5 = (f32[80,80]{1,0:T(8,128)S(1)}, f32[80,80]{1,0:T(8,128)S(1)}, u32[]{:S(2)}, u32[]{:S(2)}) collective-permute-start(f32[80,80]{1,0:T(8,128)S(1)} %get-tuple-element.47._.own), channel_id=1, source_target_pairs={{0,8},{4,12},{8,0},{12,4},{16,24},{20,28},{24,16},{28,20},{1,9},{5... | collective-permute-start | bytes 76808 | tf_op jit(solution)/shard_map/ppermute | solution.py:382
  17.8 0.0 collective-permute-done.1.other
  17.8 0.3 join_1.1
  18.1 2.6 %collective-permute-start.4 = (f32[56,128]{1,0:T(8,128)S(1)}, f32[56,128]{1,0:T(8,128)S(1)}, u32[]{:S(2)}, u32[]{:S(2)}) collective-permute-start(f32[56,128]{1,0:T(8,128)S(1)} %get-tuple-element.49._), channel_id=1, source_target_pairs={{0,16},{4,20},{8,24},{12,28},{16,0},{20,4},{24,8},{28,12},{1,17},{... | collective-permute-start | bytes 86024 | tf_op jit(solution)/shard_map/ppermute | solution.py:382
  20.7 0.0 collective-permute-done.5.other
  20.7 0.3 pass_1.1
  21.0 2.1 %collective-permute-start.6 = (f32[56,128]{1,0:T(8,128)S(1)}, f32[56,128]{1,0:T(8,128)S(1)}, u32[]{:S(2)}, u32[]{:S(2)}) collective-permute-start(f32[56,128]{1,0:T(8,128)S(1)} %get-tuple-element.52._), channel_id=1, source_target_pairs={{0,16},{4,20},{8,24},{12,28},{16,0},{20,4},{24,8},{28,12},{1,17},{... | collective-permute-start | bytes 86024 | tf_op jit(solution)/shard_map/ppermute | solution.py:382
  23.2 0.0 collective-permute-done.4.other
  23.2 0.2 entering.1.later
  23.4 0.9 %carries.1 = (bf16[6,240,240]{2,1,0:T(8,128)(2,1)S(1)}, bf16[6,240,240]{2,1,0:T(8,128)(2,1)S(1)}, bf16[2,1280,80]{2,1,0:T(8,128)(2,1)S(1)}) custom-call(f32[1280,80]{1,0:T(8,128)S(1)} %get-tuple-element.38.suffixes, f32[80,80]{1,0:T(8,128)S(1)} %entering.1.later, f32[56,128]{1,0:T(8,128)S(1)} %get-tuple-element.52._), custom_call_target="tpu_custom_call" | custom-call | flops 900000000 | bytes 2700000 | tf_op jit(solution)/shard_map/carries/pallas_call | solution.py:458
  24.3 2.7 %smoothed.1 = (bf16[16,80,2048]{2,1,0:T(8,128)(2,1)}, f32[8,128]{1,0:T(8,128)S(1)}) custom-call(bf16[6,240,240]{2,1,0:T(8,128)(2,1)S(1)} %get-tuple-element.53.factors, bf16[6,80,2048]{2,1,0:T(8,128)(2,1)S(1)} %get-tuple-element.36.ens.refs_0_, bf16[10,80,2048]{2,1,0:T(8,128)(2,1)S(1)} %get-tuple-element.54.refs_1_, ...), custom_call_target="tpu_custom_call" | custom-call | flops 500000000 | bytes 1500000 | tf_op jit(solution)/shard_map/smoothed/pallas_call | solution.py:465
  27.0 0.0 collective-permute-done.6.other
  27.0 0.0 collective-permute-done.7.__
  27.0 0.2 pass_last.1
  27.3 0.1 collective-permute-start.9
  27.3 0.5 %collective-permute-start.8 = (f32[80,80]{1,0:T(8,128)S(1)}, f32[80,80]{1,0:T(8,128)S(1)}, u32[]{:S(2)}, u32[]{:S(2)}) collective-permute-start(f32[80,80]{1,0:T(8,128)S(1)} %get-tuple-element.62._.left), channel_id=1, source_target_pairs={{0,1},{1,0},{2,3},{3,2},{4,5},{5,4},{6,7},{7,6},{8,9},{9,8},{10,11... | collective-permute-start | bytes 76808 | tf_op jit(solution)/shard_map/ppermute | solution.py:382
  27.8 0.9 %windows.1._.steps = bf16[2,2560,80]{2,1,0:T(8,128)(2,1)S(1)} custom-call(f32[16,80,80]{2,1,0:T(8,128)S(1)} %get-tuple-element.63.kept, f32[80,80]{1,0:T(8,128)S(1)} %get-tuple-element.62._.left), custom_call_target="tpu_custom_call" | custom-call | flops 1000000000 | bytes 3000000 | tf_op jit(solution)/shard_map/windows/pallas_call | solution.py:483
  28.7 0.2 collective-permute-done.8.right
  28.9 1.6 %collective-permute-start.10 = (f32[80,80]{1,0:T(8,128)S(1)}, f32[80,80]{1,0:T(8,128)S(1)}, u32[]{:S(2)}, u32[]{:S(2)}) collective-permute-start(f32[80,80]{1,0:T(8,128)S(1)} %chip_carry.1.refs_2_.refs_0_), channel_id=1, source_target_pairs={{0,2},{1,3},{2,0},{3,1},{4,6},{5,7},{6,4},{7,5},{8,10},{9,11},{10,... | collective-permute-start | bytes 76808 | tf_op jit(solution)/shard_map/ppermute | solution.py:386
  30.5 2.7 %ensemble_grad.1 = (bf16[16,80,2048]{2,1,0:T(8,128)(2,1)}, f32[8,128]{1,0:T(8,128)S(1)}) custom-call(bf16[6,240,240]{2,1,0:T(8,128)(2,1)S(1)} %get-tuple-element.57.factors, bf16[6,80,2048]{2,1,0:T(8,128)(2,1)S(1)} %get-tuple-element.37.cot.refs_0_, bf16[10,80,2048]{2,1,0:T(8,128)(2,1)S(1)} %get-tuple-element.58.refs_1_, f32[80,80]{1,0:T(8,128)S(1)} %chip_carry.1.refs_2_.refs_0_), custom_call_target="tpu_custom_call" | custom-call | flops 500000000 | bytes 1500000 | tf_op jit(solution)/shard_map/ensemble_grad/pallas_call | solution.py:465
  33.2 0.0 collective-permute-done.10.refs_1_
  33.2 0.0 collective-permute-done.9.gram_core
  33.2 2.2 %transform_grad.1 = f32[16,80,80]{2,1,0:T(8,128)} custom-call(f32[40,1408]{1,0:T(8,128)S(1)} %add.3.gram, f32[40,1408]{1,0:T(8,128)S(1)} %collective-permute-done.9.gram_core, bf16[2,1280,80]{2,1,0:T(8,128)(2,1)S(1)} %get-tuple-element.55.refs_2_.follow, bf16[2,2560,80]{2,1,0:T(8,128)(2,1)S(1)} %windows.1._.steps, f32[8,128]{1,0:T(8,128)S(1)} %get-tuple-element.66._, ...), custom_call_target="tpu_custom_call" | custom-call | flops 2500000000 | bytes 7500000 | tf_op jit(solution)/shard_map/transform_grad/pallas_call | solution.py:493
  (5 shorter events, 0.1 us)
Async XLA Ops:
  3.4 8.6 %collective-permute-start = (f32[80,80]{1,0:T(8,128)S(1)}, f32[80,80]{1,0:T(8,128)S(1)}, u32[]{:S(2)}, u32[]{:S(2)}) collective-permute-start(f32[80,80]{1,0:T(8,128)S(1)} %get-tuple-element.39.total), channel_id=1, source_target_pairs={{0,4},{4,0},{8,12},{12,8},{16,20},{20,16},{24,28},{28,24},{1,5},{5... | collective-permute-start | bytes 76808 | tf_op jit(solution)/shard_map/ppermute | solution.py:382
  11.8 2.6 %collective-permute-start.3 = (f32[40,1408]{1,0:T(8,128)S(1)}, f32[40,1408]{1,0:T(8,128)S(1)}, u32[]{:S(2)}, u32[]{:S(2)}) collective-permute-start(f32[40,1408]{1,0:T(8,128)S(1)} %get-tuple-element.46), channel_id=1, source_target_pairs={{0,1},{1,0},{2,3},{3,2},{4,5},{5,4},{6,7},{7,6},{8,9},{9,8},{10,11... | collective-permute-start | bytes 675848 | tf_op jit(solution)/shard_map/ppermute | solution.py:382
  11.9 4.1 %collective-permute-start.2 = (f32[80,80]{1,0:T(8,128)S(1)}, f32[80,80]{1,0:T(8,128)S(1)}, u32[]{:S(2)}, u32[]{:S(2)}) collective-permute-start(f32[80,80]{1,0:T(8,128)S(1)} %get-tuple-element.40._.own), channel_id=1, source_target_pairs={{0,4},{4,0},{8,12},{12,8},{16,20},{20,16},{24,28},{28,24},{1,5},{5... | collective-permute-start | bytes 76808 | tf_op jit(solution)/shard_map/ppermute | solution.py:382
  12.2 5.6 %collective-permute-start.1 = (f32[80,80]{1,0:T(8,128)S(1)}, f32[80,80]{1,0:T(8,128)S(1)}, u32[]{:S(2)}, u32[]{:S(2)}) collective-permute-start(f32[80,80]{1,0:T(8,128)S(1)} %get-tuple-element.41._.total), channel_id=1, source_target_pairs={{0,8},{4,12},{8,0},{12,4},{16,24},{20,28},{24,16},{28,20},{1,9},{5... | collective-permute-start | bytes 76808 | tf_op jit(solution)/shard_map/ppermute | solution.py:382
  14.4 12.6 %collective-permute-start.7 = (f32[40,1408]{1,0:T(8,128)S(1)}, f32[40,1408]{1,0:T(8,128)S(1)}, u32[]{:S(2)}, u32[]{:S(2)}) collective-permute-start(f32[40,1408]{1,0:T(8,128)S(1)} %chip_gram.1._), channel_id=1, source_target_pairs={{0,2},{1,3},{2,0},{3,1},{4,6},{5,7},{6,4},{7,5},{8,10},{9,11},{10,... | collective-permute-start | bytes 675848 | tf_op jit(solution)/shard_map/ppermute | solution.py:386
  16.2 4.5 %collective-permute-start.5 = (f32[80,80]{1,0:T(8,128)S(1)}, f32[80,80]{1,0:T(8,128)S(1)}, u32[]{:S(2)}, u32[]{:S(2)}) collective-permute-start(f32[80,80]{1,0:T(8,128)S(1)} %get-tuple-element.47._.own), channel_id=1, source_target_pairs={{0,8},{4,12},{8,0},{12,4},{16,24},{20,28},{24,16},{28,20},{1,9},{5... | collective-permute-start | bytes 76808 | tf_op jit(solution)/shard_map/ppermute | solution.py:382
  18.1 5.1 %collective-permute-start.4 = (f32[56,128]{1,0:T(8,128)S(1)}, f32[56,128]{1,0:T(8,128)S(1)}, u32[]{:S(2)}, u32[]{:S(2)}) collective-permute-start(f32[56,128]{1,0:T(8,128)S(1)} %get-tuple-element.49._), channel_id=1, source_target_pairs={{0,16},{4,20},{8,24},{12,28},{16,0},{20,4},{24,8},{28,12},{1,17},{... | collective-permute-start | bytes 86024 | tf_op jit(solution)/shard_map/ppermute | solution.py:382
  21.0 6.0 %collective-permute-start.6 = (f32[56,128]{1,0:T(8,128)S(1)}, f32[56,128]{1,0:T(8,128)S(1)}, u32[]{:S(2)}, u32[]{:S(2)}) collective-permute-start(f32[56,128]{1,0:T(8,128)S(1)} %get-tuple-element.52._), channel_id=1, source_target_pairs={{0,16},{4,20},{8,24},{12,28},{16,0},{20,4},{24,8},{28,12},{1,17},{... | collective-permute-start | bytes 86024 | tf_op jit(solution)/shard_map/ppermute | solution.py:382
  27.3 5.9 %collective-permute-start.9 = (f32[40,1408]{1,0:T(8,128)S(1)}, f32[40,1408]{1,0:T(8,128)S(1)}, u32[]{:S(2)}, u32[]{:S(2)}) collective-permute-start(f32[40,1408]{1,0:T(8,128)S(1)} %add.3.gram), channel_id=1, source_target_pairs={{0,1},{1,0},{2,3},{3,2},{4,5},{5,4},{6,7},{7,6},{8,9},{9,8},{10,11... | collective-permute-start | bytes 675848 | tf_op jit(solution)/shard_map/ppermute | solution.py:382
  27.3 1.5 %collective-permute-start.8 = (f32[80,80]{1,0:T(8,128)S(1)}, f32[80,80]{1,0:T(8,128)S(1)}, u32[]{:S(2)}, u32[]{:S(2)}) collective-permute-start(f32[80,80]{1,0:T(8,128)S(1)} %get-tuple-element.62._.left), channel_id=1, source_target_pairs={{0,1},{1,0},{2,3},{3,2},{4,5},{5,4},{6,7},{7,6},{8,9},{9,8},{10,11... | collective-permute-start | bytes 76808 | tf_op jit(solution)/shard_map/ppermute | solution.py:382
  28.9 4.3 %collective-permute-start.10 = (f32[80,80]{1,0:T(8,128)S(1)}, f32[80,80]{1,0:T(8,128)S(1)}, u32[]{:S(2)}, u32[]{:S(2)}) collective-permute-start(f32[80,80]{1,0:T(8,128)S(1)} %chip_carry.1.refs_2_.refs_0_), channel_id=1, source_target_pairs={{0,2},{1,3},{2,0},{3,1},{4,6},{5,7},{6,4},{7,5},{8,10},{9,11},{10,... | collective-permute-start | bytes 76808 | tf_op jit(solution)/shard_map/ppermute | solution.py:386

commit v19 on v18

--- a/solution.py
+++ b/solution.py
@@ -141,9 +141,8 @@
     more += loads(plan, 0, cotangents, cot, cot_sem, slice(1, None))
     for at in range(count):
         suffixes[plan.rows(at, at + 1)] = kept[at]
-    suffix_scan(suffixes, count, members, count // 2)
-    middle = suffixes[plan.rows(count // 2, count // 2 + 1)]
-    total[...] = mul_exact(suffixes[plan.rows(0, 1)], middle)
+    suffix_scan(suffixes, count, members, count)
+    total[...] = suffixes[plan.rows(0, 1)]
     for copy in more:
         copy.wait()
 
@@ -200,21 +199,21 @@
 
 
 def gram_kernel(
-    plan, ensembles, cotangents, halves, ens, cot,
-    kept, sent, offsets, suffixes, next_ens, next_cot, whole, ens_sem, cot_sem,
+    plan, ensembles, cotangents, suffixes, ens, cot,
+    kept, sent, offsets, next_ens, next_cot, whole, ens_sem, cot_sem,
 ):
-    waiting = iter(list(zip(
-        loads(plan, 1, ensembles, next_ens, ens_sem), loads(plan, 1, cotangents, next_cot, cot_sem)
-    )))
+    pairs = []
+    for at in range(len(plan.piece_groups[1])):
+        pairs.append(
+            loads(plan, 1, ensembles, next_ens, ens_sem, slice(at, at + 1))
+            + loads(plan, 1, cotangents, next_cot, cot_sem, slice(at, at + 1))
+        )
+    waiting = iter(pairs)
 
     def ready():
         for copy in next(waiting):
             copy.wait()
 
-    count, middle = plan.count, plan.count // 2
-    first, last = plan.rows(0, middle), plan.rows(middle, count)
-    suffixes[first] = mul_exact(halves[first], halves[plan.rows(middle, middle + 1)])
-    suffixes[last] = halves[last]
     total = gram_of(plan, 0, cot, ens, suffixes, whole)
     offsets[...] = total + gram_of(plan, 1, next_cot, next_ens, suffixes, whole, ready)
     half = plan.members // 2
@@ -418,10 +417,10 @@
         return total, later, before
 
     other = exchange(total, "tm", blocks, 1)
-    gram, gram_sent, own, suffixes, *second_part = call(
+    gram, gram_sent, own, *second_part = call(
         functools.partial(gram_kernel, plan),
-        [wide, wide, square, shape(count * members, members)] + [piece_shape(1)] * 2,
-        [HBM] * 2 + [VMEM] * 3, [VMEM] * 6,
+        [wide, wide, square] + [piece_shape(1)] * 2,
+        [HBM] * 2 + [VMEM] * 3, [VMEM] * 5,
         [pltpu.VMEM((members, plan.width), F32)] + piece_sems(1), 4.5, "gram",
     )(ensembles, cotangents, suffixes, *first_part)
     parts = [first_part, second_part]

time: 35.6 us -> 34.5 us (0.969)
  Pallas kernels: 19 us -> 17.9 us
    pallas_call x1, Pallas kernels: 5.39 us -> 4.32 us  [shards(): call(functools.partial(gram_kernel, plan), [wide, wide, square] + [piece_...]
  transfers between devices with their start and end apart: 11 -> 11, of which waited for: 1 -> 1; matrix products, arithmetic and copies ran while one was open for 0% -> 0% of each run, Pallas kernels for 39% -> 37%
where the time goes in v19:
time: 34.5 us; the launch traced here: 34.4 us
  Pallas kernels  17.9 us (52%)
  starting transfers between devices  15.4 us (45%)
  between operations  0.77 us (2%)
    ppermute x9, starting transfers between devices, exchange(): return lax.ppermute(value, axis, [(at, at ^ bit) for at in range(size)])  12.2 us
    pallas_call x2, Pallas kernels, apply(): call(functools.partial(apply_kernel, plan), [shape(count, members, cells,...  5.43 us
    pallas_call x1, Pallas kernels, shards(): call(functools.partial(gram_kernel, plan), [wide, wide, square] + [piece_...  4.32 us
    ppermute x2, starting transfers between devices, around(): lax.ppermute(value, 'space', [(at, (at + 2 * d) % lanes) for at in range(...  3.17 us
    pallas_call x1, Pallas kernels, shards(): call(functools.partial(chain_kernel, plan), [shape(count * members, membe...  2.78 us
    pallas_call x1, Pallas kernels, shards(): call(functools.partial(final_kernel, plan, scale), shape(count, members,...  2.21 us
    pallas_call x1, Pallas kernels, shards(): call(functools.partial(windows_kernel, plan), shape(2, count_steps(count)...  0.87 us
    pallas_call x1, Pallas kernels, shards(): call(functools.partial(carry_kernel, plan), [shape(len(plan.groups), size...  0.86 us
  transfers between devices with their start and end apart: 11, of which 1 were waited for; matrix products, arithmetic and copies ran while one was open for 0% of the time, Pallas kernels for 37%

profile of v19, /device:TPU:0, one launch (start us, length us, event | category | flops | bytes accessed | tf_op | source)
XLA Modules:
  0.0 34.4 jit_solution(4549083962158913267)
XLA Ops:
  0.6 2.8 %transform_chain.1 = (f32[1280,80]{1,0:T(8,128)S(1)}, f32[80,80]{1,0:T(8,128)S(1)}, f32[16,80,80]{2,1,0:T(8,128)S(1)}, bf16[6,80,2048]{2,1,0:T(8,128)(2,1)S(1)}, bf16[6,80,2048]{2,1,0:T(8,128)(2,1)S(1)}) custom-call(f32[16,80,80]{2,1,0:T(8,128)} %transforms.1, bf16[16,80,2048]{2,1,0:T(8,128)(2,1)} %ensembles.3, bf16[16,80,2048]{2,1,0:T(8,128)(2,1)} %cotangents.3), custom_call_target="tpu_custom_call" | custom-call | flops 3500000000 | bytes 10500000 | tf_op jit(solution)/shard_map/transform_chain/pallas_call | solution.py:396
  3.4 3.0 %collective-permute-start = (f32[80,80]{1,0:T(8,128)S(1)}, f32[80,80]{1,0:T(8,128)S(1)}, u32[]{:S(2)}, u32[]{:S(2)}) collective-permute-start(f32[80,80]{1,0:T(8,128)S(1)} %get-tuple-element.35.total), channel_id=1, source_target_pairs={{0,4},{4,0},{8,12},{12,8},{16,20},{20,16},{24,28},{28,24},{1,5},{5... | collective-permute-start | bytes 76808 | tf_op jit(solution)/shard_map/ppermute | solution.py:381
  6.4 4.3 %gram.1 = (f32[40,1408]{1,0:T(8,128)S(1)}, f32[40,1408]{1,0:T(8,128)S(1)}, f32[80,80]{1,0:T(8,128)S(1)}, bf16[10,80,2048]{2,1,0:T(8,128)(2,1)S(1)}, bf16[10,80,2048]{2,1,0:T(8,128)(2,1)S(1)}) custom-call(bf16[16,80,2048]{2,1,0:T(8,128)(2,1)} %ensembles.3, bf16[16,80,2048]{2,1,0:T(8,128)(2,1)} %cotangents.3, f32[1280,80]{1,0:T(8,128)S(1)} %get-tuple-element.34.suffixes, ...), custom_call_target="tpu_custom_call" | custom-call | flops 4499999744 | bytes 13500000 | tf_op jit(solution)/shard_map/gram/pallas_call | solution.py:420
  10.7 0.1 collective-permute-start.3
  10.8 0.1 collective-permute-start.2
  10.9 0.0 collective-permute-done.other
  10.9 0.2 join_0.1
  11.2 2.1 %collective-permute-start.1 = (f32[80,80]{1,0:T(8,128)S(1)}, f32[80,80]{1,0:T(8,128)S(1)}, u32[]{:S(2)}, u32[]{:S(2)}) collective-permute-start(f32[80,80]{1,0:T(8,128)S(1)} %get-tuple-element.39._.total), channel_id=1, source_target_pairs={{0,8},{4,12},{8,0},{12,4},{16,24},{20,28},{24,16},{28,20},{1,9},{5... | collective-permute-start | bytes 76808 | tf_op jit(solution)/shard_map/ppermute | solution.py:381
  13.3 0.0 collective-permute-done.3.right
  13.3 1.6 %collective-permute-start.7 = (f32[40,1408]{1,0:T(8,128)S(1)}, f32[40,1408]{1,0:T(8,128)S(1)}, u32[]{:S(2)}, u32[]{:S(2)}) collective-permute-start(f32[40,1408]{1,0:T(8,128)S(1)} %chip_gram.1._), channel_id=1, source_target_pairs={{0,2},{1,3},{2,0},{3,1},{4,6},{5,7},{6,4},{7,5},{8,10},{9,11},{10,... | collective-permute-start | bytes 675848 | tf_op jit(solution)/shard_map/ppermute | solution.py:385
  14.9 0.0 collective-permute-done.2.other
  14.9 0.2 pass_0.1
  15.1 1.6 %collective-permute-start.5 = (f32[80,80]{1,0:T(8,128)S(1)}, f32[80,80]{1,0:T(8,128)S(1)}, u32[]{:S(2)}, u32[]{:S(2)}) collective-permute-start(f32[80,80]{1,0:T(8,128)S(1)} %get-tuple-element.45._.own), channel_id=1, source_target_pairs={{0,8},{4,12},{8,0},{12,4},{16,24},{20,28},{24,16},{28,20},{1,9},{5... | collective-permute-start | bytes 76808 | tf_op jit(solution)/shard_map/ppermute | solution.py:381
  16.7 0.0 collective-permute-done.1.other
  16.7 0.3 join_1.1
  17.0 2.6 %collective-permute-start.4 = (f32[56,128]{1,0:T(8,128)S(1)}, f32[56,128]{1,0:T(8,128)S(1)}, u32[]{:S(2)}, u32[]{:S(2)}) collective-permute-start(f32[56,128]{1,0:T(8,128)S(1)} %get-tuple-element.47._), channel_id=1, source_target_pairs={{0,16},{4,20},{8,24},{12,28},{16,0},{20,4},{24,8},{28,12},{1,17},{... | collective-permute-start | bytes 86024 | tf_op jit(solution)/shard_map/ppermute | solution.py:381
  19.6 0.0 collective-permute-done.5.other
  19.6 0.3 pass_1.1
  19.9 2.2 %collective-permute-start.6 = (f32[56,128]{1,0:T(8,128)S(1)}, f32[56,128]{1,0:T(8,128)S(1)}, u32[]{:S(2)}, u32[]{:S(2)}) collective-permute-start(f32[56,128]{1,0:T(8,128)S(1)} %get-tuple-element.50._), channel_id=1, source_target_pairs={{0,16},{4,20},{8,24},{12,28},{16,0},{20,4},{24,8},{28,12},{1,17},{... | collective-permute-start | bytes 86024 | tf_op jit(solution)/shard_map/ppermute | solution.py:381
  22.1 0.0 collective-permute-done.4.other
  22.1 0.2 entering.1.later
  22.3 0.9 %carries.1 = (bf16[6,240,240]{2,1,0:T(8,128)(2,1)S(1)}, bf16[6,240,240]{2,1,0:T(8,128)(2,1)S(1)}, bf16[2,1280,80]{2,1,0:T(8,128)(2,1)S(1)}) custom-call(f32[1280,80]{1,0:T(8,128)S(1)} %get-tuple-element.34.suffixes, f32[80,80]{1,0:T(8,128)S(1)} %entering.1.later, f32[56,128]{1,0:T(8,128)S(1)} %get-tuple-element.50._), custom_call_target="tpu_custom_call" | custom-call | flops 900000000 | bytes 2700000 | tf_op jit(solution)/shard_map/carries/pallas_call | solution.py:457
  23.2 2.7 %smoothed.1 = (bf16[16,80,2048]{2,1,0:T(8,128)(2,1)}, f32[8,128]{1,0:T(8,128)S(1)}) custom-call(bf16[6,240,240]{2,1,0:T(8,128)(2,1)S(1)} %get-tuple-element.51.factors, bf16[6,80,2048]{2,1,0:T(8,128)(2,1)S(1)} %get-tuple-element.36.ens.refs_0_, bf16[10,80,2048]{2,1,0:T(8,128)(2,1)S(1)} %get-tuple-element.52.refs_1_, ...), custom_call_target="tpu_custom_call" | custom-call | flops 500000000 | bytes 1500000 | tf_op jit(solution)/shard_map/smoothed/pallas_call | solution.py:464
  25.9 0.0 collective-permute-done.6.other
  25.9 0.0 collective-permute-done.7.__
  25.9 0.2 pass_last.1
  26.2 0.1 collective-permute-start.9
  26.3 0.5 %collective-permute-start.8 = (f32[80,80]{1,0:T(8,128)S(1)}, f32[80,80]{1,0:T(8,128)S(1)}, u32[]{:S(2)}, u32[]{:S(2)}) collective-permute-start(f32[80,80]{1,0:T(8,128)S(1)} %get-tuple-element.60._.left), channel_id=1, source_target_pairs={{0,1},{1,0},{2,3},{3,2},{4,5},{5,4},{6,7},{7,6},{8,9},{9,8},{10,11... | collective-permute-start | bytes 76808 | tf_op jit(solution)/shard_map/ppermute | solution.py:381
  26.8 0.9 %windows.1._.steps = bf16[2,2560,80]{2,1,0:T(8,128)(2,1)S(1)} custom-call(f32[16,80,80]{2,1,0:T(8,128)S(1)} %get-tuple-element.61.kept, f32[80,80]{1,0:T(8,128)S(1)} %get-tuple-element.60._.left), custom_call_target="tpu_custom_call" | custom-call | flops 1000000000 | bytes 3000000 | tf_op jit(solution)/shard_map/windows/pallas_call | solution.py:482
  27.6 0.2 collective-permute-done.8.right
  27.8 1.6 %collective-permute-start.10 = (f32[80,80]{1,0:T(8,128)S(1)}, f32[80,80]{1,0:T(8,128)S(1)}, u32[]{:S(2)}, u32[]{:S(2)}) collective-permute-start(f32[80,80]{1,0:T(8,128)S(1)} %chip_carry.1.refs_2_.refs_0_), channel_id=1, source_target_pairs={{0,2},{1,3},{2,0},{3,1},{4,6},{5,7},{6,4},{7,5},{8,10},{9,11},{10,... | collective-permute-start | bytes 76808 | tf_op jit(solution)/shard_map/ppermute | solution.py:385
  29.4 2.7 %ensemble_grad.1 = (bf16[16,80,2048]{2,1,0:T(8,128)(2,1)}, f32[8,128]{1,0:T(8,128)S(1)}) custom-call(bf16[6,240,240]{2,1,0:T(8,128)(2,1)S(1)} %get-tuple-element.55.factors, bf16[6,80,2048]{2,1,0:T(8,128)(2,1)S(1)} %get-tuple-element.37.cot.refs_0_, bf16[10,80,2048]{2,1,0:T(8,128)(2,1)S(1)} %get-tuple-element.56.refs_1_, f32[80,80]{1,0:T(8,128)S(1)} %chip_carry.1.refs_2_.refs_0_), custom_call_target="tpu_custom_call" | custom-call | flops 500000000 | bytes 1500000 | tf_op jit(solution)/shard_map/ensemble_grad/pallas_call | solution.py:464
  32.1 0.0 collective-permute-done.10.refs_1_
  32.1 0.0 collective-permute-done.9.gram_core
  32.1 2.2 %transform_grad.1 = f32[16,80,80]{2,1,0:T(8,128)} custom-call(f32[40,1408]{1,0:T(8,128)S(1)} %add.3.gram, f32[40,1408]{1,0:T(8,128)S(1)} %collective-permute-done.9.gram_core, bf16[2,1280,80]{2,1,0:T(8,128)(2,1)S(1)} %get-tuple-element.53.refs_2_.follow, bf16[2,2560,80]{2,1,0:T(8,128)(2,1)S(1)} %windows.1._.steps, f32[8,128]{1,0:T(8,128)S(1)} %get-tuple-element.64._, ...), custom_call_target="tpu_custom_call" | custom-call | flops 2500000000 | bytes 7500000 | tf_op jit(solution)/shard_map/transform_grad/pallas_call | solution.py:492
  (5 shorter events, 0.1 us)
Async XLA Ops:
  3.4 7.5 %collective-permute-start = (f32[80,80]{1,0:T(8,128)S(1)}, f32[80,80]{1,0:T(8,128)S(1)}, u32[]{:S(2)}, u32[]{:S(2)}) collective-permute-start(f32[80,80]{1,0:T(8,128)S(1)} %get-tuple-element.35.total), channel_id=1, source_target_pairs={{0,4},{4,0},{8,12},{12,8},{16,20},{20,16},{24,28},{28,24},{1,5},{5... | collective-permute-start | bytes 76808 | tf_op jit(solution)/shard_map/ppermute | solution.py:381
  10.7 2.6 %collective-permute-start.3 = (f32[40,1408]{1,0:T(8,128)S(1)}, f32[40,1408]{1,0:T(8,128)S(1)}, u32[]{:S(2)}, u32[]{:S(2)}) collective-permute-start(f32[40,1408]{1,0:T(8,128)S(1)} %get-tuple-element.44), channel_id=1, source_target_pairs={{0,1},{1,0},{2,3},{3,2},{4,5},{5,4},{6,7},{7,6},{8,9},{9,8},{10,11... | collective-permute-start | bytes 675848 | tf_op jit(solution)/shard_map/ppermute | solution.py:381
  10.8 4.1 %collective-permute-start.2 = (f32[80,80]{1,0:T(8,128)S(1)}, f32[80,80]{1,0:T(8,128)S(1)}, u32[]{:S(2)}, u32[]{:S(2)}) collective-permute-start(f32[80,80]{1,0:T(8,128)S(1)} %get-tuple-element.38._.own), channel_id=1, source_target_pairs={{0,4},{4,0},{8,12},{12,8},{16,20},{20,16},{24,28},{28,24},{1,5},{5... | collective-permute-start | bytes 76808 | tf_op jit(solution)/shard_map/ppermute | solution.py:381
  11.2 5.6 %collective-permute-start.1 = (f32[80,80]{1,0:T(8,128)S(1)}, f32[80,80]{1,0:T(8,128)S(1)}, u32[]{:S(2)}, u32[]{:S(2)}) collective-permute-start(f32[80,80]{1,0:T(8,128)S(1)} %get-tuple-element.39._.total), channel_id=1, source_target_pairs={{0,8},{4,12},{8,0},{12,4},{16,24},{20,28},{24,16},{28,20},{1,9},{5... | collective-permute-start | bytes 76808 | tf_op jit(solution)/shard_map/ppermute | solution.py:381
  13.3 12.6 %collective-permute-start.7 = (f32[40,1408]{1,0:T(8,128)S(1)}, f32[40,1408]{1,0:T(8,128)S(1)}, u32[]{:S(2)}, u32[]{:S(2)}) collective-permute-start(f32[40,1408]{1,0:T(8,128)S(1)} %chip_gram.1._), channel_id=1, source_target_pairs={{0,2},{1,3},{2,0},{3,1},{4,6},{5,7},{6,4},{7,5},{8,10},{9,11},{10,... | collective-permute-start | bytes 675848 | tf_op jit(solution)/shard_map/ppermute | solution.py:385
  15.1 4.5 %collective-permute-start.5 = (f32[80,80]{1,0:T(8,128)S(1)}, f32[80,80]{1,0:T(8,128)S(1)}, u32[]{:S(2)}, u32[]{:S(2)}) collective-permute-start(f32[80,80]{1,0:T(8,128)S(1)} %get-tuple-element.45._.own), channel_id=1, source_target_pairs={{0,8},{4,12},{8,0},{12,4},{16,24},{20,28},{24,16},{28,20},{1,9},{5... | collective-permute-start | bytes 76808 | tf_op jit(solution)/shard_map/ppermute | solution.py:381
  17.0 5.1 %collective-permute-start.4 = (f32[56,128]{1,0:T(8,128)S(1)}, f32[56,128]{1,0:T(8,128)S(1)}, u32[]{:S(2)}, u32[]{:S(2)}) collective-permute-start(f32[56,128]{1,0:T(8,128)S(1)} %get-tuple-element.47._), channel_id=1, source_target_pairs={{0,16},{4,20},{8,24},{12,28},{16,0},{20,4},{24,8},{28,12},{1,17},{... | collective-permute-start | bytes 86024 | tf_op jit(solution)/shard_map/ppermute | solution.py:381
  19.9 6.0 %collective-permute-start.6 = (f32[56,128]{1,0:T(8,128)S(1)}, f32[56,128]{1,0:T(8,128)S(1)}, u32[]{:S(2)}, u32[]{:S(2)}) collective-permute-start(f32[56,128]{1,0:T(8,128)S(1)} %get-tuple-element.50._), channel_id=1, source_target_pairs={{0,16},{4,20},{8,24},{12,28},{16,0},{20,4},{24,8},{28,12},{1,17},{... | collective-permute-start | bytes 86024 | tf_op jit(solution)/shard_map/ppermute | solution.py:381
  26.2 5.9 %collective-permute-start.9 = (f32[40,1408]{1,0:T(8,128)S(1)}, f32[40,1408]{1,0:T(8,128)S(1)}, u32[]{:S(2)}, u32[]{:S(2)}) collective-permute-start(f32[40,1408]{1,0:T(8,128)S(1)} %add.3.gram), channel_id=1, source_target_pairs={{0,1},{1,0},{2,3},{3,2},{4,5},{5,4},{6,7},{7,6},{8,9},{9,8},{10,11... | collective-permute-start | bytes 675848 | tf_op jit(solution)/shard_map/ppermute | solution.py:381
  26.3 1.5 %collective-permute-start.8 = (f32[80,80]{1,0:T(8,128)S(1)}, f32[80,80]{1,0:T(8,128)S(1)}, u32[]{:S(2)}, u32[]{:S(2)}) collective-permute-start(f32[80,80]{1,0:T(8,128)S(1)} %get-tuple-element.60._.left), channel_id=1, source_target_pairs={{0,1},{1,0},{2,3},{3,2},{4,5},{5,4},{6,7},{7,6},{8,9},{9,8},{10,11... | collective-permute-start | bytes 76808 | tf_op jit(solution)/shard_map/ppermute | solution.py:381
  27.8 4.3 %collective-permute-start.10 = (f32[80,80]{1,0:T(8,128)S(1)}, f32[80,80]{1,0:T(8,128)S(1)}, u32[]{:S(2)}, u32[]{:S(2)}) collective-permute-start(f32[80,80]{1,0:T(8,128)S(1)} %chip_carry.1.refs_2_.refs_0_), channel_id=1, source_target_pairs={{0,2},{1,3},{2,0},{3,1},{4,6},{5,7},{6,4},{7,5},{8,10},{9,11},{10,... | collective-permute-start | bytes 76808 | tf_op jit(solution)/shard_map/ppermute | solution.py:385

commit v20 on v19

--- a/solution.py
+++ b/solution.py
@@ -147,7 +147,7 @@
         copy.wait()
 
 
-def windows_kernel(plan, kept, _, steps, runs):
+def windows_kernel(plan, kept, _, __, steps, ___, runs):
     count = plan.count
     for at in range(count - 1):
         runs[plan.rows(at + 1, at + 2)] = kept[at].T
@@ -250,7 +250,7 @@
     new_carry[...] = carry[...] + jnp.where(upper, mul_small(left, before[...]), 0.0)
 
 
-def last_pass_kernel(level, other, carry, before, _, __, new_carry, ___):
+def last_pass_kernel(level, other, carry, before, _, new_carry):
     added = mul_small(unpack(other[...], before.shape[0]), before[...])
     new_carry[...] = carry[...] + jnp.where(upper_half(level), added, 0.0)
 
@@ -460,35 +460,36 @@
         + [shape(2, count * members, members, kind=BF16)],
         [VMEM] * 2 + [ANY], [VMEM] * 3, [], 0.9, "carries",
     )(suffixes, entering, own)
-    def apply(factors, which, after, name):
+    def apply(factors, which, after, name, micros):
         return call(
             functools.partial(apply_kernel, plan),
             [shape(count, members, cells, kind=BF16), shape(8, 128)],
             [VMEM] * (1 + PIECES) + [ANY], [HBM, VMEM],
             [pltpu.VMEM((count, members, cells), BF16),
              pltpu.SemaphoreType.DMA((2 * len(plan.groups),))],
-            0.5, name,
+            micros, name,
         )(factors, *(part[which] for part in parts), after)
 
-    smoothed, done = apply(ens_factors, 0, follow, "smoothed")
-    carry, grams[0] = call(
+    smoothed, done = apply(ens_factors, 0, follow, "smoothed", 0.5)
+    carry = call(
         functools.partial(last_pass_kernel, levels - 1),
-        [square, wide], [VMEM] * 3 + [ANY] * 2, [VMEM, ANY], [], 0.2, "pass_last", aliases={4: 1},
-    )(other_own, carry, befores[-1], done, grams[0])
+        square, [VMEM] * 3 + [ANY], VMEM, [], 0.2, "pass_last",
+    )(other_own, carry, befores[-1], done)
     carry_core = exchange(carry, "space", lanes, 1)
+    steps, grams[0] = call(
+        functools.partial(windows_kernel, plan),
+        [shape(2, count_steps(count) * members, members, kind=BF16), wide],
+        [VMEM, ANY, ANY], [VMEM, ANY],
+        [pltpu.VMEM((count * members, members), F32)], 1.0, "windows", aliases={2: 1},
+    )(kept, carry, grams[0])
     for part in grams:
         gram = gram + part
     gram_core = exchange(gram, "space", lanes, 1)
-    steps = call(
-        functools.partial(windows_kernel, plan),
-        shape(2, count_steps(count) * members, members, kind=BF16), [VMEM, ANY], VMEM,
-        [pltpu.VMEM((count * members, members), F32)], 1.0, "windows",
-    )(kept, carry)
     carry = call(
         sum_kernel, square, [VMEM] * 2 + [ANY], VMEM, [], 0.1, "chip_carry",
     )(carry, carry_core, steps)
     carries = [carry] + around(carry)
-    ensemble_grad, done = apply(cot_factors, 1, carry, "ensemble_grad")
+    ensemble_grad, done = apply(cot_factors, 1, carry, "ensemble_grad", 5)
     transform_grad = call(
         functools.partial(final_kernel, plan, scale),
         shape(count, members, members),

time: 34.5 us -> 34.4 us (level)
  transfers between devices with their start and end apart: 11 -> 11, of which waited for: 1 -> 0; matrix products, arithmetic and copies ran while one was open for 0% -> 0% of each run, Pallas kernels for 37% -> 38%
where the time goes in v20:
time: 34.4 us; the launch traced here: 34.3 us
  Pallas kernels  17.9 us (52%)
  starting transfers between devices  15.5 us (45%)
  between operations  0.78 us (2%)
    ppermute x9, starting transfers between devices, exchange(): return lax.ppermute(value, axis, [(at, at ^ bit) for at in range(size)])  12.3 us
    pallas_call x2, Pallas kernels, apply(): call(functools.partial(apply_kernel, plan), [shape(count, members, cells,...  5.43 us
    pallas_call x1, Pallas kernels, shards(): call(functools.partial(gram_kernel, plan), [wide, wide, square] + [piece_...  4.32 us
    ppermute x2, starting transfers between devices, around(): lax.ppermute(value, 'space', [(at, (at + 2 * d) % lanes) for at in range(...  3.17 us
    pallas_call x1, Pallas kernels, shards(): call(functools.partial(chain_kernel, plan), [shape(count * members, membe...  2.78 us
    pallas_call x1, Pallas kernels, shards(): call(functools.partial(final_kernel, plan, scale), shape(count, members,...  2.21 us
    pallas_call x1, Pallas kernels, shards(): call(functools.partial(windows_kernel, plan), [shape(2, count_steps(count...  0.88 us
    pallas_call x1, Pallas kernels, shards(): call(functools.partial(carry_kernel, plan), [shape(len(plan.groups), size...  0.86 us
  transfers between devices with their start and end apart: 11, of which 0 were waited for; matrix products, arithmetic and copies ran while one was open for 0% of the time, Pallas kernels for 38%

profile of v20, /device:TPU:0, one launch (start us, length us, event | category | flops | bytes accessed | tf_op | source)
XLA Modules:
  0.0 34.3 jit_solution(5104896162417927072)
XLA Ops:
  0.6 2.8 %transform_chain.1 = (f32[1280,80]{1,0:T(8,128)S(1)}, f32[80,80]{1,0:T(8,128)S(1)}, f32[16,80,80]{2,1,0:T(8,128)S(1)}, bf16[6,80,2048]{2,1,0:T(8,128)(2,1)S(1)}, bf16[6,80,2048]{2,1,0:T(8,128)(2,1)S(1)}) custom-call(f32[16,80,80]{2,1,0:T(8,128)} %transforms.1, bf16[16,80,2048]{2,1,0:T(8,128)(2,1)} %ensembles.3, bf16[16,80,2048]{2,1,0:T(8,128)(2,1)} %cotangents.3), custom_call_target="tpu_custom_call" | custom-call | flops 3500000000 | bytes 10500000 | tf_op jit(solution)/shard_map/transform_chain/pallas_call | solution.py:396
  3.4 3.0 %collective-permute-start = (f32[80,80]{1,0:T(8,128)S(1)}, f32[80,80]{1,0:T(8,128)S(1)}, u32[]{:S(2)}, u32[]{:S(2)}) collective-permute-start(f32[80,80]{1,0:T(8,128)S(1)} %get-tuple-element.35.total), channel_id=1, source_target_pairs={{0,4},{4,0},{8,12},{12,8},{16,20},{20,16},{24,28},{28,24},{1,5},{5... | collective-permute-start | bytes 76808 | tf_op jit(solution)/shard_map/ppermute | solution.py:381
  6.4 4.3 %gram.1 = (f32[40,1408]{1,0:T(8,128)S(1)}, f32[40,1408]{1,0:T(8,128)S(1)}, f32[80,80]{1,0:T(8,128)S(1)}, bf16[10,80,2048]{2,1,0:T(8,128)(2,1)S(1)}, bf16[10,80,2048]{2,1,0:T(8,128)(2,1)S(1)}) custom-call(bf16[16,80,2048]{2,1,0:T(8,128)(2,1)} %ensembles.3, bf16[16,80,2048]{2,1,0:T(8,128)(2,1)} %cotangents.3, f32[1280,80]{1,0:T(8,128)S(1)} %get-tuple-element.34.suffixes, ...), custom_call_target="tpu_custom_call" | custom-call | flops 4499999744 | bytes 13500000 | tf_op jit(solution)/shard_map/gram/pallas_call | solution.py:420
  10.7 0.1 collective-permute-start.3
  10.8 0.1 collective-permute-start.2
  10.9 0.0 collective-permute-done.other
  10.9 0.2 join_0.1
  11.2 2.1 %collective-permute-start.1 = (f32[80,80]{1,0:T(8,128)S(1)}, f32[80,80]{1,0:T(8,128)S(1)}, u32[]{:S(2)}, u32[]{:S(2)}) collective-permute-start(f32[80,80]{1,0:T(8,128)S(1)} %get-tuple-element.39._.total), channel_id=1, source_target_pairs={{0,8},{4,12},{8,0},{12,4},{16,24},{20,28},{24,16},{28,20},{1,9},{5... | collective-permute-start | bytes 76808 | tf_op jit(solution)/shard_map/ppermute | solution.py:381
  13.3 0.0 collective-permute-done.3.right
  13.3 1.6 %collective-permute-start.8 = (f32[40,1408]{1,0:T(8,128)S(1)}, f32[40,1408]{1,0:T(8,128)S(1)}, u32[]{:S(2)}, u32[]{:S(2)}) collective-permute-start(f32[40,1408]{1,0:T(8,128)S(1)} %chip_gram.1._), channel_id=1, source_target_pairs={{0,2},{1,3},{2,0},{3,1},{4,6},{5,7},{6,4},{7,5},{8,10},{9,11},{10,... | collective-permute-start | bytes 675848 | tf_op jit(solution)/shard_map/ppermute | solution.py:385
  14.9 0.0 collective-permute-done.2.other
  14.9 0.2 pass_0.1
  15.1 1.6 %collective-permute-start.5 = (f32[80,80]{1,0:T(8,128)S(1)}, f32[80,80]{1,0:T(8,128)S(1)}, u32[]{:S(2)}, u32[]{:S(2)}) collective-permute-start(f32[80,80]{1,0:T(8,128)S(1)} %get-tuple-element.45._.own), channel_id=1, source_target_pairs={{0,8},{4,12},{8,0},{12,4},{16,24},{20,28},{24,16},{28,20},{1,9},{5... | collective-permute-start | bytes 76808 | tf_op jit(solution)/shard_map/ppermute | solution.py:381
  16.7 0.0 collective-permute-done.1.other
  16.7 0.3 join_1.1
  17.0 2.6 %collective-permute-start.4 = (f32[56,128]{1,0:T(8,128)S(1)}, f32[56,128]{1,0:T(8,128)S(1)}, u32[]{:S(2)}, u32[]{:S(2)}) collective-permute-start(f32[56,128]{1,0:T(8,128)S(1)} %get-tuple-element.47._), channel_id=1, source_target_pairs={{0,16},{4,20},{8,24},{12,28},{16,0},{20,4},{24,8},{28,12},{1,17},{... | collective-permute-start | bytes 86024 | tf_op jit(solution)/shard_map/ppermute | solution.py:381
  19.6 0.0 collective-permute-done.5.other
  19.6 0.3 pass_1.1
  19.9 2.2 %collective-permute-start.6 = (f32[56,128]{1,0:T(8,128)S(1)}, f32[56,128]{1,0:T(8,128)S(1)}, u32[]{:S(2)}, u32[]{:S(2)}) collective-permute-start(f32[56,128]{1,0:T(8,128)S(1)} %get-tuple-element.50._), channel_id=1, source_target_pairs={{0,16},{4,20},{8,24},{12,28},{16,0},{20,4},{24,8},{28,12},{1,17},{... | collective-permute-start | bytes 86024 | tf_op jit(solution)/shard_map/ppermute | solution.py:381
  22.1 0.0 collective-permute-done.4.other
  22.1 0.2 entering.1.later
  22.3 0.9 %carries.1 = (bf16[6,240,240]{2,1,0:T(8,128)(2,1)S(1)}, bf16[6,240,240]{2,1,0:T(8,128)(2,1)S(1)}, bf16[2,1280,80]{2,1,0:T(8,128)(2,1)S(1)}) custom-call(f32[1280,80]{1,0:T(8,128)S(1)} %get-tuple-element.34.suffixes, f32[80,80]{1,0:T(8,128)S(1)} %entering.1.later, f32[56,128]{1,0:T(8,128)S(1)} %get-tuple-element.50._), custom_call_target="tpu_custom_call" | custom-call | flops 900000000 | bytes 2700000 | tf_op jit(solution)/shard_map/carries/pallas_call | solution.py:457
  23.2 2.7 %smoothed.1 = (bf16[16,80,2048]{2,1,0:T(8,128)(2,1)}, f32[8,128]{1,0:T(8,128)S(1)}) custom-call(bf16[6,240,240]{2,1,0:T(8,128)(2,1)S(1)} %get-tuple-element.51.factors, bf16[6,80,2048]{2,1,0:T(8,128)(2,1)S(1)} %get-tuple-element.36.ens.refs_0_, bf16[10,80,2048]{2,1,0:T(8,128)(2,1)S(1)} %get-tuple-element.52.refs_1_, ...), custom_call_target="tpu_custom_call" | custom-call | flops 500000000 | bytes 1500000 | tf_op jit(solution)/shard_map/smoothed/pallas_call | solution.py:464
  25.9 0.0 collective-permute-done.6.other
  25.9 0.2 pass_last.1._.left
  26.1 0.1 collective-permute-start.7
  26.2 0.0 collective-permute-done.8.__
  26.2 0.9 %windows.1 = (bf16[2,2560,80]{2,1,0:T(8,128)(2,1)S(1)}, f32[40,1408]{1,0:T(8,128)S(1)}) custom-call(f32[16,80,80]{2,1,0:T(8,128)S(1)} %get-tuple-element.60.kept, f32[80,80]{1,0:T(8,128)S(1)} %pass_last.1._.left, f32[40,1408]{1,0:T(8,128)S(1)} %collective-permute-done.8.__), custom_call_target="tpu_custom_call", output_to_operand_aliasing={{1}: (2, {})} | custom-call | flops 1000000000 | bytes 3000000 | tf_op jit(solution)/shard_map/windows/pallas_call | solution.py:479
  27.1 0.6 %collective-permute-start.9 = (f32[40,1408]{1,0:T(8,128)S(1)}, f32[40,1408]{1,0:T(8,128)S(1)}, u32[]{:S(2)}, u32[]{:S(2)}) collective-permute-start(f32[40,1408]{1,0:T(8,128)S(1)} %add.3.gram), channel_id=1, source_target_pairs={{0,1},{1,0},{2,3},{3,2},{4,5},{5,4},{6,7},{7,6},{8,9},{9,8},{10,11... | collective-permute-start | bytes 675848 | tf_op jit(solution)/shard_map/ppermute | solution.py:381
  27.7 0.0 collective-permute-done.7.right
  27.7 1.6 %collective-permute-start.10 = (f32[80,80]{1,0:T(8,128)S(1)}, f32[80,80]{1,0:T(8,128)S(1)}, u32[]{:S(2)}, u32[]{:S(2)}) collective-permute-start(f32[80,80]{1,0:T(8,128)S(1)} %chip_carry.1.refs_2_.refs_0_), channel_id=1, source_target_pairs={{0,2},{1,3},{2,0},{3,1},{4,6},{5,7},{6,4},{7,5},{8,10},{9,11},{10,... | collective-permute-start | bytes 76808 | tf_op jit(solution)/shard_map/ppermute | solution.py:385
  29.3 2.7 %ensemble_grad.1 = (bf16[16,80,2048]{2,1,0:T(8,128)(2,1)}, f32[8,128]{1,0:T(8,128)S(1)}) custom-call(bf16[6,240,240]{2,1,0:T(8,128)(2,1)S(1)} %get-tuple-element.55.factors, bf16[6,80,2048]{2,1,0:T(8,128)(2,1)S(1)} %get-tuple-element.37.cot.refs_0_, bf16[10,80,2048]{2,1,0:T(8,128)(2,1)S(1)} %get-tuple-element.56.refs_1_, f32[80,80]{1,0:T(8,128)S(1)} %chip_carry.1.refs_2_.refs_0_), custom_call_target="tpu_custom_call" | custom-call | flops 5000000000 | bytes 15000000 | tf_op jit(solution)/shard_map/ensemble_grad/pallas_call | solution.py:464
  32.0 0.0 collective-permute-done.10.refs_1_
  32.0 0.0 collective-permute-done.9.gram_core
  32.0 2.2 %transform_grad.1 = f32[16,80,80]{2,1,0:T(8,128)} custom-call(f32[40,1408]{1,0:T(8,128)S(1)} %add.3.gram, f32[40,1408]{1,0:T(8,128)S(1)} %collective-permute-done.9.gram_core, bf16[2,1280,80]{2,1,0:T(8,128)(2,1)S(1)} %get-tuple-element.53.refs_2_.follow, bf16[2,2560,80]{2,1,0:T(8,128)(2,1)S(1)} %get-tuple-element.61._.steps, ...), custom_call_target="tpu_custom_call" | custom-call | flops 2500000000 | bytes 7500000 | tf_op jit(solution)/shard_map/transform_grad/pallas_call | solution.py:493
  (5 shorter events, 0.1 us)
Async XLA Ops:
  3.4 7.5 %collective-permute-start = (f32[80,80]{1,0:T(8,128)S(1)}, f32[80,80]{1,0:T(8,128)S(1)}, u32[]{:S(2)}, u32[]{:S(2)}) collective-permute-start(f32[80,80]{1,0:T(8,128)S(1)} %get-tuple-element.35.total), channel_id=1, source_target_pairs={{0,4},{4,0},{8,12},{12,8},{16,20},{20,16},{24,28},{28,24},{1,5},{5... | collective-permute-start | bytes 76808 | tf_op jit(solution)/shard_map/ppermute | solution.py:381
  10.7 2.6 %collective-permute-start.3 = (f32[40,1408]{1,0:T(8,128)S(1)}, f32[40,1408]{1,0:T(8,128)S(1)}, u32[]{:S(2)}, u32[]{:S(2)}) collective-permute-start(f32[40,1408]{1,0:T(8,128)S(1)} %get-tuple-element.44), channel_id=1, source_target_pairs={{0,1},{1,0},{2,3},{3,2},{4,5},{5,4},{6,7},{7,6},{8,9},{9,8},{10,11... | collective-permute-start | bytes 675848 | tf_op jit(solution)/shard_map/ppermute | solution.py:381
  10.8 4.1 %collective-permute-start.2 = (f32[80,80]{1,0:T(8,128)S(1)}, f32[80,80]{1,0:T(8,128)S(1)}, u32[]{:S(2)}, u32[]{:S(2)}) collective-permute-start(f32[80,80]{1,0:T(8,128)S(1)} %get-tuple-element.38._.own), channel_id=1, source_target_pairs={{0,4},{4,0},{8,12},{12,8},{16,20},{20,16},{24,28},{28,24},{1,5},{5... | collective-permute-start | bytes 76808 | tf_op jit(solution)/shard_map/ppermute | solution.py:381
  11.2 5.6 %collective-permute-start.1 = (f32[80,80]{1,0:T(8,128)S(1)}, f32[80,80]{1,0:T(8,128)S(1)}, u32[]{:S(2)}, u32[]{:S(2)}) collective-permute-start(f32[80,80]{1,0:T(8,128)S(1)} %get-tuple-element.39._.total), channel_id=1, source_target_pairs={{0,8},{4,12},{8,0},{12,4},{16,24},{20,28},{24,16},{28,20},{1,9},{5... | collective-permute-start | bytes 76808 | tf_op jit(solution)/shard_map/ppermute | solution.py:381
  13.3 12.9 %collective-permute-start.8 = (f32[40,1408]{1,0:T(8,128)S(1)}, f32[40,1408]{1,0:T(8,128)S(1)}, u32[]{:S(2)}, u32[]{:S(2)}) collective-permute-start(f32[40,1408]{1,0:T(8,128)S(1)} %chip_gram.1._), channel_id=1, source_target_pairs={{0,2},{1,3},{2,0},{3,1},{4,6},{5,7},{6,4},{7,5},{8,10},{9,11},{10,... | collective-permute-start | bytes 675848 | tf_op jit(solution)/shard_map/ppermute | solution.py:385
  15.1 4.5 %collective-permute-start.5 = (f32[80,80]{1,0:T(8,128)S(1)}, f32[80,80]{1,0:T(8,128)S(1)}, u32[]{:S(2)}, u32[]{:S(2)}) collective-permute-start(f32[80,80]{1,0:T(8,128)S(1)} %get-tuple-element.45._.own), channel_id=1, source_target_pairs={{0,8},{4,12},{8,0},{12,4},{16,24},{20,28},{24,16},{28,20},{1,9},{5... | collective-permute-start | bytes 76808 | tf_op jit(solution)/shard_map/ppermute | solution.py:381
  17.0 5.1 %collective-permute-start.4 = (f32[56,128]{1,0:T(8,128)S(1)}, f32[56,128]{1,0:T(8,128)S(1)}, u32[]{:S(2)}, u32[]{:S(2)}) collective-permute-start(f32[56,128]{1,0:T(8,128)S(1)} %get-tuple-element.47._), channel_id=1, source_target_pairs={{0,16},{4,20},{8,24},{12,28},{16,0},{20,4},{24,8},{28,12},{1,17},{... | collective-permute-start | bytes 86024 | tf_op jit(solution)/shard_map/ppermute | solution.py:381
  19.9 6.0 %collective-permute-start.6 = (f32[56,128]{1,0:T(8,128)S(1)}, f32[56,128]{1,0:T(8,128)S(1)}, u32[]{:S(2)}, u32[]{:S(2)}) collective-permute-start(f32[56,128]{1,0:T(8,128)S(1)} %get-tuple-element.50._), channel_id=1, source_target_pairs={{0,16},{4,20},{8,24},{12,28},{16,0},{20,4},{24,8},{28,12},{1,17},{... | collective-permute-start | bytes 86024 | tf_op jit(solution)/shard_map/ppermute | solution.py:381
  26.1 1.6 %collective-permute-start.7 = (f32[80,80]{1,0:T(8,128)S(1)}, f32[80,80]{1,0:T(8,128)S(1)}, u32[]{:S(2)}, u32[]{:S(2)}) collective-permute-start(f32[80,80]{1,0:T(8,128)S(1)} %pass_last.1._.left), channel_id=1, source_target_pairs={{0,1},{1,0},{2,3},{3,2},{4,5},{5,4},{6,7},{7,6},{8,9},{9,8},{10,11... | collective-permute-start | bytes 76808 | tf_op jit(solution)/shard_map/ppermute | solution.py:381
  27.1 4.9 %collective-permute-start.9 = (f32[40,1408]{1,0:T(8,128)S(1)}, f32[40,1408]{1,0:T(8,128)S(1)}, u32[]{:S(2)}, u32[]{:S(2)}) collective-permute-start(f32[40,1408]{1,0:T(8,128)S(1)} %add.3.gram), channel_id=1, source_target_pairs={{0,1},{1,0},{2,3},{3,2},{4,5},{5,4},{6,7},{7,6},{8,9},{9,8},{10,11... | collective-permute-start | bytes 675848 | tf_op jit(solution)/shard_map/ppermute | solution.py:381
  27.7 4.3 %collective-permute-start.10 = (f32[80,80]{1,0:T(8,128)S(1)}, f32[80,80]{1,0:T(8,128)S(1)}, u32[]{:S(2)}, u32[]{:S(2)}) collective-permute-start(f32[80,80]{1,0:T(8,128)S(1)} %chip_carry.1.refs_2_.refs_0_), channel_id=1, source_target_pairs={{0,2},{1,3},{2,0},{3,1},{4,6},{5,7},{6,4},{7,5},{8,10},{9,11},{10,... | collective-permute-start | bytes 76808 | tf_op jit(solution)/shard_map/ppermute | solution.py:385

commit v21 on v19

--- a/solution.py
+++ b/solution.py
@@ -255,14 +255,10 @@
     new_carry[...] = carry[...] + jnp.where(upper_half(level), added, 0.0)
 
 
-def enter_kernel(level, later, other, _, entering):
-    joined = mul_small(later[...], unpack(other[...], later.shape[0]))
-    entering[...] = jnp.where(upper_half(level), later[...], joined)
-
-
-def carry_kernel(plan, suffixes, later, _, ens_factors, cot_factors, follow):
+def carry_kernel(plan, level, suffixes, later, other, _, ens_factors, cot_factors, follow):
     count, members = plan.count, plan.members
-    entering = later[...]
+    joined = mul_small(later[...], unpack(other[...], members))
+    entering = jnp.where(upper_half(level), later[...], joined)
     mask = on_blocks(members, plan.stack * members)
     repeated = split(jnp.concatenate([entering] * plan.stack, axis=1))
     for at, (start, stop) in enumerate(plan.groups):
@@ -449,17 +445,13 @@
     befores.append(before)
     own, carry = pass_on(levels - 2, carry, total)
     other_own = exchange(own, "tm", blocks, blocks // 2)
-    entering = call(
-        functools.partial(enter_kernel, levels - 1),
-        square, [VMEM] * 2 + [ANY], VMEM, [], 0.2, "entering",
-    )(later, other, own)
     size = plan.stack * members
     ens_factors, cot_factors, follow = call(
-        functools.partial(carry_kernel, plan),
+        functools.partial(carry_kernel, plan, levels - 1),
         [shape(len(plan.groups), size, size, kind=BF16)] * 2
         + [shape(2, count * members, members, kind=BF16)],
-        [VMEM] * 2 + [ANY], [VMEM] * 3, [], 0.9, "carries",
-    )(suffixes, entering, own)
+        [VMEM] * 3 + [ANY], [VMEM] * 3, [], 0.9, "carries",
+    )(suffixes, later, other, own)
     def apply(factors, which, after, name):
         return call(
             functools.partial(apply_kernel, plan),

time: 34.5 us -> 34.5 us (level)
    pallas_call x2 -> x1, Pallas kernels: 1.08 us -> 1.06 us  [shards(): call(functools.partial(carry_kernel, plan, levels - 1), [shape(len(plan.g...]
where the time goes in v21:
time: 34.5 us; the launch traced here: 34.3 us
  Pallas kernels  17.9 us (52%)
  starting transfers between devices  15.4 us (45%)
  between operations  0.77 us (2%)
    ppermute x9, starting transfers between devices, exchange(): return lax.ppermute(value, axis, [(at, at ^ bit) for at in range(size)])  12.2 us
    pallas_call x2, Pallas kernels, apply(): call(functools.partial(apply_kernel, plan), [shape(count, members, cells,...  5.44 us
    pallas_call x1, Pallas kernels, shards(): call(functools.partial(gram_kernel, plan), [wide, wide, square] + [piece_...  4.32 us
    ppermute x2, starting transfers between devices, around(): lax.ppermute(value, 'space', [(at, (at + 2 * d) % lanes) for at in range(...  3.17 us
    pallas_call x1, Pallas kernels, shards(): call(functools.partial(chain_kernel, plan), [shape(count * members, membe...  2.78 us
    pallas_call x1, Pallas kernels, shards(): call(functools.partial(final_kernel, plan, scale), shape(count, members,...  2.21 us
    pallas_call x1, Pallas kernels, shards(): call(functools.partial(carry_kernel, plan, levels - 1), [shape(len(plan.g...  1.06 us
    pallas_call x1, Pallas kernels, shards(): call(functools.partial(windows_kernel, plan), shape(2, count_steps(count)...  0.87 us
  transfers between devices with their start and end apart: 11, of which 1 were waited for; matrix products, arithmetic and copies ran while one was open for 0% of the time, Pallas kernels for 37%

profile of v21, /device:TPU:0, one launch (start us, length us, event | category | flops | bytes accessed | tf_op | source)
XLA Modules:
  0.0 34.3 jit_solution(13197949089114631453)
XLA Ops:
  0.6 2.8 %transform_chain.1 = (f32[1280,80]{1,0:T(8,128)S(1)}, f32[80,80]{1,0:T(8,128)S(1)}, f32[16,80,80]{2,1,0:T(8,128)S(1)}, bf16[6,80,2048]{2,1,0:T(8,128)(2,1)S(1)}, bf16[6,80,2048]{2,1,0:T(8,128)(2,1)S(1)}) custom-call(f32[16,80,80]{2,1,0:T(8,128)} %transforms.1, bf16[16,80,2048]{2,1,0:T(8,128)(2,1)} %ensembles.3, bf16[16,80,2048]{2,1,0:T(8,128)(2,1)} %cotangents.3), custom_call_target="tpu_custom_call" | custom-call | flops 3500000000 | bytes 10500000 | tf_op jit(solution)/shard_map/transform_chain/pallas_call | solution.py:392
  3.4 3.0 %collective-permute-start = (f32[80,80]{1,0:T(8,128)S(1)}, f32[80,80]{1,0:T(8,128)S(1)}, u32[]{:S(2)}, u32[]{:S(2)}) collective-permute-start(f32[80,80]{1,0:T(8,128)S(1)} %get-tuple-element.35.total), channel_id=1, source_target_pairs={{0,4},{4,0},{8,12},{12,8},{16,20},{20,16},{24,28},{28,24},{1,5},{5... | collective-permute-start | bytes 76808 | tf_op jit(solution)/shard_map/ppermute | solution.py:377
  6.4 4.3 %gram.1 = (f32[40,1408]{1,0:T(8,128)S(1)}, f32[40,1408]{1,0:T(8,128)S(1)}, f32[80,80]{1,0:T(8,128)S(1)}, bf16[10,80,2048]{2,1,0:T(8,128)(2,1)S(1)}, bf16[10,80,2048]{2,1,0:T(8,128)(2,1)S(1)}) custom-call(bf16[16,80,2048]{2,1,0:T(8,128)(2,1)} %ensembles.3, bf16[16,80,2048]{2,1,0:T(8,128)(2,1)} %cotangents.3, f32[1280,80]{1,0:T(8,128)S(1)} %get-tuple-element.34.suffixes, ...), custom_call_target="tpu_custom_call" | custom-call | flops 4499999744 | bytes 13500000 | tf_op jit(solution)/shard_map/gram/pallas_call | solution.py:416
  10.7 0.1 collective-permute-start.3
  10.8 0.1 collective-permute-start.2
  10.9 0.0 collective-permute-done.other
  10.9 0.2 join_0.1
  11.2 2.1 %collective-permute-start.1 = (f32[80,80]{1,0:T(8,128)S(1)}, f32[80,80]{1,0:T(8,128)S(1)}, u32[]{:S(2)}, u32[]{:S(2)}) collective-permute-start(f32[80,80]{1,0:T(8,128)S(1)} %get-tuple-element.39._.total), channel_id=1, source_target_pairs={{0,8},{4,12},{8,0},{12,4},{16,24},{20,28},{24,16},{28,20},{1,9},{5... | collective-permute-start | bytes 76808 | tf_op jit(solution)/shard_map/ppermute | solution.py:377
  13.3 0.0 collective-permute-done.3.right
  13.3 1.6 %collective-permute-start.7 = (f32[40,1408]{1,0:T(8,128)S(1)}, f32[40,1408]{1,0:T(8,128)S(1)}, u32[]{:S(2)}, u32[]{:S(2)}) collective-permute-start(f32[40,1408]{1,0:T(8,128)S(1)} %chip_gram.1._), channel_id=1, source_target_pairs={{0,2},{1,3},{2,0},{3,1},{4,6},{5,7},{6,4},{7,5},{8,10},{9,11},{10,... | collective-permute-start | bytes 675848 | tf_op jit(solution)/shard_map/ppermute | solution.py:381
  14.9 0.0 collective-permute-done.2.other
  14.9 0.2 pass_0.1
  15.1 1.6 %collective-permute-start.5 = (f32[80,80]{1,0:T(8,128)S(1)}, f32[80,80]{1,0:T(8,128)S(1)}, u32[]{:S(2)}, u32[]{:S(2)}) collective-permute-start(f32[80,80]{1,0:T(8,128)S(1)} %get-tuple-element.45._.own), channel_id=1, source_target_pairs={{0,8},{4,12},{8,0},{12,4},{16,24},{20,28},{24,16},{28,20},{1,9},{5... | collective-permute-start | bytes 76808 | tf_op jit(solution)/shard_map/ppermute | solution.py:377
  16.7 0.0 collective-permute-done.1.other
  16.7 0.3 join_1.1
  17.0 2.6 %collective-permute-start.4 = (f32[56,128]{1,0:T(8,128)S(1)}, f32[56,128]{1,0:T(8,128)S(1)}, u32[]{:S(2)}, u32[]{:S(2)}) collective-permute-start(f32[56,128]{1,0:T(8,128)S(1)} %get-tuple-element.47._), channel_id=1, source_target_pairs={{0,16},{4,20},{8,24},{12,28},{16,0},{20,4},{24,8},{28,12},{1,17},{... | collective-permute-start | bytes 86024 | tf_op jit(solution)/shard_map/ppermute | solution.py:377
  19.6 0.0 collective-permute-done.5.other
  19.6 0.3 pass_1.1
  19.9 2.2 %collective-permute-start.6 = (f32[56,128]{1,0:T(8,128)S(1)}, f32[56,128]{1,0:T(8,128)S(1)}, u32[]{:S(2)}, u32[]{:S(2)}) collective-permute-start(f32[56,128]{1,0:T(8,128)S(1)} %get-tuple-element.50._), channel_id=1, source_target_pairs={{0,16},{4,20},{8,24},{12,28},{16,0},{20,4},{24,8},{28,12},{1,17},{... | collective-permute-start | bytes 86024 | tf_op jit(solution)/shard_map/ppermute | solution.py:377
  22.1 0.0 collective-permute-done.4.other
  22.1 1.1 %carries.1 = (bf16[6,240,240]{2,1,0:T(8,128)(2,1)S(1)}, bf16[6,240,240]{2,1,0:T(8,128)(2,1)S(1)}, bf16[2,1280,80]{2,1,0:T(8,128)(2,1)S(1)}) custom-call(f32[1280,80]{1,0:T(8,128)S(1)} %get-tuple-element.34.suffixes, f32[80,80]{1,0:T(8,128)S(1)} %get-tuple-element.46.later, f32[56,128]{1,0:T(8,128)S(1)} %collective-permute-done.4.other, ...), custom_call_target="tpu_custom_call" | custom-call | flops 900000000 | bytes 2700000 | tf_op jit(solution)/shard_map/carries/pallas_call | solution.py:449
  23.2 2.7 %smoothed.1 = (bf16[16,80,2048]{2,1,0:T(8,128)(2,1)}, f32[8,128]{1,0:T(8,128)S(1)}) custom-call(bf16[6,240,240]{2,1,0:T(8,128)(2,1)S(1)} %get-tuple-element.51.factors, bf16[6,80,2048]{2,1,0:T(8,128)(2,1)S(1)} %get-tuple-element.36.ens.refs_0_, bf16[10,80,2048]{2,1,0:T(8,128)(2,1)S(1)} %get-tuple-element.52.refs_1_, ...), custom_call_target="tpu_custom_call" | custom-call | flops 500000000 | bytes 1500000 | tf_op jit(solution)/shard_map/smoothed/pallas_call | solution.py:456
  25.9 0.0 collective-permute-done.6.other
  25.9 0.0 collective-permute-done.7.__
  25.9 0.2 pass_last.1
  26.2 0.1 collective-permute-start.9
  26.2 0.5 %collective-permute-start.8 = (f32[80,80]{1,0:T(8,128)S(1)}, f32[80,80]{1,0:T(8,128)S(1)}, u32[]{:S(2)}, u32[]{:S(2)}) collective-permute-start(f32[80,80]{1,0:T(8,128)S(1)} %get-tuple-element.60._.left), channel_id=1, source_target_pairs={{0,1},{1,0},{2,3},{3,2},{4,5},{5,4},{6,7},{7,6},{8,9},{9,8},{10,11... | collective-permute-start | bytes 76808 | tf_op jit(solution)/shard_map/ppermute | solution.py:377
  26.7 0.9 %windows.1._.steps = bf16[2,2560,80]{2,1,0:T(8,128)(2,1)S(1)} custom-call(f32[16,80,80]{2,1,0:T(8,128)S(1)} %get-tuple-element.61.kept, f32[80,80]{1,0:T(8,128)S(1)} %get-tuple-element.60._.left), custom_call_target="tpu_custom_call" | custom-call | flops 1000000000 | bytes 3000000 | tf_op jit(solution)/shard_map/windows/pallas_call | solution.py:474
  27.6 0.2 collective-permute-done.8.right
  27.8 1.6 %collective-permute-start.10 = (f32[80,80]{1,0:T(8,128)S(1)}, f32[80,80]{1,0:T(8,128)S(1)}, u32[]{:S(2)}, u32[]{:S(2)}) collective-permute-start(f32[80,80]{1,0:T(8,128)S(1)} %chip_carry.1.refs_2_.refs_0_), channel_id=1, source_target_pairs={{0,2},{1,3},{2,0},{3,1},{4,6},{5,7},{6,4},{7,5},{8,10},{9,11},{10,... | collective-permute-start | bytes 76808 | tf_op jit(solution)/shard_map/ppermute | solution.py:381
  29.4 2.7 %ensemble_grad.1 = (bf16[16,80,2048]{2,1,0:T(8,128)(2,1)}, f32[8,128]{1,0:T(8,128)S(1)}) custom-call(bf16[6,240,240]{2,1,0:T(8,128)(2,1)S(1)} %get-tuple-element.55.factors, bf16[6,80,2048]{2,1,0:T(8,128)(2,1)S(1)} %get-tuple-element.37.cot.refs_0_, bf16[10,80,2048]{2,1,0:T(8,128)(2,1)S(1)} %get-tuple-element.56.refs_1_, f32[80,80]{1,0:T(8,128)S(1)} %chip_carry.1.refs_2_.refs_0_), custom_call_target="tpu_custom_call" | custom-call | flops 500000000 | bytes 1500000 | tf_op jit(solution)/shard_map/ensemble_grad/pallas_call | solution.py:456
  32.1 0.0 collective-permute-done.10.refs_1_
  32.1 0.0 collective-permute-done.9.gram_core
  32.1 2.2 %transform_grad.1 = f32[16,80,80]{2,1,0:T(8,128)} custom-call(f32[40,1408]{1,0:T(8,128)S(1)} %add.3.gram, f32[40,1408]{1,0:T(8,128)S(1)} %collective-permute-done.9.gram_core, bf16[2,1280,80]{2,1,0:T(8,128)(2,1)S(1)} %get-tuple-element.53.refs_2_.follow, bf16[2,2560,80]{2,1,0:T(8,128)(2,1)S(1)} %windows.1._.steps, f32[8,128]{1,0:T(8,128)S(1)} %get-tuple-element.64._, ...), custom_call_target="tpu_custom_call" | custom-call | flops 2500000000 | bytes 7500000 | tf_op jit(solution)/shard_map/transform_grad/pallas_call | solution.py:484
  (5 shorter events, 0.1 us)
Async XLA Ops:
  3.4 7.5 %collective-permute-start = (f32[80,80]{1,0:T(8,128)S(1)}, f32[80,80]{1,0:T(8,128)S(1)}, u32[]{:S(2)}, u32[]{:S(2)}) collective-permute-start(f32[80,80]{1,0:T(8,128)S(1)} %get-tuple-element.35.total), channel_id=1, source_target_pairs={{0,4},{4,0},{8,12},{12,8},{16,20},{20,16},{24,28},{28,24},{1,5},{5... | collective-permute-start | bytes 76808 | tf_op jit(solution)/shard_map/ppermute | solution.py:377
  10.7 2.6 %collective-permute-start.3 = (f32[40,1408]{1,0:T(8,128)S(1)}, f32[40,1408]{1,0:T(8,128)S(1)}, u32[]{:S(2)}, u32[]{:S(2)}) collective-permute-start(f32[40,1408]{1,0:T(8,128)S(1)} %get-tuple-element.44), channel_id=1, source_target_pairs={{0,1},{1,0},{2,3},{3,2},{4,5},{5,4},{6,7},{7,6},{8,9},{9,8},{10,11... | collective-permute-start | bytes 675848 | tf_op jit(solution)/shard_map/ppermute | solution.py:377
  10.8 4.1 %collective-permute-start.2 = (f32[80,80]{1,0:T(8,128)S(1)}, f32[80,80]{1,0:T(8,128)S(1)}, u32[]{:S(2)}, u32[]{:S(2)}) collective-permute-start(f32[80,80]{1,0:T(8,128)S(1)} %get-tuple-element.38._.own), channel_id=1, source_target_pairs={{0,4},{4,0},{8,12},{12,8},{16,20},{20,16},{24,28},{28,24},{1,5},{5... | collective-permute-start | bytes 76808 | tf_op jit(solution)/shard_map/ppermute | solution.py:377
  11.2 5.6 %collective-permute-start.1 = (f32[80,80]{1,0:T(8,128)S(1)}, f32[80,80]{1,0:T(8,128)S(1)}, u32[]{:S(2)}, u32[]{:S(2)}) collective-permute-start(f32[80,80]{1,0:T(8,128)S(1)} %get-tuple-element.39._.total), channel_id=1, source_target_pairs={{0,8},{4,12},{8,0},{12,4},{16,24},{20,28},{24,16},{28,20},{1,9},{5... | collective-permute-start | bytes 76808 | tf_op jit(solution)/shard_map/ppermute | solution.py:377
  13.3 12.6 %collective-permute-start.7 = (f32[40,1408]{1,0:T(8,128)S(1)}, f32[40,1408]{1,0:T(8,128)S(1)}, u32[]{:S(2)}, u32[]{:S(2)}) collective-permute-start(f32[40,1408]{1,0:T(8,128)S(1)} %chip_gram.1._), channel_id=1, source_target_pairs={{0,2},{1,3},{2,0},{3,1},{4,6},{5,7},{6,4},{7,5},{8,10},{9,11},{10,... | collective-permute-start | bytes 675848 | tf_op jit(solution)/shard_map/ppermute | solution.py:381
  15.1 4.5 %collective-permute-start.5 = (f32[80,80]{1,0:T(8,128)S(1)}, f32[80,80]{1,0:T(8,128)S(1)}, u32[]{:S(2)}, u32[]{:S(2)}) collective-permute-start(f32[80,80]{1,0:T(8,128)S(1)} %get-tuple-element.45._.own), channel_id=1, source_target_pairs={{0,8},{4,12},{8,0},{12,4},{16,24},{20,28},{24,16},{28,20},{1,9},{5... | collective-permute-start | bytes 76808 | tf_op jit(solution)/shard_map/ppermute | solution.py:377
  17.0 5.1 %collective-permute-start.4 = (f32[56,128]{1,0:T(8,128)S(1)}, f32[56,128]{1,0:T(8,128)S(1)}, u32[]{:S(2)}, u32[]{:S(2)}) collective-permute-start(f32[56,128]{1,0:T(8,128)S(1)} %get-tuple-element.47._), channel_id=1, source_target_pairs={{0,16},{4,20},{8,24},{12,28},{16,0},{20,4},{24,8},{28,12},{1,17},{... | collective-permute-start | bytes 86024 | tf_op jit(solution)/shard_map/ppermute | solution.py:377
  19.9 6.0 %collective-permute-start.6 = (f32[56,128]{1,0:T(8,128)S(1)}, f32[56,128]{1,0:T(8,128)S(1)}, u32[]{:S(2)}, u32[]{:S(2)}) collective-permute-start(f32[56,128]{1,0:T(8,128)S(1)} %get-tuple-element.50._), channel_id=1, source_target_pairs={{0,16},{4,20},{8,24},{12,28},{16,0},{20,4},{24,8},{28,12},{1,17},{... | collective-permute-start | bytes 86024 | tf_op jit(solution)/shard_map/ppermute | solution.py:377
  26.2 5.9 %collective-permute-start.9 = (f32[40,1408]{1,0:T(8,128)S(1)}, f32[40,1408]{1,0:T(8,128)S(1)}, u32[]{:S(2)}, u32[]{:S(2)}) collective-permute-start(f32[40,1408]{1,0:T(8,128)S(1)} %add.3.gram), channel_id=1, source_target_pairs={{0,1},{1,0},{2,3},{3,2},{4,5},{5,4},{6,7},{7,6},{8,9},{9,8},{10,11... | collective-permute-start | bytes 675848 | tf_op jit(solution)/shard_map/ppermute | solution.py:377
  26.2 1.5 %collective-permute-start.8 = (f32[80,80]{1,0:T(8,128)S(1)}, f32[80,80]{1,0:T(8,128)S(1)}, u32[]{:S(2)}, u32[]{:S(2)}) collective-permute-start(f32[80,80]{1,0:T(8,128)S(1)} %get-tuple-element.60._.left), channel_id=1, source_target_pairs={{0,1},{1,0},{2,3},{3,2},{4,5},{5,4},{6,7},{7,6},{8,9},{9,8},{10,11... | collective-permute-start | bytes 76808 | tf_op jit(solution)/shard_map/ppermute | solution.py:377
  27.8 4.3 %collective-permute-start.10 = (f32[80,80]{1,0:T(8,128)S(1)}, f32[80,80]{1,0:T(8,128)S(1)}, u32[]{:S(2)}, u32[]{:S(2)}) collective-permute-start(f32[80,80]{1,0:T(8,128)S(1)} %chip_carry.1.refs_2_.refs_0_), channel_id=1, source_target_pairs={{0,2},{1,3},{2,0},{3,1},{4,6},{5,7},{6,4},{7,5},{8,10},{9,11},{10,... | collective-permute-start | bytes 76808 | tf_op jit(solution)/shard_map/ppermute | solution.py:381

commit v22 on v19

--- a/solution.py
+++ b/solution.py
@@ -134,11 +134,11 @@
     count, members = plan.count, plan.members
     read = pltpu.make_async_copy(transforms, kept, sem)
     read.start()
-    more = loads(plan, 0, ensembles, ens, ens_sem, slice(1))
-    more += loads(plan, 0, cotangents, cot, cot_sem, slice(1))
+    more = []
+    for at in range(len(plan.piece_groups[0])):
+        more += loads(plan, 0, ensembles, ens, ens_sem, slice(at, at + 1))
+        more += loads(plan, 0, cotangents, cot, cot_sem, slice(at, at + 1))
     read.wait()
-    more += loads(plan, 0, ensembles, ens, ens_sem, slice(1, None))
-    more += loads(plan, 0, cotangents, cot, cot_sem, slice(1, None))
     for at in range(count):
         suffixes[plan.rows(at, at + 1)] = kept[at]
     suffix_scan(suffixes, count, members, count)

time: 34.5 us -> 34.6 us (level)
  no operation moved by 1% of the time
where the time goes in v22:
time: 34.6 us; the launch traced here: 34.5 us
  Pallas kernels  18.1 us (52%)
  starting transfers between devices  15.4 us (45%)
  between operations  0.78 us (2%)
    ppermute x9, starting transfers between devices, exchange(): return lax.ppermute(value, axis, [(at, at ^ bit) for at in range(size)])  12.2 us
    pallas_call x2, Pallas kernels, apply(): call(functools.partial(apply_kernel, plan), [shape(count, members, cells,...  5.43 us
    pallas_call x1, Pallas kernels, shards(): call(functools.partial(gram_kernel, plan), [wide, wide, square] + [piece_...  4.32 us
    ppermute x2, starting transfers between devices, around(): lax.ppermute(value, 'space', [(at, (at + 2 * d) % lanes) for at in range(...  3.17 us
    pallas_call x1, Pallas kernels, shards(): call(functools.partial(chain_kernel, plan), [shape(count * members, membe...  2.9 us
    pallas_call x1, Pallas kernels, shards(): call(functools.partial(final_kernel, plan, scale), shape(count, members,...  2.21 us
    pallas_call x1, Pallas kernels, shards(): call(functools.partial(windows_kernel, plan), shape(2, count_steps(count)...  0.87 us
    pallas_call x1, Pallas kernels, shards(): call(functools.partial(carry_kernel, plan), [shape(len(plan.groups), size...  0.86 us
  transfers between devices with their start and end apart: 11, of which 1 were waited for; matrix products, arithmetic and copies ran while one was open for 0% of the time, Pallas kernels for 37%

profile of v22, /device:TPU:0, one launch (start us, length us, event | category | flops | bytes accessed | tf_op | source)
XLA Modules:
  0.0 34.5 jit_solution(4388810781591111512)
XLA Ops:
  0.6 2.9 %transform_chain.1 = (f32[1280,80]{1,0:T(8,128)S(1)}, f32[80,80]{1,0:T(8,128)S(1)}, f32[16,80,80]{2,1,0:T(8,128)S(1)}, bf16[6,80,2048]{2,1,0:T(8,128)(2,1)S(1)}, bf16[6,80,2048]{2,1,0:T(8,128)(2,1)S(1)}) custom-call(f32[16,80,80]{2,1,0:T(8,128)} %transforms.1, bf16[16,80,2048]{2,1,0:T(8,128)(2,1)} %ensembles.3, bf16[16,80,2048]{2,1,0:T(8,128)(2,1)} %cotangents.3), custom_call_target="tpu_custom_call" | custom-call | flops 3500000000 | bytes 10500000 | tf_op jit(solution)/shard_map/transform_chain/pallas_call | solution.py:396
  3.5 3.0 %collective-permute-start = (f32[80,80]{1,0:T(8,128)S(1)}, f32[80,80]{1,0:T(8,128)S(1)}, u32[]{:S(2)}, u32[]{:S(2)}) collective-permute-start(f32[80,80]{1,0:T(8,128)S(1)} %get-tuple-element.35.total), channel_id=1, source_target_pairs={{0,4},{4,0},{8,12},{12,8},{16,20},{20,16},{24,28},{28,24},{1,5},{5... | collective-permute-start | bytes 76808 | tf_op jit(solution)/shard_map/ppermute | solution.py:381
  6.5 4.3 %gram.1 = (f32[40,1408]{1,0:T(8,128)S(1)}, f32[40,1408]{1,0:T(8,128)S(1)}, f32[80,80]{1,0:T(8,128)S(1)}, bf16[10,80,2048]{2,1,0:T(8,128)(2,1)S(1)}, bf16[10,80,2048]{2,1,0:T(8,128)(2,1)S(1)}) custom-call(bf16[16,80,2048]{2,1,0:T(8,128)(2,1)} %ensembles.3, bf16[16,80,2048]{2,1,0:T(8,128)(2,1)} %cotangents.3, f32[1280,80]{1,0:T(8,128)S(1)} %get-tuple-element.34.suffixes, ...), custom_call_target="tpu_custom_call" | custom-call | flops 4499999744 | bytes 13500000 | tf_op jit(solution)/shard_map/gram/pallas_call | solution.py:420
  10.9 0.1 collective-permute-start.3
  10.9 0.1 collective-permute-start.2
  11.0 0.0 collective-permute-done.other
  11.0 0.2 join_0.1
  11.3 2.1 %collective-permute-start.1 = (f32[80,80]{1,0:T(8,128)S(1)}, f32[80,80]{1,0:T(8,128)S(1)}, u32[]{:S(2)}, u32[]{:S(2)}) collective-permute-start(f32[80,80]{1,0:T(8,128)S(1)} %get-tuple-element.39._.total), channel_id=1, source_target_pairs={{0,8},{4,12},{8,0},{12,4},{16,24},{20,28},{24,16},{28,20},{1,9},{5... | collective-permute-start | bytes 76808 | tf_op jit(solution)/shard_map/ppermute | solution.py:381
  13.4 0.0 collective-permute-done.3.right
  13.4 1.6 %collective-permute-start.7 = (f32[40,1408]{1,0:T(8,128)S(1)}, f32[40,1408]{1,0:T(8,128)S(1)}, u32[]{:S(2)}, u32[]{:S(2)}) collective-permute-start(f32[40,1408]{1,0:T(8,128)S(1)} %chip_gram.1._), channel_id=1, source_target_pairs={{0,2},{1,3},{2,0},{3,1},{4,6},{5,7},{6,4},{7,5},{8,10},{9,11},{10,... | collective-permute-start | bytes 675848 | tf_op jit(solution)/shard_map/ppermute | solution.py:385
  15.0 0.0 collective-permute-done.2.other
  15.0 0.2 pass_0.1
  15.2 1.6 %collective-permute-start.5 = (f32[80,80]{1,0:T(8,128)S(1)}, f32[80,80]{1,0:T(8,128)S(1)}, u32[]{:S(2)}, u32[]{:S(2)}) collective-permute-start(f32[80,80]{1,0:T(8,128)S(1)} %get-tuple-element.45._.own), channel_id=1, source_target_pairs={{0,8},{4,12},{8,0},{12,4},{16,24},{20,28},{24,16},{28,20},{1,9},{5... | collective-permute-start | bytes 76808 | tf_op jit(solution)/shard_map/ppermute | solution.py:381
  16.9 0.0 collective-permute-done.1.other
  16.9 0.3 join_1.1
  17.2 2.6 %collective-permute-start.4 = (f32[56,128]{1,0:T(8,128)S(1)}, f32[56,128]{1,0:T(8,128)S(1)}, u32[]{:S(2)}, u32[]{:S(2)}) collective-permute-start(f32[56,128]{1,0:T(8,128)S(1)} %get-tuple-element.47._), channel_id=1, source_target_pairs={{0,16},{4,20},{8,24},{12,28},{16,0},{20,4},{24,8},{28,12},{1,17},{... | collective-permute-start | bytes 86024 | tf_op jit(solution)/shard_map/ppermute | solution.py:381
  19.7 0.0 collective-permute-done.5.other
  19.7 0.3 pass_1.1
  20.0 2.2 %collective-permute-start.6 = (f32[56,128]{1,0:T(8,128)S(1)}, f32[56,128]{1,0:T(8,128)S(1)}, u32[]{:S(2)}, u32[]{:S(2)}) collective-permute-start(f32[56,128]{1,0:T(8,128)S(1)} %get-tuple-element.50._), channel_id=1, source_target_pairs={{0,16},{4,20},{8,24},{12,28},{16,0},{20,4},{24,8},{28,12},{1,17},{... | collective-permute-start | bytes 86024 | tf_op jit(solution)/shard_map/ppermute | solution.py:381
  22.2 0.0 collective-permute-done.4.other
  22.2 0.2 entering.1.later
  22.5 0.9 %carries.1 = (bf16[6,240,240]{2,1,0:T(8,128)(2,1)S(1)}, bf16[6,240,240]{2,1,0:T(8,128)(2,1)S(1)}, bf16[2,1280,80]{2,1,0:T(8,128)(2,1)S(1)}) custom-call(f32[1280,80]{1,0:T(8,128)S(1)} %get-tuple-element.34.suffixes, f32[80,80]{1,0:T(8,128)S(1)} %entering.1.later, f32[56,128]{1,0:T(8,128)S(1)} %get-tuple-element.50._), custom_call_target="tpu_custom_call" | custom-call | flops 900000000 | bytes 2700000 | tf_op jit(solution)/shard_map/carries/pallas_call | solution.py:457
  23.3 2.7 %smoothed.1 = (bf16[16,80,2048]{2,1,0:T(8,128)(2,1)}, f32[8,128]{1,0:T(8,128)S(1)}) custom-call(bf16[6,240,240]{2,1,0:T(8,128)(2,1)S(1)} %get-tuple-element.51.factors, bf16[6,80,2048]{2,1,0:T(8,128)(2,1)S(1)} %get-tuple-element.36.ens.refs_0_, bf16[10,80,2048]{2,1,0:T(8,128)(2,1)S(1)} %get-tuple-element.52.refs_1_, ...), custom_call_target="tpu_custom_call" | custom-call | flops 500000000 | bytes 1500000 | tf_op jit(solution)/shard_map/smoothed/pallas_call | solution.py:464
  26.1 0.0 collective-permute-done.6.other
  26.1 0.0 collective-permute-done.7.__
  26.1 0.2 pass_last.1
  26.3 0.1 collective-permute-start.9
  26.4 0.5 %collective-permute-start.8 = (f32[80,80]{1,0:T(8,128)S(1)}, f32[80,80]{1,0:T(8,128)S(1)}, u32[]{:S(2)}, u32[]{:S(2)}) collective-permute-start(f32[80,80]{1,0:T(8,128)S(1)} %get-tuple-element.60._.left), channel_id=1, source_target_pairs={{0,1},{1,0},{2,3},{3,2},{4,5},{5,4},{6,7},{7,6},{8,9},{9,8},{10,11... | collective-permute-start | bytes 76808 | tf_op jit(solution)/shard_map/ppermute | solution.py:381
  26.9 0.9 %windows.1._.steps = bf16[2,2560,80]{2,1,0:T(8,128)(2,1)S(1)} custom-call(f32[16,80,80]{2,1,0:T(8,128)S(1)} %get-tuple-element.61.kept, f32[80,80]{1,0:T(8,128)S(1)} %get-tuple-element.60._.left), custom_call_target="tpu_custom_call" | custom-call | flops 1000000000 | bytes 3000000 | tf_op jit(solution)/shard_map/windows/pallas_call | solution.py:482
  27.8 0.2 collective-permute-done.8.right
  27.9 1.6 %collective-permute-start.10 = (f32[80,80]{1,0:T(8,128)S(1)}, f32[80,80]{1,0:T(8,128)S(1)}, u32[]{:S(2)}, u32[]{:S(2)}) collective-permute-start(f32[80,80]{1,0:T(8,128)S(1)} %chip_carry.1.refs_2_.refs_0_), channel_id=1, source_target_pairs={{0,2},{1,3},{2,0},{3,1},{4,6},{5,7},{6,4},{7,5},{8,10},{9,11},{10,... | collective-permute-start | bytes 76808 | tf_op jit(solution)/shard_map/ppermute | solution.py:385
  29.5 2.7 %ensemble_grad.1 = (bf16[16,80,2048]{2,1,0:T(8,128)(2,1)}, f32[8,128]{1,0:T(8,128)S(1)}) custom-call(bf16[6,240,240]{2,1,0:T(8,128)(2,1)S(1)} %get-tuple-element.55.factors, bf16[6,80,2048]{2,1,0:T(8,128)(2,1)S(1)} %get-tuple-element.37.cot.refs_0_, bf16[10,80,2048]{2,1,0:T(8,128)(2,1)S(1)} %get-tuple-element.56.refs_1_, f32[80,80]{1,0:T(8,128)S(1)} %chip_carry.1.refs_2_.refs_0_), custom_call_target="tpu_custom_call" | custom-call | flops 500000000 | bytes 1500000 | tf_op jit(solution)/shard_map/ensemble_grad/pallas_call | solution.py:464
  32.2 0.0 collective-permute-done.10.refs_1_
  32.3 0.0 collective-permute-done.9.gram_core
  32.3 2.2 %transform_grad.1 = f32[16,80,80]{2,1,0:T(8,128)} custom-call(f32[40,1408]{1,0:T(8,128)S(1)} %add.3.gram, f32[40,1408]{1,0:T(8,128)S(1)} %collective-permute-done.9.gram_core, bf16[2,1280,80]{2,1,0:T(8,128)(2,1)S(1)} %get-tuple-element.53.refs_2_.follow, bf16[2,2560,80]{2,1,0:T(8,128)(2,1)S(1)} %windows.1._.steps, f32[8,128]{1,0:T(8,128)S(1)} %get-tuple-element.64._, ...), custom_call_target="tpu_custom_call" | custom-call | flops 2500000000 | bytes 7500000 | tf_op jit(solution)/shard_map/transform_grad/pallas_call | solution.py:492
  (5 shorter events, 0.1 us)
Async XLA Ops:
  3.5 7.5 %collective-permute-start = (f32[80,80]{1,0:T(8,128)S(1)}, f32[80,80]{1,0:T(8,128)S(1)}, u32[]{:S(2)}, u32[]{:S(2)}) collective-permute-start(f32[80,80]{1,0:T(8,128)S(1)} %get-tuple-element.35.total), channel_id=1, source_target_pairs={{0,4},{4,0},{8,12},{12,8},{16,20},{20,16},{24,28},{28,24},{1,5},{5... | collective-permute-start | bytes 76808 | tf_op jit(solution)/shard_map/ppermute | solution.py:381
  10.9 2.6 %collective-permute-start.3 = (f32[40,1408]{1,0:T(8,128)S(1)}, f32[40,1408]{1,0:T(8,128)S(1)}, u32[]{:S(2)}, u32[]{:S(2)}) collective-permute-start(f32[40,1408]{1,0:T(8,128)S(1)} %get-tuple-element.44), channel_id=1, source_target_pairs={{0,1},{1,0},{2,3},{3,2},{4,5},{5,4},{6,7},{7,6},{8,9},{9,8},{10,11... | collective-permute-start | bytes 675848 | tf_op jit(solution)/shard_map/ppermute | solution.py:381
  10.9 4.1 %collective-permute-start.2 = (f32[80,80]{1,0:T(8,128)S(1)}, f32[80,80]{1,0:T(8,128)S(1)}, u32[]{:S(2)}, u32[]{:S(2)}) collective-permute-start(f32[80,80]{1,0:T(8,128)S(1)} %get-tuple-element.38._.own), channel_id=1, source_target_pairs={{0,4},{4,0},{8,12},{12,8},{16,20},{20,16},{24,28},{28,24},{1,5},{5... | collective-permute-start | bytes 76808 | tf_op jit(solution)/shard_map/ppermute | solution.py:381
  11.3 5.6 %collective-permute-start.1 = (f32[80,80]{1,0:T(8,128)S(1)}, f32[80,80]{1,0:T(8,128)S(1)}, u32[]{:S(2)}, u32[]{:S(2)}) collective-permute-start(f32[80,80]{1,0:T(8,128)S(1)} %get-tuple-element.39._.total), channel_id=1, source_target_pairs={{0,8},{4,12},{8,0},{12,4},{16,24},{20,28},{24,16},{28,20},{1,9},{5... | collective-permute-start | bytes 76808 | tf_op jit(solution)/shard_map/ppermute | solution.py:381
  13.4 12.6 %collective-permute-start.7 = (f32[40,1408]{1,0:T(8,128)S(1)}, f32[40,1408]{1,0:T(8,128)S(1)}, u32[]{:S(2)}, u32[]{:S(2)}) collective-permute-start(f32[40,1408]{1,0:T(8,128)S(1)} %chip_gram.1._), channel_id=1, source_target_pairs={{0,2},{1,3},{2,0},{3,1},{4,6},{5,7},{6,4},{7,5},{8,10},{9,11},{10,... | collective-permute-start | bytes 675848 | tf_op jit(solution)/shard_map/ppermute | solution.py:385
  15.2 4.5 %collective-permute-start.5 = (f32[80,80]{1,0:T(8,128)S(1)}, f32[80,80]{1,0:T(8,128)S(1)}, u32[]{:S(2)}, u32[]{:S(2)}) collective-permute-start(f32[80,80]{1,0:T(8,128)S(1)} %get-tuple-element.45._.own), channel_id=1, source_target_pairs={{0,8},{4,12},{8,0},{12,4},{16,24},{20,28},{24,16},{28,20},{1,9},{5... | collective-permute-start | bytes 76808 | tf_op jit(solution)/shard_map/ppermute | solution.py:381
  17.2 5.1 %collective-permute-start.4 = (f32[56,128]{1,0:T(8,128)S(1)}, f32[56,128]{1,0:T(8,128)S(1)}, u32[]{:S(2)}, u32[]{:S(2)}) collective-permute-start(f32[56,128]{1,0:T(8,128)S(1)} %get-tuple-element.47._), channel_id=1, source_target_pairs={{0,16},{4,20},{8,24},{12,28},{16,0},{20,4},{24,8},{28,12},{1,17},{... | collective-permute-start | bytes 86024 | tf_op jit(solution)/shard_map/ppermute | solution.py:381
  20.0 6.0 %collective-permute-start.6 = (f32[56,128]{1,0:T(8,128)S(1)}, f32[56,128]{1,0:T(8,128)S(1)}, u32[]{:S(2)}, u32[]{:S(2)}) collective-permute-start(f32[56,128]{1,0:T(8,128)S(1)} %get-tuple-element.50._), channel_id=1, source_target_pairs={{0,16},{4,20},{8,24},{12,28},{16,0},{20,4},{24,8},{28,12},{1,17},{... | collective-permute-start | bytes 86024 | tf_op jit(solution)/shard_map/ppermute | solution.py:381
  26.3 5.9 %collective-permute-start.9 = (f32[40,1408]{1,0:T(8,128)S(1)}, f32[40,1408]{1,0:T(8,128)S(1)}, u32[]{:S(2)}, u32[]{:S(2)}) collective-permute-start(f32[40,1408]{1,0:T(8,128)S(1)} %add.3.gram), channel_id=1, source_target_pairs={{0,1},{1,0},{2,3},{3,2},{4,5},{5,4},{6,7},{7,6},{8,9},{9,8},{10,11... | collective-permute-start | bytes 675848 | tf_op jit(solution)/shard_map/ppermute | solution.py:381
  26.4 1.5 %collective-permute-start.8 = (f32[80,80]{1,0:T(8,128)S(1)}, f32[80,80]{1,0:T(8,128)S(1)}, u32[]{:S(2)}, u32[]{:S(2)}) collective-permute-start(f32[80,80]{1,0:T(8,128)S(1)} %get-tuple-element.60._.left), channel_id=1, source_target_pairs={{0,1},{1,0},{2,3},{3,2},{4,5},{5,4},{6,7},{7,6},{8,9},{9,8},{10,11... | collective-permute-start | bytes 76808 | tf_op jit(solution)/shard_map/ppermute | solution.py:381
  27.9 4.3 %collective-permute-start.10 = (f32[80,80]{1,0:T(8,128)S(1)}, f32[80,80]{1,0:T(8,128)S(1)}, u32[]{:S(2)}, u32[]{:S(2)}) collective-permute-start(f32[80,80]{1,0:T(8,128)S(1)} %chip_carry.1.refs_2_.refs_0_), channel_id=1, source_target_pairs={{0,2},{1,3},{2,0},{3,1},{4,6},{5,7},{6,4},{7,5},{8,10},{9,11},{10,... | collective-permute-start | bytes 76808 | tf_op jit(solution)/shard_map/ppermute | solution.py:385
